TPU v7x, 32 devices: a whole 2x2x4 slice. The times are simulated.
32 devices in a mesh: parts: 2 (over y), layer: 4 (over x, core), node: 4 (over z).
Axes of the slice: x: 2, y: 2, z: 4, core: 2. Of those that a mesh axis runs over, the one named last changes fastest.
Arguments:
- blocks: bfloat16 [16, 2048, 4096], P(('parts', 'layer'), 'node'), parts along dimension 0, may hold values from -6 to 6
- block_rows: int32 [16, 2048], P(('parts', 'layer'), 'node'), parts along dimension 0, may hold values from 0 to 7, as said below
- block_cols: int32 [16, 2048], P(('parts', 'layer'), 'node'), parts along dimension 0, may hold values from 0 to 31
- counts: int32 [16, 4], P(('parts', 'layer'), 'node'), parts along dimension 0, may hold values from 256 to 512, as said below
- start: float32 [16, 32, 2048], P(('parts', 'layer'), None, 'node'), parts along dimension 0, may hold values from -6 to 6
Outputs:
- joint_basis: float32 [16, 32, 2048], P(('parts', 'layer'), None, 'node'), parts along dimension 0
- scores: float32 [16, 32, 32], P(('parts', 'layer')), parts along dimension 0
There are 2 independent parts, one for each index of `parts`. A program takes and returns all parts, laid end to end along the dimension named above; each array names one. Nothing has to cross between parts.
Inputs may be any that keep to these rules, and one draw needn't show every extreme that they name: `block_rows`: each device's 512 slots of one layer name each of its 8 block rows exactly 64 times. `counts`: in every layer one device has all 512 slots live and another exactly half of them.
All inputs are finite; a program needn't handle non-finite values.
Results may differ from a plain program's by a relative error of at most 0.0014.
The roundings to bfloat16 on the way count: a program that leaves them out, or rounds other values in their place, can miss the bound.
Values may be sent and summed in bfloat16 or wider, within the bound.
No kernel may reach another device: no remote copies, remote signals or barrier semaphores. Data moves between devices by JAX's collectives and lax.ppermute only.
A program may use at most 128 MiB of HBM per device.

v0:
```python
import jax
import jax.numpy as jnp
from jax import lax
from jax.sharding import PartitionSpec as P

BLK = 64
ITERS = 2
ROWS_DEV = 512


def apply_one(values, rows_l, cols_l, live_count, gathered_l):
    slot_count = values.shape[0]
    width = gathered_l.shape[0]
    column_table = gathered_l.reshape(width, gathered_l.shape[1] // BLK, BLK)
    picked = jnp.take(column_table, cols_l, axis=1)
    products = jnp.einsum(
        "ksj,sij->ski",
        picked,
        values.reshape(slot_count, BLK, BLK),
        preferred_element_type=jnp.float32,
    )
    live_mask = jnp.arange(slot_count, dtype=jnp.int32) < live_count
    block_total = ROWS_DEV // BLK
    onehot = (
        (rows_l[:, None] == jnp.arange(block_total, dtype=jnp.int32)[None, :]) & live_mask[:, None]
    ).astype(jnp.float32)
    result = jnp.einsum("ski,sb->kbi", products, onehot, precision=lax.Precision.HIGHEST)
    return result.reshape(width, ROWS_DEV)


def solve_lower(gram_matrix, matrix):
    lower_factor = jnp.linalg.cholesky(gram_matrix)
    return lax.linalg.triangular_solve(lower_factor, matrix, left_side=True, lower=True)


def per_device(blocks, block_rows, block_cols, counts, start):
    group_layers = start.shape[0]

    def apply_all(basis):
        gathered = lax.all_gather(basis.astype(jnp.bfloat16), "node", axis=2, tiled=True)
        results = []
        for layer_idx in range(group_layers):
            results.append(
                apply_one(
                    blocks[layer_idx],
                    block_rows[layer_idx],
                    block_cols[layer_idx],
                    counts[layer_idx, 0],
                    gathered[layer_idx],
                )
            )
        return jnp.stack(results)

    current = start
    for step_idx in range(ITERS):
        orthonormal_image = apply_all(current)
        orthonormal_gram_local = jnp.einsum(
            "lki,lmi->lkm", orthonormal_image, orthonormal_image, precision=lax.Precision.HIGHEST
        )
        orthonormal_gram_total = lax.psum(orthonormal_gram_local, "node")
        solved = []
        for orthonormal_layer_idx in range(group_layers):
            solved.append(
                solve_lower(
                    orthonormal_gram_total[orthonormal_layer_idx],
                    orthonormal_image[orthonormal_layer_idx],
                )
            )
        current = jnp.stack(solved)
    collected = lax.all_gather(current, "layer", axis=0, tiled=True)
    flattened = collected.reshape(-1, collected.shape[2])
    gram_local = jnp.dot(flattened, flattened.T, precision=lax.Precision.HIGHEST)
    gram_total = lax.psum(gram_local, "node")
    joint_full = solve_lower(gram_total, flattened).reshape(collected.shape)
    joint_basis = lax.dynamic_slice_in_dim(
        joint_full, lax.axis_index("layer") * group_layers, group_layers, 0
    )
    image = apply_all(joint_basis)
    partial_scores = jnp.einsum("lki,lmi->lkm", joint_basis, image, precision=lax.Precision.HIGHEST)
    scores = lax.psum(partial_scores, "node")
    return (joint_basis, scores)


def solution(mesh):
    in_specs = (
        P(("parts", "layer"), "node", None),
        P(("parts", "layer"), "node"),
        P(("parts", "layer"), "node"),
        P(("parts", "layer"), "node"),
        P(("parts", "layer"), None, "node"),
    )
    out_specs = (P(("parts", "layer"), None, "node"), P(("parts", "layer"), None, None))
    return jax.shard_map(
        per_device, mesh=mesh, in_specs=in_specs, out_specs=out_specs, check_vma=False
    )
```

profile of v0, /device:TPU:0, one launch (start us, length us, event | category | flops | bytes accessed | tf_op | source)
XLA Modules:
  0.0 457.0 jit_solution(18435084481801582235)
XLA Ops:
  20.5 13.0 %copy.63 = bf16[512,64,64]{2,1,0:T(8,128)(2,1)} copy(bf16[512,64,64]{0,2,1:T(8,128)(2,1)} %bitcast.153) | data formatting | bytes 8388608 | tf_op jit(solution)/shard_map/reshape;squeeze | solution.py:19
  33.5 15.6 %all_gather.12 = bf16[2,32,2048]{2,1,0:T(8,128)(2,1)S(1)} all-gather(bf16[2,32,512]{2,1,0:T(8,128)(2,1)S(1)} %convert_element_type.4), channel_id=1, replica_groups=mesh['parts'=2,'layer'=4,'node'=4] {'node'}, dimensions={2}, use_global_device_ids=true | all-gather | bytes 327680 | tf_op jit(solution)/shard_map/all_gather | solution.py:40
  54.5 12.4 %fusion.20 = f32[512,32,64]{2,1,0:T(8,128)} fusion(bf16[512,64,64]{2,1,0:T(8,128)(2,1)} %copy.63, bf16[512,32,64]{2,1,0:T(8,128)(2,1)} %gather_fusion.1, pred[512]{0:T(512)(128)(4,1)S(1)} %compare_and_fusion.1), kind=kOutput, calls=%fused_computation.28 | convolution fusion | flops 135266304 | bytes 10486272 | tf_op jit(solution)/shard_map/ksj,sij->ski/dot_general | solution.py:16
  66.8 10.4 %fusion.45 = f32[32,8,64]{2,1,0:T(8,128)S(1)} fusion(f32[512,32,64]{2,1,0:T(8,128)} %fusion.20, s32[512]{0:T(512)S(1)} %bitcast.162, pred[512]{0:T(512)(128)(4,1)S(1)} %iota_compare_fusion.7), kind=kOutput, calls=%fused_computation.52 | convolution fusion | flops 100671488 | bytes 4262400 | tf_op jit(solution)/shard_map/ski,sb->kbi/dot_general | solution.py:27
  84.3 12.9 %copy.59 = bf16[512,64,64]{2,1,0:T(8,128)(2,1)} copy(bf16[512,64,64]{0,2,1:T(8,128)(2,1)} %bitcast.154) | data formatting | bytes 8388608 | tf_op jit(solution)/shard_map/reshape;squeeze | solution.py:19
  101.8 12.4 %fusion.22 = f32[512,32,64]{2,1,0:T(8,128)} fusion(bf16[512,64,64]{2,1,0:T(8,128)(2,1)} %copy.59, bf16[512,32,64]{2,1,0:T(8,128)(2,1)} %gather_fusion, pred[512]{0:T(512)(128)(4,1)S(1)} %compare_and_fusion), kind=kOutput, calls=%fused_computation.30 | convolution fusion | flops 135266304 | bytes 10486272 | tf_op jit(solution)/shard_map/ksj,sij->ski/dot_general | solution.py:16
  114.2 10.4 %fusion.42 = f32[32,8,64]{2,1,0:T(8,128)S(1)} fusion(f32[512,32,64]{2,1,0:T(8,128)} %fusion.22, s32[512]{0:T(512)S(1)} %bitcast.159, pred[512]{0:T(512)(128)(4,1)S(1)} %iota_compare_fusion.8), kind=kOutput, calls=%fused_computation.51 | convolution fusion | flops 100671488 | bytes 4262400 | tf_op jit(solution)/shard_map/ski,sb->kbi/dot_general | solution.py:27
  125.0 19.8 %psum.28 = f32[2,32,32]{1,2,0:T(8,128)S(1)} all-reduce(f32[2,32,32]{1,2,0:T(8,128)S(1)} %fusion.63), channel_id=1, replica_groups=mesh['parts'=2,'layer'=4,'node'=4] {'node'}, use_global_device_ids=true, to_apply=%region_0.0 | all-reduce | flops 2048 | bytes 16384 | tf_op jit(solution)/shard_map/psum | solution.py:60
  159.0 13.8 %all_gather.13 = bf16[2,32,2048]{2,1,0:T(8,128)(2,1)S(1)} all-gather(bf16[2,32,512]{2,1,0:T(8,128)(2,1)S(1)} %pad_maximum_fusion.2), channel_id=1, replica_groups=mesh['parts'=2,'layer'=4,'node'=4] {'node'}, dimensions={2}, use_global_device_ids=true | all-gather | bytes 327680 | tf_op jit(solution)/shard_map/all_gather | solution.py:40
  176.7 12.4 %fusion.16 = f32[512,32,64]{2,1,0:T(8,128)} fusion(bf16[512,64,64]{2,1,0:T(8,128)(2,1)} %copy.63, bf16[512,32,64]{2,1,0:T(8,128)(2,1)} %gather_fusion.3, pred[512]{0:T(512)(128)(4,1)S(1)} %compare_and_fusion.1), kind=kOutput, calls=%fused_computation.24 | convolution fusion | flops 135266304 | bytes 10486272 | tf_op jit(solution)/shard_map/ksj,sij->ski/dot_general | solution.py:16
  189.0 10.4 %fusion.51 = f32[32,8,64]{2,1,0:T(8,128)S(1)} fusion(f32[512,32,64]{2,1,0:T(8,128)} %fusion.16, s32[512]{0:T(512)S(1)} %bitcast.163, pred[512]{0:T(512)(128)(4,1)S(1)} %iota_compare_fusion.7), kind=kOutput, calls=%fused_computation.54 | convolution fusion | flops 100671488 | bytes 4262400 | tf_op jit(solution)/shard_map/ski,sb->kbi/dot_general | solution.py:27
  203.9 12.4 %fusion.18 = f32[512,32,64]{2,1,0:T(8,128)} fusion(bf16[512,64,64]{2,1,0:T(8,128)(2,1)} %copy.59, bf16[512,32,64]{2,1,0:T(8,128)(2,1)} %gather_fusion.2, pred[512]{0:T(512)(128)(4,1)S(1)} %compare_and_fusion), kind=kOutput, calls=%fused_computation.26 | convolution fusion | flops 135266304 | bytes 10486272 | tf_op jit(solution)/shard_map/ksj,sij->ski/dot_general | solution.py:16
  216.3 10.4 %fusion.48 = f32[32,8,64]{2,1,0:T(8,128)S(1)} fusion(f32[512,32,64]{2,1,0:T(8,128)} %fusion.18, s32[512]{0:T(512)S(1)} %bitcast.160, pred[512]{0:T(512)(128)(4,1)S(1)} %iota_compare_fusion.8), kind=kOutput, calls=%fused_computation.53 | convolution fusion | flops 100671488 | bytes 4262400 | tf_op jit(solution)/shard_map/ski,sb->kbi/dot_general | solution.py:27
  227.1 16.1 %psum.29 = f32[2,32,32]{1,2,0:T(8,128)S(1)} all-reduce(f32[2,32,32]{1,2,0:T(8,128)S(1)} %fusion.67), channel_id=1, replica_groups=mesh['parts'=2,'layer'=4,'node'=4] {'node'}, use_global_device_ids=true, to_apply=%region_3.0 | all-reduce | flops 2048 | bytes 16384 | tf_op jit(solution)/shard_map/psum | solution.py:60
  265.9 34.2 %all-reduce.3.cloned.1.call-done = f32[256,256]{0,1:T(8,128)} async-done(((f32[256,256]{0,1:T(8,128)}), f32[256,256]{0,1:T(8,128)}) %all-reduce.3.cloned.1.call-update) | async-done | bytes 262160 | tf_op jit(solution)/shard_map/psum | solution.py:73
  302.2 11.7 %cholesky.77 = f32[128,128]{1,0:T(8,128)S(1)} custom-call(f32[128,128]{1,0:T(8,128)S(1)} %cholesky.234), custom_call_target="Cholesky" | custom-call | tf_op jit(solution)/shard_map/jit(cholesky)/cholesky | solution.py:32
  324.2 11.7 %cholesky.132 = f32[128,128]{1,0:T(8,128)S(1)} custom-call(f32[128,128]{1,0:T(8,128)S(1)} %convolution_subtract_fusion.1), custom_call_target="Cholesky" | custom-call | tf_op jit(solution)/shard_map/jit(cholesky)/cholesky | solution.py:32
  342.2 19.7 %custom-call.20 = f32[2,128,128]{1,2,0:T(8,128)S(1)} custom-call(f32[2,128,128]{2,1,0:T(8,128)S(1)} %get-tuple-element.12), custom_call_target="InvertDiagBlocksLowerTriangular" | custom-call | tf_op jit(solution)/shard_map/triangular_solve | solution.py:33
  363.2 14.4 %all_gather.15 = bf16[2,32,2048]{2,1,0:T(8,128)(2,1)S(1)} all-gather(bf16[2,32,512]{2,1,0:T(8,128)(2,1)S(1)} %get-tuple-element.21), channel_id=1, replica_groups=mesh['parts'=2,'layer'=4,'node'=4] {'node'}, dimensions={2}, use_global_device_ids=true | all-gather | bytes 327680 | tf_op jit(solution)/shard_map/all_gather | solution.py:40
  381.4 12.4 %fusion.12 = f32[512,32,64]{2,1,0:T(8,128)} fusion(bf16[512,64,64]{2,1,0:T(8,128)(2,1)} %copy.63, bf16[512,32,64]{2,1,0:T(8,128)(2,1)} %gather_fusion.5, pred[512]{0:T(512)(128)(4,1)S(1)} %compare_and_fusion.1), kind=kOutput, calls=%fused_computation.20 | convolution fusion | flops 135266304 | bytes 10486272 | tf_op jit(solution)/shard_map/ksj,sij->ski/dot_general | solution.py:16
  393.8 10.4 %fusion.57 = f32[32,8,64]{2,1,0:T(8,128)S(1)} fusion(f32[512,32,64]{2,1,0:T(8,128)} %fusion.12, s32[512]{0:T(512)S(1)} %bitcast.164, pred[512]{0:T(512)(128)(4,1)S(1)} %iota_compare_fusion.7), kind=kOutput, calls=%fused_computation.56 | convolution fusion | flops 100671488 | bytes 4262400 | tf_op jit(solution)/shard_map/ski,sb->kbi/dot_general | solution.py:27
  408.3 12.4 %fusion.14 = f32[512,32,64]{2,1,0:T(8,128)} fusion(bf16[512,64,64]{2,1,0:T(8,128)(2,1)} %copy.59, bf16[512,32,64]{2,1,0:T(8,128)(2,1)} %gather_fusion.4, pred[512]{0:T(512)(128)(4,1)S(1)} %compare_and_fusion), kind=kOutput, calls=%fused_computation.22 | convolution fusion | flops 135266304 | bytes 10486272 | tf_op jit(solution)/shard_map/ksj,sij->ski/dot_general | solution.py:16
  420.7 10.4 %fusion.54 = f32[32,8,64]{2,1,0:T(8,128)S(1)} fusion(f32[512,32,64]{2,1,0:T(8,128)} %fusion.14, s32[512]{0:T(512)S(1)} %bitcast.161, pred[512]{0:T(512)(128)(4,1)S(1)} %iota_compare_fusion.8), kind=kOutput, calls=%fused_computation.55 | convolution fusion | flops 100671488 | bytes 4262400 | tf_op jit(solution)/shard_map/ski,sb->kbi/dot_general | solution.py:27
  431.4 18.5 %psum.31 = f32[2,32,32]{2,1,0:T(8,128)} all-reduce(f32[2,32,32]{2,1,0:T(8,128)S(1)} %fusion.71), channel_id=1, replica_groups=mesh['parts'=2,'layer'=4,'node'=4] {'node'}, use_global_device_ids=true, to_apply=%region_9.13 | all-reduce | flops 2048 | bytes 16384 | tf_op jit(solution)/shard_map/psum | solution.py:80
  (122 shorter events, 106.7 us)
Async XLA Ops:
  7.2 292.9 %all-reduce.3.cloned.1.call-start = ((), (), s32[]{:S(2)}) async-start(), calls=%async_computation | async-start | bytes 524288 | tf_op jit(solution)/shard_map/psum | solution.py:73
  20.5 13.0 %copy-start.1 = (f32[2,32,512]{2,1,0:T(8,128)S(1)}, f32[2,32,512]{2,1,0:T(8,128)}, u32[]{:S(2)}) copy-start(f32[2,32,512]{2,1,0:T(8,128)} %param.14) | copy-start | bytes 393220
  20.5 29.0 %copy-start.2 = (s32[2,512]{1,0:T(2,128)S(1)}, s32[2,512]{1,0:T(2,128)}, u32[]{:S(2)}) copy-start(s32[2,512]{1,0:T(2,128)} %param.11) | copy-start | bytes 12292
  20.5 29.1 %copy-start.3 = (s32[2,1]{0,1:T(1,128)S(1)}, s32[2,1]{0,1:T(1,128)}, u32[]{:S(2)}) copy-start(s32[2,1]{0,1:T(1,128)} %param.13) | copy-start | bytes 28
  363.2 68.0 %copy-start = (f32[2,32,512]{2,1,0:T(8,128)}, f32[2,32,512]{2,1,0:T(8,128)S(1)}, u32[]{:S(2)}) copy-start(f32[2,32,512]{2,1,0:T(8,128)S(1)} %get-tuple-element.22) | copy-start | bytes 393220
Sparse Core Ops, SparseCore 0:
  266.0 34.0 all-reduce.2
where the time goes:
time: 461 us; the launch traced here: 457 us
  matrix products  142 us (31%)
  blocking collectives  105 us (23%)
  other arithmetic  82.8 us (18%)
  local copies, waits for them, and re-layouts  76.6 us (17%)
  waiting for transfers between devices  34.2 us (7%)
  between operations  15.9 us (3%)
    dot_general x6, matrix products, apply_one(): jnp.einsum('ksj,sij->ski', picked, values.reshape(slot_count, BLK, BLK),...  74.3 us
    dot_general x6, matrix products, apply_one(): jnp.einsum('ski,sb->kbi', products, onehot, precision=lax.Precision.HIGHEST)  62.4 us
    another operation x18, other arithmetic, solve_lower(): lower_factor = jnp.linalg.cholesky(gram_matrix)  48.4 us
    all_gather x3, blocking collectives, apply_all(): lax.all_gather(basis.astype(jnp.bfloat16), 'node', axis=2, tiled=True)  43.8 us
    psum x2, blocking collectives, per_device(): orthonormal_gram_total = lax.psum(orthonormal_gram_local, 'node')  35.9 us
    psum x1, waiting for transfers between devices, per_device(): gram_total = lax.psum(gram_local, 'node')  34.2 us
    another operation x12, other arithmetic, solve_lower(): lax.linalg.triangular_solve(lower_factor, matrix, left_side=True, lower=T...  32.1 us
    another operation x2, local copies, waits for them, and re-layouts, apply_one(): values.reshape(slot_count, BLK, BLK)  25.9 us
  transfers between devices with their start and end apart: 1, of which 1 were waited for; matrix products, arithmetic and copies ran while one was open for 0% of the time, Pallas kernels for 0%

commit v1 on v0

v1 whole, which is shorter than its diff:
```python
import functools

import jax
import jax.numpy as jnp
from jax import lax
from jax.experimental import pallas as pl
from jax.experimental.pallas import tpu as pltpu
from jax.sharding import PartitionSpec as P

BLK = 64
ROWS_DEV = 512
BROWS = ROWS_DEV // BLK
CHUNK_COLS = 8
CHUNK_LANES = CHUNK_COLS * 2 * BLK
TALL = BROWS * BLK // 2
MIB = 1024 * 1024
F32 = jnp.float32
BF16 = jnp.bfloat16
HIGHEST = lax.Precision.HIGHEST
TRANS_B = (((1,), (1,)), ((), ()))
TRANS_A = (((0,), (0,)), ((), ()))


def params(mib):
    return pltpu.CompilerParams(vmem_limit_bytes=mib * MIB)


def vmem_specs(count):
    return [pl.BlockSpec(memory_space=pltpu.VMEM)] * count


def build_kernel(key_ref, blocks_ref, hi_ref, lo_ref):
    chunks = hi_ref.shape[1]
    slots = key_ref.shape[2]
    positions = chunks * CHUNK_COLS * BROWS
    base = pl.program_id(1) * positions
    position = lax.broadcasted_iota(jnp.int32, (positions, slots), 0) + base
    onehot = jnp.where(position == key_ref[0], 1.0, 0.0).astype(BF16)

    def step(u, carry):
        cols = pl.ds(pl.multiple_of(u * 256, 256), 256)
        z = jnp.dot(onehot, blocks_ref[0, :, cols], preferred_element_type=F32)
        out_rows = pl.ds(pl.multiple_of(u * 16, 16), 16)
        for c in range(chunks * CHUNK_COLS):
            piece = z[c * 8 : c * 8 + 8]
            piece = jnp.concatenate([piece[:, :128], piece[:, 128:]], axis=0)
            hi = piece.astype(BF16)
            lo = (piece - hi.astype(F32)).astype(BF16)
            lanes = slice((c % CHUNK_COLS) * 128, (c % CHUNK_COLS) * 128 + 128)
            hi_ref[0, c // CHUNK_COLS, out_rows, lanes] = hi
            lo_ref[0, c // CHUNK_COLS, out_rows, lanes] = lo
        return carry

    lax.fori_loop(0, BLK * BLK // 256, step, 0)


def build_dense(key, blocks, chunk_total):
    layers, slots, width = blocks.shape
    per_step = min(4, chunk_total)
    dense = jax.ShapeDtypeStruct((layers, chunk_total, TALL, CHUNK_LANES), BF16)
    out_spec = pl.BlockSpec((1, per_step, TALL, CHUNK_LANES), lambda l, s: (l, s, 0, 0))
    return pl.pallas_call(
        build_kernel,
        grid=(layers, chunk_total // per_step),
        in_specs=[
            pl.BlockSpec((1, 1, slots), lambda l, s: (l, 0, 0)),
            pl.BlockSpec((1, slots, width), lambda l, s: (l, 0, 0)),
        ],
        out_specs=[out_spec, out_spec],
        out_shape=[dense, dense],
        compiler_params=params(40),
        name="build_dense",
    )(key.reshape(layers, 1, slots), blocks)


def split3(x):
    a = x.astype(BF16)
    r = x - a.astype(F32)
    b = r.astype(BF16)
    c = (r - b.astype(F32)).astype(BF16)
    return a, b, c


def apply_kernel(mode, piece_count, *refs):
    pieces = refs[:piece_count]
    refs = refs[piece_count:]
    if mode == "score":
        left_ref, refs = refs[0], refs[1:]
    hi_ref, lo_ref, out_ref = refs[:3]
    gram_ref = refs[3] if mode != "plain" else None
    basis, perm, acc = refs[-3:]
    layer, chunk = pl.program_id(0), pl.program_id(1)
    k = pieces[0].shape[1]

    @pl.when((layer == 0) & (chunk == 0))
    def _():
        at = 0
        for piece in pieces:
            basis[:, :, at : at + piece.shape[2]] = piece[...].astype(BF16)
            at += piece.shape[2]
        row = lax.broadcasted_iota(jnp.int32, (ROWS_DEV, ROWS_DEV), 0)
        col = lax.broadcasted_iota(jnp.int32, (ROWS_DEV, ROWS_DEV), 1)
        target = (row % 8) * BLK + 2 * ((row % TALL) // 8) + row // TALL
        perm[...] = jnp.where(target == col, 1.0, 0.0).astype(BF16)

    width = CHUNK_COLS * BLK
    here = basis[layer, :, pl.ds(pl.multiple_of(chunk * width, width), width)].astype(F32)
    low = lax.broadcasted_iota(jnp.int32, (k, 128), 1) < BLK
    first, second = [], []
    for q in range(width // 128):
        b = here[:, q * 128 : q * 128 + 128]
        br = pltpu.roll(b, BLK, 1)
        first += [jnp.where(low, b, 0.0), jnp.where(low, br, 0.0)]
        second += [jnp.where(low, 0.0, br), jnp.where(low, 0.0, b)]
    weights = jnp.concatenate(
        [
            jnp.concatenate(first, axis=1),
            jnp.concatenate(second, axis=1),
            jnp.zeros((128 - 2 * k, CHUNK_LANES), F32),
        ],
        axis=0,
    ).astype(BF16)
    total = lax.dot_general(hi_ref[0, 0], weights, TRANS_B, preferred_element_type=F32)
    total += lax.dot_general(lo_ref[0, 0], weights, TRANS_B, preferred_element_type=F32)

    @pl.when(chunk == 0)
    def _():
        acc[...] = total

    @pl.when(chunk > 0)
    def _():
        acc[...] += total

    @pl.when(chunk == pl.num_programs(1) - 1)
    def _():
        turned = acc[...].T
        wide = jnp.concatenate([turned[:k], turned[k : 2 * k]], axis=1)
        parts = jnp.concatenate(split3(wide), axis=0)
        moved = jnp.dot(parts, perm[...], preferred_element_type=F32)
        image = moved[:k] + moved[k : 2 * k] + moved[2 * k :]
        out_ref[0] = image
        if mode == "gram":
            gram_ref[0] = lax.dot_general(image, image, TRANS_B, precision=HIGHEST, preferred_element_type=F32)
        if mode == "score":
            gram_ref[0] = lax.dot_general(
                left_ref[0], image, TRANS_B, precision=HIGHEST, preferred_element_type=F32
            )


def apply_dense(mode, pieces, hi, lo, left=None):
    layers, chunks = hi.shape[:2]
    k = pieces[0].shape[1]
    nodes = sum(piece.shape[2] for piece in pieces)
    dense_spec = pl.BlockSpec((1, 1, TALL, CHUNK_LANES), lambda l, s: (l, s, 0, 0))
    image_spec = pl.BlockSpec((1, k, ROWS_DEV), lambda l, s: (l, 0, 0))
    small_spec = pl.BlockSpec((1, k, k), lambda l, s: (l, 0, 0))
    out_shape = [jax.ShapeDtypeStruct((layers, k, ROWS_DEV), F32)]
    out_specs = [image_spec]
    if mode != "plain":
        out_shape.append(jax.ShapeDtypeStruct((layers, k, k), F32))
        out_specs.append(small_spec)
    operands = list(pieces) + ([left] if mode == "score" else []) + [hi, lo]
    in_specs = vmem_specs(len(pieces)) + ([image_spec] if mode == "score" else []) + [dense_spec, dense_spec]
    return pl.pallas_call(
        functools.partial(apply_kernel, mode, len(pieces)),
        grid=(layers, chunks),
        in_specs=in_specs,
        out_specs=out_specs,
        out_shape=out_shape,
        scratch_shapes=[
            pltpu.VMEM((layers, k, nodes), BF16),
            pltpu.VMEM((ROWS_DEV, ROWS_DEV), BF16),
            pltpu.VMEM((TALL, 128), F32),
        ],
        compiler_params=params(40),
        name="apply_" + mode,
    )(*operands)


def eliminate(panel, tail, offset):
    k = panel.shape[0]
    row_at = lax.broadcasted_iota(jnp.int32, (k, 1), 0)
    for j in range(k):
        row = panel[j : j + 1]
        pivot = row[:, offset + j : offset + j + 1]
        column = panel[:, offset + j : offset + j + 1]
        factor = jnp.where(row_at > j, column / pivot, 0.0)
        panel = panel - factor * row
        tail = tail - factor * tail[j : j + 1]
    lane = lax.broadcasted_iota(jnp.int32, panel.shape, 1)
    sub = lax.broadcasted_iota(jnp.int32, panel.shape, 0)
    diagonal = jnp.sum(jnp.where(lane == sub + offset, panel, 0.0), axis=1, keepdims=True)
    scale = 1.0 / jnp.sqrt(diagonal)
    return panel * scale, tail * scale


def solve_kernel(piece_count, *refs):
    grams, image_ref, out_ref = refs[:piece_count], refs[piece_count], refs[piece_count + 1]
    layers, k = image_ref.shape[:2]
    lane = lax.broadcasted_iota(jnp.int32, (k, 128), 1)
    sub = lax.broadcasted_iota(jnp.int32, (k, 128), 0)
    eye = jnp.where(lane == sub, 1.0, 0.0)
    for layer in range(layers):
        values = [ref[layer] for ref in grams]
        if piece_count == 4:
            gram = (values[0] + values[2]) + (values[1] + values[3])
        else:
            gram = values[0]
        gram = jnp.concatenate([gram, jnp.zeros((k, 128 - k), F32)], axis=1)
        inverse = eliminate(gram, eye, 0)[1][:, :k]
        solved = jnp.dot(inverse, image_ref[layer], precision=HIGHEST, preferred_element_type=F32)
        out_ref[layer] = solved.astype(BF16)


def solve(grams, image):
    return pl.pallas_call(
        functools.partial(solve_kernel, len(grams)),
        in_specs=vmem_specs(len(grams) + 1),
        out_specs=pl.BlockSpec(memory_space=pltpu.VMEM),
        out_shape=jax.ShapeDtypeStruct(image.shape, BF16),
        name="solve_layers",
    )(*grams, image)


def stack_rows(refs, scratch):
    g = lax.axis_index("layer")
    rows = scratch.shape[0] // len(refs)
    for d, ref in enumerate(refs):
        at = lax.rem(g + d, len(refs)) * rows
        scratch[pl.ds(pl.multiple_of(at, rows), rows)] = ref[...].reshape(rows, ref.shape[-1])


def cross_kernel(piece_count, *refs):
    pieces, out_ref, stacked = refs[:piece_count], refs[piece_count], refs[piece_count + 1]
    stack_rows(pieces, stacked)
    own = pieces[0][...].reshape(-1, stacked.shape[1])
    out_ref[...] = lax.dot_general(
        own, stacked[...], TRANS_B, precision=HIGHEST, preferred_element_type=F32
    )


def cross(pieces):
    layers, k, width = pieces[0].shape
    rows = layers * k
    return pl.pallas_call(
        functools.partial(cross_kernel, len(pieces)),
        in_specs=vmem_specs(len(pieces)),
        out_specs=pl.BlockSpec(memory_space=pltpu.VMEM),
        out_shape=jax.ShapeDtypeStruct((rows, rows * len(pieces)), F32),
        scratch_shapes=[pltpu.VMEM((rows * len(pieces), width), F32)],
        name="cross_gram",
    )(*pieces)


def joint_kernel(piece_count, k, *refs):
    gram_refs, image_refs = refs[:piece_count], refs[piece_count : 2 * piece_count]
    out_ref, rounded_ref, work, stacked = refs[2 * piece_count :]
    stack_rows(gram_refs, work)
    stack_rows(image_refs, stacked)
    size = work.shape[0]
    steps = size // k
    lane = lax.broadcasted_iota(jnp.int32, (k, size), 1)
    sub = lax.broadcasted_iota(jnp.int32, (k, size), 0)
    lane_all = lax.broadcasted_iota(jnp.int32, (size, size), 1)
    for s in range(steps):
        lo, hi = s * k, (s + 1) * k
        here = (lane >= lo) & (lane < hi)
        panel = work[lo:hi]
        tail = jnp.where(here, jnp.where(lane == sub + lo, 1.0, 0.0), 0.0)
        panel, tail = eliminate(panel, tail, lo)
        panel = jnp.where(here, tail, panel)
        work[lo:hi] = jnp.where(lane < hi, panel, 0.0)
        if s + 1 < steps:
            ahead = jnp.where(lane >= hi, panel, 0.0)
            update = lax.dot_general(ahead, panel, TRANS_A, precision=HIGHEST, preferred_element_type=F32)
            rest = work[hi:]
            rest = jnp.where((lane_all[hi:] >= lo) & (lane_all[hi:] < hi), 0.0, rest)
            work[hi:] = rest - update[hi:]
    rows = size // piece_count
    own = work[pl.ds(pl.multiple_of(lax.axis_index("layer") * rows, rows), rows)]
    joint = jnp.dot(own, stacked[...], precision=HIGHEST, preferred_element_type=F32)
    joint = joint.reshape(out_ref.shape)
    out_ref[...] = joint
    rounded_ref[...] = joint.astype(BF16)


def joint_solve(grams, images):
    layers, k, width = images[0].shape
    size = layers * k * len(images)
    return pl.pallas_call(
        functools.partial(joint_kernel, len(images), k),
        in_specs=vmem_specs(2 * len(images)),
        out_specs=vmem_specs(2),
        out_shape=[
            jax.ShapeDtypeStruct(images[0].shape, F32),
            jax.ShapeDtypeStruct(images[0].shape, BF16),
        ],
        scratch_shapes=[pltpu.VMEM((size, size), F32), pltpu.VMEM((size, width), F32)],
        compiler_params=params(32),
        name="joint_solve",
    )(*grams, *images)


def around(x, axis, count):
    pieces = [x]
    for d in range(1, count):
        pieces.append(lax.ppermute(x, axis, [((m + d) % count, m) for m in range(count)]))
    return pieces


def add4(pieces):
    return (pieces[0] + pieces[2]) + (pieces[1] + pieces[3])


def per_device(shards, groups, blocks, block_rows, block_cols, counts, start):
    relative = shards == 4
    cols_total = shards * BROWS
    live = jnp.arange(block_rows.shape[1], dtype=jnp.int32)[None, :] < counts
    cols = block_cols
    if relative:
        cols = (cols - lax.axis_index("node") * BROWS + cols_total) % cols_total
    key = jnp.where(live, cols * BROWS + block_rows, -1)

    def gather(x):
        if relative:
            return around(x, "node", shards)
        return [lax.all_gather(x, "node", axis=2, tiled=True)]

    def total(x):
        return add4(around(x, "node", shards)) if relative else lax.psum(x, "node")

    first = gather(start.astype(BF16))
    hi, lo = build_dense(key, blocks, cols_total // CHUNK_COLS)
    image, gram = apply_dense("gram", first, hi, lo)
    grams = around(gram, "node", shards) if relative else [lax.psum(gram, "node")]
    (image,) = apply_dense("plain", gather(solve(grams, image)), hi, lo)
    images = around(image, "layer", groups)
    grams = around(total(cross(images)), "layer", groups)
    joint_basis, rounded = joint_solve(grams, images)
    _, partial = apply_dense("score", gather(rounded), hi, lo, joint_basis)
    return joint_basis, total(partial)


def solution(mesh):
    in_specs = (
        P(("parts", "layer"), "node", None),
        P(("parts", "layer"), "node"),
        P(("parts", "layer"), "node"),
        P(("parts", "layer"), "node"),
        P(("parts", "layer"), None, "node"),
    )
    out_specs = (P(("parts", "layer"), None, "node"), P(("parts", "layer"), None, None))
    return jax.shard_map(
        functools.partial(per_device, mesh.shape["node"], mesh.shape["layer"]),
        mesh=mesh,
        in_specs=in_specs,
        out_specs=out_specs,
        check_vma=False,
    )
```

time: 461 us -> 142 us (0.31)
  matrix products: 142 us -> 0 us
  blocking collectives: 105 us -> 0 us
  other arithmetic: 82.8 us -> 3.17 us
  local copies, waits for them, and re-layouts: 76.6 us -> 16.1 us
  Pallas kernels: 0 us -> 59.1 us
  starting transfers between devices: 0.04 us -> 32.4 us
  between operations: 15.9 us -> 0.76 us
    dot_general x16 -> x0, matrix products: 139 us -> none  [the longest x6 74.3 us: apply_one(): jnp.einsum('ksj,sij->ski', picked, values.reshape(slot_count, BLK, BLK),...]
    another operation x32 -> x0, other arithmetic: 80.5 us -> none  [the longest x18 48.4 us: solve_lower(): lower_factor = jnp.linalg.cholesky(gram_matrix)]
    pallas_call x0 -> x7, Pallas kernels: none -> 59.1 us  [the longest x1 26.1 us: joint_solve(): pl.pallas_call(functools.partial(joint_kernel, len(images), k), in_specs=...]
    psum x3 -> x0, blocking collectives: 54.5 us -> none  [the longest x2 35.9 us: per_device(): orthonormal_gram_total = lax.psum(orthonormal_gram_local, 'node')]
    all_gather x4 -> x0, blocking collectives: 51 us -> none  [the longest x3 43.8 us: apply_all(): lax.all_gather(basis.astype(jnp.bfloat16), 'node', axis=2, tiled=True)]
    psum x1 -> x0, waiting for transfers between devices: 34.2 us -> none  [per_device(): gram_total = lax.psum(gram_local, 'node')]
    another operation x34 -> x0, local copies, waits for them, and re-layouts: 32.8 us -> none  [the longest x2 25.9 us: apply_one(): values.reshape(slot_count, BLK, BLK)]
    ppermute x0 -> x24, starting transfers between devices: none -> 32.4 us  [around(): lax.ppermute(x, axis, [((m + d) % count, m) for m in range(count)])]
  transfers between devices with their start and end apart: 1 -> 24, of which waited for: 1 -> 16; matrix products, arithmetic and copies ran while one was open for 0% -> 1% of each run, Pallas kernels for 0% -> 7%
where the time goes in v1:
time: 142 us; the launch traced here: 141 us
  Pallas kernels  59.1 us (42%)
  starting transfers between devices  32.4 us (23%)
  waiting for transfers between devices  29.8 us (21%)
  local copies, waits for them, and re-layouts  16.1 us (11%)
  other arithmetic  3.17 us (2%)
    ppermute x24, starting transfers between devices, around(): lax.ppermute(x, axis, [((m + d) % count, m) for m in range(count)])  32.4 us
    ppermute x24, waiting for transfers between devices, around(): lax.ppermute(x, axis, [((m + d) % count, m) for m in range(count)])  29.8 us
    pallas_call x1, Pallas kernels, joint_solve(): pl.pallas_call(functools.partial(joint_kernel, len(images), k), in_specs=...  26.1 us
    unnamed x42, local copies, waits for them, and re-layouts  16.1 us
    pallas_call x3, Pallas kernels, apply_dense(): pl.pallas_call(functools.partial(apply_kernel, mode, len(pieces)), grid=(...  16 us
    pallas_call x1, Pallas kernels, build_dense(): pl.pallas_call(build_kernel, grid=(layers, chunk_total // per_step), in_s...  10.1 us
    pallas_call x1, Pallas kernels, solve(): pl.pallas_call(functools.partial(solve_kernel, len(grams)), in_specs=vmem...  4.55 us
  transfers between devices with their start and end apart: 24, of which 16 were waited for; matrix products, arithmetic and copies ran while one was open for 1% of the time, Pallas kernels for 7%

profile of v1, /device:TPU:0, one launch (start us, length us, event | category | flops | bytes accessed | tf_op | source)
XLA Modules:
  0.0 141.3 jit_solution(7774161581979462034)
XLA Ops:
  1.5 3.1 %collective-permute-start.2 = (bf16[2,32,512]{2,1,0:T(8,128)(2,1)S(1)}, bf16[2,32,512]{2,1,0:T(8,128)(2,1)S(1)}, u32[]{:S(2)}, u32[]{:S(2)}) collective-permute-start(bf16[2,32,512]{2,1,0:T(8,128)(2,1)S(1)} %convert_element_type.3.refs_0_), channel_id=1, source_target_pairs={{3,0},{0,1},{1,2},{2,3},{7,4},{4,5},{5,6},{6,7},{11,8},{8,9},{9,10... | collective-permute-start | bytes 196616 | tf_op jit(solution)/shard_map/ppermute | solution.py:307
  4.6 2.6 %collective-permute-start.1 = (bf16[2,32,512]{2,1,0:T(8,128)(2,1)S(1)}, bf16[2,32,512]{2,1,0:T(8,128)(2,1)S(1)}, u32[]{:S(2)}, u32[]{:S(2)}) collective-permute-start(bf16[2,32,512]{2,1,0:T(8,128)(2,1)S(1)} %convert_element_type.3.refs_0_), channel_id=1, source_target_pairs={{2,0},{3,1},{0,2},{1,3},{6,4},{7,5},{4,6},{5,7},{10,8},{11,9},{8,1... | collective-permute-start | bytes 196616 | tf_op jit(solution)/shard_map/ppermute | solution.py:307
  9.3 10.1 %build_dense.1 = (bf16[2,4,256,1024]{3,2,1,0:T(8,128)(2,1)S(1)}, bf16[2,4,256,1024]{3,2,1,0:T(8,128)(2,1)S(1)}) custom-call(s32[2,1,512]{2,1,0:T(1,128)S(1)} %reshape.7.key_ref, bf16[2,512,4096]{2,1,0:T(8,128)(2,1)} %blocks_ref.1), custom_call_target="tpu_custom_call" | custom-call | tf_op jit(solution)/shard_map/build_dense/pallas_call | solution.py:62
  19.5 5.2 %apply_gram.1 = (f32[2,32,512]{2,1,0:T(8,128)S(1)}, f32[2,32,32]{2,1,0:T(8,128)S(1)}) custom-call(bf16[2,32,512]{2,1,0:T(8,128)(2,1)S(1)} %convert_element_type.3.refs_0_, bf16[2,32,512]{2,1,0:T(8,128)(2,1)S(1)} %collective-permute-done.refs_1_, bf16[2,32,512]{2,1,0:T(8,128)(2,1)S(1)} %collective-permute-done.1.refs_2_, ...), custom_call_target="tpu_custom_call" | custom-call | tf_op jit(solution)/shard_map/apply_gram/pallas_call | solution.py:164
  26.4 2.8 %collective-permute-start.3 = (f32[2,32,32]{2,1,0:T(8,128)S(1)}, f32[2,32,32]{2,1,0:T(8,128)S(1)}, u32[]{:S(2)}, u32[]{:S(2)}) collective-permute-start(f32[2,32,32]{2,1,0:T(8,128)S(1)} %get-tuple-element.11.refs_0_), channel_id=1, source_target_pairs={{1,0},{2,1},{3,2},{0,3},{5,4},{6,5},{7,6},{4,7},{9,8},{10,9},{11,1... | collective-permute-start | bytes 24584 | tf_op jit(solution)/shard_map/ppermute | solution.py:307
  32.4 4.6 %solve_layers.1.refs_0_ = bf16[2,32,512]{2,1,0:T(8,128)(2,1)} custom-call(f32[2,32,32]{2,1,0:T(8,128)} %copy-done.17, f32[2,32,32]{2,1,0:T(8,128)} %copy-done.20, f32[2,32,32]{2,1,0:T(8,128)} %copy-done.19, f32[2,32,32]{2,1,0:T(8,128)} %copy-done.18, f32[2,32,512]{2,1,0:T(8,128)} %copy-done.16), custom_call_target="tpu_custom_call" | custom-call | tf_op jit(solution)/shard_map/solve_layers/pallas_call | solution.py:216
  41.2 2.0 %collective-permute-done.8.refs_3_ = bf16[2,32,512]{2,1,0:T(8,128)(2,1)S(1)} collective-permute-done((bf16[2,32,512]{2,1,0:T(8,128)(2,1)}, bf16[2,32,512]{2,1,0:T(8,128)(2,1)S(1)}, u32[]{:S(2)}, u32[]{:S(2)}) %collective-permute-start.8) | collective-permute-done | bytes 65568 | tf_op jit(solution)/shard_map/ppermute | solution.py:307
  45.3 2.2 %copy-done.1 = bf16[2,4,256,1024]{3,2,1,0:T(8,128)(2,1)S(1)} copy-done((bf16[2,4,256,1024]{3,2,1,0:T(8,128)(2,1)S(1)}, bf16[2,4,256,1024]{3,2,1,0:T(8,128)(2,1)}, u32[]{:S(2)}) %copy-start.1) | copy-done | bytes 4194328
  47.5 2.2 %copy-done.4 = bf16[2,4,256,1024]{3,2,1,0:T(8,128)(2,1)S(1)} copy-done((bf16[2,4,256,1024]{3,2,1,0:T(8,128)(2,1)S(1)}, bf16[2,4,256,1024]{3,2,1,0:T(8,128)(2,1)}, u32[]{:S(2)}) %copy-start.4) | copy-done | bytes 4194328
  50.5 4.8 %apply_plain.1.refs_0_.refs_4_ = f32[2,32,512]{2,1,0:T(8,128)S(1)} custom-call(bf16[2,32,512]{2,1,0:T(8,128)(2,1)S(1)} %copy-done.14, bf16[2,32,512]{2,1,0:T(8,128)(2,1)S(1)} %collective-permute-done.6.refs_1_, bf16[2,32,512]{2,1,0:T(8,128)(2,1)S(1)} %collective-permute-done.7.refs_2_, bf16[2,32,512]{2,1,0:T(8,128)(2,1)S(1)} %collective-permute-done.8.refs_3_, ...), custom_call_target="tpu_custom_call" | custom-call | tf_op jit(solution)/shard_map/apply_plain/pallas_call | solution.py:164
  58.3 2.2 %collective-permute-done.11.refs_3_.refs_7_ = f32[2,32,512]{2,1,0:T(8,128)S(1)} collective-permute-done((f32[2,32,512]{2,1,0:T(8,128)S(1)}, f32[2,32,512]{2,1,0:T(8,128)S(1)}, u32[]{:S(2)}, u32[]{:S(2)}) %collective-permute-start.11) | collective-permute-done | bytes 131104 | tf_op jit(solution)/shard_map/ppermute | solution.py:307
  63.6 2.4 %cross_gram.1 = f32[64,256]{1,0:T(8,128)} custom-call(f32[2,32,512]{2,1,0:T(8,128)} %copy-done.6, f32[2,32,512]{2,1,0:T(8,128)} %copy-done.12, f32[2,32,512]{2,1,0:T(8,128)} %copy-done.10, f32[2,32,512]{2,1,0:T(8,128)} %copy-done.8), custom_call_target="tpu_custom_call" | custom-call | tf_op jit(solution)/shard_map/cross_gram/pallas_call | solution.py:245
  66.5 3.3 %collective-permute-start.13 = (f32[64,256]{1,0:T(8,128)}, f32[64,256]{1,0:T(8,128)S(1)}, u32[]{:S(2)}, u32[]{:S(2)}) collective-permute-start(f32[64,256]{1,0:T(8,128)} %cross_gram.1), channel_id=1, source_target_pairs={{1,0},{2,1},{3,2},{0,3},{5,4},{6,5},{7,6},{4,7},{9,8},{10,9},{11,1... | collective-permute-start | bytes 196616 | tf_op jit(solution)/shard_map/ppermute | solution.py:307
  69.8 3.2 %collective-permute-done.14 = f32[64,256]{1,0:T(8,128)S(1)} collective-permute-done((f32[64,256]{1,0:T(8,128)}, f32[64,256]{1,0:T(8,128)S(1)}, u32[]{:S(2)}, u32[]{:S(2)}) %collective-permute-start.14) | collective-permute-done | bytes 65568 | tf_op jit(solution)/shard_map/ppermute | solution.py:307
  73.0 3.6 %collective-permute-done.12 = f32[64,256]{1,0:T(8,128)S(1)} collective-permute-done((f32[64,256]{1,0:T(8,128)}, f32[64,256]{1,0:T(8,128)S(1)}, u32[]{:S(2)}, u32[]{:S(2)}) %collective-permute-start.12) | collective-permute-done | bytes 65568 | tf_op jit(solution)/shard_map/ppermute | solution.py:307
  85.9 26.1 %joint_solve.1 = (f32[2,32,512]{2,1,0:T(8,128)}, bf16[2,32,512]{2,1,0:T(8,128)(2,1)S(1)}) custom-call(f32[64,256]{1,0:T(8,128)S(1)} %add_add_fusion.refs_0_, f32[64,256]{1,0:T(8,128)S(1)} %collective-permute-done.15.refs_1_, f32[64,256]{1,0:T(8,128)S(1)} %collective-permute-done.16.refs_2_, f32[64,256]{1,0:T(8,128)S(1)} %collective-permute-done.17.refs_3_, ...), custom_call_target="tpu_custom_call" | custom-call | tf_op jit(solution)/shard_map/joint_solve/pallas_call | solution.py:290
  112.1 2.6 %collective-permute-start.19 = (bf16[2,32,512]{2,1,0:T(8,128)(2,1)S(1)}, bf16[2,32,512]{2,1,0:T(8,128)(2,1)S(1)}, u32[]{:S(2)}, u32[]{:S(2)}) collective-permute-start(bf16[2,32,512]{2,1,0:T(8,128)(2,1)S(1)} %get-tuple-element.14.refs_0_), channel_id=1, source_target_pairs={{2,0},{3,1},{0,2},{1,3},{6,4},{7,5},{4,6},{5,7},{10,8},{11,9},{8,1... | collective-permute-start | bytes 196616 | tf_op jit(solution)/shard_map/ppermute | solution.py:307
  115.9 3.0 %collective-permute-done.20.refs_3_ = bf16[2,32,512]{2,1,0:T(8,128)(2,1)S(1)} collective-permute-done((bf16[2,32,512]{2,1,0:T(8,128)(2,1)S(1)}, bf16[2,32,512]{2,1,0:T(8,128)(2,1)S(1)}, u32[]{:S(2)}, u32[]{:S(2)}) %collective-permute-start.20) | collective-permute-done | bytes 65568 | tf_op jit(solution)/shard_map/ppermute | solution.py:307
  120.7 2.2 %copy-done.2 = bf16[2,4,256,1024]{3,2,1,0:T(8,128)(2,1)S(1)} copy-done((bf16[2,4,256,1024]{3,2,1,0:T(8,128)(2,1)S(1)}, bf16[2,4,256,1024]{3,2,1,0:T(8,128)(2,1)}, u32[]{:S(2)}) %copy-start.2) | copy-done | bytes 4194328
  122.9 2.2 %copy-done.5 = bf16[2,4,256,1024]{3,2,1,0:T(8,128)(2,1)S(1)} copy-done((bf16[2,4,256,1024]{3,2,1,0:T(8,128)(2,1)S(1)}, bf16[2,4,256,1024]{3,2,1,0:T(8,128)(2,1)}, u32[]{:S(2)}) %copy-start.5) | copy-done | bytes 4194328
  126.0 6.0 %apply_score.1 = (f32[2,32,512]{2,1,0:T(8,128)}, f32[2,32,32]{2,1,0:T(8,128)S(1)}) custom-call(bf16[2,32,512]{2,1,0:T(8,128)(2,1)S(1)} %get-tuple-element.14.refs_0_, bf16[2,32,512]{2,1,0:T(8,128)(2,1)S(1)} %collective-permute-done.18.refs_1_, bf16[2,32,512]{2,1,0:T(8,128)(2,1)S(1)} %collective-permute-done.19.refs_2_, ...), custom_call_target="tpu_custom_call" | custom-call | tf_op jit(solution)/shard_map/apply_score/pallas_call | solution.py:164
  133.9 2.0 %collective-permute-start.22 = (f32[2,32,32]{2,1,0:T(8,128)S(1)}, f32[2,32,32]{2,1,0:T(8,128)S(1)}, u32[]{:S(2)}, u32[]{:S(2)}) collective-permute-start(f32[2,32,32]{2,1,0:T(8,128)S(1)} %get-tuple-element.15), channel_id=1, source_target_pairs={{1,0},{2,1},{3,2},{0,3},{5,4},{6,5},{7,6},{4,7},{9,8},{10,9},{11,1... | collective-permute-start | bytes 24584 | tf_op jit(solution)/shard_map/ppermute | solution.py:307
  135.9 2.2 %collective-permute-done.23 = f32[2,32,32]{2,1,0:T(8,128)S(1)} collective-permute-done((f32[2,32,32]{2,1,0:T(8,128)S(1)}, f32[2,32,32]{2,1,0:T(8,128)S(1)}, u32[]{:S(2)}, u32[]{:S(2)}) %collective-permute-start.23) | collective-permute-done | bytes 8224 | tf_op jit(solution)/shard_map/ppermute | solution.py:307
  138.1 2.5 %collective-permute-done.21 = f32[2,32,32]{2,1,0:T(8,128)S(1)} collective-permute-done((f32[2,32,32]{2,1,0:T(8,128)S(1)}, f32[2,32,32]{2,1,0:T(8,128)S(1)}, u32[]{:S(2)}, u32[]{:S(2)}) %collective-permute-start.21) | collective-permute-done | bytes 8224 | tf_op jit(solution)/shard_map/ppermute | solution.py:307
  (78 shorter events, 37.6 us)
Async XLA Ops:
  1.5 17.9 %collective-permute-start.2 = (bf16[2,32,512]{2,1,0:T(8,128)(2,1)S(1)}, bf16[2,32,512]{2,1,0:T(8,128)(2,1)S(1)}, u32[]{:S(2)}, u32[]{:S(2)}) collective-permute-start(bf16[2,32,512]{2,1,0:T(8,128)(2,1)S(1)} %convert_element_type.3.refs_0_), channel_id=1, source_target_pairs={{3,0},{0,1},{1,2},{2,3},{7,4},{4,5},{5,6},{6,7},{11,8},{8,9},{9,10... | collective-permute-start | bytes 196616 | tf_op jit(solution)/shard_map/ppermute | solution.py:307
  4.6 14.8 %collective-permute-start.1 = (bf16[2,32,512]{2,1,0:T(8,128)(2,1)S(1)}, bf16[2,32,512]{2,1,0:T(8,128)(2,1)S(1)}, u32[]{:S(2)}, u32[]{:S(2)}) collective-permute-start(bf16[2,32,512]{2,1,0:T(8,128)(2,1)S(1)} %convert_element_type.3.refs_0_), channel_id=1, source_target_pairs={{2,0},{3,1},{0,2},{1,3},{6,4},{7,5},{4,6},{5,7},{10,8},{11,9},{8,1... | collective-permute-start | bytes 196616 | tf_op jit(solution)/shard_map/ppermute | solution.py:307
  7.2 12.2 %collective-permute-start = (bf16[2,32,512]{2,1,0:T(8,128)(2,1)S(1)}, bf16[2,32,512]{2,1,0:T(8,128)(2,1)S(1)}, u32[]{:S(2)}, u32[]{:S(2)}) collective-permute-start(bf16[2,32,512]{2,1,0:T(8,128)(2,1)S(1)} %convert_element_type.3.refs_0_), channel_id=1, source_target_pairs={{1,0},{2,1},{3,2},{0,3},{5,4},{6,5},{7,6},{4,7},{9,8},{10,9},{11,1... | collective-permute-start | bytes 196616 | tf_op jit(solution)/shard_map/ppermute | solution.py:307
  25.4 5.8 %collective-permute-start.5 = (f32[2,32,32]{2,1,0:T(8,128)S(1)}, f32[2,32,32]{2,1,0:T(8,128)S(1)}, u32[]{:S(2)}, u32[]{:S(2)}) collective-permute-start(f32[2,32,32]{2,1,0:T(8,128)S(1)} %get-tuple-element.11.refs_0_), channel_id=1, source_target_pairs={{3,0},{0,1},{1,2},{2,3},{7,4},{4,5},{5,6},{6,7},{11,8},{8,9},{9,10... | collective-permute-start | bytes 24584 | tf_op jit(solution)/shard_map/ppermute | solution.py:307
  26.1 5.7 %collective-permute-start.4 = (f32[2,32,32]{2,1,0:T(8,128)S(1)}, f32[2,32,32]{2,1,0:T(8,128)S(1)}, u32[]{:S(2)}, u32[]{:S(2)}) collective-permute-start(f32[2,32,32]{2,1,0:T(8,128)S(1)} %get-tuple-element.11.refs_0_), channel_id=1, source_target_pairs={{2,0},{3,1},{0,2},{1,3},{6,4},{7,5},{4,6},{5,7},{10,8},{11,9},{8,1... | collective-permute-start | bytes 24584 | tf_op jit(solution)/shard_map/ppermute | solution.py:307
  26.4 5.4 %collective-permute-start.3 = (f32[2,32,32]{2,1,0:T(8,128)S(1)}, f32[2,32,32]{2,1,0:T(8,128)S(1)}, u32[]{:S(2)}, u32[]{:S(2)}) collective-permute-start(f32[2,32,32]{2,1,0:T(8,128)S(1)} %get-tuple-element.11.refs_0_), channel_id=1, source_target_pairs={{1,0},{2,1},{3,2},{0,3},{5,4},{6,5},{7,6},{4,7},{9,8},{10,9},{11,1... | collective-permute-start | bytes 24584 | tf_op jit(solution)/shard_map/ppermute | solution.py:307
  36.9 6.3 %collective-permute-start.8 = (bf16[2,32,512]{2,1,0:T(8,128)(2,1)}, bf16[2,32,512]{2,1,0:T(8,128)(2,1)S(1)}, u32[]{:S(2)}, u32[]{:S(2)}) collective-permute-start(bf16[2,32,512]{2,1,0:T(8,128)(2,1)} %solve_layers.1.refs_0_), channel_id=1, source_target_pairs={{3,0},{0,1},{1,2},{2,3},{7,4},{4,5},{5,6},{6,7},{11,8},{8,9},{9,10... | collective-permute-start | bytes 196616 | tf_op jit(solution)/shard_map/ppermute | solution.py:307
  38.9 5.8 %collective-permute-start.7 = (bf16[2,32,512]{2,1,0:T(8,128)(2,1)}, bf16[2,32,512]{2,1,0:T(8,128)(2,1)S(1)}, u32[]{:S(2)}, u32[]{:S(2)}) collective-permute-start(bf16[2,32,512]{2,1,0:T(8,128)(2,1)} %solve_layers.1.refs_0_), channel_id=1, source_target_pairs={{2,0},{3,1},{0,2},{1,3},{6,4},{7,5},{4,6},{5,7},{10,8},{11,9},{8,1... | collective-permute-start | bytes 196616 | tf_op jit(solution)/shard_map/ppermute | solution.py:307
  40.7 4.7 %collective-permute-start.6 = (bf16[2,32,512]{2,1,0:T(8,128)(2,1)}, bf16[2,32,512]{2,1,0:T(8,128)(2,1)S(1)}, u32[]{:S(2)}, u32[]{:S(2)}) collective-permute-start(bf16[2,32,512]{2,1,0:T(8,128)(2,1)} %solve_layers.1.refs_0_), channel_id=1, source_target_pairs={{1,0},{2,1},{3,2},{0,3},{5,4},{6,5},{7,6},{4,7},{9,8},{10,9},{11,1... | collective-permute-start | bytes 196616 | tf_op jit(solution)/shard_map/ppermute | solution.py:307
  55.3 5.2 %collective-permute-start.11 = (f32[2,32,512]{2,1,0:T(8,128)S(1)}, f32[2,32,512]{2,1,0:T(8,128)S(1)}, u32[]{:S(2)}, u32[]{:S(2)}) collective-permute-start(f32[2,32,512]{2,1,0:T(8,128)S(1)} %apply_plain.1.refs_0_.refs_4_), channel_id=1, source_target_pairs={{12,0},{0,4},{4,8},{8,12},{13,1},{1,5},{5,9},{9,13},{14,2},{2,6},{... | collective-permute-start | bytes 393224 | tf_op jit(solution)/shard_map/ppermute | solution.py:307
  55.3 6.4 %collective-permute-start.10 = (f32[2,32,512]{2,1,0:T(8,128)S(1)}, f32[2,32,512]{2,1,0:T(8,128)S(1)}, u32[]{:S(2)}, u32[]{:S(2)}) collective-permute-start(f32[2,32,512]{2,1,0:T(8,128)S(1)} %apply_plain.1.refs_0_.refs_4_), channel_id=1, source_target_pairs={{8,0},{12,4},{0,8},{4,12},{9,1},{13,5},{1,9},{5,13},{10,2},{14,6},... | collective-permute-start | bytes 393224 | tf_op jit(solution)/shard_map/ppermute | solution.py:307
  56.9 6.1 %collective-permute-start.9 = (f32[2,32,512]{2,1,0:T(8,128)S(1)}, f32[2,32,512]{2,1,0:T(8,128)S(1)}, u32[]{:S(2)}, u32[]{:S(2)}) collective-permute-start(f32[2,32,512]{2,1,0:T(8,128)S(1)} %apply_plain.1.refs_0_.refs_4_), channel_id=1, source_target_pairs={{4,0},{8,4},{12,8},{0,12},{5,1},{9,5},{13,9},{1,13},{6,2},{10,6},{... | collective-permute-start | bytes 393224 | tf_op jit(solution)/shard_map/ppermute | solution.py:307
  66.0 7.0 %collective-permute-start.14 = (f32[64,256]{1,0:T(8,128)}, f32[64,256]{1,0:T(8,128)S(1)}, u32[]{:S(2)}, u32[]{:S(2)}) collective-permute-start(f32[64,256]{1,0:T(8,128)} %cross_gram.1), channel_id=1, source_target_pairs={{3,0},{0,1},{1,2},{2,3},{7,4},{4,5},{5,6},{6,7},{11,8},{8,9},{9,10... | collective-permute-start | bytes 196616 | tf_op jit(solution)/shard_map/ppermute | solution.py:307
  66.5 6.5 %collective-permute-start.13 = (f32[64,256]{1,0:T(8,128)}, f32[64,256]{1,0:T(8,128)S(1)}, u32[]{:S(2)}, u32[]{:S(2)}) collective-permute-start(f32[64,256]{1,0:T(8,128)} %cross_gram.1), channel_id=1, source_target_pairs={{1,0},{2,1},{3,2},{0,3},{5,4},{6,5},{7,6},{4,7},{9,8},{10,9},{11,1... | collective-permute-start | bytes 196616 | tf_op jit(solution)/shard_map/ppermute | solution.py:307
  69.8 6.8 %collective-permute-start.12 = (f32[64,256]{1,0:T(8,128)}, f32[64,256]{1,0:T(8,128)S(1)}, u32[]{:S(2)}, u32[]{:S(2)}) collective-permute-start(f32[64,256]{1,0:T(8,128)} %cross_gram.1), channel_id=1, source_target_pairs={{2,0},{3,1},{0,2},{1,3},{6,4},{7,5},{4,6},{5,7},{10,8},{11,9},{8,1... | collective-permute-start | bytes 196616 | tf_op jit(solution)/shard_map/ppermute | solution.py:307
  77.5 3.8 %collective-permute-start.17 = (f32[64,256]{1,0:T(8,128)S(1)}, f32[64,256]{1,0:T(8,128)S(1)}, u32[]{:S(2)}, u32[]{:S(2)}) collective-permute-start(f32[64,256]{1,0:T(8,128)S(1)} %add_add_fusion.refs_0_), channel_id=1, source_target_pairs={{12,0},{0,4},{4,8},{8,12},{13,1},{1,5},{5,9},{9,13},{14,2},{2,6},{... | collective-permute-start | bytes 196616 | tf_op jit(solution)/shard_map/ppermute | solution.py:307
  77.5 4.8 %collective-permute-start.16 = (f32[64,256]{1,0:T(8,128)S(1)}, f32[64,256]{1,0:T(8,128)S(1)}, u32[]{:S(2)}, u32[]{:S(2)}) collective-permute-start(f32[64,256]{1,0:T(8,128)S(1)} %add_add_fusion.refs_0_), channel_id=1, source_target_pairs={{8,0},{12,4},{0,8},{4,12},{9,1},{13,5},{1,9},{5,13},{10,2},{14,6},... | collective-permute-start | bytes 196616 | tf_op jit(solution)/shard_map/ppermute | solution.py:307
  78.9 3.4 %collective-permute-start.15 = (f32[64,256]{1,0:T(8,128)S(1)}, f32[64,256]{1,0:T(8,128)S(1)}, u32[]{:S(2)}, u32[]{:S(2)}) collective-permute-start(f32[64,256]{1,0:T(8,128)S(1)} %add_add_fusion.refs_0_), channel_id=1, source_target_pairs={{4,0},{8,4},{12,8},{0,12},{5,1},{9,5},{13,9},{1,13},{6,2},{10,6},{... | collective-permute-start | bytes 196616 | tf_op jit(solution)/shard_map/ppermute | solution.py:307
  112.1 6.9 %collective-permute-start.20 = (bf16[2,32,512]{2,1,0:T(8,128)(2,1)S(1)}, bf16[2,32,512]{2,1,0:T(8,128)(2,1)S(1)}, u32[]{:S(2)}, u32[]{:S(2)}) collective-permute-start(bf16[2,32,512]{2,1,0:T(8,128)(2,1)S(1)} %get-tuple-element.14.refs_0_), channel_id=1, source_target_pairs={{3,0},{0,1},{1,2},{2,3},{7,4},{4,5},{5,6},{6,7},{11,8},{8,9},{9,10... | collective-permute-start | bytes 196616 | tf_op jit(solution)/shard_map/ppermute | solution.py:307
  112.1 8.7 %collective-permute-start.19 = (bf16[2,32,512]{2,1,0:T(8,128)(2,1)S(1)}, bf16[2,32,512]{2,1,0:T(8,128)(2,1)S(1)}, u32[]{:S(2)}, u32[]{:S(2)}) collective-permute-start(bf16[2,32,512]{2,1,0:T(8,128)(2,1)S(1)} %get-tuple-element.14.refs_0_), channel_id=1, source_target_pairs={{2,0},{3,1},{0,2},{1,3},{6,4},{7,5},{4,6},{5,7},{10,8},{11,9},{8,1... | collective-permute-start | bytes 196616 | tf_op jit(solution)/shard_map/ppermute | solution.py:307
  114.6 6.1 %collective-permute-start.18 = (bf16[2,32,512]{2,1,0:T(8,128)(2,1)S(1)}, bf16[2,32,512]{2,1,0:T(8,128)(2,1)S(1)}, u32[]{:S(2)}, u32[]{:S(2)}) collective-permute-start(bf16[2,32,512]{2,1,0:T(8,128)(2,1)S(1)} %get-tuple-element.14.refs_0_), channel_id=1, source_target_pairs={{1,0},{2,1},{3,2},{0,3},{5,4},{6,5},{7,6},{4,7},{9,8},{10,9},{11,1... | collective-permute-start | bytes 196616 | tf_op jit(solution)/shard_map/ppermute | solution.py:307
  132.0 6.1 %collective-permute-start.23 = (f32[2,32,32]{2,1,0:T(8,128)S(1)}, f32[2,32,32]{2,1,0:T(8,128)S(1)}, u32[]{:S(2)}, u32[]{:S(2)}) collective-permute-start(f32[2,32,32]{2,1,0:T(8,128)S(1)} %get-tuple-element.15), channel_id=1, source_target_pairs={{3,0},{0,1},{1,2},{2,3},{7,4},{4,5},{5,6},{6,7},{11,8},{8,9},{9,10... | collective-permute-start | bytes 24584 | tf_op jit(solution)/shard_map/ppermute | solution.py:307
  133.9 4.3 %collective-permute-start.22 = (f32[2,32,32]{2,1,0:T(8,128)S(1)}, f32[2,32,32]{2,1,0:T(8,128)S(1)}, u32[]{:S(2)}, u32[]{:S(2)}) collective-permute-start(f32[2,32,32]{2,1,0:T(8,128)S(1)} %get-tuple-element.15), channel_id=1, source_target_pairs={{1,0},{2,1},{3,2},{0,3},{5,4},{6,5},{7,6},{4,7},{9,8},{10,9},{11,1... | collective-permute-start | bytes 24584 | tf_op jit(solution)/shard_map/ppermute | solution.py:307
  135.9 4.8 %collective-permute-start.21 = (f32[2,32,32]{2,1,0:T(8,128)S(1)}, f32[2,32,32]{2,1,0:T(8,128)S(1)}, u32[]{:S(2)}, u32[]{:S(2)}) collective-permute-start(f32[2,32,32]{2,1,0:T(8,128)S(1)} %get-tuple-element.15), channel_id=1, source_target_pairs={{2,0},{3,1},{0,2},{1,3},{6,4},{7,5},{4,6},{5,7},{10,8},{11,9},{8,1... | collective-permute-start | bytes 24584 | tf_op jit(solution)/shard_map/ppermute | solution.py:307
  (21 other events, 45.5 us)

commit v2 on v1

--- a/solution.py
+++ b/solution.py
@@ -68,7 +68,7 @@
         ],
         out_specs=[out_spec, out_spec],
         out_shape=[dense, dense],
-        compiler_params=params(40),
+        compiler_params=params(24),
         name="build_dense",
     )(key.reshape(layers, 1, slots), blocks)
 
@@ -172,7 +172,7 @@
             pltpu.VMEM((ROWS_DEV, ROWS_DEV), BF16),
             pltpu.VMEM((TALL, 128), F32),
         ],
-        compiler_params=params(40),
+        compiler_params=params(12),
         name="apply_" + mode,
     )(*operands)
 
@@ -218,6 +218,7 @@
         in_specs=vmem_specs(len(grams) + 1),
         out_specs=pl.BlockSpec(memory_space=pltpu.VMEM),
         out_shape=jax.ShapeDtypeStruct(image.shape, BF16),
+        compiler_params=params(4),
         name="solve_layers",
     )(*grams, image)
 
@@ -248,6 +249,7 @@
         out_specs=pl.BlockSpec(memory_space=pltpu.VMEM),
         out_shape=jax.ShapeDtypeStruct((rows, rows * len(pieces)), F32),
         scratch_shapes=[pltpu.VMEM((rows * len(pieces), width), F32)],
+        compiler_params=params(6),
         name="cross_gram",
     )(*pieces)
 
@@ -296,7 +298,7 @@
             jax.ShapeDtypeStruct(images[0].shape, BF16),
         ],
         scratch_shapes=[pltpu.VMEM((size, size), F32), pltpu.VMEM((size, width), F32)],
-        compiler_params=params(32),
+        compiler_params=params(8),
         name="joint_solve",
     )(*grams, *images)
 

time: 142 us -> 123 us (0.87)
  local copies, waits for them, and re-layouts: 16.1 us -> 4.29 us
  Pallas kernels: 59.1 us -> 53.5 us
    unnamed x42 -> x4, local copies, waits for them, and re-layouts: 16.1 us -> 4.29 us
    pallas_call x1, Pallas kernels: 10.1 us -> 7.86 us  [build_dense(): pl.pallas_call(build_kernel, grid=(layers, chunk_total // per_step), in_s...]
    pallas_call x1, Pallas kernels: 2.36 us -> 0.64 us  [cross(): pl.pallas_call(functools.partial(cross_kernel, len(pieces)), in_specs=vme...]
    pallas_call x1, Pallas kernels: 4.55 us -> 2.92 us  [solve(): pl.pallas_call(functools.partial(solve_kernel, len(grams)), in_specs=vmem...]
  transfers between devices with their start and end apart: 24 -> 24, of which waited for: 16 -> 16; matrix products, arithmetic and copies ran while one was open for 1% -> 1% of each run, Pallas kernels for 7% -> 6%
where the time goes in v2:
time: 123 us
  Pallas kernels  53.5 us (43%)
  starting transfers between devices  32 us (26%)
  waiting for transfers between devices  30 us (24%)
  local copies, waits for them, and re-layouts  4.29 us (3%)
  other arithmetic  2.33 us (2%)
    ppermute x24, starting transfers between devices, around(): lax.ppermute(x, axis, [((m + d) % count, m) for m in range(count)])  32 us
    ppermute x24, waiting for transfers between devices, around(): lax.ppermute(x, axis, [((m + d) % count, m) for m in range(count)])  30 us
    pallas_call x1, Pallas kernels, joint_solve(): pl.pallas_call(functools.partial(joint_kernel, len(images), k), in_specs=...  26.1 us
    pallas_call x3, Pallas kernels, apply_dense(): pl.pallas_call(functools.partial(apply_kernel, mode, len(pieces)), grid=(...  16 us
    pallas_call x1, Pallas kernels, build_dense(): pl.pallas_call(build_kernel, grid=(layers, chunk_total // per_step), in_s...  7.86 us
    unnamed x4, local copies, waits for them, and re-layouts  4.29 us
    pallas_call x1, Pallas kernels, solve(): pl.pallas_call(functools.partial(solve_kernel, len(grams)), in_specs=vmem...  2.92 us
  transfers between devices with their start and end apart: 24, of which 16 were waited for; matrix products, arithmetic and copies ran while one was open for 1% of the time, Pallas kernels for 6%

profile of v2, /device:TPU:0, one launch (start us, length us, event | category | flops | bytes accessed | tf_op | source)
XLA Modules:
  0.0 122.8 jit_solution(9857343814806618275)
XLA Ops:
  1.5 3.1 %collective-permute-start.2 = (bf16[2,32,512]{2,1,0:T(8,128)(2,1)S(1)}, bf16[2,32,512]{2,1,0:T(8,128)(2,1)S(1)}, u32[]{:S(2)}, u32[]{:S(2)}) collective-permute-start(bf16[2,32,512]{2,1,0:T(8,128)(2,1)S(1)} %convert_element_type.3.refs_0_), channel_id=1, source_target_pairs={{3,0},{0,1},{1,2},{2,3},{7,4},{4,5},{5,6},{6,7},{11,8},{8,9},{9,10... | collective-permute-start | bytes 196616 | tf_op jit(solution)/shard_map/ppermute | solution.py:309
  4.6 2.6 %collective-permute-start.1 = (bf16[2,32,512]{2,1,0:T(8,128)(2,1)S(1)}, bf16[2,32,512]{2,1,0:T(8,128)(2,1)S(1)}, u32[]{:S(2)}, u32[]{:S(2)}) collective-permute-start(bf16[2,32,512]{2,1,0:T(8,128)(2,1)S(1)} %convert_element_type.3.refs_0_), channel_id=1, source_target_pairs={{2,0},{3,1},{0,2},{1,3},{6,4},{7,5},{4,6},{5,7},{10,8},{11,9},{8,1... | collective-permute-start | bytes 196616 | tf_op jit(solution)/shard_map/ppermute | solution.py:309
  9.3 3.4 %copy-done = bf16[2,512,4096]{2,1,0:T(8,128)(2,1)S(1)} copy-done((bf16[2,512,4096]{2,1,0:T(8,128)(2,1)S(1)}, bf16[2,512,4096]{2,1,0:T(8,128)(2,1)}, u32[]{:S(2)}) %copy-start) | copy-done | bytes 8388632
  12.7 7.9 %build_dense.1 = (bf16[2,4,256,1024]{3,2,1,0:T(8,128)(2,1)S(1)}, bf16[2,4,256,1024]{3,2,1,0:T(8,128)(2,1)S(1)}) custom-call(s32[2,1,512]{2,1,0:T(1,128)S(1)} %reshape.7.key_ref, bf16[2,512,4096]{2,1,0:T(8,128)(2,1)S(1)} %copy-done), custom_call_target="tpu_custom_call" | custom-call | tf_op jit(solution)/shard_map/build_dense/pallas_call | solution.py:62
  20.6 5.2 %apply_gram.1 = (f32[2,32,512]{2,1,0:T(8,128)S(1)}, f32[2,32,32]{2,1,0:T(8,128)S(1)}) custom-call(bf16[2,32,512]{2,1,0:T(8,128)(2,1)S(1)} %convert_element_type.3.refs_0_, bf16[2,32,512]{2,1,0:T(8,128)(2,1)S(1)} %collective-permute-done.refs_1_, bf16[2,32,512]{2,1,0:T(8,128)(2,1)S(1)} %collective-permute-done.1.refs_2_, ...), custom_call_target="tpu_custom_call" | custom-call | tf_op jit(solution)/shard_map/apply_gram/pallas_call | solution.py:164
  26.9 2.8 %collective-permute-start.3 = (f32[2,32,32]{2,1,0:T(8,128)S(1)}, f32[2,32,32]{2,1,0:T(8,128)S(1)}, u32[]{:S(2)}, u32[]{:S(2)}) collective-permute-start(f32[2,32,32]{2,1,0:T(8,128)S(1)} %get-tuple-element.11.refs_0_), channel_id=1, source_target_pairs={{1,0},{2,1},{3,2},{0,3},{5,4},{6,5},{7,6},{4,7},{9,8},{10,9},{11,1... | collective-permute-start | bytes 24584 | tf_op jit(solution)/shard_map/ppermute | solution.py:309
  29.7 2.0 %collective-permute-done.5.refs_3_ = f32[2,32,32]{2,1,0:T(8,128)S(1)} collective-permute-done((f32[2,32,32]{2,1,0:T(8,128)S(1)}, f32[2,32,32]{2,1,0:T(8,128)S(1)}, u32[]{:S(2)}, u32[]{:S(2)}) %collective-permute-start.5) | collective-permute-done | bytes 8224 | tf_op jit(solution)/shard_map/ppermute | solution.py:309
  32.2 2.9 %solve_layers.1.refs_0_ = bf16[2,32,512]{2,1,0:T(8,128)(2,1)S(1)} custom-call(f32[2,32,32]{2,1,0:T(8,128)S(1)} %get-tuple-element.11.refs_0_, f32[2,32,32]{2,1,0:T(8,128)S(1)} %collective-permute-done.3.refs_1_, f32[2,32,32]{2,1,0:T(8,128)S(1)} %collective-permute-done.4.refs_2_, f32[2,32,32]{2,1,0:T(8,128)S(1)} %collective-permute-done.5.refs_3_, ...), custom_call_target="tpu_custom_call" | custom-call | tf_op jit(solution)/shard_map/solve_layers/pallas_call | solution.py:216
  35.2 1.9 %collective-permute-start.8 = (bf16[2,32,512]{2,1,0:T(8,128)(2,1)S(1)}, bf16[2,32,512]{2,1,0:T(8,128)(2,1)S(1)}, u32[]{:S(2)}, u32[]{:S(2)}) collective-permute-start(bf16[2,32,512]{2,1,0:T(8,128)(2,1)S(1)} %solve_layers.1.refs_0_), channel_id=1, source_target_pairs={{3,0},{0,1},{1,2},{2,3},{7,4},{4,5},{5,6},{6,7},{11,8},{8,9},{9,10... | collective-permute-start | bytes 196616 | tf_op jit(solution)/shard_map/ppermute | solution.py:309
  37.1 1.8 %collective-permute-start.7 = (bf16[2,32,512]{2,1,0:T(8,128)(2,1)S(1)}, bf16[2,32,512]{2,1,0:T(8,128)(2,1)S(1)}, u32[]{:S(2)}, u32[]{:S(2)}) collective-permute-start(bf16[2,32,512]{2,1,0:T(8,128)(2,1)S(1)} %solve_layers.1.refs_0_), channel_id=1, source_target_pairs={{2,0},{3,1},{0,2},{1,3},{6,4},{7,5},{4,6},{5,7},{10,8},{11,9},{8,1... | collective-permute-start | bytes 196616 | tf_op jit(solution)/shard_map/ppermute | solution.py:309
  43.3 4.8 %apply_plain.1.refs_0_.refs_4_ = f32[2,32,512]{2,1,0:T(8,128)S(1)} custom-call(bf16[2,32,512]{2,1,0:T(8,128)(2,1)S(1)} %solve_layers.1.refs_0_, bf16[2,32,512]{2,1,0:T(8,128)(2,1)S(1)} %collective-permute-done.6.refs_1_, bf16[2,32,512]{2,1,0:T(8,128)(2,1)S(1)} %collective-permute-done.7.refs_2_, bf16[2,32,512]{2,1,0:T(8,128)(2,1)S(1)} %collective-permute-done.8.refs_3_, ...), custom_call_target="tpu_custom_call" | custom-call | tf_op jit(solution)/shard_map/apply_plain/pallas_call | solution.py:164
  51.1 2.3 %collective-permute-done.11.refs_3_.refs_7_ = f32[2,32,512]{2,1,0:T(8,128)S(1)} collective-permute-done((f32[2,32,512]{2,1,0:T(8,128)S(1)}, f32[2,32,512]{2,1,0:T(8,128)S(1)}, u32[]{:S(2)}, u32[]{:S(2)}) %collective-permute-start.11) | collective-permute-done | bytes 131104 | tf_op jit(solution)/shard_map/ppermute | solution.py:309
  57.0 3.3 %collective-permute-start.13 = (f32[64,256]{1,0:T(8,128)S(1)}, f32[64,256]{1,0:T(8,128)S(1)}, u32[]{:S(2)}, u32[]{:S(2)}) collective-permute-start(f32[64,256]{1,0:T(8,128)S(1)} %cross_gram.1), channel_id=1, source_target_pairs={{1,0},{2,1},{3,2},{0,3},{5,4},{6,5},{7,6},{4,7},{9,8},{10,9},{11,1... | collective-permute-start | bytes 196616 | tf_op jit(solution)/shard_map/ppermute | solution.py:309
  60.3 3.0 %collective-permute-done.14 = f32[64,256]{1,0:T(8,128)S(1)} collective-permute-done((f32[64,256]{1,0:T(8,128)S(1)}, f32[64,256]{1,0:T(8,128)S(1)}, u32[]{:S(2)}, u32[]{:S(2)}) %collective-permute-start.14) | collective-permute-done | bytes 65568 | tf_op jit(solution)/shard_map/ppermute | solution.py:309
  63.3 3.6 %collective-permute-done.12 = f32[64,256]{1,0:T(8,128)S(1)} collective-permute-done((f32[64,256]{1,0:T(8,128)S(1)}, f32[64,256]{1,0:T(8,128)S(1)}, u32[]{:S(2)}, u32[]{:S(2)}) %collective-permute-start.12) | collective-permute-done | bytes 65568 | tf_op jit(solution)/shard_map/ppermute | solution.py:309
  71.9 26.1 %joint_solve.1 = (f32[2,32,512]{2,1,0:T(8,128)}, bf16[2,32,512]{2,1,0:T(8,128)(2,1)S(1)}) custom-call(f32[64,256]{1,0:T(8,128)S(1)} %add_add_fusion.refs_0_, f32[64,256]{1,0:T(8,128)S(1)} %collective-permute-done.15.refs_1_, f32[64,256]{1,0:T(8,128)S(1)} %collective-permute-done.16.refs_2_, f32[64,256]{1,0:T(8,128)S(1)} %collective-permute-done.17.refs_3_, ...), custom_call_target="tpu_custom_call" | custom-call | tf_op jit(solution)/shard_map/joint_solve/pallas_call | solution.py:292
  98.0 2.5 %collective-permute-start.19 = (bf16[2,32,512]{2,1,0:T(8,128)(2,1)S(1)}, bf16[2,32,512]{2,1,0:T(8,128)(2,1)S(1)}, u32[]{:S(2)}, u32[]{:S(2)}) collective-permute-start(bf16[2,32,512]{2,1,0:T(8,128)(2,1)S(1)} %get-tuple-element.14.refs_0_), channel_id=1, source_target_pairs={{2,0},{3,1},{0,2},{1,3},{6,4},{7,5},{4,6},{5,7},{10,8},{11,9},{8,1... | collective-permute-start | bytes 196616 | tf_op jit(solution)/shard_map/ppermute | solution.py:309
  101.9 2.9 %collective-permute-done.20.refs_3_ = bf16[2,32,512]{2,1,0:T(8,128)(2,1)S(1)} collective-permute-done((bf16[2,32,512]{2,1,0:T(8,128)(2,1)S(1)}, bf16[2,32,512]{2,1,0:T(8,128)(2,1)S(1)}, u32[]{:S(2)}, u32[]{:S(2)}) %collective-permute-start.20) | collective-permute-done | bytes 65568 | tf_op jit(solution)/shard_map/ppermute | solution.py:309
  104.8 1.8 %collective-permute-done.19.refs_2_ = bf16[2,32,512]{2,1,0:T(8,128)(2,1)S(1)} collective-permute-done((bf16[2,32,512]{2,1,0:T(8,128)(2,1)S(1)}, bf16[2,32,512]{2,1,0:T(8,128)(2,1)S(1)}, u32[]{:S(2)}, u32[]{:S(2)}) %collective-permute-start.19) | collective-permute-done | bytes 65568 | tf_op jit(solution)/shard_map/ppermute | solution.py:309
  107.5 6.0 %apply_score.1 = (f32[2,32,512]{2,1,0:T(8,128)}, f32[2,32,32]{2,1,0:T(8,128)S(1)}) custom-call(bf16[2,32,512]{2,1,0:T(8,128)(2,1)S(1)} %get-tuple-element.14.refs_0_, bf16[2,32,512]{2,1,0:T(8,128)(2,1)S(1)} %collective-permute-done.18.refs_1_, bf16[2,32,512]{2,1,0:T(8,128)(2,1)S(1)} %collective-permute-done.19.refs_2_, ...), custom_call_target="tpu_custom_call" | custom-call | tf_op jit(solution)/shard_map/apply_score/pallas_call | solution.py:164
  113.5 1.7 %collective-permute-start.23 = (f32[2,32,32]{2,1,0:T(8,128)S(1)}, f32[2,32,32]{2,1,0:T(8,128)S(1)}, u32[]{:S(2)}, u32[]{:S(2)}) collective-permute-start(f32[2,32,32]{2,1,0:T(8,128)S(1)} %get-tuple-element.15), channel_id=1, source_target_pairs={{3,0},{0,1},{1,2},{2,3},{7,4},{4,5},{5,6},{6,7},{11,8},{8,9},{9,10... | collective-permute-start | bytes 24584 | tf_op jit(solution)/shard_map/ppermute | solution.py:309
  115.2 2.1 %collective-permute-start.22 = (f32[2,32,32]{2,1,0:T(8,128)S(1)}, f32[2,32,32]{2,1,0:T(8,128)S(1)}, u32[]{:S(2)}, u32[]{:S(2)}) collective-permute-start(f32[2,32,32]{2,1,0:T(8,128)S(1)} %get-tuple-element.15), channel_id=1, source_target_pairs={{1,0},{2,1},{3,2},{0,3},{5,4},{6,5},{7,6},{4,7},{9,8},{10,9},{11,1... | collective-permute-start | bytes 24584 | tf_op jit(solution)/shard_map/ppermute | solution.py:309
  117.3 2.2 %collective-permute-done.23 = f32[2,32,32]{2,1,0:T(8,128)S(1)} collective-permute-done((f32[2,32,32]{2,1,0:T(8,128)S(1)}, f32[2,32,32]{2,1,0:T(8,128)S(1)}, u32[]{:S(2)}, u32[]{:S(2)}) %collective-permute-start.23) | collective-permute-done | bytes 8224 | tf_op jit(solution)/shard_map/ppermute | solution.py:309
  119.5 2.7 %collective-permute-done.21 = f32[2,32,32]{2,1,0:T(8,128)S(1)} collective-permute-done((f32[2,32,32]{2,1,0:T(8,128)S(1)}, f32[2,32,32]{2,1,0:T(8,128)S(1)}, u32[]{:S(2)}, u32[]{:S(2)}) %collective-permute-start.21) | collective-permute-done | bytes 8224 | tf_op jit(solution)/shard_map/ppermute | solution.py:309
  (40 shorter events, 23.7 us)
Async XLA Ops:
  1.5 19.0 %collective-permute-start.2 = (bf16[2,32,512]{2,1,0:T(8,128)(2,1)S(1)}, bf16[2,32,512]{2,1,0:T(8,128)(2,1)S(1)}, u32[]{:S(2)}, u32[]{:S(2)}) collective-permute-start(bf16[2,32,512]{2,1,0:T(8,128)(2,1)S(1)} %convert_element_type.3.refs_0_), channel_id=1, source_target_pairs={{3,0},{0,1},{1,2},{2,3},{7,4},{4,5},{5,6},{6,7},{11,8},{8,9},{9,10... | collective-permute-start | bytes 196616 | tf_op jit(solution)/shard_map/ppermute | solution.py:309
  4.6 16.0 %collective-permute-start.1 = (bf16[2,32,512]{2,1,0:T(8,128)(2,1)S(1)}, bf16[2,32,512]{2,1,0:T(8,128)(2,1)S(1)}, u32[]{:S(2)}, u32[]{:S(2)}) collective-permute-start(bf16[2,32,512]{2,1,0:T(8,128)(2,1)S(1)} %convert_element_type.3.refs_0_), channel_id=1, source_target_pairs={{2,0},{3,1},{0,2},{1,3},{6,4},{7,5},{4,6},{5,7},{10,8},{11,9},{8,1... | collective-permute-start | bytes 196616 | tf_op jit(solution)/shard_map/ppermute | solution.py:309
  7.2 13.4 %collective-permute-start = (bf16[2,32,512]{2,1,0:T(8,128)(2,1)S(1)}, bf16[2,32,512]{2,1,0:T(8,128)(2,1)S(1)}, u32[]{:S(2)}, u32[]{:S(2)}) collective-permute-start(bf16[2,32,512]{2,1,0:T(8,128)(2,1)S(1)} %convert_element_type.3.refs_0_), channel_id=1, source_target_pairs={{1,0},{2,1},{3,2},{0,3},{5,4},{6,5},{7,6},{4,7},{9,8},{10,9},{11,1... | collective-permute-start | bytes 196616 | tf_op jit(solution)/shard_map/ppermute | solution.py:309
  25.8 5.8 %collective-permute-start.5 = (f32[2,32,32]{2,1,0:T(8,128)S(1)}, f32[2,32,32]{2,1,0:T(8,128)S(1)}, u32[]{:S(2)}, u32[]{:S(2)}) collective-permute-start(f32[2,32,32]{2,1,0:T(8,128)S(1)} %get-tuple-element.11.refs_0_), channel_id=1, source_target_pairs={{3,0},{0,1},{1,2},{2,3},{7,4},{4,5},{5,6},{6,7},{11,8},{8,9},{9,10... | collective-permute-start | bytes 24584 | tf_op jit(solution)/shard_map/ppermute | solution.py:309
  26.5 5.7 %collective-permute-start.4 = (f32[2,32,32]{2,1,0:T(8,128)S(1)}, f32[2,32,32]{2,1,0:T(8,128)S(1)}, u32[]{:S(2)}, u32[]{:S(2)}) collective-permute-start(f32[2,32,32]{2,1,0:T(8,128)S(1)} %get-tuple-element.11.refs_0_), channel_id=1, source_target_pairs={{2,0},{3,1},{0,2},{1,3},{6,4},{7,5},{4,6},{5,7},{10,8},{11,9},{8,1... | collective-permute-start | bytes 24584 | tf_op jit(solution)/shard_map/ppermute | solution.py:309
  26.9 5.4 %collective-permute-start.3 = (f32[2,32,32]{2,1,0:T(8,128)S(1)}, f32[2,32,32]{2,1,0:T(8,128)S(1)}, u32[]{:S(2)}, u32[]{:S(2)}) collective-permute-start(f32[2,32,32]{2,1,0:T(8,128)S(1)} %get-tuple-element.11.refs_0_), channel_id=1, source_target_pairs={{1,0},{2,1},{3,2},{0,3},{5,4},{6,5},{7,6},{4,7},{9,8},{10,9},{11,1... | collective-permute-start | bytes 24584 | tf_op jit(solution)/shard_map/ppermute | solution.py:309
  35.2 6.1 %collective-permute-start.8 = (bf16[2,32,512]{2,1,0:T(8,128)(2,1)S(1)}, bf16[2,32,512]{2,1,0:T(8,128)(2,1)S(1)}, u32[]{:S(2)}, u32[]{:S(2)}) collective-permute-start(bf16[2,32,512]{2,1,0:T(8,128)(2,1)S(1)} %solve_layers.1.refs_0_), channel_id=1, source_target_pairs={{3,0},{0,1},{1,2},{2,3},{7,4},{4,5},{5,6},{6,7},{11,8},{8,9},{9,10... | collective-permute-start | bytes 196616 | tf_op jit(solution)/shard_map/ppermute | solution.py:309
  37.1 5.6 %collective-permute-start.7 = (bf16[2,32,512]{2,1,0:T(8,128)(2,1)S(1)}, bf16[2,32,512]{2,1,0:T(8,128)(2,1)S(1)}, u32[]{:S(2)}, u32[]{:S(2)}) collective-permute-start(bf16[2,32,512]{2,1,0:T(8,128)(2,1)S(1)} %solve_layers.1.refs_0_), channel_id=1, source_target_pairs={{2,0},{3,1},{0,2},{1,3},{6,4},{7,5},{4,6},{5,7},{10,8},{11,9},{8,1... | collective-permute-start | bytes 196616 | tf_op jit(solution)/shard_map/ppermute | solution.py:309
  38.9 4.4 %collective-permute-start.6 = (bf16[2,32,512]{2,1,0:T(8,128)(2,1)S(1)}, bf16[2,32,512]{2,1,0:T(8,128)(2,1)S(1)}, u32[]{:S(2)}, u32[]{:S(2)}) collective-permute-start(bf16[2,32,512]{2,1,0:T(8,128)(2,1)S(1)} %solve_layers.1.refs_0_), channel_id=1, source_target_pairs={{1,0},{2,1},{3,2},{0,3},{5,4},{6,5},{7,6},{4,7},{9,8},{10,9},{11,1... | collective-permute-start | bytes 196616 | tf_op jit(solution)/shard_map/ppermute | solution.py:309
  48.1 5.3 %collective-permute-start.11 = (f32[2,32,512]{2,1,0:T(8,128)S(1)}, f32[2,32,512]{2,1,0:T(8,128)S(1)}, u32[]{:S(2)}, u32[]{:S(2)}) collective-permute-start(f32[2,32,512]{2,1,0:T(8,128)S(1)} %apply_plain.1.refs_0_.refs_4_), channel_id=1, source_target_pairs={{12,0},{0,4},{4,8},{8,12},{13,1},{1,5},{5,9},{9,13},{14,2},{2,6},{... | collective-permute-start | bytes 393224 | tf_op jit(solution)/shard_map/ppermute | solution.py:309
  48.1 6.4 %collective-permute-start.10 = (f32[2,32,512]{2,1,0:T(8,128)S(1)}, f32[2,32,512]{2,1,0:T(8,128)S(1)}, u32[]{:S(2)}, u32[]{:S(2)}) collective-permute-start(f32[2,32,512]{2,1,0:T(8,128)S(1)} %apply_plain.1.refs_0_.refs_4_), channel_id=1, source_target_pairs={{8,0},{12,4},{0,8},{4,12},{9,1},{13,5},{1,9},{5,13},{10,2},{14,6},... | collective-permute-start | bytes 393224 | tf_op jit(solution)/shard_map/ppermute | solution.py:309
  49.7 6.1 %collective-permute-start.9 = (f32[2,32,512]{2,1,0:T(8,128)S(1)}, f32[2,32,512]{2,1,0:T(8,128)S(1)}, u32[]{:S(2)}, u32[]{:S(2)}) collective-permute-start(f32[2,32,512]{2,1,0:T(8,128)S(1)} %apply_plain.1.refs_0_.refs_4_), channel_id=1, source_target_pairs={{4,0},{8,4},{12,8},{0,12},{5,1},{9,5},{13,9},{1,13},{6,2},{10,6},{... | collective-permute-start | bytes 393224 | tf_op jit(solution)/shard_map/ppermute | solution.py:309
  56.4 6.9 %collective-permute-start.14 = (f32[64,256]{1,0:T(8,128)S(1)}, f32[64,256]{1,0:T(8,128)S(1)}, u32[]{:S(2)}, u32[]{:S(2)}) collective-permute-start(f32[64,256]{1,0:T(8,128)S(1)} %cross_gram.1), channel_id=1, source_target_pairs={{3,0},{0,1},{1,2},{2,3},{7,4},{4,5},{5,6},{6,7},{11,8},{8,9},{9,10... | collective-permute-start | bytes 196616 | tf_op jit(solution)/shard_map/ppermute | solution.py:309
  57.0 6.2 %collective-permute-start.13 = (f32[64,256]{1,0:T(8,128)S(1)}, f32[64,256]{1,0:T(8,128)S(1)}, u32[]{:S(2)}, u32[]{:S(2)}) collective-permute-start(f32[64,256]{1,0:T(8,128)S(1)} %cross_gram.1), channel_id=1, source_target_pairs={{1,0},{2,1},{3,2},{0,3},{5,4},{6,5},{7,6},{4,7},{9,8},{10,9},{11,1... | collective-permute-start | bytes 196616 | tf_op jit(solution)/shard_map/ppermute | solution.py:309
  60.3 6.6 %collective-permute-start.12 = (f32[64,256]{1,0:T(8,128)S(1)}, f32[64,256]{1,0:T(8,128)S(1)}, u32[]{:S(2)}, u32[]{:S(2)}) collective-permute-start(f32[64,256]{1,0:T(8,128)S(1)} %cross_gram.1), channel_id=1, source_target_pairs={{2,0},{3,1},{0,2},{1,3},{6,4},{7,5},{4,6},{5,7},{10,8},{11,9},{8,1... | collective-permute-start | bytes 196616 | tf_op jit(solution)/shard_map/ppermute | solution.py:309
  66.8 3.8 %collective-permute-start.17 = (f32[64,256]{1,0:T(8,128)S(1)}, f32[64,256]{1,0:T(8,128)S(1)}, u32[]{:S(2)}, u32[]{:S(2)}) collective-permute-start(f32[64,256]{1,0:T(8,128)S(1)} %add_add_fusion.refs_0_), channel_id=1, source_target_pairs={{12,0},{0,4},{4,8},{8,12},{13,1},{1,5},{5,9},{9,13},{14,2},{2,6},{... | collective-permute-start | bytes 196616 | tf_op jit(solution)/shard_map/ppermute | solution.py:309
  66.9 5.0 %collective-permute-start.16 = (f32[64,256]{1,0:T(8,128)S(1)}, f32[64,256]{1,0:T(8,128)S(1)}, u32[]{:S(2)}, u32[]{:S(2)}) collective-permute-start(f32[64,256]{1,0:T(8,128)S(1)} %add_add_fusion.refs_0_), channel_id=1, source_target_pairs={{8,0},{12,4},{0,8},{4,12},{9,1},{13,5},{1,9},{5,13},{10,2},{14,6},... | collective-permute-start | bytes 196616 | tf_op jit(solution)/shard_map/ppermute | solution.py:309
  67.7 4.2 %collective-permute-start.15 = (f32[64,256]{1,0:T(8,128)S(1)}, f32[64,256]{1,0:T(8,128)S(1)}, u32[]{:S(2)}, u32[]{:S(2)}) collective-permute-start(f32[64,256]{1,0:T(8,128)S(1)} %add_add_fusion.refs_0_), channel_id=1, source_target_pairs={{4,0},{8,4},{12,8},{0,12},{5,1},{9,5},{13,9},{1,13},{6,2},{10,6},{... | collective-permute-start | bytes 196616 | tf_op jit(solution)/shard_map/ppermute | solution.py:309
  98.0 6.8 %collective-permute-start.20 = (bf16[2,32,512]{2,1,0:T(8,128)(2,1)S(1)}, bf16[2,32,512]{2,1,0:T(8,128)(2,1)S(1)}, u32[]{:S(2)}, u32[]{:S(2)}) collective-permute-start(bf16[2,32,512]{2,1,0:T(8,128)(2,1)S(1)} %get-tuple-element.14.refs_0_), channel_id=1, source_target_pairs={{3,0},{0,1},{1,2},{2,3},{7,4},{4,5},{5,6},{6,7},{11,8},{8,9},{9,10... | collective-permute-start | bytes 196616 | tf_op jit(solution)/shard_map/ppermute | solution.py:309
  98.0 8.6 %collective-permute-start.19 = (bf16[2,32,512]{2,1,0:T(8,128)(2,1)S(1)}, bf16[2,32,512]{2,1,0:T(8,128)(2,1)S(1)}, u32[]{:S(2)}, u32[]{:S(2)}) collective-permute-start(bf16[2,32,512]{2,1,0:T(8,128)(2,1)S(1)} %get-tuple-element.14.refs_0_), channel_id=1, source_target_pairs={{2,0},{3,1},{0,2},{1,3},{6,4},{7,5},{4,6},{5,7},{10,8},{11,9},{8,1... | collective-permute-start | bytes 196616 | tf_op jit(solution)/shard_map/ppermute | solution.py:309
  100.5 6.1 %collective-permute-start.18 = (bf16[2,32,512]{2,1,0:T(8,128)(2,1)S(1)}, bf16[2,32,512]{2,1,0:T(8,128)(2,1)S(1)}, u32[]{:S(2)}, u32[]{:S(2)}) collective-permute-start(bf16[2,32,512]{2,1,0:T(8,128)(2,1)S(1)} %get-tuple-element.14.refs_0_), channel_id=1, source_target_pairs={{1,0},{2,1},{3,2},{0,3},{5,4},{6,5},{7,6},{4,7},{9,8},{10,9},{11,1... | collective-permute-start | bytes 196616 | tf_op jit(solution)/shard_map/ppermute | solution.py:309
  113.5 6.0 %collective-permute-start.23 = (f32[2,32,32]{2,1,0:T(8,128)S(1)}, f32[2,32,32]{2,1,0:T(8,128)S(1)}, u32[]{:S(2)}, u32[]{:S(2)}) collective-permute-start(f32[2,32,32]{2,1,0:T(8,128)S(1)} %get-tuple-element.15), channel_id=1, source_target_pairs={{3,0},{0,1},{1,2},{2,3},{7,4},{4,5},{5,6},{6,7},{11,8},{8,9},{9,10... | collective-permute-start | bytes 24584 | tf_op jit(solution)/shard_map/ppermute | solution.py:309
  115.2 4.3 %collective-permute-start.22 = (f32[2,32,32]{2,1,0:T(8,128)S(1)}, f32[2,32,32]{2,1,0:T(8,128)S(1)}, u32[]{:S(2)}, u32[]{:S(2)}) collective-permute-start(f32[2,32,32]{2,1,0:T(8,128)S(1)} %get-tuple-element.15), channel_id=1, source_target_pairs={{1,0},{2,1},{3,2},{0,3},{5,4},{6,5},{7,6},{4,7},{9,8},{10,9},{11,1... | collective-permute-start | bytes 24584 | tf_op jit(solution)/shard_map/ppermute | solution.py:309
  117.3 4.8 %collective-permute-start.21 = (f32[2,32,32]{2,1,0:T(8,128)S(1)}, f32[2,32,32]{2,1,0:T(8,128)S(1)}, u32[]{:S(2)}, u32[]{:S(2)}) collective-permute-start(f32[2,32,32]{2,1,0:T(8,128)S(1)} %get-tuple-element.15), channel_id=1, source_target_pairs={{2,0},{3,1},{0,2},{1,3},{6,4},{7,5},{4,6},{5,7},{10,8},{11,9},{8,1... | collective-permute-start | bytes 24584 | tf_op jit(solution)/shard_map/ppermute | solution.py:309
  (2 other events, 4.3 us)

commit v3 on v2

--- a/solution.py
+++ b/solution.py
@@ -81,30 +81,29 @@
     return a, b, c
 
 
-def apply_kernel(mode, piece_count, *refs):
-    pieces = refs[:piece_count]
-    refs = refs[piece_count:]
+def spread_copies(x, ref):
+    return jnp.broadcast_to(x[None, None], ref.shape)
+
+
+def apply_kernel(mode, *refs):
+    pieces, refs = refs[0], refs[1:]
     if mode == "score":
         left_ref, refs = refs[0], refs[1:]
     hi_ref, lo_ref, out_ref = refs[:3]
     gram_ref = refs[3] if mode != "plain" else None
-    basis, perm, acc = refs[-3:]
+    perm, acc = refs[-2:]
     layer, chunk = pl.program_id(0), pl.program_id(1)
-    k = pieces[0].shape[1]
+    k = pieces.shape[2]
 
     @pl.when((layer == 0) & (chunk == 0))
     def _():
-        at = 0
-        for piece in pieces:
-            basis[:, :, at : at + piece.shape[2]] = piece[...].astype(BF16)
-            at += piece.shape[2]
         row = lax.broadcasted_iota(jnp.int32, (ROWS_DEV, ROWS_DEV), 0)
         col = lax.broadcasted_iota(jnp.int32, (ROWS_DEV, ROWS_DEV), 1)
         target = (row % 8) * BLK + 2 * ((row % TALL) // 8) + row // TALL
         perm[...] = jnp.where(target == col, 1.0, 0.0).astype(BF16)
 
     width = CHUNK_COLS * BLK
-    here = basis[layer, :, pl.ds(pl.multiple_of(chunk * width, width), width)].astype(F32)
+    here = pieces[chunk, layer].astype(F32)
     low = lax.broadcasted_iota(jnp.int32, (k, 128), 1) < BLK
     first, second = [], []
     for q in range(width // 128):
@@ -140,87 +139,144 @@
         image = moved[:k] + moved[k : 2 * k] + moved[2 * k :]
         out_ref[0] = image
         if mode == "gram":
-            gram_ref[0] = lax.dot_general(image, image, TRANS_B, precision=HIGHEST, preferred_element_type=F32)
+            gram_ref[...] = spread_copies(lax.dot_general(image, image, TRANS_B, precision=HIGHEST, preferred_element_type=F32), gram_ref)
         if mode == "score":
-            gram_ref[0] = lax.dot_general(
-                left_ref[0], image, TRANS_B, precision=HIGHEST, preferred_element_type=F32
-            )
-
-
-def apply_dense(mode, pieces, hi, lo, left=None):
+            gram_ref[...] = spread_copies(lax.dot_general(left_ref[0], image, TRANS_B, precision=HIGHEST, preferred_element_type=F32), gram_ref)
+
+
+def apply_dense(mode, basis, hi, lo, left=None):
     layers, chunks = hi.shape[:2]
-    k = pieces[0].shape[1]
-    nodes = sum(piece.shape[2] for piece in pieces)
+    k = basis.shape[2]
     dense_spec = pl.BlockSpec((1, 1, TALL, CHUNK_LANES), lambda l, s: (l, s, 0, 0))
     image_spec = pl.BlockSpec((1, k, ROWS_DEV), lambda l, s: (l, 0, 0))
-    small_spec = pl.BlockSpec((1, k, k), lambda l, s: (l, 0, 0))
+    small_spec = pl.BlockSpec((chunks, 1, k, k), lambda l, s: (0, l, 0, 0))
     out_shape = [jax.ShapeDtypeStruct((layers, k, ROWS_DEV), F32)]
     out_specs = [image_spec]
     if mode != "plain":
-        out_shape.append(jax.ShapeDtypeStruct((layers, k, k), F32))
+        out_shape.append(jax.ShapeDtypeStruct((chunks, layers, k, k), F32))
         out_specs.append(small_spec)
-    operands = list(pieces) + ([left] if mode == "score" else []) + [hi, lo]
-    in_specs = vmem_specs(len(pieces)) + ([image_spec] if mode == "score" else []) + [dense_spec, dense_spec]
+    operands = [basis] + ([left] if mode == "score" else []) + [hi, lo]
+    in_specs = vmem_specs(1) + ([image_spec] if mode == "score" else []) + [dense_spec, dense_spec]
     return pl.pallas_call(
-        functools.partial(apply_kernel, mode, len(pieces)),
+        functools.partial(apply_kernel, mode),
         grid=(layers, chunks),
         in_specs=in_specs,
         out_specs=out_specs,
         out_shape=out_shape,
-        scratch_shapes=[
-            pltpu.VMEM((layers, k, nodes), BF16),
-            pltpu.VMEM((ROWS_DEV, ROWS_DEV), BF16),
-            pltpu.VMEM((TALL, 128), F32),
-        ],
+        scratch_shapes=[pltpu.VMEM((ROWS_DEV, ROWS_DEV), BF16), pltpu.VMEM((TALL, 128), F32)],
         compiler_params=params(12),
         name="apply_" + mode,
     )(*operands)
 
 
-def eliminate(panel, tail, offset):
-    k = panel.shape[0]
-    row_at = lax.broadcasted_iota(jnp.int32, (k, 1), 0)
-    for j in range(k):
-        row = panel[j : j + 1]
-        pivot = row[:, offset + j : offset + j + 1]
-        column = panel[:, offset + j : offset + j + 1]
-        factor = jnp.where(row_at > j, column / pivot, 0.0)
-        panel = panel - factor * row
-        tail = tail - factor * tail[j : j + 1]
-    lane = lax.broadcasted_iota(jnp.int32, panel.shape, 1)
-    sub = lax.broadcasted_iota(jnp.int32, panel.shape, 0)
-    diagonal = jnp.sum(jnp.where(lane == sub + offset, panel, 0.0), axis=1, keepdims=True)
-    scale = 1.0 / jnp.sqrt(diagonal)
-    return panel * scale, tail * scale
-
-
-def solve_kernel(piece_count, *refs):
-    grams, image_ref, out_ref = refs[:piece_count], refs[piece_count], refs[piece_count + 1]
+def reciprocal(x):
+    r = pl.reciprocal(x, approx=True)
+    r = r * (2.0 - x * r)
+    return r * (2.0 - x * r)
+
+
+def eliminate(rows, offset):
+    k, width = rows.shape
+    groups = [rows[g * 8 : g * 8 + 8] for g in range(k // 8)]
+    sub = lax.broadcasted_iota(jnp.int32, (8, 128), 0)
+
+    def spread(x, size):
+        return jnp.broadcast_to(x, (8, size))
+
+    for base in range(0, k, 4):
+        active = range(base // 8, k // 8)
+        home, at = base // 8, base % 8
+        cols = [
+            {g: spread(groups[g][:, offset + base + q : offset + base + q + 1], 128) for g in active}
+            for q in range(4)
+        ]
+        row = [spread(groups[home][at + q : at + q + 1], width) for q in range(4)]
+        cell = {}
+        for q in range(4):
+            for p in range(q + 1):
+                cell[p, q] = spread(cols[p][home][at + q : at + q + 1], 128)
+        pairs = []
+        for m in (0, 2):
+            a, b, c = cell[m, m], cell[m, m + 1], cell[m + 1, m + 1]
+            r = reciprocal(a * c - b * b)
+            i00, i01, i11 = c * r, -b * r, a * r
+            f0 = {g: cols[m][g] * i00 + cols[m + 1][g] * i01 for g in active}
+            f1 = {g: cols[m][g] * i01 + cols[m + 1][g] * i11 for g in active}
+            if m == 0:
+                e0 = [cell[0, q] * i00 + cell[1, q] * i01 for q in (2, 3)]
+                e1 = [cell[0, q] * i01 + cell[1, q] * i11 for q in (2, 3)]
+                for q in (2, 3):
+                    for p in range(2, q + 1):
+                        cell[p, q] = cell[p, q] - e0[p - 2] * cell[0, q] - e1[p - 2] * cell[1, q]
+                    cols[q] = {g: cols[q][g] - f0[g] * cell[0, q] - f1[g] * cell[1, q] for g in active}
+                    row[q] = (
+                        row[q]
+                        - jnp.tile(e0[q - 2], (1, width // 128)) * row[0]
+                        - jnp.tile(e1[q - 2], (1, width // 128)) * row[1]
+                    )
+            f0 = {g: jnp.where(sub > base + m + 1 - 8 * g, f0[g], 0.0) for g in active}
+            f1 = {g: jnp.where(sub > base + m + 1 - 8 * g, f1[g], 0.0) for g in active}
+            f0[home] = jnp.where(sub == at + m + 1, b * reciprocal(a), f0[home])
+            pairs.append((f0, f1))
+        for g in active:
+            x = groups[g]
+            for m, (f0, f1) in enumerate(pairs):
+                x = x - jnp.tile(f0[g], (1, width // 128)) * row[2 * m]
+                x = x - jnp.tile(f1[g], (1, width // 128)) * row[2 * m + 1]
+            groups[g] = x
+    rows = jnp.concatenate(groups, axis=0)
+    tile = offset // 128 * 128
+    diagonal = diagonal_of(rows[:, tile : tile + 128], offset - tile)
+    return rows * (1.0 / jnp.sqrt(diagonal))
+
+
+def diagonal_of(block, offset):
+    lane = lax.broadcasted_iota(jnp.int32, block.shape, 1)
+    sub = lax.broadcasted_iota(jnp.int32, block.shape, 0)
+    return jnp.sum(jnp.where(lane == sub + offset, block, 0.0), axis=1, keepdims=True)
+
+
+def unit_scale(gram):
+    lane = lax.broadcasted_iota(jnp.int32, gram.shape, 1)
+    sub = lax.broadcasted_iota(jnp.int32, gram.shape, 0)
+    kept = jnp.where(lane == sub, gram, 0.0)
+    down = 1.0 / jnp.sqrt(jnp.sum(kept, axis=1, keepdims=True))
+    across = jnp.sum(kept, axis=0, keepdims=True)
+    across = 1.0 / jnp.sqrt(jnp.where(across == 0.0, 1.0, across))
+    return gram * down * across, across
+
+
+def gram_update(left, right):
+    a, b = split3(left), split3(right)
+    left = jnp.concatenate([a[0], a[0], a[1], a[1], a[0], a[2]], axis=0)
+    right = jnp.concatenate([b[0], b[1], b[0], b[1], b[2], b[0]], axis=0)
+    return lax.dot_general(left, right, TRANS_A, preferred_element_type=F32)
+
+
+def solve_kernel(grams_ref, image_ref, out_ref):
     layers, k = image_ref.shape[:2]
     lane = lax.broadcasted_iota(jnp.int32, (k, 128), 1)
     sub = lax.broadcasted_iota(jnp.int32, (k, 128), 0)
     eye = jnp.where(lane == sub, 1.0, 0.0)
     for layer in range(layers):
-        values = [ref[layer] for ref in grams]
-        if piece_count == 4:
-            gram = (values[0] + values[2]) + (values[1] + values[3])
-        else:
-            gram = values[0]
+        gram = sum(grams_ref[m, layer] for m in range(grams_ref.shape[0]))
         gram = jnp.concatenate([gram, jnp.zeros((k, 128 - k), F32)], axis=1)
-        inverse = eliminate(gram, eye, 0)[1][:, :k]
-        solved = jnp.dot(inverse, image_ref[layer], precision=HIGHEST, preferred_element_type=F32)
-        out_ref[layer] = solved.astype(BF16)
-
-
-def solve(grams, image):
+        gram, across = unit_scale(gram)
+        inverse = eliminate(jnp.concatenate([gram, eye], axis=1), 0)[:, 128:] * across
+        solved = jnp.dot(inverse[:, :k], image_ref[layer], precision=HIGHEST, preferred_element_type=F32)
+        for copy in range(out_ref.shape[0]):
+            out_ref[copy, layer] = solved.astype(BF16)
+
+
+def solve(grams, image, copies):
     return pl.pallas_call(
-        functools.partial(solve_kernel, len(grams)),
-        in_specs=vmem_specs(len(grams) + 1),
+        solve_kernel,
+        in_specs=vmem_specs(2),
         out_specs=pl.BlockSpec(memory_space=pltpu.VMEM),
-        out_shape=jax.ShapeDtypeStruct(image.shape, BF16),
-        compiler_params=params(4),
+        out_shape=jax.ShapeDtypeStruct((copies, *image.shape), BF16),
+        compiler_params=params(6),
         name="solve_layers",
-    )(*grams, image)
+    )(grams, image)
 
 
 def stack_rows(refs, scratch):
@@ -262,31 +318,34 @@
     size = work.shape[0]
     steps = size // k
     lane = lax.broadcasted_iota(jnp.int32, (k, size), 1)
-    sub = lax.broadcasted_iota(jnp.int32, (k, size), 0)
-    lane_all = lax.broadcasted_iota(jnp.int32, (size, size), 1)
+    lane_128 = lax.broadcasted_iota(jnp.int32, (k, 128), 1)
+    sub_128 = lax.broadcasted_iota(jnp.int32, (k, 128), 0)
+    gram, across = unit_scale(work[...])
+    work[...] = gram
     for s in range(steps):
         lo, hi = s * k, (s + 1) * k
         here = (lane >= lo) & (lane < hi)
+        eye = jnp.where(lane_128 == sub_128 + lo % 128, 1.0, 0.0)
         panel = work[lo:hi]
-        tail = jnp.where(here, jnp.where(lane == sub + lo, 1.0, 0.0), 0.0)
-        panel, tail = eliminate(panel, tail, lo)
-        panel = jnp.where(here, tail, panel)
+        solved = eliminate(jnp.concatenate([panel, eye], axis=1), lo)
+        panel, tail = solved[:, :size], solved[:, size:]
+        panel = jnp.where(here, jnp.concatenate([tail] * (size // 128), axis=1), panel)
         work[lo:hi] = jnp.where(lane < hi, panel, 0.0)
         if s + 1 < steps:
-            ahead = jnp.where(lane >= hi, panel, 0.0)
-            update = lax.dot_general(ahead, panel, TRANS_A, precision=HIGHEST, preferred_element_type=F32)
-            rest = work[hi:]
-            rest = jnp.where((lane_all[hi:] >= lo) & (lane_all[hi:] < hi), 0.0, rest)
-            work[hi:] = rest - update[hi:]
+            update = gram_update(jnp.where(lane >= hi, panel, 0.0), panel)
+            for r in range(s + 1, steps):
+                rows = work[r * k : r * k + k]
+                work[r * k : r * k + k] = jnp.where(here, 0.0, rows) - update[r * k : r * k + k]
     rows = size // piece_count
-    own = work[pl.ds(pl.multiple_of(lax.axis_index("layer") * rows, rows), rows)]
+    own = work[pl.ds(pl.multiple_of(lax.axis_index("layer") * rows, rows), rows)] * across
     joint = jnp.dot(own, stacked[...], precision=HIGHEST, preferred_element_type=F32)
     joint = joint.reshape(out_ref.shape)
     out_ref[...] = joint
-    rounded_ref[...] = joint.astype(BF16)
-
-
-def joint_solve(grams, images):
+    for copy in range(rounded_ref.shape[0]):
+        rounded_ref[copy] = joint.astype(BF16)
+
+
+def joint_solve(grams, images, copies):
     layers, k, width = images[0].shape
     size = layers * k * len(images)
     return pl.pallas_call(
@@ -295,7 +354,7 @@
         out_specs=vmem_specs(2),
         out_shape=[
             jax.ShapeDtypeStruct(images[0].shape, F32),
-            jax.ShapeDtypeStruct(images[0].shape, BF16),
+            jax.ShapeDtypeStruct((copies, *images[0].shape), BF16),
         ],
         scratch_shapes=[pltpu.VMEM((size, size), F32), pltpu.VMEM((size, width), F32)],
         compiler_params=params(8),
@@ -310,37 +369,27 @@
     return pieces
 
 
-def add4(pieces):
-    return (pieces[0] + pieces[2]) + (pieces[1] + pieces[3])
+def gather(copies):
+    return lax.all_to_all(copies, "node", 0, 0)
 
 
 def per_device(shards, groups, blocks, block_rows, block_cols, counts, start):
-    relative = shards == 4
     cols_total = shards * BROWS
     live = jnp.arange(block_rows.shape[1], dtype=jnp.int32)[None, :] < counts
-    cols = block_cols
-    if relative:
-        cols = (cols - lax.axis_index("node") * BROWS + cols_total) % cols_total
-    key = jnp.where(live, cols * BROWS + block_rows, -1)
-
-    def gather(x):
-        if relative:
-            return around(x, "node", shards)
-        return [lax.all_gather(x, "node", axis=2, tiled=True)]
-
-    def total(x):
-        return add4(around(x, "node", shards)) if relative else lax.psum(x, "node")
-
-    first = gather(start.astype(BF16))
+    key = jnp.where(live, block_cols * BROWS + block_rows, -1)
+
+    def copied(x):
+        return jnp.broadcast_to(x[None], (shards, *x.shape))
+
+    first = gather(copied(start.astype(BF16)))
     hi, lo = build_dense(key, blocks, cols_total // CHUNK_COLS)
     image, gram = apply_dense("gram", first, hi, lo)
-    grams = around(gram, "node", shards) if relative else [lax.psum(gram, "node")]
-    (image,) = apply_dense("plain", gather(solve(grams, image)), hi, lo)
+    (image,) = apply_dense("plain", gather(solve(gather(gram), image, shards)), hi, lo)
     images = around(image, "layer", groups)
-    grams = around(total(cross(images)), "layer", groups)
-    joint_basis, rounded = joint_solve(grams, images)
+    grams = around(jnp.sum(gather(copied(cross(images))), axis=0), "layer", groups)
+    joint_basis, rounded = joint_solve(grams, images, shards)
     _, partial = apply_dense("score", gather(rounded), hi, lo, joint_basis)
-    return joint_basis, total(partial)
+    return joint_basis, jnp.sum(gather(partial), axis=0)
 
 
 def solution(mesh):

time: 123 us -> 142 us (1.15)
  blocking collectives: 0 us -> 53.1 us
  waiting for transfers between devices: 30 us -> 7.69 us
  starting transfers between devices: 32 us -> 11.3 us
  local copies, waits for them, and re-layouts: 4.29 us -> 23.1 us
  Pallas kernels: 53.5 us -> 41.4 us
  other arithmetic: 2.33 us -> 3.79 us
    all_to_all x0 -> x5, blocking collectives: none -> 53.1 us  [gather(): return lax.all_to_all(copies, 'node', 0, 0)]
    ppermute x24 -> x6, starting transfers between devices: 32 us -> 5.01 us  [around(): lax.ppermute(x, axis, [((m + d) % count, m) for m in range(count)])]
    ppermute x24 -> x6, waiting for transfers between devices: 30 us -> 7.68 us  [around(): lax.ppermute(x, axis, [((m + d) % count, m) for m in range(count)])]
    unnamed x4 -> x24, local copies, waits for them, and re-layouts: 4.29 us -> 21.7 us
    pallas_call x1, Pallas kernels: 26.1 us -> 13.9 us  [joint_solve(): pl.pallas_call(functools.partial(joint_kernel, len(images), k), in_specs=...]
    all_to_all x0 -> x1, starting transfers between devices: none -> 6.32 us  [gather(): return lax.all_to_all(copies, 'node', 0, 0)]
    all_to_all x0 -> x2, other arithmetic: none -> 1.46 us  [gather(): return lax.all_to_all(copies, 'node', 0, 0)]
  transfers between devices with their start and end apart: 24 -> 7, of which waited for: 16 -> 5; matrix products, arithmetic and copies ran while one was open for 1% -> 1% of each run, Pallas kernels for 6% -> 6%
where the time goes in v3:
time: 142 us; the launch traced here: 141 us
  blocking collectives  53.1 us (37%)
  Pallas kernels  41.4 us (29%)
  local copies, waits for them, and re-layouts  23.1 us (16%)
  starting transfers between devices  11.3 us (8%)
  waiting for transfers between devices  7.69 us (5%)
  other arithmetic  3.79 us (3%)
    all_to_all x5, blocking collectives, gather(): return lax.all_to_all(copies, 'node', 0, 0)  53.1 us
    unnamed x24, local copies, waits for them, and re-layouts  21.7 us
    pallas_call x3, Pallas kernels, apply_dense(): pl.pallas_call(functools.partial(apply_kernel, mode), grid=(layers, chunk...  16 us
    pallas_call x1, Pallas kernels, joint_solve(): pl.pallas_call(functools.partial(joint_kernel, len(images), k), in_specs=...  13.9 us
    pallas_call x1, Pallas kernels, build_dense(): pl.pallas_call(build_kernel, grid=(layers, chunk_total // per_step), in_s...  7.86 us
    ppermute x6, waiting for transfers between devices, around(): lax.ppermute(x, axis, [((m + d) % count, m) for m in range(count)])  7.68 us
    all_to_all x1, starting transfers between devices, gather(): return lax.all_to_all(copies, 'node', 0, 0)  6.32 us
    ppermute x6, starting transfers between devices, around(): lax.ppermute(x, axis, [((m + d) % count, m) for m in range(count)])  5.01 us
  transfers between devices with their start and end apart: 7, of which 5 were waited for; matrix products, arithmetic and copies ran while one was open for 1% of the time, Pallas kernels for 6%

profile of v3, /device:TPU:0, one launch (start us, length us, event | category | flops | bytes accessed | tf_op | source)
XLA Modules:
  0.0 141.1 jit_solution(13436909508998600970)
XLA Ops:
  2.3 6.3 %all-to-all-start = ((bf16[4,2,32,512]{3,2,1,0:T(8,128)(2,1)}), bf16[4,2,32,512]{3,2,1,0:T(8,128)(2,1)S(1)}, u32[]{:S(2)}, u32[]{:S(2)}) async-start(bf16[4,2,32,512]{3,2,1,0:T(8,128)(2,1)} %broadcast_in_dim.8), calls=%async_computation | async-start | bytes 524288 | tf_op jit(solution)/shard_map/all_to_all | solution.py:373
  9.4 3.4 %copy-done.8 = bf16[2,512,4096]{2,1,0:T(8,128)(2,1)S(1)} copy-done((bf16[2,512,4096]{2,1,0:T(8,128)(2,1)S(1)}, bf16[2,512,4096]{2,1,0:T(8,128)(2,1)}, u32[]{:S(2)}) %copy-start.8) | copy-done | bytes 8388632
  12.8 7.9 %build_dense.1 = (bf16[2,4,256,1024]{3,2,1,0:T(8,128)(2,1)S(1)}, bf16[2,4,256,1024]{3,2,1,0:T(8,128)(2,1)S(1)}) custom-call(s32[2,1,512]{2,1,0:T(1,128)S(1)} %reshape.9.key_ref, bf16[2,512,4096]{2,1,0:T(8,128)(2,1)S(1)} %copy-done.8), custom_call_target="tpu_custom_call" | custom-call | tf_op jit(solution)/shard_map/build_dense/pallas_call | solution.py:62
  20.7 1.9 %copy-done = bf16[2,4,256,1024]{3,2,1,0:T(8,128)(2,1)} copy-done((bf16[2,4,256,1024]{3,2,1,0:T(8,128)(2,1)}, bf16[2,4,256,1024]{3,2,1,0:T(8,128)(2,1)S(1)}, u32[]{:S(2)}) %copy-start) | copy-done | bytes 4194328
  22.6 2.0 %copy-done.4 = bf16[2,4,256,1024]{3,2,1,0:T(8,128)(2,1)} copy-done((bf16[2,4,256,1024]{3,2,1,0:T(8,128)(2,1)}, bf16[2,4,256,1024]{3,2,1,0:T(8,128)(2,1)S(1)}, u32[]{:S(2)}) %copy-start.4) | copy-done | bytes 4194328
  24.6 2.2 %copy-done.1 = bf16[2,4,256,1024]{3,2,1,0:T(8,128)(2,1)S(1)} copy-done((bf16[2,4,256,1024]{3,2,1,0:T(8,128)(2,1)S(1)}, bf16[2,4,256,1024]{3,2,1,0:T(8,128)(2,1)}, u32[]{:S(2)}) %copy-start.1) | copy-done | bytes 4194328
  26.8 2.2 %copy-done.5 = bf16[2,4,256,1024]{3,2,1,0:T(8,128)(2,1)S(1)} copy-done((bf16[2,4,256,1024]{3,2,1,0:T(8,128)(2,1)S(1)}, bf16[2,4,256,1024]{3,2,1,0:T(8,128)(2,1)}, u32[]{:S(2)}) %copy-start.5) | copy-done | bytes 4194328
  29.0 5.3 %apply_gram.1 = (f32[2,32,512]{2,1,0:T(8,128)S(1)}, f32[4,2,32,32]{3,2,1,0:T(8,128)S(1)}) custom-call(bf16[4,2,32,512]{3,2,1,0:T(8,128)(2,1)S(1)} %all-to-all-done.refs_0_, bf16[2,4,256,1024]{3,2,1,0:T(8,128)(2,1)S(1)} %copy-done.1, bf16[2,4,256,1024]{3,2,1,0:T(8,128)(2,1)S(1)} %copy-done.5), custom_call_target="tpu_custom_call" | custom-call | tf_op jit(solution)/shard_map/apply_gram/pallas_call | solution.py:160
  34.4 10.5 %all_to_all.30 = f32[4,1,2048]{2,1,0:T(1,128)S(1)} all-to-all(f32[4,1,2048]{2,1,0:T(1,128)S(1)} %reshape.10), channel_id=1, replica_groups=mesh['parts'=2,'layer'=4,'node'=4] {'node'}, dimensions={0} | all-to-all | bytes 65536 | tf_op jit(solution)/shard_map/all_to_all | solution.py:373
  46.2 3.0 %solve_layers.1 = bf16[4,2,32,512]{3,2,1,0:T(8,128)(2,1)S(1)} custom-call(f32[4,2,32,32]{3,2,1,0:T(8,128)S(1)} %reshape.11.grams_ref, f32[2,32,512]{2,1,0:T(8,128)S(1)} %get-tuple-element.12.image_ref), custom_call_target="tpu_custom_call" | custom-call | tf_op jit(solution)/shard_map/solve_layers/pallas_call | solution.py:272
  49.3 9.5 %all_to_all.31.refs_0_ = bf16[4,2,32,512]{3,2,1,0:T(8,128)(2,1)S(1)} all-to-all(bf16[4,2,32,512]{3,2,1,0:T(8,128)(2,1)S(1)} %solve_layers.1), channel_id=1, replica_groups=mesh['parts'=2,'layer'=4,'node'=4] {'node'}, dimensions={0} | all-to-all | bytes 524288 | tf_op jit(solution)/shard_map/all_to_all | solution.py:373
  58.8 2.2 %copy-done.2 = bf16[2,4,256,1024]{3,2,1,0:T(8,128)(2,1)S(1)} copy-done((bf16[2,4,256,1024]{3,2,1,0:T(8,128)(2,1)S(1)}, bf16[2,4,256,1024]{3,2,1,0:T(8,128)(2,1)}, u32[]{:S(2)}) %copy-start.2) | copy-done | bytes 4194328
  61.0 2.2 %copy-done.6 = bf16[2,4,256,1024]{3,2,1,0:T(8,128)(2,1)S(1)} copy-done((bf16[2,4,256,1024]{3,2,1,0:T(8,128)(2,1)S(1)}, bf16[2,4,256,1024]{3,2,1,0:T(8,128)(2,1)}, u32[]{:S(2)}) %copy-start.6) | copy-done | bytes 4194328
  63.2 4.7 %apply_plain.1.refs_0_.refs_4_ = f32[2,32,512]{2,1,0:T(8,128)S(1)} custom-call(bf16[4,2,32,512]{3,2,1,0:T(8,128)(2,1)S(1)} %all_to_all.31.refs_0_, bf16[2,4,256,1024]{3,2,1,0:T(8,128)(2,1)S(1)} %copy-done.2, bf16[2,4,256,1024]{3,2,1,0:T(8,128)(2,1)S(1)} %copy-done.6), custom_call_target="tpu_custom_call" | custom-call | tf_op jit(solution)/shard_map/apply_plain/pallas_call | solution.py:160
  67.9 1.6 %collective-permute-start.1 = (f32[2,32,512]{2,1,0:T(8,128)S(1)}, f32[2,32,512]{2,1,0:T(8,128)S(1)}, u32[]{:S(2)}, u32[]{:S(2)}) collective-permute-start(f32[2,32,512]{2,1,0:T(8,128)S(1)} %apply_plain.1.refs_0_.refs_4_), channel_id=1, source_target_pairs={{8,0},{12,4},{0,8},{4,12},{9,1},{13,5},{1,9},{5,13},{10,2},{14,6},... | collective-permute-start | bytes 393224 | tf_op jit(solution)/shard_map/ppermute | solution.py:368
  70.9 2.3 %collective-permute-done.2.refs_3_.refs_7_ = f32[2,32,512]{2,1,0:T(8,128)S(1)} collective-permute-done((f32[2,32,512]{2,1,0:T(8,128)S(1)}, f32[2,32,512]{2,1,0:T(8,128)S(1)}, u32[]{:S(2)}, u32[]{:S(2)}) %collective-permute-start.2) | collective-permute-done | bytes 131104 | tf_op jit(solution)/shard_map/ppermute | solution.py:368
  76.2 12.5 %all_to_all.32 = f32[4,64,256]{2,1,0:T(8,128)S(1)} all-to-all(f32[4,64,256]{2,1,0:T(8,128)S(1)} %broadcast_in_dim.10), channel_id=1, replica_groups=mesh['parts'=2,'layer'=4,'node'=4] {'node'}, dimensions={0} | all-to-all | bytes 524288 | tf_op jit(solution)/shard_map/all_to_all | solution.py:373
  90.8 1.8 %collective-permute-done.5.refs_3_ = f32[64,256]{1,0:T(8,128)S(1)} collective-permute-done((f32[64,256]{1,0:T(8,128)S(1)}, f32[64,256]{1,0:T(8,128)S(1)}, u32[]{:S(2)}, u32[]{:S(2)}) %collective-permute-start.5) | collective-permute-done | bytes 65568 | tf_op jit(solution)/shard_map/ppermute | solution.py:368
  93.8 13.9 %joint_solve.1 = (f32[2,32,512]{2,1,0:T(8,128)}, bf16[4,2,32,512]{3,2,1,0:T(8,128)(2,1)S(1)}) custom-call(f32[64,256]{1,0:T(8,128)S(1)} %reduce_sum.18.refs_0_, f32[64,256]{1,0:T(8,128)S(1)} %collective-permute-done.3.refs_1_, f32[64,256]{1,0:T(8,128)S(1)} %collective-permute-done.4.refs_2_, f32[64,256]{1,0:T(8,128)S(1)} %collective-permute-done.5.refs_3_, ...), custom_call_target="tpu_custom_call" | custom-call | tf_op jit(solution)/shard_map/joint_solve/pallas_call | solution.py:351
  107.8 12.3 %all_to_all.33.refs_0_ = bf16[4,2,32,512]{3,2,1,0:T(8,128)(2,1)S(1)} all-to-all(bf16[4,2,32,512]{3,2,1,0:T(8,128)(2,1)S(1)} %get-tuple-element.14), channel_id=1, replica_groups=mesh['parts'=2,'layer'=4,'node'=4] {'node'}, dimensions={0} | all-to-all | bytes 524288 | tf_op jit(solution)/shard_map/all_to_all | solution.py:373
  120.1 2.2 %copy-done.3 = bf16[2,4,256,1024]{3,2,1,0:T(8,128)(2,1)S(1)} copy-done((bf16[2,4,256,1024]{3,2,1,0:T(8,128)(2,1)S(1)}, bf16[2,4,256,1024]{3,2,1,0:T(8,128)(2,1)}, u32[]{:S(2)}) %copy-start.3) | copy-done | bytes 4194328
  122.3 2.2 %copy-done.7 = bf16[2,4,256,1024]{3,2,1,0:T(8,128)(2,1)S(1)} copy-done((bf16[2,4,256,1024]{3,2,1,0:T(8,128)(2,1)S(1)}, bf16[2,4,256,1024]{3,2,1,0:T(8,128)(2,1)}, u32[]{:S(2)}) %copy-start.7) | copy-done | bytes 4194328
  125.3 6.0 %apply_score.1 = (f32[2,32,512]{2,1,0:T(8,128)}, f32[4,2,32,32]{3,2,1,0:T(8,128)S(1)}) custom-call(bf16[4,2,32,512]{3,2,1,0:T(8,128)(2,1)S(1)} %all_to_all.33.refs_0_, f32[2,32,512]{2,1,0:T(8,128)S(1)} %copy-done.9, bf16[2,4,256,1024]{3,2,1,0:T(8,128)(2,1)S(1)} %copy-done.3, bf16[2,4,256,1024]{3,2,1,0:T(8,128)(2,1)S(1)} %copy-done.7), custom_call_target="tpu_custom_call" | custom-call | tf_op jit(solution)/shard_map/apply_score/pallas_call | solution.py:160
  131.5 8.2 %all_to_all.34 = f32[4,1,2048]{2,1,0:T(1,128)S(1)} all-to-all(f32[4,1,2048]{2,1,0:T(1,128)S(1)} %reshape.12), channel_id=1, replica_groups=mesh['parts'=2,'layer'=4,'node'=4] {'node'}, dimensions={0} | all-to-all | bytes 65536 | tf_op jit(solution)/shard_map/all_to_all | solution.py:373
  (36 shorter events, 14.1 us)
Async XLA Ops:
  2.3 22.3 %all-to-all-start = ((bf16[4,2,32,512]{3,2,1,0:T(8,128)(2,1)}), bf16[4,2,32,512]{3,2,1,0:T(8,128)(2,1)S(1)}, u32[]{:S(2)}, u32[]{:S(2)}) async-start(bf16[4,2,32,512]{3,2,1,0:T(8,128)(2,1)} %broadcast_in_dim.8), calls=%async_computation | async-start | bytes 524288 | tf_op jit(solution)/shard_map/all_to_all | solution.py:373
  9.4 3.4 %copy-start.8 = (bf16[2,512,4096]{2,1,0:T(8,128)(2,1)S(1)}, bf16[2,512,4096]{2,1,0:T(8,128)(2,1)}, u32[]{:S(2)}) copy-start(bf16[2,512,4096]{2,1,0:T(8,128)(2,1)} %blocks_ref.1) | copy-start | bytes 25165828
  20.7 1.9 %copy-start = (bf16[2,4,256,1024]{3,2,1,0:T(8,128)(2,1)}, bf16[2,4,256,1024]{3,2,1,0:T(8,128)(2,1)S(1)}, u32[]{:S(2)}) copy-start(bf16[2,4,256,1024]{3,2,1,0:T(8,128)(2,1)S(1)} %get-tuple-element.9.refs_1_.refs_2_) | copy-start | bytes 12582916
  22.6 2.0 %copy-start.4 = (bf16[2,4,256,1024]{3,2,1,0:T(8,128)(2,1)}, bf16[2,4,256,1024]{3,2,1,0:T(8,128)(2,1)S(1)}, u32[]{:S(2)}) copy-start(bf16[2,4,256,1024]{3,2,1,0:T(8,128)(2,1)S(1)} %get-tuple-element.10.refs_2_.refs_3_) | copy-start | bytes 12582916
  24.6 2.2 %copy-start.1 = (bf16[2,4,256,1024]{3,2,1,0:T(8,128)(2,1)S(1)}, bf16[2,4,256,1024]{3,2,1,0:T(8,128)(2,1)}, u32[]{:S(2)}) copy-start(bf16[2,4,256,1024]{3,2,1,0:T(8,128)(2,1)} %copy-done) | copy-start | bytes 12582916
  26.8 2.2 %copy-start.5 = (bf16[2,4,256,1024]{3,2,1,0:T(8,128)(2,1)S(1)}, bf16[2,4,256,1024]{3,2,1,0:T(8,128)(2,1)}, u32[]{:S(2)}) copy-start(bf16[2,4,256,1024]{3,2,1,0:T(8,128)(2,1)} %copy-done.4) | copy-start | bytes 12582916
  58.8 2.2 %copy-start.2 = (bf16[2,4,256,1024]{3,2,1,0:T(8,128)(2,1)S(1)}, bf16[2,4,256,1024]{3,2,1,0:T(8,128)(2,1)}, u32[]{:S(2)}) copy-start(bf16[2,4,256,1024]{3,2,1,0:T(8,128)(2,1)} %copy-done) | copy-start | bytes 12582916
  61.0 2.2 %copy-start.6 = (bf16[2,4,256,1024]{3,2,1,0:T(8,128)(2,1)S(1)}, bf16[2,4,256,1024]{3,2,1,0:T(8,128)(2,1)}, u32[]{:S(2)}) copy-start(bf16[2,4,256,1024]{3,2,1,0:T(8,128)(2,1)} %copy-done.4) | copy-start | bytes 12582916
  67.9 5.3 %collective-permute-start.2 = (f32[2,32,512]{2,1,0:T(8,128)S(1)}, f32[2,32,512]{2,1,0:T(8,128)S(1)}, u32[]{:S(2)}, u32[]{:S(2)}) collective-permute-start(f32[2,32,512]{2,1,0:T(8,128)S(1)} %apply_plain.1.refs_0_.refs_4_), channel_id=1, source_target_pairs={{12,0},{0,4},{4,8},{8,12},{13,1},{1,5},{5,9},{9,13},{14,2},{2,6},{... | collective-permute-start | bytes 393224 | tf_op jit(solution)/shard_map/ppermute | solution.py:368
  67.9 6.4 %collective-permute-start.1 = (f32[2,32,512]{2,1,0:T(8,128)S(1)}, f32[2,32,512]{2,1,0:T(8,128)S(1)}, u32[]{:S(2)}, u32[]{:S(2)}) collective-permute-start(f32[2,32,512]{2,1,0:T(8,128)S(1)} %apply_plain.1.refs_0_.refs_4_), channel_id=1, source_target_pairs={{8,0},{12,4},{0,8},{4,12},{9,1},{13,5},{1,9},{5,13},{10,2},{14,6},... | collective-permute-start | bytes 393224 | tf_op jit(solution)/shard_map/ppermute | solution.py:368
  69.5 6.1 %collective-permute-start = (f32[2,32,512]{2,1,0:T(8,128)S(1)}, f32[2,32,512]{2,1,0:T(8,128)S(1)}, u32[]{:S(2)}, u32[]{:S(2)}) collective-permute-start(f32[2,32,512]{2,1,0:T(8,128)S(1)} %apply_plain.1.refs_0_.refs_4_), channel_id=1, source_target_pairs={{4,0},{8,4},{12,8},{0,12},{5,1},{9,5},{13,9},{1,13},{6,2},{10,6},{... | collective-permute-start | bytes 393224 | tf_op jit(solution)/shard_map/ppermute | solution.py:368
  88.8 3.8 %collective-permute-start.5 = (f32[64,256]{1,0:T(8,128)S(1)}, f32[64,256]{1,0:T(8,128)S(1)}, u32[]{:S(2)}, u32[]{:S(2)}) collective-permute-start(f32[64,256]{1,0:T(8,128)S(1)} %reduce_sum.18.refs_0_), channel_id=1, source_target_pairs={{12,0},{0,4},{4,8},{8,12},{13,1},{1,5},{5,9},{9,13},{14,2},{2,6},{... | collective-permute-start | bytes 196616 | tf_op jit(solution)/shard_map/ppermute | solution.py:368
  88.8 5.0 %collective-permute-start.4 = (f32[64,256]{1,0:T(8,128)S(1)}, f32[64,256]{1,0:T(8,128)S(1)}, u32[]{:S(2)}, u32[]{:S(2)}) collective-permute-start(f32[64,256]{1,0:T(8,128)S(1)} %reduce_sum.18.refs_0_), channel_id=1, source_target_pairs={{8,0},{12,4},{0,8},{4,12},{9,1},{13,5},{1,9},{5,13},{10,2},{14,6},... | collective-permute-start | bytes 196616 | tf_op jit(solution)/shard_map/ppermute | solution.py:368
  89.6 4.2 %collective-permute-start.3 = (f32[64,256]{1,0:T(8,128)S(1)}, f32[64,256]{1,0:T(8,128)S(1)}, u32[]{:S(2)}, u32[]{:S(2)}) collective-permute-start(f32[64,256]{1,0:T(8,128)S(1)} %reduce_sum.18.refs_0_), channel_id=1, source_target_pairs={{4,0},{8,4},{12,8},{0,12},{5,1},{9,5},{13,9},{1,13},{6,2},{10,6},{... | collective-permute-start | bytes 196616 | tf_op jit(solution)/shard_map/ppermute | solution.py:368
  120.1 2.2 %copy-start.3 = (bf16[2,4,256,1024]{3,2,1,0:T(8,128)(2,1)S(1)}, bf16[2,4,256,1024]{3,2,1,0:T(8,128)(2,1)}, u32[]{:S(2)}) copy-start(bf16[2,4,256,1024]{3,2,1,0:T(8,128)(2,1)} %copy-done) | copy-start | bytes 12582916
  122.3 2.2 %copy-start.7 = (bf16[2,4,256,1024]{3,2,1,0:T(8,128)(2,1)S(1)}, bf16[2,4,256,1024]{3,2,1,0:T(8,128)(2,1)}, u32[]{:S(2)}) copy-start(bf16[2,4,256,1024]{3,2,1,0:T(8,128)(2,1)} %copy-done.4) | copy-start | bytes 12582916
  124.4 0.9 copy-start.9

commit v4 on v2

v4 whole, which is shorter than its diff:
```python
import functools

import jax
import jax.numpy as jnp
from jax import lax
from jax.experimental import pallas as pl
from jax.experimental.pallas import tpu as pltpu
from jax.sharding import PartitionSpec as P

BLK = 64
ROWS_DEV = 512
BROWS = ROWS_DEV // BLK
CHUNK_COLS = 8
CHUNK_LANES = CHUNK_COLS * 2 * BLK
TALL = BROWS * BLK // 2
MIB = 1024 * 1024
F32 = jnp.float32
BF16 = jnp.bfloat16
HIGHEST = lax.Precision.HIGHEST
TRANS_B = (((1,), (1,)), ((), ()))
TRANS_A = (((0,), (0,)), ((), ()))


def params(mib):
    return pltpu.CompilerParams(vmem_limit_bytes=mib * MIB)


def vmem_specs(count):
    return [pl.BlockSpec(memory_space=pltpu.VMEM)] * count


def place(z, chunks, u, hi_ref, lo_ref, layer):
    out_rows = pl.ds(pl.multiple_of(u * 16, 16), 16)
    for c in range(chunks * CHUNK_COLS):
        piece = z[c * 8 : c * 8 + 8]
        piece = jnp.concatenate([piece[:, :128], piece[:, 128:]], axis=0)
        hi = piece.astype(BF16)
        lo = (piece - hi.astype(F32)).astype(BF16)
        lanes = slice((c % CHUNK_COLS) * 128, (c % CHUNK_COLS) * 128 + 128)
        hi_ref[layer, c // CHUNK_COLS, out_rows, lanes] = hi
        lo_ref[layer, c // CHUNK_COLS, out_rows, lanes] = lo


def one_hot(key, base, positions):
    position = lax.broadcasted_iota(jnp.int32, (positions, key.shape[1]), 0) + base
    return jnp.where(position == key, 1.0, 0.0).astype(BF16)


def build_kernel(key_ref, blocks_ref, hi_ref, lo_ref):
    chunks = hi_ref.shape[1]
    positions = chunks * CHUNK_COLS * BROWS
    onehot = one_hot(key_ref[0], pl.program_id(1) * positions, positions)

    def step(u, carry):
        cols = pl.ds(pl.multiple_of(u * 256, 256), 256)
        z = jnp.dot(onehot, blocks_ref[0, :, cols], preferred_element_type=F32)
        place(z, chunks, u, hi_ref, lo_ref, 0)
        return carry

    lax.fori_loop(0, BLK * BLK // 256, step, 0)


def build_whole_kernel(key_ref, blocks_ref, hi_ref, lo_ref, held, arrived):
    layers, chunks = hi_ref.shape[:2]
    pieces = arrived.shape[1]
    width = held.shape[2] // pieces
    inner = width // 256

    def fetch(layer, piece):
        cols = pl.ds(pl.multiple_of(piece * width, width), width)
        return pltpu.make_async_copy(
            blocks_ref.at[layer, :, cols], held.at[layer, :, cols], arrived.at[layer, piece]
        )

    for layer in range(layers):
        for piece in range(pieces):
            fetch(layer, piece).start()
    for layer in range(layers):
        onehot = one_hot(key_ref[layer], 0, chunks * CHUNK_COLS * BROWS)

        def step(piece, carry):
            fetch(layer, piece).wait()
            for v in range(inner):
                cols = pl.ds(pl.multiple_of(piece * width + v * 256, 256), 256)
                z = jnp.dot(onehot, held[layer, :, cols], preferred_element_type=F32)
                place(z, chunks, piece * inner + v, hi_ref, lo_ref, layer)
            return carry

        lax.fori_loop(0, pieces, step, 0)


def build_dense(key, blocks, chunk_total):
    layers, slots, width = blocks.shape
    dense = jax.ShapeDtypeStruct((layers, chunk_total, TALL, CHUNK_LANES), BF16)
    key = key.reshape(layers, 1, slots)
    if chunk_total <= 4:
        pieces = 4
        return pl.pallas_call(
            build_whole_kernel,
            in_specs=[pl.BlockSpec(memory_space=pltpu.VMEM), pl.BlockSpec(memory_space=pltpu.HBM)],
            out_specs=vmem_specs(2),
            out_shape=[dense, dense],
            scratch_shapes=[pltpu.VMEM(blocks.shape, BF16), pltpu.SemaphoreType.DMA((layers, pieces))],
            compiler_params=params(24),
            name="build_dense",
        )(key, blocks)
    out_spec = pl.BlockSpec((1, 4, TALL, CHUNK_LANES), lambda l, s: (l, s, 0, 0))
    return pl.pallas_call(
        build_kernel,
        grid=(layers, chunk_total // 4),
        in_specs=[
            pl.BlockSpec((1, 1, slots), lambda l, s: (l, 0, 0)),
            pl.BlockSpec((1, slots, width), lambda l, s: (l, 0, 0)),
        ],
        out_specs=[out_spec, out_spec],
        out_shape=[dense, dense],
        compiler_params=params(24),
        name="build_dense",
    )(key, blocks)


def split3(x):
    a = x.astype(BF16)
    r = x - a.astype(F32)
    b = r.astype(BF16)
    c = (r - b.astype(F32)).astype(BF16)
    return a, b, c


def image_part(basis, hi, lo):
    k, width = basis.shape
    basis = basis.astype(F32)
    low = lax.broadcasted_iota(jnp.int32, (k, 128), 1) < BLK
    first, second = [], []
    for q in range(width // 128):
        b = basis[:, q * 128 : q * 128 + 128]
        br = pltpu.roll(b, BLK, 1)
        first += [jnp.where(low, b, 0.0), jnp.where(low, br, 0.0)]
        second += [jnp.where(low, 0.0, br), jnp.where(low, 0.0, b)]
    weights = jnp.concatenate(
        [
            jnp.concatenate(first, axis=1),
            jnp.concatenate(second, axis=1),
            jnp.zeros((128 - 2 * k, CHUNK_LANES), F32),
        ],
        axis=0,
    ).astype(BF16)
    total = lax.dot_general(hi, weights, TRANS_B, preferred_element_type=F32)
    return total + lax.dot_general(lo, weights, TRANS_B, preferred_element_type=F32)


def node_order():
    row = lax.broadcasted_iota(jnp.int32, (ROWS_DEV, ROWS_DEV), 0)
    col = lax.broadcasted_iota(jnp.int32, (ROWS_DEV, ROWS_DEV), 1)
    target = (row % 8) * BLK + 2 * ((row % TALL) // 8) + row // TALL
    return jnp.where(target == col, 1.0, 0.0).astype(BF16)


def to_wide(total, perm, k):
    turned = total.T
    wide = jnp.concatenate([turned[:k], turned[k : 2 * k]], axis=1)
    moved = jnp.dot(jnp.concatenate(split3(wide), axis=0), perm, preferred_element_type=F32)
    return moved[:k] + moved[k : 2 * k] + moved[2 * k :]


def dot_rows(a, b):
    return lax.dot_general(a, b, TRANS_B, precision=HIGHEST, preferred_element_type=F32)


def apply_kernel(mode, *refs):
    basis_ref, refs = refs[0], refs[1:]
    if mode == "score":
        left_ref, refs = refs[0], refs[1:]
    hi_ref, lo_ref, out_ref = refs[:3]
    perm, acc = refs[-2:]
    layer, chunk = pl.program_id(0), pl.program_id(1)

    @pl.when((layer == 0) & (chunk == 0))
    def _():
        perm[...] = node_order()

    total = image_part(basis_ref[chunk, layer], hi_ref[0, 0], lo_ref[0, 0])

    @pl.when(chunk == 0)
    def _():
        acc[...] = total

    @pl.when(chunk > 0)
    def _():
        acc[...] += total

    @pl.when(chunk == pl.num_programs(1) - 1)
    def _():
        image = to_wide(acc[...], perm[...], basis_ref.shape[2])
        if mode != "score":
            out_ref[0] = image
        if mode == "gram":
            refs[3][0] = dot_rows(image, image)
        if mode == "score":
            out_ref[0] = dot_rows(left_ref[0], image)


def apply_whole_kernel(mode, piece_count, *refs):
    pieces, refs = refs[:piece_count], refs[piece_count:]
    if mode == "score":
        left_ref, refs = refs[0], refs[1:]
    hi_ref, lo_ref, out_ref = refs[:3]
    perm = node_order()
    for layer in range(hi_ref.shape[0]):
        total = sum(
            image_part(piece[layer], hi_ref[layer, chunk], lo_ref[layer, chunk])
            for chunk, piece in enumerate(pieces)
        )
        image = to_wide(total, perm, pieces[0].shape[1])
        if mode != "score":
            out_ref[layer] = image
        if mode == "gram":
            refs[3][layer] = dot_rows(image, image)
        if mode == "score":
            out_ref[layer] = dot_rows(left_ref[layer], image)


def apply_dense(mode, pieces, hi, lo, left=None):
    layers, chunks = hi.shape[:2]
    k = pieces[0].shape[-2]
    image = jax.ShapeDtypeStruct((layers, k, ROWS_DEV), F32)
    small = jax.ShapeDtypeStruct((layers, k, k), F32)
    out_shape = {"gram": [image, small], "plain": [image], "score": [small]}[mode]
    operands = list(pieces) + ([left] if mode == "score" else []) + [hi, lo]
    if len(pieces) == chunks:
        return pl.pallas_call(
            functools.partial(apply_whole_kernel, mode, chunks),
            in_specs=vmem_specs(len(operands)),
            out_specs=vmem_specs(len(out_shape)),
            out_shape=out_shape,
            compiler_params=params(14),
            name="apply_" + mode,
        )(*operands)
    dense_spec = pl.BlockSpec((1, 1, TALL, CHUNK_LANES), lambda l, s: (l, s, 0, 0))
    image_spec = pl.BlockSpec((1, k, ROWS_DEV), lambda l, s: (l, 0, 0))
    small_spec = pl.BlockSpec((1, k, k), lambda l, s: (l, 0, 0))
    return pl.pallas_call(
        functools.partial(apply_kernel, mode),
        grid=(layers, chunks),
        in_specs=vmem_specs(1) + ([image_spec] if mode == "score" else []) + [dense_spec, dense_spec],
        out_specs={"gram": [image_spec, small_spec], "plain": [image_spec], "score": [small_spec]}[mode],
        out_shape=out_shape,
        scratch_shapes=[pltpu.VMEM((ROWS_DEV, ROWS_DEV), BF16), pltpu.VMEM((TALL, 128), F32)],
        compiler_params=params(12),
        name="apply_" + mode,
    )(*operands)


def spread(x):
    return jnp.broadcast_to(x, (8, 128))


def eliminate(rows, offset):
    groups, tiles = len(rows), len(rows[0])
    rows = [list(row) for row in rows]
    home, at = offset // 128, offset % 128
    sub = lax.broadcasted_iota(jnp.int32, (8, 128), 0)
    solved = []
    for h in range(groups):
        below = range(h + 1, groups)
        lane = at + 8 * h
        col = [{g: spread(rows[g][home][:, lane + q : lane + q + 1]) for g in range(h, groups)} for q in range(8)]
        cell = {(p, q): spread(col[p][h][q : q + 1]) for q in range(8) for p in range(q + 1)}
        row = [[spread(rows[h][t][q : q + 1]) for t in range(tiles)] for q in range(8)]
        done = []
        for m in range(0, 8, 2):
            n = m + 1
            a, b, c = cell[m, m], cell[m, n], cell[n, n]
            det = a * c - b * b
            r = pl.reciprocal(det, approx=True)
            later = range(m + 2, 8)
            u = {q: c * cell[m, q] - b * cell[n, q] for q in later}
            v = {q: a * cell[n, q] - b * cell[m, q] for q in later}
            for q in later:
                for p in range(m + 2, q + 1):
                    cell[p, q] = cell[p, q] - r * (cell[m, p] * u[q] + cell[n, p] * v[q])
            for q in later:
                for g in below:
                    col[q][g] = col[q][g] - r * (col[m][g] * u[q] + col[n][g] * v[q])
            for t in range(tiles):
                x = r * (c * row[m][t] - b * row[n][t])
                y = r * (a * row[n][t] - b * row[m][t])
                for q in later:
                    row[q][t] = row[q][t] - (cell[m, q] * x + cell[n, q] * y)
                for g in below:
                    rows[g][t] = rows[g][t] - (col[m][g] * x + col[n][g] * y)
            over = pl.reciprocal(a, approx=True)
            done.append([lax.rsqrt(a) * x for x in row[m]])
            scale = lax.rsqrt(det * over)
            done.append([scale * (x - (b * over) * w) for x, w in zip(row[n], row[m])])
        finished = []
        for t in range(tiles):
            x = done[7][t]
            for q in range(7):
                x = jnp.where(sub == q, done[q][t], x)
            finished.append(x)
        solved.append(finished)
    return solved


def tiled(x):
    return [
        [x[g * 8 : g * 8 + 8, t * 128 : t * 128 + 128] for t in range(x.shape[1] // 128)]
        for g in range(x.shape[0] // 8)
    ]


def joined(tiles):
    return jnp.concatenate([jnp.concatenate(row, axis=1) for row in tiles], axis=0)


def unit_scale(gram):
    lane = lax.broadcasted_iota(jnp.int32, gram.shape, 1)
    sub = lax.broadcasted_iota(jnp.int32, gram.shape, 0)
    kept = jnp.where(lane == sub, gram, 0.0)
    down = 1.0 / jnp.sqrt(jnp.sum(kept, axis=1, keepdims=True))
    across = jnp.sum(kept, axis=0, keepdims=True)
    across = 1.0 / jnp.sqrt(jnp.where(across == 0.0, 1.0, across))
    return gram * down * across, across


def gram_update(panel, first):
    a, b, c = split3(panel)
    left = jnp.concatenate([a, a, b, b, a, c], axis=0)
    right = jnp.concatenate([a, b, a, b, c, a], axis=0)
    parts = {
        at: lax.dot_general(left[:, at : at + 128], right, TRANS_A, preferred_element_type=F32)
        for at in range(first, panel.shape[1], 128)
    }
    return lambda at, count: parts[at // 128 * 128][at % 128 : at % 128 + count]


def solve_kernel(piece_count, *refs):
    grams, image_ref, out_ref = refs[:piece_count], refs[piece_count], refs[piece_count + 1]
    layers, k = image_ref.shape[:2]
    lane = lax.broadcasted_iota(jnp.int32, (k, 128), 1)
    sub = lax.broadcasted_iota(jnp.int32, (k, 128), 0)
    eye = jnp.where(lane == sub, 1.0, 0.0)
    for layer in range(layers):
        gram = add_pieces([ref[layer] for ref in grams])
        gram = jnp.concatenate([gram, jnp.zeros((k, 128 - k), F32)], axis=1)
        gram, across = unit_scale(gram)
        solved = eliminate(tiled(jnp.concatenate([gram, eye], axis=1)), 0)
        inverse = joined(solved)[:, 128:] * across
        solved = jnp.dot(inverse[:, :k], image_ref[layer], precision=HIGHEST, preferred_element_type=F32)
        out_ref[layer] = solved.astype(BF16)


def solve(grams, image):
    return pl.pallas_call(
        functools.partial(solve_kernel, len(grams)),
        in_specs=vmem_specs(len(grams) + 1),
        out_specs=pl.BlockSpec(memory_space=pltpu.VMEM),
        out_shape=jax.ShapeDtypeStruct(image.shape, BF16),
        compiler_params=params(4),
        name="solve_layers",
    )(*grams, image)


def stack_rows(refs, scratch):
    g = lax.axis_index("layer")
    rows = scratch.shape[0] // len(refs)
    for d, ref in enumerate(refs):
        at = lax.rem(g + d, len(refs)) * rows
        scratch[pl.ds(pl.multiple_of(at, rows), rows)] = ref[...].reshape(rows, ref.shape[-1])


def cross_kernel(piece_count, *refs):
    pieces, out_ref, stacked = refs[:piece_count], refs[piece_count], refs[piece_count + 1]
    stack_rows(pieces, stacked)
    own = pieces[0][...].reshape(-1, stacked.shape[1])
    out_ref[...] = lax.dot_general(
        own, stacked[...], TRANS_B, precision=HIGHEST, preferred_element_type=F32
    )


def cross(pieces):
    layers, k, width = pieces[0].shape
    rows = layers * k
    return pl.pallas_call(
        functools.partial(cross_kernel, len(pieces)),
        in_specs=vmem_specs(len(pieces)),
        out_specs=pl.BlockSpec(memory_space=pltpu.VMEM),
        out_shape=jax.ShapeDtypeStruct((rows, rows * len(pieces)), F32),
        scratch_shapes=[pltpu.VMEM((rows * len(pieces), width), F32)],
        compiler_params=params(6),
        name="cross_gram",
    )(*pieces)


def joint_kernel(piece_count, k, *refs):
    gram_refs, image_refs = refs[:piece_count], refs[piece_count : 2 * piece_count]
    out_ref, rounded_ref, work, stacked = refs[2 * piece_count :]
    stack_rows(gram_refs, work)
    stack_rows(image_refs, stacked)
    size = work.shape[0]
    steps = size // k
    lane = lax.broadcasted_iota(jnp.int32, (k, size), 1)
    lane_128 = lax.broadcasted_iota(jnp.int32, (k, 128), 1)
    sub_128 = lax.broadcasted_iota(jnp.int32, (k, 128), 0)
    gram, across = unit_scale(work[...])
    work[...] = gram
    for s in range(steps):
        lo, hi = s * k, (s + 1) * k
        here = (lane >= lo) & (lane < hi)
        eye = jnp.where(lane_128 == sub_128 + lo % 128, 1.0, 0.0)
        solved = joined(eliminate(tiled(jnp.concatenate([work[lo:hi], eye], axis=1)), lo))
        panel, tail = solved[:, :size], solved[:, size:]
        panel = jnp.where(here, jnp.concatenate([tail] * (size // 128), axis=1), panel)
        work[lo:hi] = jnp.where(lane < hi, panel, 0.0)
        if s + 1 < steps:
            update = gram_update(panel, hi // 128 * 128)
            for r in range(s + 1, steps):
                rows = work[r * k : r * k + k]
                work[r * k : r * k + k] = jnp.where(here, 0.0, rows) - update(r * k, k)
    rows = size // piece_count
    own = work[pl.ds(pl.multiple_of(lax.axis_index("layer") * rows, rows), rows)] * across
    joint = jnp.dot(own, stacked[...], precision=HIGHEST, preferred_element_type=F32)
    joint = joint.reshape(out_ref.shape)
    out_ref[...] = joint
    rounded_ref[...] = joint.astype(BF16)


def joint_solve(grams, images):
    layers, k, width = images[0].shape
    size = layers * k * len(images)
    return pl.pallas_call(
        functools.partial(joint_kernel, len(images), k),
        in_specs=vmem_specs(2 * len(images)),
        out_specs=vmem_specs(2),
        out_shape=[
            jax.ShapeDtypeStruct(images[0].shape, F32),
            jax.ShapeDtypeStruct(images[0].shape, BF16),
        ],
        scratch_shapes=[pltpu.VMEM((size, size), F32), pltpu.VMEM((size, width), F32)],
        compiler_params=params(8),
        name="joint_solve",
    )(*grams, *images)


def around(x, axis, count):
    pieces = [x]
    for d in range(1, count):
        pieces.append(lax.ppermute(x, axis, [((m + d) % count, m) for m in range(count)]))
    return pieces


def add_pieces(pieces):
    if len(pieces) == 1:
        return pieces[0]
    return (pieces[0] + pieces[2]) + (pieces[1] + pieces[3])


def per_device(shards, groups, blocks, block_rows, block_cols, counts, start):
    few = shards == 4
    cols_total = shards * BROWS
    live = jnp.arange(block_rows.shape[1], dtype=jnp.int32)[None, :] < counts
    cols = block_cols
    if few:
        cols = (cols - lax.axis_index("node") * BROWS + cols_total) % cols_total
    key = jnp.where(live, cols * BROWS + block_rows, -1)

    def gather(x):
        return around(x, "node", shards) if few else [lax.all_gather(x, "node")]

    def partials(x):
        return around(x, "node", shards) if few else [lax.psum(x, "node")]

    first = gather(start.astype(BF16))
    hi, lo = build_dense(key, blocks, cols_total // CHUNK_COLS)
    image, gram = apply_dense("gram", first, hi, lo)
    (image,) = apply_dense("plain", gather(solve(partials(gram), image)), hi, lo)
    images = around(image, "layer", groups)
    grams = around(add_pieces(partials(cross(images))), "layer", groups)
    joint_basis, rounded = joint_solve(grams, images)
    (partial,) = apply_dense("score", gather(rounded), hi, lo, joint_basis)
    return joint_basis, add_pieces(partials(partial))


def solution(mesh):
    in_specs = (
        P(("parts", "layer"), "node", None),
        P(("parts", "layer"), "node"),
        P(("parts", "layer"), "node"),
        P(("parts", "layer"), "node"),
        P(("parts", "layer"), None, "node"),
    )
    out_specs = (P(("parts", "layer"), None, "node"), P(("parts", "layer"), None, None))
    return jax.shard_map(
        functools.partial(per_device, mesh.shape["node"], mesh.shape["layer"]),
        mesh=mesh,
        in_specs=in_specs,
        out_specs=out_specs,
        check_vma=False,
    )
```

time: 123 us -> 103 us (0.84)
  Pallas kernels: 53.5 us -> 33.3 us
    pallas_call x1, Pallas kernels: 26.1 us -> 9.49 us  [joint_solve(): pl.pallas_call(functools.partial(joint_kernel, len(images), k), in_specs=...]
    pallas_call x4, Pallas kernels: 23.8 us -> 21.3 us  [the longest x3 15.9 us: apply_dense(): pl.pallas_call(functools.partial(apply_whole_kernel, mode, chunks), in_sp...]
  transfers between devices with their start and end apart: 24 -> 24, of which waited for: 16 -> 16; matrix products, arithmetic and copies ran while one was open for 1% -> 1% of each run, Pallas kernels for 6% -> 5%
where the time goes in v4:
time: 103 us
  Pallas kernels  33.3 us (32%)
  starting transfers between devices  32 us (31%)
  waiting for transfers between devices  30 us (29%)
  local copies, waits for them, and re-layouts  4.29 us (4%)
  other arithmetic  2.33 us (2%)
    ppermute x24, starting transfers between devices, around(): lax.ppermute(x, axis, [((m + d) % count, m) for m in range(count)])  32 us
    ppermute x24, waiting for transfers between devices, around(): lax.ppermute(x, axis, [((m + d) % count, m) for m in range(count)])  30 us
    pallas_call x3, Pallas kernels, apply_dense(): pl.pallas_call(functools.partial(apply_whole_kernel, mode, chunks), in_sp...  15.9 us
    pallas_call x1, Pallas kernels, joint_solve(): pl.pallas_call(functools.partial(joint_kernel, len(images), k), in_specs=...  9.49 us
    pallas_call x1, Pallas kernels, build_dense(): pl.pallas_call(build_whole_kernel, in_specs=[pl.BlockSpec(memory_space=pl...  5.39 us
    unnamed x4, local copies, waits for them, and re-layouts  4.29 us
  transfers between devices with their start and end apart: 24, of which 16 were waited for; matrix products, arithmetic and copies ran while one was open for 1% of the time, Pallas kernels for 5%

profile of v4, /device:TPU:0, one launch (start us, length us, event | category | flops | bytes accessed | tf_op | source)
XLA Modules:
  0.0 102.6 jit_solution(14379690186767739107)
XLA Ops:
  1.5 3.1 %collective-permute-start.2 = (bf16[2,32,512]{2,1,0:T(8,128)(2,1)S(1)}, bf16[2,32,512]{2,1,0:T(8,128)(2,1)S(1)}, u32[]{:S(2)}, u32[]{:S(2)}) collective-permute-start(bf16[2,32,512]{2,1,0:T(8,128)(2,1)S(1)} %convert_element_type.3.refs_0_), channel_id=1, source_target_pairs={{3,0},{0,1},{1,2},{2,3},{7,4},{4,5},{5,6},{6,7},{11,8},{8,9},{9,10... | collective-permute-start | bytes 196616 | tf_op jit(solution)/shard_map/ppermute | solution.py:449
  4.6 2.6 %collective-permute-start.1 = (bf16[2,32,512]{2,1,0:T(8,128)(2,1)S(1)}, bf16[2,32,512]{2,1,0:T(8,128)(2,1)S(1)}, u32[]{:S(2)}, u32[]{:S(2)}) collective-permute-start(bf16[2,32,512]{2,1,0:T(8,128)(2,1)S(1)} %convert_element_type.3.refs_0_), channel_id=1, source_target_pairs={{2,0},{3,1},{0,2},{1,3},{6,4},{7,5},{4,6},{5,7},{10,8},{11,9},{8,1... | collective-permute-start | bytes 196616 | tf_op jit(solution)/shard_map/ppermute | solution.py:449
  9.3 3.4 %copy-done = bf16[2,512,4096]{2,1,0:T(8,128)(2,1)S(1)} copy-done((bf16[2,512,4096]{2,1,0:T(8,128)(2,1)S(1)}, bf16[2,512,4096]{2,1,0:T(8,128)(2,1)}, u32[]{:S(2)}) %copy-start) | copy-done | bytes 8388632
  12.7 5.4 %build_dense.1 = (bf16[2,4,256,1024]{3,2,1,0:T(8,128)(2,1)S(1)}, bf16[2,4,256,1024]{3,2,1,0:T(8,128)(2,1)S(1)}) custom-call(s32[2,1,512]{2,1,0:T(1,128)S(1)} %reshape.7.key_ref, bf16[2,512,4096]{2,1,0:T(8,128)(2,1)S(1)} %copy-done), custom_call_target="tpu_custom_call" | custom-call | tf_op jit(solution)/shard_map/build_dense/pallas_call | solution.py:98
  18.2 5.4 %apply_gram.1 = (f32[2,32,512]{2,1,0:T(8,128)S(1)}, f32[2,32,32]{2,1,0:T(8,128)S(1)}) custom-call(bf16[2,32,512]{2,1,0:T(8,128)(2,1)S(1)} %convert_element_type.3.refs_0_, bf16[2,32,512]{2,1,0:T(8,128)(2,1)S(1)} %collective-permute-done.refs_1_, bf16[2,32,512]{2,1,0:T(8,128)(2,1)S(1)} %collective-permute-done.1.refs_2_, ...), custom_call_target="tpu_custom_call" | custom-call | tf_op jit(solution)/shard_map/apply_gram/pallas_call | solution.py:231
  24.6 2.8 %collective-permute-start.3 = (f32[2,32,32]{2,1,0:T(8,128)S(1)}, f32[2,32,32]{2,1,0:T(8,128)S(1)}, u32[]{:S(2)}, u32[]{:S(2)}) collective-permute-start(f32[2,32,32]{2,1,0:T(8,128)S(1)} %get-tuple-element.10.refs_0_), channel_id=1, source_target_pairs={{1,0},{2,1},{3,2},{0,3},{5,4},{6,5},{7,6},{4,7},{9,8},{10,9},{11,1... | collective-permute-start | bytes 24584 | tf_op jit(solution)/shard_map/ppermute | solution.py:449
  27.4 2.0 %collective-permute-done.5.refs_3_ = f32[2,32,32]{2,1,0:T(8,128)S(1)} collective-permute-done((f32[2,32,32]{2,1,0:T(8,128)S(1)}, f32[2,32,32]{2,1,0:T(8,128)S(1)}, u32[]{:S(2)}, u32[]{:S(2)}) %collective-permute-start.5) | collective-permute-done | bytes 8224 | tf_op jit(solution)/shard_map/ppermute | solution.py:449
  30.0 1.9 %solve_layers.1.refs_0_ = bf16[2,32,512]{2,1,0:T(8,128)(2,1)S(1)} custom-call(f32[2,32,32]{2,1,0:T(8,128)S(1)} %get-tuple-element.10.refs_0_, f32[2,32,32]{2,1,0:T(8,128)S(1)} %collective-permute-done.3.refs_1_, f32[2,32,32]{2,1,0:T(8,128)S(1)} %collective-permute-done.4.refs_2_, f32[2,32,32]{2,1,0:T(8,128)S(1)} %collective-permute-done.5.refs_3_, ...), custom_call_target="tpu_custom_call" | custom-call | tf_op jit(solution)/shard_map/solve_layers/pallas_call | solution.py:355
  31.9 2.0 %collective-permute-start.8 = (bf16[2,32,512]{2,1,0:T(8,128)(2,1)S(1)}, bf16[2,32,512]{2,1,0:T(8,128)(2,1)S(1)}, u32[]{:S(2)}, u32[]{:S(2)}) collective-permute-start(bf16[2,32,512]{2,1,0:T(8,128)(2,1)S(1)} %solve_layers.1.refs_0_), channel_id=1, source_target_pairs={{3,0},{0,1},{1,2},{2,3},{7,4},{4,5},{5,6},{6,7},{11,8},{8,9},{9,10... | collective-permute-start | bytes 196616 | tf_op jit(solution)/shard_map/ppermute | solution.py:449
  33.8 1.8 %collective-permute-start.7 = (bf16[2,32,512]{2,1,0:T(8,128)(2,1)S(1)}, bf16[2,32,512]{2,1,0:T(8,128)(2,1)S(1)}, u32[]{:S(2)}, u32[]{:S(2)}) collective-permute-start(bf16[2,32,512]{2,1,0:T(8,128)(2,1)S(1)} %solve_layers.1.refs_0_), channel_id=1, source_target_pairs={{2,0},{3,1},{0,2},{1,3},{6,4},{7,5},{4,6},{5,7},{10,8},{11,9},{8,1... | collective-permute-start | bytes 196616 | tf_op jit(solution)/shard_map/ppermute | solution.py:449
  40.0 5.1 %apply_plain.1.refs_0_.refs_4_ = f32[2,32,512]{2,1,0:T(8,128)S(1)} custom-call(bf16[2,32,512]{2,1,0:T(8,128)(2,1)S(1)} %solve_layers.1.refs_0_, bf16[2,32,512]{2,1,0:T(8,128)(2,1)S(1)} %collective-permute-done.6.refs_1_, bf16[2,32,512]{2,1,0:T(8,128)(2,1)S(1)} %collective-permute-done.7.refs_2_, bf16[2,32,512]{2,1,0:T(8,128)(2,1)S(1)} %collective-permute-done.8.refs_3_, ...), custom_call_target="tpu_custom_call" | custom-call | tf_op jit(solution)/shard_map/apply_plain/pallas_call | solution.py:231
  48.1 2.3 %collective-permute-done.11.refs_3_.refs_7_ = f32[2,32,512]{2,1,0:T(8,128)S(1)} collective-permute-done((f32[2,32,512]{2,1,0:T(8,128)S(1)}, f32[2,32,512]{2,1,0:T(8,128)S(1)}, u32[]{:S(2)}, u32[]{:S(2)}) %collective-permute-start.11) | collective-permute-done | bytes 131104 | tf_op jit(solution)/shard_map/ppermute | solution.py:449
  54.0 3.3 %collective-permute-start.13 = (f32[64,256]{1,0:T(8,128)S(1)}, f32[64,256]{1,0:T(8,128)S(1)}, u32[]{:S(2)}, u32[]{:S(2)}) collective-permute-start(f32[64,256]{1,0:T(8,128)S(1)} %cross_gram.1), channel_id=1, source_target_pairs={{1,0},{2,1},{3,2},{0,3},{5,4},{6,5},{7,6},{4,7},{9,8},{10,9},{11,1... | collective-permute-start | bytes 196616 | tf_op jit(solution)/shard_map/ppermute | solution.py:449
  57.3 3.0 %collective-permute-done.14 = f32[64,256]{1,0:T(8,128)S(1)} collective-permute-done((f32[64,256]{1,0:T(8,128)S(1)}, f32[64,256]{1,0:T(8,128)S(1)}, u32[]{:S(2)}, u32[]{:S(2)}) %collective-permute-start.14) | collective-permute-done | bytes 65568 | tf_op jit(solution)/shard_map/ppermute | solution.py:449
  60.3 3.6 %collective-permute-done.12 = f32[64,256]{1,0:T(8,128)S(1)} collective-permute-done((f32[64,256]{1,0:T(8,128)S(1)}, f32[64,256]{1,0:T(8,128)S(1)}, u32[]{:S(2)}, u32[]{:S(2)}) %collective-permute-start.12) | collective-permute-done | bytes 65568 | tf_op jit(solution)/shard_map/ppermute | solution.py:449
  68.9 9.5 %joint_solve.1 = (f32[2,32,512]{2,1,0:T(8,128)}, bf16[2,32,512]{2,1,0:T(8,128)(2,1)S(1)}) custom-call(f32[64,256]{1,0:T(8,128)S(1)} %add_add_fusion.refs_0_, f32[64,256]{1,0:T(8,128)S(1)} %collective-permute-done.15.refs_1_, f32[64,256]{1,0:T(8,128)S(1)} %collective-permute-done.16.refs_2_, f32[64,256]{1,0:T(8,128)S(1)} %collective-permute-done.17.refs_3_, ...), custom_call_target="tpu_custom_call" | custom-call | tf_op jit(solution)/shard_map/joint_solve/pallas_call | solution.py:432
  78.4 2.5 %collective-permute-start.19 = (bf16[2,32,512]{2,1,0:T(8,128)(2,1)S(1)}, bf16[2,32,512]{2,1,0:T(8,128)(2,1)S(1)}, u32[]{:S(2)}, u32[]{:S(2)}) collective-permute-start(bf16[2,32,512]{2,1,0:T(8,128)(2,1)S(1)} %get-tuple-element.13.refs_0_), channel_id=1, source_target_pairs={{2,0},{3,1},{0,2},{1,3},{6,4},{7,5},{4,6},{5,7},{10,8},{11,9},{8,1... | collective-permute-start | bytes 196616 | tf_op jit(solution)/shard_map/ppermute | solution.py:449
  82.2 2.9 %collective-permute-done.20.refs_3_ = bf16[2,32,512]{2,1,0:T(8,128)(2,1)S(1)} collective-permute-done((bf16[2,32,512]{2,1,0:T(8,128)(2,1)S(1)}, bf16[2,32,512]{2,1,0:T(8,128)(2,1)S(1)}, u32[]{:S(2)}, u32[]{:S(2)}) %collective-permute-start.20) | collective-permute-done | bytes 65568 | tf_op jit(solution)/shard_map/ppermute | solution.py:449
  85.2 1.8 %collective-permute-done.19.refs_2_ = bf16[2,32,512]{2,1,0:T(8,128)(2,1)S(1)} collective-permute-done((bf16[2,32,512]{2,1,0:T(8,128)(2,1)S(1)}, bf16[2,32,512]{2,1,0:T(8,128)(2,1)S(1)}, u32[]{:S(2)}, u32[]{:S(2)}) %collective-permute-start.19) | collective-permute-done | bytes 65568 | tf_op jit(solution)/shard_map/ppermute | solution.py:449
  87.9 5.4 %apply_score.1 = f32[2,32,32]{2,1,0:T(8,128)S(1)} custom-call(bf16[2,32,512]{2,1,0:T(8,128)(2,1)S(1)} %get-tuple-element.13.refs_0_, bf16[2,32,512]{2,1,0:T(8,128)(2,1)S(1)} %collective-permute-done.18.refs_1_, bf16[2,32,512]{2,1,0:T(8,128)(2,1)S(1)} %collective-permute-done.19.refs_2_, bf16[2,32,512]{2,1,0:T(8,128)(2,1)S(1)} %collective-permute-done.20.refs_3_, ...), custom_call_target="tpu_custom_call" | custom-call | tf_op jit(solution)/shard_map/apply_score/pallas_call | solution.py:231
  93.3 1.7 %collective-permute-start.23 = (f32[2,32,32]{2,1,0:T(8,128)S(1)}, f32[2,32,32]{2,1,0:T(8,128)S(1)}, u32[]{:S(2)}, u32[]{:S(2)}) collective-permute-start(f32[2,32,32]{2,1,0:T(8,128)S(1)} %apply_score.1), channel_id=1, source_target_pairs={{3,0},{0,1},{1,2},{2,3},{7,4},{4,5},{5,6},{6,7},{11,8},{8,9},{9,10... | collective-permute-start | bytes 24584 | tf_op jit(solution)/shard_map/ppermute | solution.py:449
  95.0 2.1 %collective-permute-start.22 = (f32[2,32,32]{2,1,0:T(8,128)S(1)}, f32[2,32,32]{2,1,0:T(8,128)S(1)}, u32[]{:S(2)}, u32[]{:S(2)}) collective-permute-start(f32[2,32,32]{2,1,0:T(8,128)S(1)} %apply_score.1), channel_id=1, source_target_pairs={{1,0},{2,1},{3,2},{0,3},{5,4},{6,5},{7,6},{4,7},{9,8},{10,9},{11,1... | collective-permute-start | bytes 24584 | tf_op jit(solution)/shard_map/ppermute | solution.py:449
  97.2 2.2 %collective-permute-done.23 = f32[2,32,32]{2,1,0:T(8,128)S(1)} collective-permute-done((f32[2,32,32]{2,1,0:T(8,128)S(1)}, f32[2,32,32]{2,1,0:T(8,128)S(1)}, u32[]{:S(2)}, u32[]{:S(2)}) %collective-permute-start.23) | collective-permute-done | bytes 8224 | tf_op jit(solution)/shard_map/ppermute | solution.py:449
  99.3 2.7 %collective-permute-done.21 = f32[2,32,32]{2,1,0:T(8,128)S(1)} collective-permute-done((f32[2,32,32]{2,1,0:T(8,128)S(1)}, f32[2,32,32]{2,1,0:T(8,128)S(1)}, u32[]{:S(2)}, u32[]{:S(2)}) %collective-permute-start.21) | collective-permute-done | bytes 8224 | tf_op jit(solution)/shard_map/ppermute | solution.py:449
  (40 shorter events, 23.6 us)
Async XLA Ops:
  1.5 16.6 %collective-permute-start.2 = (bf16[2,32,512]{2,1,0:T(8,128)(2,1)S(1)}, bf16[2,32,512]{2,1,0:T(8,128)(2,1)S(1)}, u32[]{:S(2)}, u32[]{:S(2)}) collective-permute-start(bf16[2,32,512]{2,1,0:T(8,128)(2,1)S(1)} %convert_element_type.3.refs_0_), channel_id=1, source_target_pairs={{3,0},{0,1},{1,2},{2,3},{7,4},{4,5},{5,6},{6,7},{11,8},{8,9},{9,10... | collective-permute-start | bytes 196616 | tf_op jit(solution)/shard_map/ppermute | solution.py:449
  4.6 13.5 %collective-permute-start.1 = (bf16[2,32,512]{2,1,0:T(8,128)(2,1)S(1)}, bf16[2,32,512]{2,1,0:T(8,128)(2,1)S(1)}, u32[]{:S(2)}, u32[]{:S(2)}) collective-permute-start(bf16[2,32,512]{2,1,0:T(8,128)(2,1)S(1)} %convert_element_type.3.refs_0_), channel_id=1, source_target_pairs={{2,0},{3,1},{0,2},{1,3},{6,4},{7,5},{4,6},{5,7},{10,8},{11,9},{8,1... | collective-permute-start | bytes 196616 | tf_op jit(solution)/shard_map/ppermute | solution.py:449
  7.2 10.9 %collective-permute-start = (bf16[2,32,512]{2,1,0:T(8,128)(2,1)S(1)}, bf16[2,32,512]{2,1,0:T(8,128)(2,1)S(1)}, u32[]{:S(2)}, u32[]{:S(2)}) collective-permute-start(bf16[2,32,512]{2,1,0:T(8,128)(2,1)S(1)} %convert_element_type.3.refs_0_), channel_id=1, source_target_pairs={{1,0},{2,1},{3,2},{0,3},{5,4},{6,5},{7,6},{4,7},{9,8},{10,9},{11,1... | collective-permute-start | bytes 196616 | tf_op jit(solution)/shard_map/ppermute | solution.py:449
  23.6 5.8 %collective-permute-start.5 = (f32[2,32,32]{2,1,0:T(8,128)S(1)}, f32[2,32,32]{2,1,0:T(8,128)S(1)}, u32[]{:S(2)}, u32[]{:S(2)}) collective-permute-start(f32[2,32,32]{2,1,0:T(8,128)S(1)} %get-tuple-element.10.refs_0_), channel_id=1, source_target_pairs={{3,0},{0,1},{1,2},{2,3},{7,4},{4,5},{5,6},{6,7},{11,8},{8,9},{9,10... | collective-permute-start | bytes 24584 | tf_op jit(solution)/shard_map/ppermute | solution.py:449
  24.3 5.7 %collective-permute-start.4 = (f32[2,32,32]{2,1,0:T(8,128)S(1)}, f32[2,32,32]{2,1,0:T(8,128)S(1)}, u32[]{:S(2)}, u32[]{:S(2)}) collective-permute-start(f32[2,32,32]{2,1,0:T(8,128)S(1)} %get-tuple-element.10.refs_0_), channel_id=1, source_target_pairs={{2,0},{3,1},{0,2},{1,3},{6,4},{7,5},{4,6},{5,7},{10,8},{11,9},{8,1... | collective-permute-start | bytes 24584 | tf_op jit(solution)/shard_map/ppermute | solution.py:449
  24.6 5.4 %collective-permute-start.3 = (f32[2,32,32]{2,1,0:T(8,128)S(1)}, f32[2,32,32]{2,1,0:T(8,128)S(1)}, u32[]{:S(2)}, u32[]{:S(2)}) collective-permute-start(f32[2,32,32]{2,1,0:T(8,128)S(1)} %get-tuple-element.10.refs_0_), channel_id=1, source_target_pairs={{1,0},{2,1},{3,2},{0,3},{5,4},{6,5},{7,6},{4,7},{9,8},{10,9},{11,1... | collective-permute-start | bytes 24584 | tf_op jit(solution)/shard_map/ppermute | solution.py:449
  31.9 6.1 %collective-permute-start.8 = (bf16[2,32,512]{2,1,0:T(8,128)(2,1)S(1)}, bf16[2,32,512]{2,1,0:T(8,128)(2,1)S(1)}, u32[]{:S(2)}, u32[]{:S(2)}) collective-permute-start(bf16[2,32,512]{2,1,0:T(8,128)(2,1)S(1)} %solve_layers.1.refs_0_), channel_id=1, source_target_pairs={{3,0},{0,1},{1,2},{2,3},{7,4},{4,5},{5,6},{6,7},{11,8},{8,9},{9,10... | collective-permute-start | bytes 196616 | tf_op jit(solution)/shard_map/ppermute | solution.py:449
  33.8 5.6 %collective-permute-start.7 = (bf16[2,32,512]{2,1,0:T(8,128)(2,1)S(1)}, bf16[2,32,512]{2,1,0:T(8,128)(2,1)S(1)}, u32[]{:S(2)}, u32[]{:S(2)}) collective-permute-start(bf16[2,32,512]{2,1,0:T(8,128)(2,1)S(1)} %solve_layers.1.refs_0_), channel_id=1, source_target_pairs={{2,0},{3,1},{0,2},{1,3},{6,4},{7,5},{4,6},{5,7},{10,8},{11,9},{8,1... | collective-permute-start | bytes 196616 | tf_op jit(solution)/shard_map/ppermute | solution.py:449
  35.6 4.4 %collective-permute-start.6 = (bf16[2,32,512]{2,1,0:T(8,128)(2,1)S(1)}, bf16[2,32,512]{2,1,0:T(8,128)(2,1)S(1)}, u32[]{:S(2)}, u32[]{:S(2)}) collective-permute-start(bf16[2,32,512]{2,1,0:T(8,128)(2,1)S(1)} %solve_layers.1.refs_0_), channel_id=1, source_target_pairs={{1,0},{2,1},{3,2},{0,3},{5,4},{6,5},{7,6},{4,7},{9,8},{10,9},{11,1... | collective-permute-start | bytes 196616 | tf_op jit(solution)/shard_map/ppermute | solution.py:449
  45.1 5.2 %collective-permute-start.11 = (f32[2,32,512]{2,1,0:T(8,128)S(1)}, f32[2,32,512]{2,1,0:T(8,128)S(1)}, u32[]{:S(2)}, u32[]{:S(2)}) collective-permute-start(f32[2,32,512]{2,1,0:T(8,128)S(1)} %apply_plain.1.refs_0_.refs_4_), channel_id=1, source_target_pairs={{12,0},{0,4},{4,8},{8,12},{13,1},{1,5},{5,9},{9,13},{14,2},{2,6},{... | collective-permute-start | bytes 393224 | tf_op jit(solution)/shard_map/ppermute | solution.py:449
  45.1 6.4 %collective-permute-start.10 = (f32[2,32,512]{2,1,0:T(8,128)S(1)}, f32[2,32,512]{2,1,0:T(8,128)S(1)}, u32[]{:S(2)}, u32[]{:S(2)}) collective-permute-start(f32[2,32,512]{2,1,0:T(8,128)S(1)} %apply_plain.1.refs_0_.refs_4_), channel_id=1, source_target_pairs={{8,0},{12,4},{0,8},{4,12},{9,1},{13,5},{1,9},{5,13},{10,2},{14,6},... | collective-permute-start | bytes 393224 | tf_op jit(solution)/shard_map/ppermute | solution.py:449
  46.7 6.1 %collective-permute-start.9 = (f32[2,32,512]{2,1,0:T(8,128)S(1)}, f32[2,32,512]{2,1,0:T(8,128)S(1)}, u32[]{:S(2)}, u32[]{:S(2)}) collective-permute-start(f32[2,32,512]{2,1,0:T(8,128)S(1)} %apply_plain.1.refs_0_.refs_4_), channel_id=1, source_target_pairs={{4,0},{8,4},{12,8},{0,12},{5,1},{9,5},{13,9},{1,13},{6,2},{10,6},{... | collective-permute-start | bytes 393224 | tf_op jit(solution)/shard_map/ppermute | solution.py:449
  53.4 6.9 %collective-permute-start.14 = (f32[64,256]{1,0:T(8,128)S(1)}, f32[64,256]{1,0:T(8,128)S(1)}, u32[]{:S(2)}, u32[]{:S(2)}) collective-permute-start(f32[64,256]{1,0:T(8,128)S(1)} %cross_gram.1), channel_id=1, source_target_pairs={{3,0},{0,1},{1,2},{2,3},{7,4},{4,5},{5,6},{6,7},{11,8},{8,9},{9,10... | collective-permute-start | bytes 196616 | tf_op jit(solution)/shard_map/ppermute | solution.py:449
  54.0 6.2 %collective-permute-start.13 = (f32[64,256]{1,0:T(8,128)S(1)}, f32[64,256]{1,0:T(8,128)S(1)}, u32[]{:S(2)}, u32[]{:S(2)}) collective-permute-start(f32[64,256]{1,0:T(8,128)S(1)} %cross_gram.1), channel_id=1, source_target_pairs={{1,0},{2,1},{3,2},{0,3},{5,4},{6,5},{7,6},{4,7},{9,8},{10,9},{11,1... | collective-permute-start | bytes 196616 | tf_op jit(solution)/shard_map/ppermute | solution.py:449
  57.3 6.6 %collective-permute-start.12 = (f32[64,256]{1,0:T(8,128)S(1)}, f32[64,256]{1,0:T(8,128)S(1)}, u32[]{:S(2)}, u32[]{:S(2)}) collective-permute-start(f32[64,256]{1,0:T(8,128)S(1)} %cross_gram.1), channel_id=1, source_target_pairs={{2,0},{3,1},{0,2},{1,3},{6,4},{7,5},{4,6},{5,7},{10,8},{11,9},{8,1... | collective-permute-start | bytes 196616 | tf_op jit(solution)/shard_map/ppermute | solution.py:449
  63.9 3.8 %collective-permute-start.17 = (f32[64,256]{1,0:T(8,128)S(1)}, f32[64,256]{1,0:T(8,128)S(1)}, u32[]{:S(2)}, u32[]{:S(2)}) collective-permute-start(f32[64,256]{1,0:T(8,128)S(1)} %add_add_fusion.refs_0_), channel_id=1, source_target_pairs={{12,0},{0,4},{4,8},{8,12},{13,1},{1,5},{5,9},{9,13},{14,2},{2,6},{... | collective-permute-start | bytes 196616 | tf_op jit(solution)/shard_map/ppermute | solution.py:449
  63.9 5.0 %collective-permute-start.16 = (f32[64,256]{1,0:T(8,128)S(1)}, f32[64,256]{1,0:T(8,128)S(1)}, u32[]{:S(2)}, u32[]{:S(2)}) collective-permute-start(f32[64,256]{1,0:T(8,128)S(1)} %add_add_fusion.refs_0_), channel_id=1, source_target_pairs={{8,0},{12,4},{0,8},{4,12},{9,1},{13,5},{1,9},{5,13},{10,2},{14,6},... | collective-permute-start | bytes 196616 | tf_op jit(solution)/shard_map/ppermute | solution.py:449
  64.7 4.2 %collective-permute-start.15 = (f32[64,256]{1,0:T(8,128)S(1)}, f32[64,256]{1,0:T(8,128)S(1)}, u32[]{:S(2)}, u32[]{:S(2)}) collective-permute-start(f32[64,256]{1,0:T(8,128)S(1)} %add_add_fusion.refs_0_), channel_id=1, source_target_pairs={{4,0},{8,4},{12,8},{0,12},{5,1},{9,5},{13,9},{1,13},{6,2},{10,6},{... | collective-permute-start | bytes 196616 | tf_op jit(solution)/shard_map/ppermute | solution.py:449
  78.4 6.8 %collective-permute-start.20 = (bf16[2,32,512]{2,1,0:T(8,128)(2,1)S(1)}, bf16[2,32,512]{2,1,0:T(8,128)(2,1)S(1)}, u32[]{:S(2)}, u32[]{:S(2)}) collective-permute-start(bf16[2,32,512]{2,1,0:T(8,128)(2,1)S(1)} %get-tuple-element.13.refs_0_), channel_id=1, source_target_pairs={{3,0},{0,1},{1,2},{2,3},{7,4},{4,5},{5,6},{6,7},{11,8},{8,9},{9,10... | collective-permute-start | bytes 196616 | tf_op jit(solution)/shard_map/ppermute | solution.py:449
  78.4 8.6 %collective-permute-start.19 = (bf16[2,32,512]{2,1,0:T(8,128)(2,1)S(1)}, bf16[2,32,512]{2,1,0:T(8,128)(2,1)S(1)}, u32[]{:S(2)}, u32[]{:S(2)}) collective-permute-start(bf16[2,32,512]{2,1,0:T(8,128)(2,1)S(1)} %get-tuple-element.13.refs_0_), channel_id=1, source_target_pairs={{2,0},{3,1},{0,2},{1,3},{6,4},{7,5},{4,6},{5,7},{10,8},{11,9},{8,1... | collective-permute-start | bytes 196616 | tf_op jit(solution)/shard_map/ppermute | solution.py:449
  80.9 6.1 %collective-permute-start.18 = (bf16[2,32,512]{2,1,0:T(8,128)(2,1)S(1)}, bf16[2,32,512]{2,1,0:T(8,128)(2,1)S(1)}, u32[]{:S(2)}, u32[]{:S(2)}) collective-permute-start(bf16[2,32,512]{2,1,0:T(8,128)(2,1)S(1)} %get-tuple-element.13.refs_0_), channel_id=1, source_target_pairs={{1,0},{2,1},{3,2},{0,3},{5,4},{6,5},{7,6},{4,7},{9,8},{10,9},{11,1... | collective-permute-start | bytes 196616 | tf_op jit(solution)/shard_map/ppermute | solution.py:449
  93.3 6.0 %collective-permute-start.23 = (f32[2,32,32]{2,1,0:T(8,128)S(1)}, f32[2,32,32]{2,1,0:T(8,128)S(1)}, u32[]{:S(2)}, u32[]{:S(2)}) collective-permute-start(f32[2,32,32]{2,1,0:T(8,128)S(1)} %apply_score.1), channel_id=1, source_target_pairs={{3,0},{0,1},{1,2},{2,3},{7,4},{4,5},{5,6},{6,7},{11,8},{8,9},{9,10... | collective-permute-start | bytes 24584 | tf_op jit(solution)/shard_map/ppermute | solution.py:449
  95.0 4.3 %collective-permute-start.22 = (f32[2,32,32]{2,1,0:T(8,128)S(1)}, f32[2,32,32]{2,1,0:T(8,128)S(1)}, u32[]{:S(2)}, u32[]{:S(2)}) collective-permute-start(f32[2,32,32]{2,1,0:T(8,128)S(1)} %apply_score.1), channel_id=1, source_target_pairs={{1,0},{2,1},{3,2},{0,3},{5,4},{6,5},{7,6},{4,7},{9,8},{10,9},{11,1... | collective-permute-start | bytes 24584 | tf_op jit(solution)/shard_map/ppermute | solution.py:449
  97.2 4.8 %collective-permute-start.21 = (f32[2,32,32]{2,1,0:T(8,128)S(1)}, f32[2,32,32]{2,1,0:T(8,128)S(1)}, u32[]{:S(2)}, u32[]{:S(2)}) collective-permute-start(f32[2,32,32]{2,1,0:T(8,128)S(1)} %apply_score.1), channel_id=1, source_target_pairs={{2,0},{3,1},{0,2},{1,3},{6,4},{7,5},{4,6},{5,7},{10,8},{11,9},{8,1... | collective-permute-start | bytes 24584 | tf_op jit(solution)/shard_map/ppermute | solution.py:449
  (2 other events, 4.3 us)

commit v5 on v4

--- a/solution.py
+++ b/solution.py
@@ -29,39 +29,42 @@
     return [pl.BlockSpec(memory_space=pltpu.VMEM)] * count
 
 
-def place(z, chunks, u, hi_ref, lo_ref, layer):
-    out_rows = pl.ds(pl.multiple_of(u * 16, 16), 16)
+def place(z, chunks, u, dense_ref, layer):
     for c in range(chunks * CHUNK_COLS):
         piece = z[c * 8 : c * 8 + 8]
         piece = jnp.concatenate([piece[:, :128], piece[:, 128:]], axis=0)
         hi = piece.astype(BF16)
         lo = (piece - hi.astype(F32)).astype(BF16)
         lanes = slice((c % CHUNK_COLS) * 128, (c % CHUNK_COLS) * 128 + 128)
-        hi_ref[layer, c // CHUNK_COLS, out_rows, lanes] = hi
-        lo_ref[layer, c // CHUNK_COLS, out_rows, lanes] = lo
-
-
-def one_hot(key, base, positions):
+        dense_ref[layer, c // CHUNK_COLS, pl.ds(pl.multiple_of(u * 16, 16), 16), lanes] = hi
+        dense_ref[layer, c // CHUNK_COLS, pl.ds(pl.multiple_of(u * 16 + TALL, 16), 16), lanes] = lo
+
+
+def one_hot(rows_ref, cols_ref, counts_ref, layer, flip, base, positions):
+    slot = lax.broadcasted_iota(jnp.int32, (1, rows_ref.shape[2]), 1)
+    key = (cols_ref[layer] ^ flip) * BROWS + rows_ref[layer]
+    key = jnp.where(slot < counts_ref[layer], key, -1)
     position = lax.broadcasted_iota(jnp.int32, (positions, key.shape[1]), 0) + base
     return jnp.where(position == key, 1.0, 0.0).astype(BF16)
 
 
-def build_kernel(key_ref, blocks_ref, hi_ref, lo_ref):
-    chunks = hi_ref.shape[1]
+def build_kernel(rows_ref, cols_ref, counts_ref, blocks_ref, dense_ref):
+    chunks = dense_ref.shape[1]
     positions = chunks * CHUNK_COLS * BROWS
-    onehot = one_hot(key_ref[0], pl.program_id(1) * positions, positions)
+    base = pl.program_id(1) * positions
+    onehot = one_hot(rows_ref, cols_ref, counts_ref, pl.program_id(0), 0, base, positions)
 
     def step(u, carry):
         cols = pl.ds(pl.multiple_of(u * 256, 256), 256)
         z = jnp.dot(onehot, blocks_ref[0, :, cols], preferred_element_type=F32)
-        place(z, chunks, u, hi_ref, lo_ref, 0)
+        place(z, chunks, u, dense_ref, 0)
         return carry
 
     lax.fori_loop(0, BLK * BLK // 256, step, 0)
 
 
-def build_whole_kernel(key_ref, blocks_ref, hi_ref, lo_ref, held, arrived):
-    layers, chunks = hi_ref.shape[:2]
+def build_whole_kernel(rows_ref, cols_ref, counts_ref, blocks_ref, dense_ref, held, arrived):
+    layers, chunks = dense_ref.shape[:2]
     pieces = arrived.shape[1]
     width = held.shape[2] // pieces
     inner = width // 256
@@ -75,48 +78,50 @@
     for layer in range(layers):
         for piece in range(pieces):
             fetch(layer, piece).start()
+    flip = lax.axis_index("node") * CHUNK_COLS
     for layer in range(layers):
-        onehot = one_hot(key_ref[layer], 0, chunks * CHUNK_COLS * BROWS)
+        onehot = one_hot(rows_ref, cols_ref, counts_ref, layer, flip, 0, chunks * CHUNK_COLS * BROWS)
 
         def step(piece, carry):
             fetch(layer, piece).wait()
             for v in range(inner):
                 cols = pl.ds(pl.multiple_of(piece * width + v * 256, 256), 256)
                 z = jnp.dot(onehot, held[layer, :, cols], preferred_element_type=F32)
-                place(z, chunks, piece * inner + v, hi_ref, lo_ref, layer)
+                place(z, chunks, piece * inner + v, dense_ref, layer)
             return carry
 
         lax.fori_loop(0, pieces, step, 0)
 
 
-def build_dense(key, blocks, chunk_total):
+def build_dense(block_rows, block_cols, counts, blocks, chunk_total):
     layers, slots, width = blocks.shape
-    dense = jax.ShapeDtypeStruct((layers, chunk_total, TALL, CHUNK_LANES), BF16)
-    key = key.reshape(layers, 1, slots)
+    dense = jax.ShapeDtypeStruct((layers, chunk_total, 2 * TALL, CHUNK_LANES), BF16)
+    operands = (block_rows[:, None], block_cols[:, None], counts[:, 0], pltpu.with_memory_space_constraint(blocks, pltpu.HBM))
     if chunk_total <= 4:
         pieces = 4
         return pl.pallas_call(
             build_whole_kernel,
-            in_specs=[pl.BlockSpec(memory_space=pltpu.VMEM), pl.BlockSpec(memory_space=pltpu.HBM)],
-            out_specs=vmem_specs(2),
-            out_shape=[dense, dense],
+            in_specs=vmem_specs(2)
+            + [pl.BlockSpec(memory_space=pltpu.SMEM), pl.BlockSpec(memory_space=pltpu.HBM)],
+            out_specs=pl.BlockSpec(memory_space=pltpu.VMEM),
+            out_shape=dense,
             scratch_shapes=[pltpu.VMEM(blocks.shape, BF16), pltpu.SemaphoreType.DMA((layers, pieces))],
-            compiler_params=params(24),
+            compiler_params=params(28),
             name="build_dense",
-        )(key, blocks)
-    out_spec = pl.BlockSpec((1, 4, TALL, CHUNK_LANES), lambda l, s: (l, s, 0, 0))
+        )(*operands)
     return pl.pallas_call(
         build_kernel,
         grid=(layers, chunk_total // 4),
-        in_specs=[
-            pl.BlockSpec((1, 1, slots), lambda l, s: (l, 0, 0)),
+        in_specs=vmem_specs(2)
+        + [
+            pl.BlockSpec(memory_space=pltpu.SMEM),
             pl.BlockSpec((1, slots, width), lambda l, s: (l, 0, 0)),
         ],
-        out_specs=[out_spec, out_spec],
-        out_shape=[dense, dense],
+        out_specs=pl.BlockSpec((1, 4, 2 * TALL, CHUNK_LANES), lambda l, s: (l, s, 0, 0)),
+        out_shape=dense,
         compiler_params=params(24),
         name="build_dense",
-    )(key, blocks)
+    )(*operands)
 
 
 def split3(x):
@@ -127,40 +132,26 @@
     return a, b, c
 
 
-def image_part(basis, hi, lo):
+def image_part(basis, dense):
     k, width = basis.shape
     basis = basis.astype(F32)
-    low = lax.broadcasted_iota(jnp.int32, (k, 128), 1) < BLK
-    first, second = [], []
-    for q in range(width // 128):
-        b = basis[:, q * 128 : q * 128 + 128]
-        br = pltpu.roll(b, BLK, 1)
-        first += [jnp.where(low, b, 0.0), jnp.where(low, br, 0.0)]
-        second += [jnp.where(low, 0.0, br), jnp.where(low, 0.0, b)]
-    weights = jnp.concatenate(
-        [
-            jnp.concatenate(first, axis=1),
-            jnp.concatenate(second, axis=1),
-            jnp.zeros((128 - 2 * k, CHUNK_LANES), F32),
-        ],
-        axis=0,
-    ).astype(BF16)
-    total = lax.dot_general(hi, weights, TRANS_B, preferred_element_type=F32)
-    return total + lax.dot_general(lo, weights, TRANS_B, preferred_element_type=F32)
-
-
-def node_order():
-    row = lax.broadcasted_iota(jnp.int32, (ROWS_DEV, ROWS_DEV), 0)
-    col = lax.broadcasted_iota(jnp.int32, (ROWS_DEV, ROWS_DEV), 1)
-    target = (row % 8) * BLK + 2 * ((row % TALL) // 8) + row // TALL
-    return jnp.where(target == col, 1.0, 0.0).astype(BF16)
-
-
-def to_wide(total, perm, k):
-    turned = total.T
-    wide = jnp.concatenate([turned[:k], turned[k : 2 * k]], axis=1)
-    moved = jnp.dot(jnp.concatenate(split3(wide), axis=0), perm, preferred_element_type=F32)
-    return moved[:k] + moved[k : 2 * k] + moved[2 * k :]
+    tall = jnp.concatenate([basis, basis, jnp.zeros((128 - 2 * k, width), F32)], axis=0).T
+    lane = lax.broadcasted_iota(jnp.int32, tall.shape, 1)
+    first = jnp.where(lane < k, tall, 0.0).astype(BF16)
+    second = jnp.where(lane < k, 0.0, tall).astype(BF16)
+    weights = []
+    for c in range(width // BLK):
+        weights += [first[c * BLK : c * BLK + BLK], second[c * BLK : c * BLK + BLK]]
+    return jnp.dot(dense, jnp.concatenate(weights, axis=0), preferred_element_type=F32)
+
+
+def to_wide(total, k, halves, tall):
+    halves[...] = total[:TALL] + total[TALL:]
+    for b in range(BROWS):
+        part = halves[pl.ds(b, BLK // 2, stride=BROWS), :]
+        tall[pl.ds(BLK * b, BLK // 2, stride=2), :] = part
+        tall[pl.ds(BLK * b + 1, BLK // 2, stride=2), :] = pltpu.roll(part, 128 - k, 1)
+    return tall[...].T[:k]
 
 
 def dot_rows(a, b):
@@ -171,15 +162,10 @@
     basis_ref, refs = refs[0], refs[1:]
     if mode == "score":
         left_ref, refs = refs[0], refs[1:]
-    hi_ref, lo_ref, out_ref = refs[:3]
-    perm, acc = refs[-2:]
+    dense_ref, out_ref = refs[:2]
+    halves, tall, acc = refs[-3:]
     layer, chunk = pl.program_id(0), pl.program_id(1)
-
-    @pl.when((layer == 0) & (chunk == 0))
-    def _():
-        perm[...] = node_order()
-
-    total = image_part(basis_ref[chunk, layer], hi_ref[0, 0], lo_ref[0, 0])
+    total = image_part(basis_ref[chunk, layer], dense_ref[0, 0])
 
     @pl.when(chunk == 0)
     def _():
@@ -191,11 +177,11 @@
 
     @pl.when(chunk == pl.num_programs(1) - 1)
     def _():
-        image = to_wide(acc[...], perm[...], basis_ref.shape[2])
+        image = to_wide(acc[...], basis_ref.shape[2], halves, tall)
         if mode != "score":
             out_ref[0] = image
         if mode == "gram":
-            refs[3][0] = dot_rows(image, image)
+            refs[2][0] = dot_rows(image, image)
         if mode == "score":
             out_ref[0] = dot_rows(left_ref[0], image)
 
@@ -204,48 +190,52 @@
     pieces, refs = refs[:piece_count], refs[piece_count:]
     if mode == "score":
         left_ref, refs = refs[0], refs[1:]
-    hi_ref, lo_ref, out_ref = refs[:3]
-    perm = node_order()
-    for layer in range(hi_ref.shape[0]):
+    dense_ref, out_ref = refs[:2]
+    halves, tall = refs[-2:]
+    for layer in range(dense_ref.shape[0]):
         total = sum(
-            image_part(piece[layer], hi_ref[layer, chunk], lo_ref[layer, chunk])
-            for chunk, piece in enumerate(pieces)
+            image_part(piece[layer], dense_ref[layer, chunk]) for chunk, piece in enumerate(pieces)
         )
-        image = to_wide(total, perm, pieces[0].shape[1])
+        image = to_wide(total, pieces[0].shape[1], halves.at[layer], tall.at[layer])
         if mode != "score":
             out_ref[layer] = image
         if mode == "gram":
-            refs[3][layer] = dot_rows(image, image)
+            refs[2][layer] = dot_rows(image, image)
         if mode == "score":
             out_ref[layer] = dot_rows(left_ref[layer], image)
 
 
-def apply_dense(mode, pieces, hi, lo, left=None):
-    layers, chunks = hi.shape[:2]
+def apply_dense(mode, pieces, dense, left=None):
+    layers, chunks = dense.shape[:2]
     k = pieces[0].shape[-2]
     image = jax.ShapeDtypeStruct((layers, k, ROWS_DEV), F32)
     small = jax.ShapeDtypeStruct((layers, k, k), F32)
     out_shape = {"gram": [image, small], "plain": [image], "score": [small]}[mode]
-    operands = list(pieces) + ([left] if mode == "score" else []) + [hi, lo]
+    operands = list(pieces) + ([left] if mode == "score" else []) + [dense]
     if len(pieces) == chunks:
         return pl.pallas_call(
             functools.partial(apply_whole_kernel, mode, chunks),
             in_specs=vmem_specs(len(operands)),
             out_specs=vmem_specs(len(out_shape)),
             out_shape=out_shape,
+            scratch_shapes=[pltpu.VMEM((layers, TALL, 128), F32), pltpu.VMEM((layers, ROWS_DEV, 128), F32)],
             compiler_params=params(14),
             name="apply_" + mode,
         )(*operands)
-    dense_spec = pl.BlockSpec((1, 1, TALL, CHUNK_LANES), lambda l, s: (l, s, 0, 0))
+    dense_spec = pl.BlockSpec((1, 1, 2 * TALL, CHUNK_LANES), lambda l, s: (l, s, 0, 0))
     image_spec = pl.BlockSpec((1, k, ROWS_DEV), lambda l, s: (l, 0, 0))
     small_spec = pl.BlockSpec((1, k, k), lambda l, s: (l, 0, 0))
     return pl.pallas_call(
         functools.partial(apply_kernel, mode),
         grid=(layers, chunks),
-        in_specs=vmem_specs(1) + ([image_spec] if mode == "score" else []) + [dense_spec, dense_spec],
+        in_specs=vmem_specs(1) + ([image_spec] if mode == "score" else []) + [dense_spec],
         out_specs={"gram": [image_spec, small_spec], "plain": [image_spec], "score": [small_spec]}[mode],
         out_shape=out_shape,
-        scratch_shapes=[pltpu.VMEM((ROWS_DEV, ROWS_DEV), BF16), pltpu.VMEM((TALL, 128), F32)],
+        scratch_shapes=[
+            pltpu.VMEM((TALL, 128), F32),
+            pltpu.VMEM((ROWS_DEV, 128), F32),
+            pltpu.VMEM((2 * TALL, 128), F32),
+        ],
         compiler_params=params(12),
         name="apply_" + mode,
     )(*operands)
@@ -366,7 +356,7 @@
     g = lax.axis_index("layer")
     rows = scratch.shape[0] // len(refs)
     for d, ref in enumerate(refs):
-        at = lax.rem(g + d, len(refs)) * rows
+        at = (g ^ d) * rows
         scratch[pl.ds(pl.multiple_of(at, rows), rows)] = ref[...].reshape(rows, ref.shape[-1])
 
 
@@ -395,7 +385,7 @@
 
 def joint_kernel(piece_count, k, *refs):
     gram_refs, image_refs = refs[:piece_count], refs[piece_count : 2 * piece_count]
-    out_ref, rounded_ref, work, stacked = refs[2 * piece_count :]
+    out_ref, again_ref, rounded_ref, work, stacked = refs[2 * piece_count :]
     stack_rows(gram_refs, work)
     stack_rows(image_refs, stacked)
     size = work.shape[0]
@@ -423,6 +413,7 @@
     joint = jnp.dot(own, stacked[...], precision=HIGHEST, preferred_element_type=F32)
     joint = joint.reshape(out_ref.shape)
     out_ref[...] = joint
+    again_ref[...] = joint
     rounded_ref[...] = joint.astype(BF16)
 
 
@@ -432,8 +423,9 @@
     return pl.pallas_call(
         functools.partial(joint_kernel, len(images), k),
         in_specs=vmem_specs(2 * len(images)),
-        out_specs=vmem_specs(2),
+        out_specs=vmem_specs(3),
         out_shape=[
+            jax.ShapeDtypeStruct(images[0].shape, F32),
             jax.ShapeDtypeStruct(images[0].shape, F32),
             jax.ShapeDtypeStruct(images[0].shape, BF16),
         ],
@@ -446,24 +438,18 @@
 def around(x, axis, count):
     pieces = [x]
     for d in range(1, count):
-        pieces.append(lax.ppermute(x, axis, [((m + d) % count, m) for m in range(count)]))
+        pieces.append(lax.ppermute(x, axis, [(m ^ d, m) for m in range(count)]))
     return pieces
 
 
 def add_pieces(pieces):
     if len(pieces) == 1:
         return pieces[0]
-    return (pieces[0] + pieces[2]) + (pieces[1] + pieces[3])
+    return (pieces[0] + pieces[1]) + (pieces[2] + pieces[3])
 
 
 def per_device(shards, groups, blocks, block_rows, block_cols, counts, start):
     few = shards == 4
-    cols_total = shards * BROWS
-    live = jnp.arange(block_rows.shape[1], dtype=jnp.int32)[None, :] < counts
-    cols = block_cols
-    if few:
-        cols = (cols - lax.axis_index("node") * BROWS + cols_total) % cols_total
-    key = jnp.where(live, cols * BROWS + block_rows, -1)
 
     def gather(x):
         return around(x, "node", shards) if few else [lax.all_gather(x, "node")]
@@ -472,13 +458,13 @@
         return around(x, "node", shards) if few else [lax.psum(x, "node")]
 
     first = gather(start.astype(BF16))
-    hi, lo = build_dense(key, blocks, cols_total // CHUNK_COLS)
-    image, gram = apply_dense("gram", first, hi, lo)
-    (image,) = apply_dense("plain", gather(solve(partials(gram), image)), hi, lo)
+    dense = build_dense(block_rows, block_cols, counts, blocks, shards * BROWS // CHUNK_COLS)
+    image, gram = apply_dense("gram", first, dense)
+    (image,) = apply_dense("plain", gather(solve(partials(gram), image)), dense)
     images = around(image, "layer", groups)
     grams = around(add_pieces(partials(cross(images))), "layer", groups)
-    joint_basis, rounded = joint_solve(grams, images)
-    (partial,) = apply_dense("score", gather(rounded), hi, lo, joint_basis)
+    joint_basis, again, rounded = joint_solve(grams, images)
+    (partial,) = apply_dense("score", gather(rounded), dense, again)
     return joint_basis, add_pieces(partials(partial))
 
 

time: 103 us -> 97.1 us (0.943)
  local copies, waits for them, and re-layouts: 4.29 us -> 2.03 us
  Pallas kernels: 33.3 us -> 31.6 us
    unnamed x4 -> x2, local copies, waits for them, and re-layouts: 4.29 us -> 0.65 us
    pallas_call x3, Pallas kernels: 15.9 us -> 13.5 us  [apply_dense(): pl.pallas_call(functools.partial(apply_whole_kernel, mode, chunks), in_sp...]
    broadcast_in_dim x0 -> x2, local copies, waits for them, and re-layouts: none -> 1.38 us  [the longest x1 0.69 us: build_dense(): block_rows[:, None]]
  transfers between devices with their start and end apart: 24 -> 24, of which waited for: 16 -> 14; matrix products, arithmetic and copies ran while one was open for 1% -> 1% of each run, Pallas kernels for 5% -> 6%
where the time goes in v5:
time: 97.1 us; the launch traced here: 96.9 us
  starting transfers between devices  31.7 us (33%)
  Pallas kernels  31.6 us (33%)
  waiting for transfers between devices  29.3 us (30%)
  local copies, waits for them, and re-layouts  2.03 us (2%)
  other arithmetic  1.56 us (2%)
    ppermute x24, starting transfers between devices, around(): pieces.append(lax.ppermute(x, axis, [(m ^ d, m) for m in range(count)]))  31.7 us
    ppermute x24, waiting for transfers between devices, around(): pieces.append(lax.ppermute(x, axis, [(m ^ d, m) for m in range(count)]))  29.3 us
    pallas_call x3, Pallas kernels, apply_dense(): pl.pallas_call(functools.partial(apply_whole_kernel, mode, chunks), in_sp...  13.5 us
    pallas_call x1, Pallas kernels, joint_solve(): pl.pallas_call(functools.partial(joint_kernel, len(images), k), in_specs=...  9.65 us
    pallas_call x1, Pallas kernels, build_dense(): pl.pallas_call(build_whole_kernel, in_specs=vmem_specs(2) + [pl.BlockSpec...  5.96 us
  transfers between devices with their start and end apart: 24, of which 14 were waited for; matrix products, arithmetic and copies ran while one was open for 1% of the time, Pallas kernels for 6%

profile of v5, /device:TPU:0, one launch (start us, length us, event | category | flops | bytes accessed | tf_op | source)
XLA Modules:
  0.0 96.9 jit_solution(3885406210455058419)
XLA Ops:
  1.5 5.1 %collective-permute-start.2 = (bf16[2,32,512]{2,1,0:T(8,128)(2,1)S(1)}, bf16[2,32,512]{2,1,0:T(8,128)(2,1)S(1)}, u32[]{:S(2)}, u32[]{:S(2)}) collective-permute-start(bf16[2,32,512]{2,1,0:T(8,128)(2,1)S(1)} %convert_element_type.3.refs_0_), channel_id=1, source_target_pairs={{3,0},{2,1},{1,2},{0,3},{7,4},{6,5},{5,6},{4,7},{11,8},{10,9},{9,1... | collective-permute-start | bytes 196616 | tf_op jit(solution)/shard_map/ppermute | solution.py:441
  9.3 6.0 %build_dense.1.refs_4_.refs_5_ = bf16[2,4,512,1024]{3,2,1,0:T(8,128)(2,1)S(1)} custom-call(s32[2,1,512]{2,1,0:T(1,128)S(1)} %broadcast_in_dim.6.rows_ref, s32[2,1,512]{2,1,0:T(1,128)S(1)} %broadcast_in_dim.7.cols_ref, s32[2]{0:T(128)S(1)} %bitcast.1, bf16[2,512,4096]{2,1,0:T(8,128)(2,1)} %blocks_ref.1), custom_call_target="tpu_custom_call" | custom-call | tf_op jit(solution)/shard_map/build_dense/pallas_call | solution.py:102
  15.3 5.4 %apply_gram.1 = (f32[2,32,512]{2,1,0:T(8,128)S(1)}, f32[2,32,32]{2,1,0:T(8,128)S(1)}) custom-call(bf16[2,32,512]{2,1,0:T(8,128)(2,1)S(1)} %convert_element_type.3.refs_0_, bf16[2,32,512]{2,1,0:T(8,128)(2,1)S(1)} %collective-permute-done.refs_1_, bf16[2,32,512]{2,1,0:T(8,128)(2,1)S(1)} %collective-permute-done.1.refs_2_, ...), custom_call_target="tpu_custom_call" | custom-call | tf_op jit(solution)/shard_map/apply_gram/pallas_call | solution.py:216
  20.7 3.8 %collective-permute-start.5 = (f32[2,32,32]{2,1,0:T(8,128)S(1)}, f32[2,32,32]{2,1,0:T(8,128)S(1)}, u32[]{:S(2)}, u32[]{:S(2)}) collective-permute-start(f32[2,32,32]{2,1,0:T(8,128)S(1)} %get-tuple-element.7.refs_0_), channel_id=1, source_target_pairs={{3,0},{2,1},{1,2},{0,3},{7,4},{6,5},{5,6},{4,7},{11,8},{10,9},{9,1... | collective-permute-start | bytes 24584 | tf_op jit(solution)/shard_map/ppermute | solution.py:441
  26.5 2.8 %collective-permute-done.4.refs_2_ = f32[2,32,32]{2,1,0:T(8,128)S(1)} collective-permute-done((f32[2,32,32]{2,1,0:T(8,128)S(1)}, f32[2,32,32]{2,1,0:T(8,128)S(1)}, u32[]{:S(2)}, u32[]{:S(2)}) %collective-permute-start.4) | collective-permute-done | bytes 8224 | tf_op jit(solution)/shard_map/ppermute | solution.py:441
  29.3 1.9 %solve_layers.1.refs_0_ = bf16[2,32,512]{2,1,0:T(8,128)(2,1)S(1)} custom-call(f32[2,32,32]{2,1,0:T(8,128)S(1)} %get-tuple-element.7.refs_0_, f32[2,32,32]{2,1,0:T(8,128)S(1)} %collective-permute-done.3.refs_1_, f32[2,32,32]{2,1,0:T(8,128)S(1)} %collective-permute-done.4.refs_2_, f32[2,32,32]{2,1,0:T(8,128)S(1)} %collective-permute-done.5.refs_3_, ...), custom_call_target="tpu_custom_call" | custom-call | tf_op jit(solution)/shard_map/solve_layers/pallas_call | solution.py:345
  33.3 2.3 %collective-permute-start.6 = (bf16[2,32,512]{2,1,0:T(8,128)(2,1)S(1)}, bf16[2,32,512]{2,1,0:T(8,128)(2,1)S(1)}, u32[]{:S(2)}, u32[]{:S(2)}) collective-permute-start(bf16[2,32,512]{2,1,0:T(8,128)(2,1)S(1)} %solve_layers.1.refs_0_), channel_id=1, source_target_pairs={{1,0},{0,1},{3,2},{2,3},{5,4},{4,5},{7,6},{6,7},{9,8},{8,9},{11,10... | collective-permute-start | bytes 196616 | tf_op jit(solution)/shard_map/ppermute | solution.py:441
  35.6 1.7 %collective-permute-done.8.refs_3_ = bf16[2,32,512]{2,1,0:T(8,128)(2,1)S(1)} collective-permute-done((bf16[2,32,512]{2,1,0:T(8,128)(2,1)S(1)}, bf16[2,32,512]{2,1,0:T(8,128)(2,1)S(1)}, u32[]{:S(2)}, u32[]{:S(2)}) %collective-permute-start.8) | collective-permute-done | bytes 65568 | tf_op jit(solution)/shard_map/ppermute | solution.py:441
  38.7 2.7 %apply_plain.1.refs_0_.refs_4_ = f32[2,32,512]{2,1,0:T(8,128)S(1)} custom-call(bf16[2,32,512]{2,1,0:T(8,128)(2,1)S(1)} %solve_layers.1.refs_0_, bf16[2,32,512]{2,1,0:T(8,128)(2,1)S(1)} %collective-permute-done.6.refs_1_, bf16[2,32,512]{2,1,0:T(8,128)(2,1)S(1)} %collective-permute-done.7.refs_2_, bf16[2,32,512]{2,1,0:T(8,128)(2,1)S(1)} %collective-permute-done.8.refs_3_, ...), custom_call_target="tpu_custom_call" | custom-call | tf_op jit(solution)/shard_map/apply_plain/pallas_call | solution.py:216
  43.3 3.9 %collective-permute-done.11.refs_3_.refs_7_ = f32[2,32,512]{2,1,0:T(8,128)S(1)} collective-permute-done((f32[2,32,512]{2,1,0:T(8,128)S(1)}, f32[2,32,512]{2,1,0:T(8,128)S(1)}, u32[]{:S(2)}, u32[]{:S(2)}) %collective-permute-start.11) | collective-permute-done | bytes 131104 | tf_op jit(solution)/shard_map/ppermute | solution.py:441
  47.2 2.9 %collective-permute-done.10.refs_2_.refs_6_ = f32[2,32,512]{2,1,0:T(8,128)S(1)} collective-permute-done((f32[2,32,512]{2,1,0:T(8,128)S(1)}, f32[2,32,512]{2,1,0:T(8,128)S(1)}, u32[]{:S(2)}, u32[]{:S(2)}) %collective-permute-start.10) | collective-permute-done | bytes 131104 | tf_op jit(solution)/shard_map/ppermute | solution.py:441
  50.7 2.5 %collective-permute-start.14 = (f32[64,256]{1,0:T(8,128)S(1)}, f32[64,256]{1,0:T(8,128)S(1)}, u32[]{:S(2)}, u32[]{:S(2)}) collective-permute-start(f32[64,256]{1,0:T(8,128)S(1)} %cross_gram.1), channel_id=1, source_target_pairs={{3,0},{2,1},{1,2},{0,3},{7,4},{6,5},{5,6},{4,7},{11,8},{10,9},{9,1... | collective-permute-start | bytes 196616 | tf_op jit(solution)/shard_map/ppermute | solution.py:441
  53.4 1.7 %collective-permute-start.12 = (f32[64,256]{1,0:T(8,128)S(1)}, f32[64,256]{1,0:T(8,128)S(1)}, u32[]{:S(2)}, u32[]{:S(2)}) collective-permute-start(f32[64,256]{1,0:T(8,128)S(1)} %cross_gram.1), channel_id=1, source_target_pairs={{1,0},{0,1},{3,2},{2,3},{5,4},{4,5},{7,6},{6,7},{9,8},{8,9},{11,10... | collective-permute-start | bytes 196616 | tf_op jit(solution)/shard_map/ppermute | solution.py:441
  55.2 2.3 %collective-permute-done.14 = f32[64,256]{1,0:T(8,128)S(1)} collective-permute-done((f32[64,256]{1,0:T(8,128)S(1)}, f32[64,256]{1,0:T(8,128)S(1)}, u32[]{:S(2)}, u32[]{:S(2)}) %collective-permute-start.14) | collective-permute-done | bytes 65568 | tf_op jit(solution)/shard_map/ppermute | solution.py:441
  57.4 2.4 %collective-permute-done.13 = f32[64,256]{1,0:T(8,128)S(1)} collective-permute-done((f32[64,256]{1,0:T(8,128)S(1)}, f32[64,256]{1,0:T(8,128)S(1)}, u32[]{:S(2)}, u32[]{:S(2)}) %collective-permute-start.13) | collective-permute-done | bytes 65568 | tf_op jit(solution)/shard_map/ppermute | solution.py:441
  61.8 2.5 %collective-permute-done.17.refs_3_ = f32[64,256]{1,0:T(8,128)S(1)} collective-permute-done((f32[64,256]{1,0:T(8,128)S(1)}, f32[64,256]{1,0:T(8,128)S(1)}, u32[]{:S(2)}, u32[]{:S(2)}) %collective-permute-start.17) | collective-permute-done | bytes 65568 | tf_op jit(solution)/shard_map/ppermute | solution.py:441
  65.7 9.7 %joint_solve.1 = (f32[2,32,512]{2,1,0:T(8,128)}, f32[2,32,512]{2,1,0:T(8,128)S(1)}, bf16[2,32,512]{2,1,0:T(8,128)(2,1)S(1)}) custom-call(f32[64,256]{1,0:T(8,128)S(1)} %add_add_fusion.refs_0_, f32[64,256]{1,0:T(8,128)S(1)} %collective-permute-done.15.refs_1_, f32[64,256]{1,0:T(8,128)S(1)} %collective-permute-done.16.refs_2_, ...), custom_call_target="tpu_custom_call" | custom-call | tf_op jit(solution)/shard_map/joint_solve/pallas_call | solution.py:423
  75.4 2.0 %collective-permute-start.20 = (bf16[2,32,512]{2,1,0:T(8,128)(2,1)S(1)}, bf16[2,32,512]{2,1,0:T(8,128)(2,1)S(1)}, u32[]{:S(2)}, u32[]{:S(2)}) collective-permute-start(bf16[2,32,512]{2,1,0:T(8,128)(2,1)S(1)} %get-tuple-element.10.refs_0_), channel_id=1, source_target_pairs={{3,0},{2,1},{1,2},{0,3},{7,4},{6,5},{5,6},{4,7},{11,8},{10,9},{9,1... | collective-permute-start | bytes 196616 | tf_op jit(solution)/shard_map/ppermute | solution.py:441
  77.4 2.4 %collective-permute-start.18 = (bf16[2,32,512]{2,1,0:T(8,128)(2,1)S(1)}, bf16[2,32,512]{2,1,0:T(8,128)(2,1)S(1)}, u32[]{:S(2)}, u32[]{:S(2)}) collective-permute-start(bf16[2,32,512]{2,1,0:T(8,128)(2,1)S(1)} %get-tuple-element.10.refs_0_), channel_id=1, source_target_pairs={{1,0},{0,1},{3,2},{2,3},{5,4},{4,5},{7,6},{6,7},{9,8},{8,9},{11,10... | collective-permute-start | bytes 196616 | tf_op jit(solution)/shard_map/ppermute | solution.py:441
  79.8 2.4 %collective-permute-done.20.refs_3_ = bf16[2,32,512]{2,1,0:T(8,128)(2,1)S(1)} collective-permute-done((bf16[2,32,512]{2,1,0:T(8,128)(2,1)S(1)}, bf16[2,32,512]{2,1,0:T(8,128)(2,1)S(1)}, u32[]{:S(2)}, u32[]{:S(2)}) %collective-permute-start.20) | collective-permute-done | bytes 65568 | tf_op jit(solution)/shard_map/ppermute | solution.py:441
  82.2 1.9 %collective-permute-done.19.refs_2_ = bf16[2,32,512]{2,1,0:T(8,128)(2,1)S(1)} collective-permute-done((bf16[2,32,512]{2,1,0:T(8,128)(2,1)S(1)}, bf16[2,32,512]{2,1,0:T(8,128)(2,1)S(1)}, u32[]{:S(2)}, u32[]{:S(2)}) %collective-permute-start.19) | collective-permute-done | bytes 65568 | tf_op jit(solution)/shard_map/ppermute | solution.py:441
  84.1 5.4 %apply_score.1 = f32[2,32,32]{2,1,0:T(8,128)S(1)} custom-call(bf16[2,32,512]{2,1,0:T(8,128)(2,1)S(1)} %get-tuple-element.10.refs_0_, bf16[2,32,512]{2,1,0:T(8,128)(2,1)S(1)} %collective-permute-done.18.refs_1_, bf16[2,32,512]{2,1,0:T(8,128)(2,1)S(1)} %collective-permute-done.19.refs_2_, bf16[2,32,512]{2,1,0:T(8,128)(2,1)S(1)} %collective-permute-done.20.refs_3_, ...), custom_call_target="tpu_custom_call" | custom-call | tf_op jit(solution)/shard_map/apply_score/pallas_call | solution.py:216
  89.5 1.9 %collective-permute-start.23 = (f32[2,32,32]{2,1,0:T(8,128)S(1)}, f32[2,32,32]{2,1,0:T(8,128)S(1)}, u32[]{:S(2)}, u32[]{:S(2)}) collective-permute-start(f32[2,32,32]{2,1,0:T(8,128)S(1)} %apply_score.1), channel_id=1, source_target_pairs={{3,0},{2,1},{1,2},{0,3},{7,4},{6,5},{5,6},{4,7},{11,8},{10,9},{9,1... | collective-permute-start | bytes 24584 | tf_op jit(solution)/shard_map/ppermute | solution.py:441
  91.4 2.5 %collective-permute-start.21 = (f32[2,32,32]{2,1,0:T(8,128)S(1)}, f32[2,32,32]{2,1,0:T(8,128)S(1)}, u32[]{:S(2)}, u32[]{:S(2)}) collective-permute-start(f32[2,32,32]{2,1,0:T(8,128)S(1)} %apply_score.1), channel_id=1, source_target_pairs={{1,0},{0,1},{3,2},{2,3},{5,4},{4,5},{7,6},{6,7},{9,8},{8,9},{11,10... | collective-permute-start | bytes 24584 | tf_op jit(solution)/shard_map/ppermute | solution.py:441
  (38 shorter events, 18.2 us)
Async XLA Ops:
  1.5 13.8 %collective-permute-start.2 = (bf16[2,32,512]{2,1,0:T(8,128)(2,1)S(1)}, bf16[2,32,512]{2,1,0:T(8,128)(2,1)S(1)}, u32[]{:S(2)}, u32[]{:S(2)}) collective-permute-start(bf16[2,32,512]{2,1,0:T(8,128)(2,1)S(1)} %convert_element_type.3.refs_0_), channel_id=1, source_target_pairs={{3,0},{2,1},{1,2},{0,3},{7,4},{6,5},{5,6},{4,7},{11,8},{10,9},{9,1... | collective-permute-start | bytes 196616 | tf_op jit(solution)/shard_map/ppermute | solution.py:441
  6.7 8.7 %collective-permute-start.1 = (bf16[2,32,512]{2,1,0:T(8,128)(2,1)S(1)}, bf16[2,32,512]{2,1,0:T(8,128)(2,1)S(1)}, u32[]{:S(2)}, u32[]{:S(2)}) collective-permute-start(bf16[2,32,512]{2,1,0:T(8,128)(2,1)S(1)} %convert_element_type.3.refs_0_), channel_id=1, source_target_pairs={{2,0},{3,1},{0,2},{1,3},{6,4},{7,5},{4,6},{5,7},{10,8},{11,9},{8,1... | collective-permute-start | bytes 196616 | tf_op jit(solution)/shard_map/ppermute | solution.py:441
  6.7 8.7 %collective-permute-start = (bf16[2,32,512]{2,1,0:T(8,128)(2,1)S(1)}, bf16[2,32,512]{2,1,0:T(8,128)(2,1)S(1)}, u32[]{:S(2)}, u32[]{:S(2)}) collective-permute-start(bf16[2,32,512]{2,1,0:T(8,128)(2,1)S(1)} %convert_element_type.3.refs_0_), channel_id=1, source_target_pairs={{1,0},{0,1},{3,2},{2,3},{5,4},{4,5},{7,6},{6,7},{9,8},{8,9},{11,10... | collective-permute-start | bytes 196616 | tf_op jit(solution)/shard_map/ppermute | solution.py:441
  20.7 5.8 %collective-permute-start.5 = (f32[2,32,32]{2,1,0:T(8,128)S(1)}, f32[2,32,32]{2,1,0:T(8,128)S(1)}, u32[]{:S(2)}, u32[]{:S(2)}) collective-permute-start(f32[2,32,32]{2,1,0:T(8,128)S(1)} %get-tuple-element.7.refs_0_), channel_id=1, source_target_pairs={{3,0},{2,1},{1,2},{0,3},{7,4},{6,5},{5,6},{4,7},{11,8},{10,9},{9,1... | collective-permute-start | bytes 24584 | tf_op jit(solution)/shard_map/ppermute | solution.py:441
  24.5 4.8 %collective-permute-start.4 = (f32[2,32,32]{2,1,0:T(8,128)S(1)}, f32[2,32,32]{2,1,0:T(8,128)S(1)}, u32[]{:S(2)}, u32[]{:S(2)}) collective-permute-start(f32[2,32,32]{2,1,0:T(8,128)S(1)} %get-tuple-element.7.refs_0_), channel_id=1, source_target_pairs={{2,0},{3,1},{0,2},{1,3},{6,4},{7,5},{4,6},{5,7},{10,8},{11,9},{8,1... | collective-permute-start | bytes 24584 | tf_op jit(solution)/shard_map/ppermute | solution.py:441
  24.5 4.8 %collective-permute-start.3 = (f32[2,32,32]{2,1,0:T(8,128)S(1)}, f32[2,32,32]{2,1,0:T(8,128)S(1)}, u32[]{:S(2)}, u32[]{:S(2)}) collective-permute-start(f32[2,32,32]{2,1,0:T(8,128)S(1)} %get-tuple-element.7.refs_0_), channel_id=1, source_target_pairs={{1,0},{0,1},{3,2},{2,3},{5,4},{4,5},{7,6},{6,7},{9,8},{8,9},{11,10... | collective-permute-start | bytes 24584 | tf_op jit(solution)/shard_map/ppermute | solution.py:441
  31.2 6.1 %collective-permute-start.8 = (bf16[2,32,512]{2,1,0:T(8,128)(2,1)S(1)}, bf16[2,32,512]{2,1,0:T(8,128)(2,1)S(1)}, u32[]{:S(2)}, u32[]{:S(2)}) collective-permute-start(bf16[2,32,512]{2,1,0:T(8,128)(2,1)S(1)} %solve_layers.1.refs_0_), channel_id=1, source_target_pairs={{3,0},{2,1},{1,2},{0,3},{7,4},{6,5},{5,6},{4,7},{11,8},{10,9},{9,1... | collective-permute-start | bytes 196616 | tf_op jit(solution)/shard_map/ppermute | solution.py:441
  32.7 6.0 %collective-permute-start.7 = (bf16[2,32,512]{2,1,0:T(8,128)(2,1)S(1)}, bf16[2,32,512]{2,1,0:T(8,128)(2,1)S(1)}, u32[]{:S(2)}, u32[]{:S(2)}) collective-permute-start(bf16[2,32,512]{2,1,0:T(8,128)(2,1)S(1)} %solve_layers.1.refs_0_), channel_id=1, source_target_pairs={{2,0},{3,1},{0,2},{1,3},{6,4},{7,5},{4,6},{5,7},{10,8},{11,9},{8,1... | collective-permute-start | bytes 196616 | tf_op jit(solution)/shard_map/ppermute | solution.py:441
  33.3 5.4 %collective-permute-start.6 = (bf16[2,32,512]{2,1,0:T(8,128)(2,1)S(1)}, bf16[2,32,512]{2,1,0:T(8,128)(2,1)S(1)}, u32[]{:S(2)}, u32[]{:S(2)}) collective-permute-start(bf16[2,32,512]{2,1,0:T(8,128)(2,1)S(1)} %solve_layers.1.refs_0_), channel_id=1, source_target_pairs={{1,0},{0,1},{3,2},{2,3},{5,4},{4,5},{7,6},{6,7},{9,8},{8,9},{11,10... | collective-permute-start | bytes 196616 | tf_op jit(solution)/shard_map/ppermute | solution.py:441
  41.4 5.8 %collective-permute-start.11 = (f32[2,32,512]{2,1,0:T(8,128)S(1)}, f32[2,32,512]{2,1,0:T(8,128)S(1)}, u32[]{:S(2)}, u32[]{:S(2)}) collective-permute-start(f32[2,32,512]{2,1,0:T(8,128)S(1)} %apply_plain.1.refs_0_.refs_4_), channel_id=1, source_target_pairs={{12,0},{8,4},{4,8},{0,12},{13,1},{9,5},{5,9},{1,13},{14,2},{10,6},... | collective-permute-start | bytes 393224 | tf_op jit(solution)/shard_map/ppermute | solution.py:441
  41.5 8.6 %collective-permute-start.10 = (f32[2,32,512]{2,1,0:T(8,128)S(1)}, f32[2,32,512]{2,1,0:T(8,128)S(1)}, u32[]{:S(2)}, u32[]{:S(2)}) collective-permute-start(f32[2,32,512]{2,1,0:T(8,128)S(1)} %apply_plain.1.refs_0_.refs_4_), channel_id=1, source_target_pairs={{8,0},{12,4},{0,8},{4,12},{9,1},{13,5},{1,9},{5,13},{10,2},{14,6},... | collective-permute-start | bytes 393224 | tf_op jit(solution)/shard_map/ppermute | solution.py:441
  43.0 7.0 %collective-permute-start.9 = (f32[2,32,512]{2,1,0:T(8,128)S(1)}, f32[2,32,512]{2,1,0:T(8,128)S(1)}, u32[]{:S(2)}, u32[]{:S(2)}) collective-permute-start(f32[2,32,512]{2,1,0:T(8,128)S(1)} %apply_plain.1.refs_0_.refs_4_), channel_id=1, source_target_pairs={{4,0},{0,4},{12,8},{8,12},{5,1},{1,5},{13,9},{9,13},{6,2},{2,6},{1... | collective-permute-start | bytes 393224 | tf_op jit(solution)/shard_map/ppermute | solution.py:441
  50.7 6.7 %collective-permute-start.14 = (f32[64,256]{1,0:T(8,128)S(1)}, f32[64,256]{1,0:T(8,128)S(1)}, u32[]{:S(2)}, u32[]{:S(2)}) collective-permute-start(f32[64,256]{1,0:T(8,128)S(1)} %cross_gram.1), channel_id=1, source_target_pairs={{3,0},{2,1},{1,2},{0,3},{7,4},{6,5},{5,6},{4,7},{11,8},{10,9},{9,1... | collective-permute-start | bytes 196616 | tf_op jit(solution)/shard_map/ppermute | solution.py:441
  53.2 6.7 %collective-permute-start.13 = (f32[64,256]{1,0:T(8,128)S(1)}, f32[64,256]{1,0:T(8,128)S(1)}, u32[]{:S(2)}, u32[]{:S(2)}) collective-permute-start(f32[64,256]{1,0:T(8,128)S(1)} %cross_gram.1), channel_id=1, source_target_pairs={{2,0},{3,1},{0,2},{1,3},{6,4},{7,5},{4,6},{5,7},{10,8},{11,9},{8,1... | collective-permute-start | bytes 196616 | tf_op jit(solution)/shard_map/ppermute | solution.py:441
  53.4 6.5 %collective-permute-start.12 = (f32[64,256]{1,0:T(8,128)S(1)}, f32[64,256]{1,0:T(8,128)S(1)}, u32[]{:S(2)}, u32[]{:S(2)}) collective-permute-start(f32[64,256]{1,0:T(8,128)S(1)} %cross_gram.1), channel_id=1, source_target_pairs={{1,0},{0,1},{3,2},{2,3},{5,4},{4,5},{7,6},{6,7},{9,8},{8,9},{11,10... | collective-permute-start | bytes 196616 | tf_op jit(solution)/shard_map/ppermute | solution.py:441
  59.9 4.4 %collective-permute-start.17 = (f32[64,256]{1,0:T(8,128)S(1)}, f32[64,256]{1,0:T(8,128)S(1)}, u32[]{:S(2)}, u32[]{:S(2)}) collective-permute-start(f32[64,256]{1,0:T(8,128)S(1)} %add_add_fusion.refs_0_), channel_id=1, source_target_pairs={{12,0},{8,4},{4,8},{0,12},{13,1},{9,5},{5,9},{1,13},{14,2},{10,6},... | collective-permute-start | bytes 196616 | tf_op jit(solution)/shard_map/ppermute | solution.py:441
  60.0 5.8 %collective-permute-start.16 = (f32[64,256]{1,0:T(8,128)S(1)}, f32[64,256]{1,0:T(8,128)S(1)}, u32[]{:S(2)}, u32[]{:S(2)}) collective-permute-start(f32[64,256]{1,0:T(8,128)S(1)} %add_add_fusion.refs_0_), channel_id=1, source_target_pairs={{8,0},{12,4},{0,8},{4,12},{9,1},{13,5},{1,9},{5,13},{10,2},{14,6},... | collective-permute-start | bytes 196616 | tf_op jit(solution)/shard_map/ppermute | solution.py:441
  61.4 4.3 %collective-permute-start.15 = (f32[64,256]{1,0:T(8,128)S(1)}, f32[64,256]{1,0:T(8,128)S(1)}, u32[]{:S(2)}, u32[]{:S(2)}) collective-permute-start(f32[64,256]{1,0:T(8,128)S(1)} %add_add_fusion.refs_0_), channel_id=1, source_target_pairs={{4,0},{0,4},{12,8},{8,12},{5,1},{1,5},{13,9},{9,13},{6,2},{2,6},{1... | collective-permute-start | bytes 196616 | tf_op jit(solution)/shard_map/ppermute | solution.py:441
  75.4 6.8 %collective-permute-start.20 = (bf16[2,32,512]{2,1,0:T(8,128)(2,1)S(1)}, bf16[2,32,512]{2,1,0:T(8,128)(2,1)S(1)}, u32[]{:S(2)}, u32[]{:S(2)}) collective-permute-start(bf16[2,32,512]{2,1,0:T(8,128)(2,1)S(1)} %get-tuple-element.10.refs_0_), channel_id=1, source_target_pairs={{3,0},{2,1},{1,2},{0,3},{7,4},{6,5},{5,6},{4,7},{11,8},{10,9},{9,1... | collective-permute-start | bytes 196616 | tf_op jit(solution)/shard_map/ppermute | solution.py:441
  77.4 6.7 %collective-permute-start.19 = (bf16[2,32,512]{2,1,0:T(8,128)(2,1)S(1)}, bf16[2,32,512]{2,1,0:T(8,128)(2,1)S(1)}, u32[]{:S(2)}, u32[]{:S(2)}) collective-permute-start(bf16[2,32,512]{2,1,0:T(8,128)(2,1)S(1)} %get-tuple-element.10.refs_0_), channel_id=1, source_target_pairs={{2,0},{3,1},{0,2},{1,3},{6,4},{7,5},{4,6},{5,7},{10,8},{11,9},{8,1... | collective-permute-start | bytes 196616 | tf_op jit(solution)/shard_map/ppermute | solution.py:441
  77.4 6.7 %collective-permute-start.18 = (bf16[2,32,512]{2,1,0:T(8,128)(2,1)S(1)}, bf16[2,32,512]{2,1,0:T(8,128)(2,1)S(1)}, u32[]{:S(2)}, u32[]{:S(2)}) collective-permute-start(bf16[2,32,512]{2,1,0:T(8,128)(2,1)S(1)} %get-tuple-element.10.refs_0_), channel_id=1, source_target_pairs={{1,0},{0,1},{3,2},{2,3},{5,4},{4,5},{7,6},{6,7},{9,8},{8,9},{11,10... | collective-permute-start | bytes 196616 | tf_op jit(solution)/shard_map/ppermute | solution.py:441
  89.5 5.8 %collective-permute-start.23 = (f32[2,32,32]{2,1,0:T(8,128)S(1)}, f32[2,32,32]{2,1,0:T(8,128)S(1)}, u32[]{:S(2)}, u32[]{:S(2)}) collective-permute-start(f32[2,32,32]{2,1,0:T(8,128)S(1)} %apply_score.1), channel_id=1, source_target_pairs={{3,0},{2,1},{1,2},{0,3},{7,4},{6,5},{5,6},{4,7},{11,8},{10,9},{9,1... | collective-permute-start | bytes 24584 | tf_op jit(solution)/shard_map/ppermute | solution.py:441
  91.4 4.9 %collective-permute-start.22 = (f32[2,32,32]{2,1,0:T(8,128)S(1)}, f32[2,32,32]{2,1,0:T(8,128)S(1)}, u32[]{:S(2)}, u32[]{:S(2)}) collective-permute-start(f32[2,32,32]{2,1,0:T(8,128)S(1)} %apply_score.1), channel_id=1, source_target_pairs={{2,0},{3,1},{0,2},{1,3},{6,4},{7,5},{4,6},{5,7},{10,8},{11,9},{8,1... | collective-permute-start | bytes 24584 | tf_op jit(solution)/shard_map/ppermute | solution.py:441
  91.4 4.9 %collective-permute-start.21 = (f32[2,32,32]{2,1,0:T(8,128)S(1)}, f32[2,32,32]{2,1,0:T(8,128)S(1)}, u32[]{:S(2)}, u32[]{:S(2)}) collective-permute-start(f32[2,32,32]{2,1,0:T(8,128)S(1)} %apply_score.1), channel_id=1, source_target_pairs={{1,0},{0,1},{3,2},{2,3},{5,4},{4,5},{7,6},{6,7},{9,8},{8,9},{11,10... | collective-permute-start | bytes 24584 | tf_op jit(solution)/shard_map/ppermute | solution.py:441
  (1 other events, 0.7 us)

commit v6 on v5

--- a/solution.py
+++ b/solution.py
@@ -41,9 +41,9 @@
 
 
 def one_hot(rows_ref, cols_ref, counts_ref, layer, flip, base, positions):
-    slot = lax.broadcasted_iota(jnp.int32, (1, rows_ref.shape[2]), 1)
-    key = (cols_ref[layer] ^ flip) * BROWS + rows_ref[layer]
-    key = jnp.where(slot < counts_ref[layer], key, -1)
+    slot = lax.broadcasted_iota(jnp.int32, (1, rows_ref.shape[1]), 1)
+    key = (cols_ref[pl.ds(layer, 1), :] ^ flip) * BROWS + rows_ref[pl.ds(layer, 1), :]
+    key = jnp.where(slot < counts_ref[0, layer], key, -1)
     position = lax.broadcasted_iota(jnp.int32, (positions, key.shape[1]), 0) + base
     return jnp.where(position == key, 1.0, 0.0).astype(BF16)
 
@@ -96,8 +96,9 @@
 def build_dense(block_rows, block_cols, counts, blocks, chunk_total):
     layers, slots, width = blocks.shape
     dense = jax.ShapeDtypeStruct((layers, chunk_total, 2 * TALL, CHUNK_LANES), BF16)
-    operands = (block_rows[:, None], block_cols[:, None], counts[:, 0], pltpu.with_memory_space_constraint(blocks, pltpu.HBM))
+    operands = (block_rows, block_cols, counts.T, blocks)
     if chunk_total <= 4:
+        operands = (*operands[:3], pltpu.with_memory_space_constraint(blocks, pltpu.HBM))
         pieces = 4
         return pl.pallas_call(
             build_whole_kernel,
@@ -154,8 +155,15 @@
     return tall[...].T[:k]
 
 
-def dot_rows(a, b):
-    return lax.dot_general(a, b, TRANS_B, precision=HIGHEST, preferred_element_type=F32)
+def against(left, tall):
+    k = left.shape[0]
+    lane = lax.broadcasted_iota(jnp.int32, tall.shape, 1)
+    a, b, c = split3(jnp.where(lane < k, tall, 0.0))
+    right = a.astype(F32) + pltpu.roll(b.astype(F32), k, 1) + pltpu.roll(c.astype(F32), 2 * k, 1)
+    pieces = jnp.dot(jnp.concatenate(split3(left), axis=0), right.astype(BF16), preferred_element_type=F32)
+    top, middle, bottom = pieces[:k], pieces[k : 2 * k], pieces[2 * k :]
+    total = top[:, :k] + (top[:, k : 2 * k] + middle[:, :k])
+    return total + (middle[:, k : 2 * k] + (top[:, 2 * k : 3 * k] + bottom[:, :k]))
 
 
 def apply_kernel(mode, *refs):
@@ -181,9 +189,9 @@
         if mode != "score":
             out_ref[0] = image
         if mode == "gram":
-            refs[2][0] = dot_rows(image, image)
+            refs[2][0] = against(image, tall[...])
         if mode == "score":
-            out_ref[0] = dot_rows(left_ref[0], image)
+            out_ref[0] = against(left_ref[0], tall[...])
 
 
 def apply_whole_kernel(mode, piece_count, *refs):
@@ -200,9 +208,9 @@
         if mode != "score":
             out_ref[layer] = image
         if mode == "gram":
-            refs[2][layer] = dot_rows(image, image)
+            refs[2][layer] = against(image, tall[layer])
         if mode == "score":
-            out_ref[layer] = dot_rows(left_ref[layer], image)
+            out_ref[layer] = against(left_ref[layer], tall[layer])
 
 
 def apply_dense(mode, pieces, dense, left=None):
@@ -332,7 +340,7 @@
     sub = lax.broadcasted_iota(jnp.int32, (k, 128), 0)
     eye = jnp.where(lane == sub, 1.0, 0.0)
     for layer in range(layers):
-        gram = add_pieces([ref[layer] for ref in grams])
+        gram = sum(ref[layer] for ref in grams)
         gram = jnp.concatenate([gram, jnp.zeros((k, 128 - k), F32)], axis=1)
         gram, across = unit_scale(gram)
         solved = eliminate(tiled(jnp.concatenate([gram, eye], axis=1)), 0)
@@ -360,34 +368,27 @@
         scratch[pl.ds(pl.multiple_of(at, rows), rows)] = ref[...].reshape(rows, ref.shape[-1])
 
 
-def cross_kernel(piece_count, *refs):
-    pieces, out_ref, stacked = refs[:piece_count], refs[piece_count], refs[piece_count + 1]
-    stack_rows(pieces, stacked)
-    own = pieces[0][...].reshape(-1, stacked.shape[1])
-    out_ref[...] = lax.dot_general(
-        own, stacked[...], TRANS_B, precision=HIGHEST, preferred_element_type=F32
-    )
-
-
-def cross(pieces):
-    layers, k, width = pieces[0].shape
-    rows = layers * k
+def cross_kernel(own_ref, all_ref, out_ref):
+    own = own_ref[...].reshape(-1, own_ref.shape[2])
+    every = all_ref[...].reshape(-1, own_ref.shape[2])
+    out_ref[...] = lax.dot_general(own, every, TRANS_B, precision=HIGHEST, preferred_element_type=F32)
+
+
+def cross(own, every):
+    rows = own.shape[0] * own.shape[1]
     return pl.pallas_call(
-        functools.partial(cross_kernel, len(pieces)),
-        in_specs=vmem_specs(len(pieces)),
+        cross_kernel,
+        in_specs=vmem_specs(2),
         out_specs=pl.BlockSpec(memory_space=pltpu.VMEM),
-        out_shape=jax.ShapeDtypeStruct((rows, rows * len(pieces)), F32),
-        scratch_shapes=[pltpu.VMEM((rows * len(pieces), width), F32)],
+        out_shape=jax.ShapeDtypeStruct((rows, every.shape[0] * every.shape[1]), F32),
         compiler_params=params(6),
         name="cross_gram",
-    )(*pieces)
+    )(own, every)
 
 
 def joint_kernel(piece_count, k, *refs):
-    gram_refs, image_refs = refs[:piece_count], refs[piece_count : 2 * piece_count]
-    out_ref, again_ref, rounded_ref, work, stacked = refs[2 * piece_count :]
+    gram_refs, (images_ref, out_ref, again_ref, rounded_ref, work) = refs[:piece_count], refs[piece_count:]
     stack_rows(gram_refs, work)
-    stack_rows(image_refs, stacked)
     size = work.shape[0]
     steps = size // k
     lane = lax.broadcasted_iota(jnp.int32, (k, size), 1)
@@ -410,7 +411,8 @@
                 work[r * k : r * k + k] = jnp.where(here, 0.0, rows) - update(r * k, k)
     rows = size // piece_count
     own = work[pl.ds(pl.multiple_of(lax.axis_index("layer") * rows, rows), rows)] * across
-    joint = jnp.dot(own, stacked[...], precision=HIGHEST, preferred_element_type=F32)
+    images = images_ref[...].reshape(size, -1)
+    joint = jnp.dot(own, images, precision=HIGHEST, preferred_element_type=F32)
     joint = joint.reshape(out_ref.shape)
     out_ref[...] = joint
     again_ref[...] = joint
@@ -418,21 +420,23 @@
 
 
 def joint_solve(grams, images):
-    layers, k, width = images[0].shape
-    size = layers * k * len(images)
+    groups = len(grams)
+    _, k, width = images.shape
+    size = grams[0].shape[1]
+    shape = (images.shape[0] // groups, k, width)
     return pl.pallas_call(
-        functools.partial(joint_kernel, len(images), k),
-        in_specs=vmem_specs(2 * len(images)),
+        functools.partial(joint_kernel, groups, k),
+        in_specs=vmem_specs(groups + 1),
         out_specs=vmem_specs(3),
         out_shape=[
-            jax.ShapeDtypeStruct(images[0].shape, F32),
-            jax.ShapeDtypeStruct(images[0].shape, F32),
-            jax.ShapeDtypeStruct(images[0].shape, BF16),
+            jax.ShapeDtypeStruct(shape, F32),
+            jax.ShapeDtypeStruct(shape, F32),
+            jax.ShapeDtypeStruct(shape, BF16),
         ],
-        scratch_shapes=[pltpu.VMEM((size, size), F32), pltpu.VMEM((size, width), F32)],
+        scratch_shapes=[pltpu.VMEM((size, size), F32)],
         compiler_params=params(8),
         name="joint_solve",
-    )(*grams, *images)
+    )(*grams, images)
 
 
 def around(x, axis, count):
@@ -443,8 +447,6 @@
 
 
 def add_pieces(pieces):
-    if len(pieces) == 1:
-        return pieces[0]
     return (pieces[0] + pieces[1]) + (pieces[2] + pieces[3])
 
 
@@ -455,17 +457,23 @@
         return around(x, "node", shards) if few else [lax.all_gather(x, "node")]
 
     def partials(x):
-        return around(x, "node", shards) if few else [lax.psum(x, "node")]
+        if not few:
+            return [lax.psum(x, "node")]
+        near = x + lax.ppermute(x, "node", [(m ^ 1, m) for m in range(shards)])
+        return [near, lax.ppermute(near, "node", [(m ^ 2, m) for m in range(shards)])]
+
+    def total(x):
+        return add_pieces(around(x, "node", shards)) if few else lax.psum(x, "node")
 
     first = gather(start.astype(BF16))
     dense = build_dense(block_rows, block_cols, counts, blocks, shards * BROWS // CHUNK_COLS)
     image, gram = apply_dense("gram", first, dense)
     (image,) = apply_dense("plain", gather(solve(partials(gram), image)), dense)
-    images = around(image, "layer", groups)
-    grams = around(add_pieces(partials(cross(images))), "layer", groups)
+    images = lax.all_gather(image, "layer", axis=0, tiled=True)
+    grams = around(total(cross(image, images)), "layer", groups)
     joint_basis, again, rounded = joint_solve(grams, images)
     (partial,) = apply_dense("score", gather(rounded), dense, again)
-    return joint_basis, add_pieces(partials(partial))
+    return joint_basis, sum(partials(partial))
 
 
 def solution(mesh):

time: 97.1 us -> 99.3 us (1.023)
  blocking collectives: 0 us -> 7.36 us
  starting transfers between devices: 31.7 us -> 25.9 us
    ppermute x0 -> x4, waiting for transfers between devices: none -> 12.8 us  [the longest x2 6.79 us: partials(): lax.ppermute(near, 'node', [(m ^ 2, m) for m in range(shards)])]
    ppermute x24 -> x15, waiting for transfers between devices: 29.3 us -> 17.2 us  [around(): pieces.append(lax.ppermute(x, axis, [(m ^ d, m) for m in range(count)]))]
    ppermute x24 -> x15, starting transfers between devices: 31.7 us -> 20.9 us  [around(): pieces.append(lax.ppermute(x, axis, [(m ^ d, m) for m in range(count)]))]
    all_gather x0 -> x1, blocking collectives: none -> 7.36 us  [per_device(): images = lax.all_gather(image, 'layer', axis=0, tiled=True)]
    ppermute x0 -> x4, starting transfers between devices: none -> 4.99 us  [the longest x2 3.1 us: partials(): lax.ppermute(near, 'node', [(m ^ 2, m) for m in range(shards)])]
    broadcast_in_dim x2 -> x0, local copies, waits for them, and re-layouts: 1.38 us -> none  [the longest x1 0.69 us: build_dense(): block_rows[:, None]]
    unnamed x2 -> x6, local copies, waits for them, and re-layouts: 0.65 us -> 2.03 us
  transfers between devices with their start and end apart: 24 -> 19, of which waited for: 14 -> 12; matrix products, arithmetic and copies ran while one was open for 1% -> 0% of each run, Pallas kernels for 6% -> 6%
where the time goes in v6:
time: 99.3 us; the launch traced here: 99.1 us
  Pallas kernels  31.6 us (32%)
  waiting for transfers between devices  29.9 us (30%)
  starting transfers between devices  25.9 us (26%)
  blocking collectives  7.36 us (7%)
  local copies, waits for them, and re-layouts  2.03 us (2%)
  other arithmetic  1.57 us (2%)
    ppermute x15, starting transfers between devices, around(): pieces.append(lax.ppermute(x, axis, [(m ^ d, m) for m in range(count)]))  20.9 us
    ppermute x15, waiting for transfers between devices, around(): pieces.append(lax.ppermute(x, axis, [(m ^ d, m) for m in range(count)]))  17.2 us
    pallas_call x3, Pallas kernels, apply_dense(): pl.pallas_call(functools.partial(apply_whole_kernel, mode, chunks), in_sp...  13.7 us
    pallas_call x1, Pallas kernels, joint_solve(): pl.pallas_call(functools.partial(joint_kernel, groups, k), in_specs=vmem_...  9.46 us
    all_gather x1, blocking collectives, per_device(): images = lax.all_gather(image, 'layer', axis=0, tiled=True)  7.36 us
    ppermute x2, waiting for transfers between devices, partials(): lax.ppermute(near, 'node', [(m ^ 2, m) for m in range(shards)])  6.79 us
    ppermute x2, waiting for transfers between devices, partials(): near = x + lax.ppermute(x, 'node', [(m ^ 1, m) for m in range(shards)])  5.98 us
    pallas_call x1, Pallas kernels, build_dense(): pl.pallas_call(build_whole_kernel, in_specs=vmem_specs(2) + [pl.BlockSpec...  5.94 us
  transfers between devices with their start and end apart: 19, of which 12 were waited for; matrix products, arithmetic and copies ran while one was open for 0% of the time, Pallas kernels for 6%

profile of v6, /device:TPU:0, one launch (start us, length us, event | category | flops | bytes accessed | tf_op | source)
XLA Modules:
  0.0 99.1 jit_solution(8031387099710607128)
XLA Ops:
  1.5 5.1 %collective-permute-start.2 = (bf16[2,32,512]{2,1,0:T(8,128)(2,1)S(1)}, bf16[2,32,512]{2,1,0:T(8,128)(2,1)S(1)}, u32[]{:S(2)}, u32[]{:S(2)}) collective-permute-start(bf16[2,32,512]{2,1,0:T(8,128)(2,1)S(1)} %convert_element_type.3.refs_0_), channel_id=1, source_target_pairs={{3,0},{2,1},{1,2},{0,3},{7,4},{6,5},{5,6},{4,7},{11,8},{10,9},{9,1... | collective-permute-start | bytes 196616 | tf_op jit(solution)/shard_map/ppermute | solution.py:445
  9.3 5.9 %build_dense.1.refs_4_.refs_5_ = bf16[2,4,512,1024]{3,2,1,0:T(8,128)(2,1)S(1)} custom-call(s32[2,512]{1,0:T(2,128)S(1)} %copy-done, s32[2,512]{1,0:T(2,128)S(1)} %copy-done.1, s32[1,2]{1,0:T(1,128)S(1)} %bitcast.1, bf16[2,512,4096]{2,1,0:T(8,128)(2,1)} %blocks_ref.1), custom_call_target="tpu_custom_call" | custom-call | tf_op jit(solution)/shard_map/build_dense/pallas_call | solution.py:103
  15.3 5.6 %apply_gram.1 = (f32[2,32,512]{2,1,0:T(8,128)S(1)}, f32[2,32,32]{2,1,0:T(8,128)S(1)}) custom-call(bf16[2,32,512]{2,1,0:T(8,128)(2,1)S(1)} %convert_element_type.3.refs_0_, bf16[2,32,512]{2,1,0:T(8,128)(2,1)S(1)} %collective-permute-done.refs_1_, bf16[2,32,512]{2,1,0:T(8,128)(2,1)S(1)} %collective-permute-done.1.refs_2_, ...), custom_call_target="tpu_custom_call" | custom-call | tf_op jit(solution)/shard_map/apply_gram/pallas_call | solution.py:224
  22.3 2.5 %collective-permute-done.3 = f32[2,32,32]{2,1,0:T(8,128)S(1)} collective-permute-done((f32[2,32,32]{2,1,0:T(8,128)S(1)}, f32[2,32,32]{2,1,0:T(8,128)S(1)}, u32[]{:S(2)}, u32[]{:S(2)}) %collective-permute-start.3) | collective-permute-done | bytes 8224 | tf_op jit(solution)/shard_map/ppermute | solution.py:462
  24.8 2.3 %collective-permute-start.4 = (f32[2,32,32]{2,1,0:T(8,128)S(1)}, f32[2,32,32]{2,1,0:T(8,128)S(1)}, u32[]{:S(2)}, u32[]{:S(2)}) collective-permute-start(f32[2,32,32]{2,1,0:T(8,128)S(1)} %add.18.refs_0_), channel_id=1, source_target_pairs={{2,0},{3,1},{0,2},{1,3},{6,4},{7,5},{4,6},{5,7},{10,8},{11,9},{8,1... | collective-permute-start | bytes 24584 | tf_op jit(solution)/shard_map/ppermute | solution.py:463
  27.1 2.5 %collective-permute-done.4.refs_1_ = f32[2,32,32]{2,1,0:T(8,128)S(1)} collective-permute-done((f32[2,32,32]{2,1,0:T(8,128)S(1)}, f32[2,32,32]{2,1,0:T(8,128)S(1)}, u32[]{:S(2)}, u32[]{:S(2)}) %collective-permute-start.4) | collective-permute-done | bytes 8224 | tf_op jit(solution)/shard_map/ppermute | solution.py:463
  29.6 1.9 %solve_layers.1.refs_0_ = bf16[2,32,512]{2,1,0:T(8,128)(2,1)S(1)} custom-call(f32[2,32,32]{2,1,0:T(8,128)S(1)} %add.18.refs_0_, f32[2,32,32]{2,1,0:T(8,128)S(1)} %collective-permute-done.4.refs_1_, f32[2,32,512]{2,1,0:T(8,128)S(1)} %get-tuple-element.8.refs_2_), custom_call_target="tpu_custom_call" | custom-call | tf_op jit(solution)/shard_map/solve_layers/pallas_call | solution.py:353
  31.5 3.8 %collective-permute-start.7 = (bf16[2,32,512]{2,1,0:T(8,128)(2,1)S(1)}, bf16[2,32,512]{2,1,0:T(8,128)(2,1)S(1)}, u32[]{:S(2)}, u32[]{:S(2)}) collective-permute-start(bf16[2,32,512]{2,1,0:T(8,128)(2,1)S(1)} %solve_layers.1.refs_0_), channel_id=1, source_target_pairs={{3,0},{2,1},{1,2},{0,3},{7,4},{6,5},{5,6},{4,7},{11,8},{10,9},{9,1... | collective-permute-start | bytes 196616 | tf_op jit(solution)/shard_map/ppermute | solution.py:445
  35.9 1.9 %collective-permute-done.7.refs_3_ = bf16[2,32,512]{2,1,0:T(8,128)(2,1)S(1)} collective-permute-done((bf16[2,32,512]{2,1,0:T(8,128)(2,1)S(1)}, bf16[2,32,512]{2,1,0:T(8,128)(2,1)S(1)}, u32[]{:S(2)}, u32[]{:S(2)}) %collective-permute-start.7) | collective-permute-done | bytes 65568 | tf_op jit(solution)/shard_map/ppermute | solution.py:445
  37.8 2.6 %collective-permute-done.6.refs_2_ = bf16[2,32,512]{2,1,0:T(8,128)(2,1)S(1)} collective-permute-done((bf16[2,32,512]{2,1,0:T(8,128)(2,1)S(1)}, bf16[2,32,512]{2,1,0:T(8,128)(2,1)S(1)}, u32[]{:S(2)}, u32[]{:S(2)}) %collective-permute-start.6) | collective-permute-done | bytes 65568 | tf_op jit(solution)/shard_map/ppermute | solution.py:445
  40.4 2.7 %apply_plain.1.own_ref = f32[2,32,512]{2,1,0:T(8,128)S(1)} custom-call(bf16[2,32,512]{2,1,0:T(8,128)(2,1)S(1)} %solve_layers.1.refs_0_, bf16[2,32,512]{2,1,0:T(8,128)(2,1)S(1)} %collective-permute-done.5.refs_1_, bf16[2,32,512]{2,1,0:T(8,128)(2,1)S(1)} %collective-permute-done.6.refs_2_, bf16[2,32,512]{2,1,0:T(8,128)(2,1)S(1)} %collective-permute-done.7.refs_3_, ...), custom_call_target="tpu_custom_call" | custom-call | tf_op jit(solution)/shard_map/apply_plain/pallas_call | solution.py:224
  43.1 7.4 %all_gather.3.all_ref.refs_4_ = f32[8,32,512]{2,1,0:T(8,128)S(1)} all-gather(f32[2,32,512]{2,1,0:T(8,128)S(1)} %apply_plain.1.own_ref), channel_id=1, replica_groups=mesh['parts'=2,'layer'=4,'node'=4] {'layer'}, dimensions={0}, use_global_device_ids=true | all-gather | bytes 655360 | tf_op jit(solution)/shard_map/all_gather | solution.py:472
  53.2 2.3 %collective-permute-start.8 = (f32[64,256]{1,0:T(8,128)S(1)}, f32[64,256]{1,0:T(8,128)S(1)}, u32[]{:S(2)}, u32[]{:S(2)}) collective-permute-start(f32[64,256]{1,0:T(8,128)S(1)} %cross_gram.1), channel_id=1, source_target_pairs={{1,0},{0,1},{3,2},{2,3},{5,4},{4,5},{7,6},{6,7},{9,8},{8,9},{11,10... | collective-permute-start | bytes 196616 | tf_op jit(solution)/shard_map/ppermute | solution.py:445
  55.5 2.4 %collective-permute-done.10 = f32[64,256]{1,0:T(8,128)S(1)} collective-permute-done((f32[64,256]{1,0:T(8,128)S(1)}, f32[64,256]{1,0:T(8,128)S(1)}, u32[]{:S(2)}, u32[]{:S(2)}) %collective-permute-start.10) | collective-permute-done | bytes 65568 | tf_op jit(solution)/shard_map/ppermute | solution.py:445
  57.9 2.2 %collective-permute-done.9 = f32[64,256]{1,0:T(8,128)S(1)} collective-permute-done((f32[64,256]{1,0:T(8,128)S(1)}, f32[64,256]{1,0:T(8,128)S(1)}, u32[]{:S(2)}, u32[]{:S(2)}) %collective-permute-start.9) | collective-permute-done | bytes 65568 | tf_op jit(solution)/shard_map/ppermute | solution.py:445
  62.0 2.3 %collective-permute-done.13.refs_3_ = f32[64,256]{1,0:T(8,128)S(1)} collective-permute-done((f32[64,256]{1,0:T(8,128)S(1)}, f32[64,256]{1,0:T(8,128)S(1)}, u32[]{:S(2)}, u32[]{:S(2)}) %collective-permute-start.13) | collective-permute-done | bytes 65568 | tf_op jit(solution)/shard_map/ppermute | solution.py:445
  66.0 9.5 %joint_solve.1 = (f32[2,32,512]{2,1,0:T(8,128)}, f32[2,32,512]{2,1,0:T(8,128)S(1)}, bf16[2,32,512]{2,1,0:T(8,128)(2,1)S(1)}) custom-call(f32[64,256]{1,0:T(8,128)S(1)} %add_add_fusion.refs_0_, f32[64,256]{1,0:T(8,128)S(1)} %collective-permute-done.11.refs_1_, f32[64,256]{1,0:T(8,128)S(1)} %collective-permute-done.12.refs_2_, ...), custom_call_target="tpu_custom_call" | custom-call | tf_op jit(solution)/shard_map/joint_solve/pallas_call | solution.py:427
  75.4 2.0 %collective-permute-start.16 = (bf16[2,32,512]{2,1,0:T(8,128)(2,1)S(1)}, bf16[2,32,512]{2,1,0:T(8,128)(2,1)S(1)}, u32[]{:S(2)}, u32[]{:S(2)}) collective-permute-start(bf16[2,32,512]{2,1,0:T(8,128)(2,1)S(1)} %get-tuple-element.10.refs_0_), channel_id=1, source_target_pairs={{3,0},{2,1},{1,2},{0,3},{7,4},{6,5},{5,6},{4,7},{11,8},{10,9},{9,1... | collective-permute-start | bytes 196616 | tf_op jit(solution)/shard_map/ppermute | solution.py:445
  77.5 2.3 %collective-permute-start.14 = (bf16[2,32,512]{2,1,0:T(8,128)(2,1)S(1)}, bf16[2,32,512]{2,1,0:T(8,128)(2,1)S(1)}, u32[]{:S(2)}, u32[]{:S(2)}) collective-permute-start(bf16[2,32,512]{2,1,0:T(8,128)(2,1)S(1)} %get-tuple-element.10.refs_0_), channel_id=1, source_target_pairs={{1,0},{0,1},{3,2},{2,3},{5,4},{4,5},{7,6},{6,7},{9,8},{8,9},{11,10... | collective-permute-start | bytes 196616 | tf_op jit(solution)/shard_map/ppermute | solution.py:445
  79.8 2.2 %collective-permute-done.16.refs_3_ = bf16[2,32,512]{2,1,0:T(8,128)(2,1)S(1)} collective-permute-done((bf16[2,32,512]{2,1,0:T(8,128)(2,1)S(1)}, bf16[2,32,512]{2,1,0:T(8,128)(2,1)S(1)}, u32[]{:S(2)}, u32[]{:S(2)}) %collective-permute-start.16) | collective-permute-done | bytes 65568 | tf_op jit(solution)/shard_map/ppermute | solution.py:445
  82.0 2.0 %collective-permute-done.15.refs_2_ = bf16[2,32,512]{2,1,0:T(8,128)(2,1)S(1)} collective-permute-done((bf16[2,32,512]{2,1,0:T(8,128)(2,1)S(1)}, bf16[2,32,512]{2,1,0:T(8,128)(2,1)S(1)}, u32[]{:S(2)}, u32[]{:S(2)}) %collective-permute-start.15) | collective-permute-done | bytes 65568 | tf_op jit(solution)/shard_map/ppermute | solution.py:445
  84.0 5.5 %apply_score.1 = f32[2,32,32]{2,1,0:T(8,128)S(1)} custom-call(bf16[2,32,512]{2,1,0:T(8,128)(2,1)S(1)} %get-tuple-element.10.refs_0_, bf16[2,32,512]{2,1,0:T(8,128)(2,1)S(1)} %collective-permute-done.14.refs_1_, bf16[2,32,512]{2,1,0:T(8,128)(2,1)S(1)} %collective-permute-done.15.refs_2_, bf16[2,32,512]{2,1,0:T(8,128)(2,1)S(1)} %collective-permute-done.16.refs_3_, ...), custom_call_target="tpu_custom_call" | custom-call | tf_op jit(solution)/shard_map/apply_score/pallas_call | solution.py:224
  90.0 3.4 %collective-permute-done.17 = f32[2,32,32]{2,1,0:T(8,128)S(1)} collective-permute-done((f32[2,32,32]{2,1,0:T(8,128)S(1)}, f32[2,32,32]{2,1,0:T(8,128)S(1)}, u32[]{:S(2)}, u32[]{:S(2)}) %collective-permute-start.17) | collective-permute-done | bytes 8224 | tf_op jit(solution)/shard_map/ppermute | solution.py:462
  94.2 4.3 %collective-permute-done.18 = f32[2,32,32]{2,1,0:T(8,128)S(1)} collective-permute-done((f32[2,32,32]{2,1,0:T(8,128)S(1)}, f32[2,32,32]{2,1,0:T(8,128)S(1)}, u32[]{:S(2)}, u32[]{:S(2)}) %collective-permute-start.18) | collective-permute-done | bytes 8224 | tf_op jit(solution)/shard_map/ppermute | solution.py:463
  (33 shorter events, 13.9 us)
Async XLA Ops:
  1.5 13.7 %collective-permute-start.2 = (bf16[2,32,512]{2,1,0:T(8,128)(2,1)S(1)}, bf16[2,32,512]{2,1,0:T(8,128)(2,1)S(1)}, u32[]{:S(2)}, u32[]{:S(2)}) collective-permute-start(bf16[2,32,512]{2,1,0:T(8,128)(2,1)S(1)} %convert_element_type.3.refs_0_), channel_id=1, source_target_pairs={{3,0},{2,1},{1,2},{0,3},{7,4},{6,5},{5,6},{4,7},{11,8},{10,9},{9,1... | collective-permute-start | bytes 196616 | tf_op jit(solution)/shard_map/ppermute | solution.py:445
  6.7 8.6 %collective-permute-start.1 = (bf16[2,32,512]{2,1,0:T(8,128)(2,1)S(1)}, bf16[2,32,512]{2,1,0:T(8,128)(2,1)S(1)}, u32[]{:S(2)}, u32[]{:S(2)}) collective-permute-start(bf16[2,32,512]{2,1,0:T(8,128)(2,1)S(1)} %convert_element_type.3.refs_0_), channel_id=1, source_target_pairs={{2,0},{3,1},{0,2},{1,3},{6,4},{7,5},{4,6},{5,7},{10,8},{11,9},{8,1... | collective-permute-start | bytes 196616 | tf_op jit(solution)/shard_map/ppermute | solution.py:445
  6.7 8.6 %collective-permute-start = (bf16[2,32,512]{2,1,0:T(8,128)(2,1)S(1)}, bf16[2,32,512]{2,1,0:T(8,128)(2,1)S(1)}, u32[]{:S(2)}, u32[]{:S(2)}) collective-permute-start(bf16[2,32,512]{2,1,0:T(8,128)(2,1)S(1)} %convert_element_type.3.refs_0_), channel_id=1, source_target_pairs={{1,0},{0,1},{3,2},{2,3},{5,4},{4,5},{7,6},{6,7},{9,8},{8,9},{11,10... | collective-permute-start | bytes 196616 | tf_op jit(solution)/shard_map/ppermute | solution.py:445
  7.3 0.7 copy-start
  8.0 0.7 copy-start.1
  8.7 0.7 copy-start.2
  20.9 3.9 %collective-permute-start.3 = (f32[2,32,32]{2,1,0:T(8,128)S(1)}, f32[2,32,32]{2,1,0:T(8,128)S(1)}, u32[]{:S(2)}, u32[]{:S(2)}) collective-permute-start(f32[2,32,32]{2,1,0:T(8,128)S(1)} %get-tuple-element.7), channel_id=1, source_target_pairs={{1,0},{0,1},{3,2},{2,3},{5,4},{4,5},{7,6},{6,7},{9,8},{8,9},{11,10... | collective-permute-start | bytes 24584 | tf_op jit(solution)/shard_map/ppermute | solution.py:462
  24.8 4.8 %collective-permute-start.4 = (f32[2,32,32]{2,1,0:T(8,128)S(1)}, f32[2,32,32]{2,1,0:T(8,128)S(1)}, u32[]{:S(2)}, u32[]{:S(2)}) collective-permute-start(f32[2,32,32]{2,1,0:T(8,128)S(1)} %add.18.refs_0_), channel_id=1, source_target_pairs={{2,0},{3,1},{0,2},{1,3},{6,4},{7,5},{4,6},{5,7},{10,8},{11,9},{8,1... | collective-permute-start | bytes 24584 | tf_op jit(solution)/shard_map/ppermute | solution.py:463
  31.5 6.3 %collective-permute-start.7 = (bf16[2,32,512]{2,1,0:T(8,128)(2,1)S(1)}, bf16[2,32,512]{2,1,0:T(8,128)(2,1)S(1)}, u32[]{:S(2)}, u32[]{:S(2)}) collective-permute-start(bf16[2,32,512]{2,1,0:T(8,128)(2,1)S(1)} %solve_layers.1.refs_0_), channel_id=1, source_target_pairs={{3,0},{2,1},{1,2},{0,3},{7,4},{6,5},{5,6},{4,7},{11,8},{10,9},{9,1... | collective-permute-start | bytes 196616 | tf_op jit(solution)/shard_map/ppermute | solution.py:445
  35.3 5.2 %collective-permute-start.6 = (bf16[2,32,512]{2,1,0:T(8,128)(2,1)S(1)}, bf16[2,32,512]{2,1,0:T(8,128)(2,1)S(1)}, u32[]{:S(2)}, u32[]{:S(2)}) collective-permute-start(bf16[2,32,512]{2,1,0:T(8,128)(2,1)S(1)} %solve_layers.1.refs_0_), channel_id=1, source_target_pairs={{2,0},{3,1},{0,2},{1,3},{6,4},{7,5},{4,6},{5,7},{10,8},{11,9},{8,1... | collective-permute-start | bytes 196616 | tf_op jit(solution)/shard_map/ppermute | solution.py:445
  35.3 5.2 %collective-permute-start.5 = (bf16[2,32,512]{2,1,0:T(8,128)(2,1)S(1)}, bf16[2,32,512]{2,1,0:T(8,128)(2,1)S(1)}, u32[]{:S(2)}, u32[]{:S(2)}) collective-permute-start(bf16[2,32,512]{2,1,0:T(8,128)(2,1)S(1)} %solve_layers.1.refs_0_), channel_id=1, source_target_pairs={{1,0},{0,1},{3,2},{2,3},{5,4},{4,5},{7,6},{6,7},{9,8},{8,9},{11,10... | collective-permute-start | bytes 196616 | tf_op jit(solution)/shard_map/ppermute | solution.py:445
  51.1 6.9 %collective-permute-start.10 = (f32[64,256]{1,0:T(8,128)S(1)}, f32[64,256]{1,0:T(8,128)S(1)}, u32[]{:S(2)}, u32[]{:S(2)}) collective-permute-start(f32[64,256]{1,0:T(8,128)S(1)} %cross_gram.1), channel_id=1, source_target_pairs={{3,0},{2,1},{1,2},{0,3},{7,4},{6,5},{5,6},{4,7},{11,8},{10,9},{9,1... | collective-permute-start | bytes 196616 | tf_op jit(solution)/shard_map/ppermute | solution.py:445
  52.8 7.3 %collective-permute-start.9 = (f32[64,256]{1,0:T(8,128)S(1)}, f32[64,256]{1,0:T(8,128)S(1)}, u32[]{:S(2)}, u32[]{:S(2)}) collective-permute-start(f32[64,256]{1,0:T(8,128)S(1)} %cross_gram.1), channel_id=1, source_target_pairs={{2,0},{3,1},{0,2},{1,3},{6,4},{7,5},{4,6},{5,7},{10,8},{11,9},{8,1... | collective-permute-start | bytes 196616 | tf_op jit(solution)/shard_map/ppermute | solution.py:445
  53.2 6.9 %collective-permute-start.8 = (f32[64,256]{1,0:T(8,128)S(1)}, f32[64,256]{1,0:T(8,128)S(1)}, u32[]{:S(2)}, u32[]{:S(2)}) collective-permute-start(f32[64,256]{1,0:T(8,128)S(1)} %cross_gram.1), channel_id=1, source_target_pairs={{1,0},{0,1},{3,2},{2,3},{5,4},{4,5},{7,6},{6,7},{9,8},{8,9},{11,10... | collective-permute-start | bytes 196616 | tf_op jit(solution)/shard_map/ppermute | solution.py:445
  60.1 4.2 %collective-permute-start.13 = (f32[64,256]{1,0:T(8,128)S(1)}, f32[64,256]{1,0:T(8,128)S(1)}, u32[]{:S(2)}, u32[]{:S(2)}) collective-permute-start(f32[64,256]{1,0:T(8,128)S(1)} %add_add_fusion.refs_0_), channel_id=1, source_target_pairs={{12,0},{8,4},{4,8},{0,12},{13,1},{9,5},{5,9},{1,13},{14,2},{10,6},... | collective-permute-start | bytes 196616 | tf_op jit(solution)/shard_map/ppermute | solution.py:445
  60.6 5.3 %collective-permute-start.12 = (f32[64,256]{1,0:T(8,128)S(1)}, f32[64,256]{1,0:T(8,128)S(1)}, u32[]{:S(2)}, u32[]{:S(2)}) collective-permute-start(f32[64,256]{1,0:T(8,128)S(1)} %add_add_fusion.refs_0_), channel_id=1, source_target_pairs={{8,0},{12,4},{0,8},{4,12},{9,1},{13,5},{1,9},{5,13},{10,2},{14,6},... | collective-permute-start | bytes 196616 | tf_op jit(solution)/shard_map/ppermute | solution.py:445
  61.8 4.1 %collective-permute-start.11 = (f32[64,256]{1,0:T(8,128)S(1)}, f32[64,256]{1,0:T(8,128)S(1)}, u32[]{:S(2)}, u32[]{:S(2)}) collective-permute-start(f32[64,256]{1,0:T(8,128)S(1)} %add_add_fusion.refs_0_), channel_id=1, source_target_pairs={{4,0},{0,4},{12,8},{8,12},{5,1},{1,5},{13,9},{9,13},{6,2},{2,6},{1... | collective-permute-start | bytes 196616 | tf_op jit(solution)/shard_map/ppermute | solution.py:445
  75.4 6.5 %collective-permute-start.16 = (bf16[2,32,512]{2,1,0:T(8,128)(2,1)S(1)}, bf16[2,32,512]{2,1,0:T(8,128)(2,1)S(1)}, u32[]{:S(2)}, u32[]{:S(2)}) collective-permute-start(bf16[2,32,512]{2,1,0:T(8,128)(2,1)S(1)} %get-tuple-element.10.refs_0_), channel_id=1, source_target_pairs={{3,0},{2,1},{1,2},{0,3},{7,4},{6,5},{5,6},{4,7},{11,8},{10,9},{9,1... | collective-permute-start | bytes 196616 | tf_op jit(solution)/shard_map/ppermute | solution.py:445
  77.5 6.5 %collective-permute-start.15 = (bf16[2,32,512]{2,1,0:T(8,128)(2,1)S(1)}, bf16[2,32,512]{2,1,0:T(8,128)(2,1)S(1)}, u32[]{:S(2)}, u32[]{:S(2)}) collective-permute-start(bf16[2,32,512]{2,1,0:T(8,128)(2,1)S(1)} %get-tuple-element.10.refs_0_), channel_id=1, source_target_pairs={{2,0},{3,1},{0,2},{1,3},{6,4},{7,5},{4,6},{5,7},{10,8},{11,9},{8,1... | collective-permute-start | bytes 196616 | tf_op jit(solution)/shard_map/ppermute | solution.py:445
  77.5 6.5 %collective-permute-start.14 = (bf16[2,32,512]{2,1,0:T(8,128)(2,1)S(1)}, bf16[2,32,512]{2,1,0:T(8,128)(2,1)S(1)}, u32[]{:S(2)}, u32[]{:S(2)}) collective-permute-start(bf16[2,32,512]{2,1,0:T(8,128)(2,1)S(1)} %get-tuple-element.10.refs_0_), channel_id=1, source_target_pairs={{1,0},{0,1},{3,2},{2,3},{5,4},{4,5},{7,6},{6,7},{9,8},{8,9},{11,10... | collective-permute-start | bytes 196616 | tf_op jit(solution)/shard_map/ppermute | solution.py:445
  89.5 3.9 %collective-permute-start.17 = (f32[2,32,32]{2,1,0:T(8,128)S(1)}, f32[2,32,32]{2,1,0:T(8,128)S(1)}, u32[]{:S(2)}, u32[]{:S(2)}) collective-permute-start(f32[2,32,32]{2,1,0:T(8,128)S(1)} %apply_score.1), channel_id=1, source_target_pairs={{1,0},{0,1},{3,2},{2,3},{5,4},{4,5},{7,6},{6,7},{9,8},{8,9},{11,10... | collective-permute-start | bytes 24584 | tf_op jit(solution)/shard_map/ppermute | solution.py:462
  93.4 5.1 %collective-permute-start.18 = (f32[2,32,32]{2,1,0:T(8,128)S(1)}, f32[2,32,32]{2,1,0:T(8,128)S(1)}, u32[]{:S(2)}, u32[]{:S(2)}) collective-permute-start(f32[2,32,32]{2,1,0:T(8,128)S(1)} %add.22), channel_id=1, source_target_pairs={{2,0},{3,1},{0,2},{1,3},{6,4},{7,5},{4,6},{5,7},{10,8},{11,9},{8,1... | collective-permute-start | bytes 24584 | tf_op jit(solution)/shard_map/ppermute | solution.py:463

commit v7 on v6

--- a/solution.py
+++ b/solution.py
@@ -63,8 +63,18 @@
     lax.fori_loop(0, BLK * BLK // 256, step, 0)
 
 
-def build_whole_kernel(rows_ref, cols_ref, counts_ref, blocks_ref, dense_ref, held, arrived):
+def build_whole_kernel(
+    rows_hbm, cols_hbm, counts_hbm, blocks_ref, dense_ref, held, rows_ref, cols_ref, counts_ref, arrived, index_arrived
+):
     layers, chunks = dense_ref.shape[:2]
+    index_copies = [
+        pltpu.make_async_copy(source, target, index_arrived.at[i])
+        for i, (source, target) in enumerate(
+            [(rows_hbm, rows_ref), (cols_hbm, cols_ref), (counts_hbm, counts_ref)]
+        )
+    ]
+    for copy in index_copies:
+        copy.start()
     pieces = arrived.shape[1]
     width = held.shape[2] // pieces
     inner = width // 256
@@ -79,6 +89,8 @@
         for piece in range(pieces):
             fetch(layer, piece).start()
     flip = lax.axis_index("node") * CHUNK_COLS
+    for copy in index_copies:
+        copy.wait()
     for layer in range(layers):
         onehot = one_hot(rows_ref, cols_ref, counts_ref, layer, flip, 0, chunks * CHUNK_COLS * BROWS)
 
@@ -98,18 +110,23 @@
     dense = jax.ShapeDtypeStruct((layers, chunk_total, 2 * TALL, CHUNK_LANES), BF16)
     operands = (block_rows, block_cols, counts.T, blocks)
     if chunk_total <= 4:
-        operands = (*operands[:3], pltpu.with_memory_space_constraint(blocks, pltpu.HBM))
         pieces = 4
         return pl.pallas_call(
             build_whole_kernel,
-            in_specs=vmem_specs(2)
-            + [pl.BlockSpec(memory_space=pltpu.SMEM), pl.BlockSpec(memory_space=pltpu.HBM)],
+            in_specs=[pl.BlockSpec(memory_space=pltpu.HBM)] * 4,
             out_specs=pl.BlockSpec(memory_space=pltpu.VMEM),
             out_shape=dense,
-            scratch_shapes=[pltpu.VMEM(blocks.shape, BF16), pltpu.SemaphoreType.DMA((layers, pieces))],
+            scratch_shapes=[
+                pltpu.VMEM(blocks.shape, BF16),
+                pltpu.VMEM(block_rows.shape, jnp.int32),
+                pltpu.VMEM(block_cols.shape, jnp.int32),
+                pltpu.SMEM((1, layers), jnp.int32),
+                pltpu.SemaphoreType.DMA((layers, pieces)),
+                pltpu.SemaphoreType.DMA((3,)),
+            ],
             compiler_params=params(28),
             name="build_dense",
-        )(*operands)
+        )(*[pltpu.with_memory_space_constraint(x, pltpu.HBM) for x in operands])
     return pl.pallas_call(
         build_kernel,
         grid=(layers, chunk_total // 4),
@@ -136,7 +153,7 @@
 def image_part(basis, dense):
     k, width = basis.shape
     basis = basis.astype(F32)
-    tall = jnp.concatenate([basis, basis, jnp.zeros((128 - 2 * k, width), F32)], axis=0).T
+    tall = jnp.concatenate([basis, basis], axis=0).T
     lane = lax.broadcasted_iota(jnp.int32, tall.shape, 1)
     first = jnp.where(lane < k, tall, 0.0).astype(BF16)
     second = jnp.where(lane < k, 0.0, tall).astype(BF16)
@@ -147,7 +164,8 @@
 
 
 def to_wide(total, k, halves, tall):
-    halves[...] = total[:TALL] + total[TALL:]
+    halves[:, : 2 * k] = total[:TALL] + total[TALL:]
+    halves[:, 2 * k :] = jnp.zeros((TALL, 128 - 2 * k), F32)
     for b in range(BROWS):
         part = halves[pl.ds(b, BLK // 2, stride=BROWS), :]
         tall[pl.ds(BLK * b, BLK // 2, stride=2), :] = part
@@ -194,23 +212,40 @@
             out_ref[0] = against(left_ref[0], tall[...])
 
 
+def product(a, b):
+    k = a.shape[0]
+    left = jnp.concatenate(split3(a), axis=0)
+    right = left if b is a else jnp.concatenate(split3(b), axis=0)
+    pieces = lax.dot_general(left, right, TRANS_B, preferred_element_type=F32)
+    top, middle, bottom = pieces[:k], pieces[k : 2 * k], pieces[2 * k :]
+    total = top[:, :k] + (top[:, k : 2 * k] + middle[:, :k])
+    return total + (middle[:, k : 2 * k] + (top[:, 2 * k : 3 * k] + bottom[:, :k]))
+
+
 def apply_whole_kernel(mode, piece_count, *refs):
     pieces, refs = refs[:piece_count], refs[piece_count:]
     if mode == "score":
         left_ref, refs = refs[0], refs[1:]
-    dense_ref, out_ref = refs[:2]
-    halves, tall = refs[-2:]
-    for layer in range(dense_ref.shape[0]):
-        total = sum(
-            image_part(piece[layer], dense_ref[layer, chunk]) for chunk, piece in enumerate(pieces)
-        )
-        image = to_wide(total, pieces[0].shape[1], halves.at[layer], tall.at[layer])
-        if mode != "score":
-            out_ref[layer] = image
-        if mode == "gram":
-            refs[2][layer] = against(image, tall[layer])
-        if mode == "score":
-            out_ref[layer] = against(left_ref[layer], tall[layer])
+    dense_ref, out_ref, halves, tall = refs
+    layers, k = pieces[0].shape[:2]
+    if mode == "solved":
+        images = [jnp.concatenate([piece[layer] for piece in pieces], axis=1) for layer in range(layers)]
+        grams = [product(image, image) for image in images]
+        inverses = [inverse_factor(gram) for gram in grams]
+        bases = [
+            jnp.dot(inverse, image, precision=HIGHEST, preferred_element_type=F32)
+            for inverse, image in zip(inverses, images)
+        ]
+        parts = [[basis[:, d * ROWS_DEV : d * ROWS_DEV + ROWS_DEV] for d in range(piece_count)] for basis in bases]
+    else:
+        parts = [[piece[layer] for piece in pieces] for layer in range(layers)]
+    totals = [
+        sum(image_part(part, dense_ref[layer, chunk]) for chunk, part in enumerate(parts[layer]))
+        for layer in range(layers)
+    ]
+    wide = [to_wide(totals[layer], k, halves.at[layer], tall.at[layer]) for layer in range(layers)]
+    for layer in range(layers):
+        out_ref[layer] = product(left_ref[layer], wide[layer]) if mode == "score" else wide[layer]
 
 
 def apply_dense(mode, pieces, dense, left=None):
@@ -218,7 +253,7 @@
     k = pieces[0].shape[-2]
     image = jax.ShapeDtypeStruct((layers, k, ROWS_DEV), F32)
     small = jax.ShapeDtypeStruct((layers, k, k), F32)
-    out_shape = {"gram": [image, small], "plain": [image], "score": [small]}[mode]
+    out_shape = {"gram": [image, small], "plain": [image], "solved": [image], "score": [small]}[mode]
     operands = list(pieces) + ([left] if mode == "score" else []) + [dense]
     if len(pieces) == chunks:
         return pl.pallas_call(
@@ -242,7 +277,7 @@
         scratch_shapes=[
             pltpu.VMEM((TALL, 128), F32),
             pltpu.VMEM((ROWS_DEV, 128), F32),
-            pltpu.VMEM((2 * TALL, 128), F32),
+            pltpu.VMEM((2 * TALL, 2 * k), F32),
         ],
         compiler_params=params(12),
         name="apply_" + mode,
@@ -333,62 +368,76 @@
     return lambda at, count: parts[at // 128 * 128][at % 128 : at % 128 + count]
 
 
-def solve_kernel(piece_count, *refs):
-    grams, image_ref, out_ref = refs[:piece_count], refs[piece_count], refs[piece_count + 1]
-    layers, k = image_ref.shape[:2]
+def inverse_factor(gram):
+    k = gram.shape[0]
     lane = lax.broadcasted_iota(jnp.int32, (k, 128), 1)
     sub = lax.broadcasted_iota(jnp.int32, (k, 128), 0)
     eye = jnp.where(lane == sub, 1.0, 0.0)
-    for layer in range(layers):
-        gram = sum(ref[layer] for ref in grams)
-        gram = jnp.concatenate([gram, jnp.zeros((k, 128 - k), F32)], axis=1)
-        gram, across = unit_scale(gram)
-        solved = eliminate(tiled(jnp.concatenate([gram, eye], axis=1)), 0)
-        inverse = joined(solved)[:, 128:] * across
-        solved = jnp.dot(inverse[:, :k], image_ref[layer], precision=HIGHEST, preferred_element_type=F32)
+    gram, across = unit_scale(jnp.concatenate([gram, jnp.zeros((k, 128 - k), F32)], axis=1))
+    solved = eliminate(tiled(jnp.concatenate([gram, eye], axis=1)), 0)
+    return (joined(solved)[:, 128:] * across)[:, :k]
+
+
+def solve_kernel(gram_ref, image_ref, out_ref):
+    for layer in range(image_ref.shape[0]):
+        inverse = inverse_factor(gram_ref[layer])
+        solved = jnp.dot(inverse, image_ref[layer], precision=HIGHEST, preferred_element_type=F32)
         out_ref[layer] = solved.astype(BF16)
 
 
-def solve(grams, image):
+def solve(gram, image):
     return pl.pallas_call(
-        functools.partial(solve_kernel, len(grams)),
-        in_specs=vmem_specs(len(grams) + 1),
+        solve_kernel,
+        in_specs=vmem_specs(2),
         out_specs=pl.BlockSpec(memory_space=pltpu.VMEM),
         out_shape=jax.ShapeDtypeStruct(image.shape, BF16),
         compiler_params=params(4),
         name="solve_layers",
-    )(*grams, image)
-
-
-def stack_rows(refs, scratch):
-    g = lax.axis_index("layer")
-    rows = scratch.shape[0] // len(refs)
-    for d, ref in enumerate(refs):
-        at = (g ^ d) * rows
-        scratch[pl.ds(pl.multiple_of(at, rows), rows)] = ref[...].reshape(rows, ref.shape[-1])
-
-
-def cross_kernel(own_ref, all_ref, out_ref):
-    own = own_ref[...].reshape(-1, own_ref.shape[2])
-    every = all_ref[...].reshape(-1, own_ref.shape[2])
-    out_ref[...] = lax.dot_general(own, every, TRANS_B, precision=HIGHEST, preferred_element_type=F32)
-
-
-def cross(own, every):
-    rows = own.shape[0] * own.shape[1]
+    )(gram, image)
+
+
+def cross_kernel(k, all_ref, out_ref):
+    every = all_ref[...].reshape(-1, all_ref.shape[2])
+    gram = lax.dot_general(every, every, TRANS_B, precision=HIGHEST, preferred_element_type=F32)
+    half = gram.shape[0] // 2
+    first, last = gram[:half, :half], gram[half:, half:]
+    row = lax.broadcasted_iota(jnp.int32, (half, half), 0) // k
+    col = lax.broadcasted_iota(jnp.int32, (half, half), 1) // k
+    out_ref[:half] = gram[:half, half:]
+    out_ref[half : 2 * half] = jnp.where(col >= row, first, last)
+    diagonal = jnp.where(col == row, last, 0.0)
+    out_ref[2 * half :] = sum(diagonal[r * k : r * k + k] for r in range(half // k))
+
+
+def cross(every):
+    _, k, _ = every.shape
+    half = every.shape[0] * k // 2
     return pl.pallas_call(
-        cross_kernel,
-        in_specs=vmem_specs(2),
+        functools.partial(cross_kernel, k),
+        in_specs=vmem_specs(1),
         out_specs=pl.BlockSpec(memory_space=pltpu.VMEM),
-        out_shape=jax.ShapeDtypeStruct((rows, every.shape[0] * every.shape[1]), F32),
+        out_shape=jax.ShapeDtypeStruct((2 * half + k, half), F32),
         compiler_params=params(6),
         name="cross_gram",
-    )(own, every)
+    )(every)
+
+
+def unpack(packed, k, work):
+    half = packed.shape[1]
+    row = lax.broadcasted_iota(jnp.int32, (half, half), 0) // k
+    col = lax.broadcasted_iota(jnp.int32, (half, half), 1) // k
+    mixed = packed[half : 2 * half]
+    under = jnp.where(col < row, mixed, 0.0)
+    diagonal = jnp.concatenate([packed[2 * half :]] * (half // k), axis=0)
+    work[:half, :half] = jnp.where(col >= row, mixed, 0.0)
+    work[:half, half:] = packed[:half]
+    work[half:, :half] = jnp.zeros((half, half), F32)
+    work[half:, half:] = under.T + jnp.where(col == row, diagonal, 0.0)
 
 
 def joint_kernel(piece_count, k, *refs):
-    gram_refs, (images_ref, out_ref, again_ref, rounded_ref, work) = refs[:piece_count], refs[piece_count:]
-    stack_rows(gram_refs, work)
+    packed_refs, (images_ref, out_ref, again_ref, rounded_ref, work) = refs[:piece_count], refs[piece_count:]
+    unpack(add_pieces([ref[...] for ref in packed_refs]), k, work)
     size = work.shape[0]
     steps = size // k
     lane = lax.broadcasted_iota(jnp.int32, (k, size), 1)
@@ -409,7 +458,7 @@
             for r in range(s + 1, steps):
                 rows = work[r * k : r * k + k]
                 work[r * k : r * k + k] = jnp.where(here, 0.0, rows) - update(r * k, k)
-    rows = size // piece_count
+    rows = out_ref.shape[0] * k
     own = work[pl.ds(pl.multiple_of(lax.axis_index("layer") * rows, rows), rows)] * across
     images = images_ref[...].reshape(size, -1)
     joint = jnp.dot(own, images, precision=HIGHEST, preferred_element_type=F32)
@@ -419,14 +468,13 @@
     rounded_ref[...] = joint.astype(BF16)
 
 
-def joint_solve(grams, images):
-    groups = len(grams)
+def joint_solve(packed, images, layers):
     _, k, width = images.shape
-    size = grams[0].shape[1]
-    shape = (images.shape[0] // groups, k, width)
+    size = images.shape[0] * k
+    shape = (layers, k, width)
     return pl.pallas_call(
-        functools.partial(joint_kernel, groups, k),
-        in_specs=vmem_specs(groups + 1),
+        functools.partial(joint_kernel, len(packed), k),
+        in_specs=vmem_specs(len(packed) + 1),
         out_specs=vmem_specs(3),
         out_shape=[
             jax.ShapeDtypeStruct(shape, F32),
@@ -436,7 +484,7 @@
         scratch_shapes=[pltpu.VMEM((size, size), F32)],
         compiler_params=params(8),
         name="joint_solve",
-    )(*grams, images)
+    )(*packed, images)
 
 
 def around(x, axis, count):
@@ -447,33 +495,32 @@
 
 
 def add_pieces(pieces):
+    if len(pieces) == 1:
+        return pieces[0]
     return (pieces[0] + pieces[1]) + (pieces[2] + pieces[3])
 
 
-def per_device(shards, groups, blocks, block_rows, block_cols, counts, start):
+def per_device(shards, blocks, block_rows, block_cols, counts, start):
     few = shards == 4
 
     def gather(x):
         return around(x, "node", shards) if few else [lax.all_gather(x, "node")]
 
     def partials(x):
-        if not few:
-            return [lax.psum(x, "node")]
-        near = x + lax.ppermute(x, "node", [(m ^ 1, m) for m in range(shards)])
-        return [near, lax.ppermute(near, "node", [(m ^ 2, m) for m in range(shards)])]
-
-    def total(x):
-        return add_pieces(around(x, "node", shards)) if few else lax.psum(x, "node")
-
-    first = gather(start.astype(BF16))
+        return around(x, "node", shards) if few else [lax.psum(x, "node")]
+
+    first = gather(start if few else start.astype(BF16))
     dense = build_dense(block_rows, block_cols, counts, blocks, shards * BROWS // CHUNK_COLS)
-    image, gram = apply_dense("gram", first, dense)
-    (image,) = apply_dense("plain", gather(solve(partials(gram), image)), dense)
+    if few:
+        (image,) = apply_dense("plain", first, dense)
+        (image,) = apply_dense("solved", gather(image), dense)
+    else:
+        image, gram = apply_dense("gram", first, dense)
+        (image,) = apply_dense("plain", gather(solve(lax.psum(gram, "node"), image)), dense)
     images = lax.all_gather(image, "layer", axis=0, tiled=True)
-    grams = around(total(cross(image, images)), "layer", groups)
-    joint_basis, again, rounded = joint_solve(grams, images)
+    joint_basis, again, rounded = joint_solve(partials(cross(images)), images, start.shape[0])
     (partial,) = apply_dense("score", gather(rounded), dense, again)
-    return joint_basis, sum(partials(partial))
+    return joint_basis, add_pieces(partials(partial))
 
 
 def solution(mesh):
@@ -486,7 +533,7 @@
     )
     out_specs = (P(("parts", "layer"), None, "node"), P(("parts", "layer"), None, None))
     return jax.shard_map(
-        functools.partial(per_device, mesh.shape["node"], mesh.shape["layer"]),
+        functools.partial(per_device, mesh.shape["node"]),
         mesh=mesh,
         in_specs=in_specs,
         out_specs=out_specs,

time: 99.3 us -> 90.1 us (0.907)
  Pallas kernels: 31.6 us -> 28 us
  starting transfers between devices: 25.9 us -> 23.8 us
  local copies, waits for them, and re-layouts: 2.03 us -> 0.01 us
    ppermute x4 -> x0, waiting for transfers between devices: 12.8 us -> none  [the longest x2 6.79 us: partials(): lax.ppermute(near, 'node', [(m ^ 2, m) for m in range(shards)])]
    ppermute x15, waiting for transfers between devices: 17.2 us -> 29.4 us  [around(): pieces.append(lax.ppermute(x, axis, [(m ^ d, m) for m in range(count)]))]
    ppermute x4 -> x0, starting transfers between devices: 4.99 us -> none  [the longest x2 3.1 us: partials(): lax.ppermute(near, 'node', [(m ^ 2, m) for m in range(shards)])]
    ppermute x15, starting transfers between devices: 20.9 us -> 23.8 us  [around(): pieces.append(lax.ppermute(x, axis, [(m ^ d, m) for m in range(count)]))]
    pallas_call x3, Pallas kernels: 13.7 us -> 11 us  [apply_dense(): pl.pallas_call(functools.partial(apply_whole_kernel, mode, chunks), in_sp...]
    unnamed x6 -> x2, local copies, waits for them, and re-layouts: 2.03 us -> 0.01 us
    pallas_call x4 -> x3, Pallas kernels: 17.9 us -> 17 us  [the longest x1 9.52 us: joint_solve(): pl.pallas_call(functools.partial(joint_kernel, len(packed), k), in_specs=...]
  transfers between devices with their start and end apart: 19 -> 15, of which waited for: 12 -> 9; matrix products, arithmetic and copies ran while one was open for 0% -> 0% of each run, Pallas kernels for 6% -> 8%
where the time goes in v7:
time: 90.1 us; the launch traced here: 89.9 us
  waiting for transfers between devices  29.4 us (33%)
  Pallas kernels  28 us (31%)
  starting transfers between devices  23.8 us (26%)
  blocking collectives  7.37 us (8%)
    ppermute x15, waiting for transfers between devices, around(): pieces.append(lax.ppermute(x, axis, [(m ^ d, m) for m in range(count)]))  29.4 us
    ppermute x15, starting transfers between devices, around(): pieces.append(lax.ppermute(x, axis, [(m ^ d, m) for m in range(count)]))  23.8 us
    pallas_call x3, Pallas kernels, apply_dense(): pl.pallas_call(functools.partial(apply_whole_kernel, mode, chunks), in_sp...  11 us
    pallas_call x1, Pallas kernels, joint_solve(): pl.pallas_call(functools.partial(joint_kernel, len(packed), k), in_specs=...  9.52 us
    all_gather x1, blocking collectives, per_device(): images = lax.all_gather(image, 'layer', axis=0, tiled=True)  7.37 us
    pallas_call x1, Pallas kernels, build_dense(): pl.pallas_call(build_whole_kernel, in_specs=[pl.BlockSpec(memory_space=pl...  6.88 us
  transfers between devices with their start and end apart: 15, of which 9 were waited for; matrix products, arithmetic and copies ran while one was open for 0% of the time, Pallas kernels for 8%

profile of v7, /device:TPU:0, one launch (start us, length us, event | category | flops | bytes accessed | tf_op | source)
XLA Modules:
  0.0 89.9 jit_solution(11543358179983786378)
XLA Ops:
  0.6 4.1 %collective-permute-start.1 = (f32[2,32,512]{2,1,0:T(8,128)}, f32[2,32,512]{2,1,0:T(8,128)S(1)}, u32[]{:S(2)}, u32[]{:S(2)}) collective-permute-start(f32[2,32,512]{2,1,0:T(8,128)} %refs_0_.1), channel_id=1, source_target_pairs={{2,0},{3,1},{0,2},{1,3},{6,4},{7,5},{4,6},{5,7},{10,8},{11,9},{8,1... | collective-permute-start | bytes 393224 | tf_op jit(solution)/shard_map/ppermute | solution.py:493
  4.7 1.6 %collective-permute-start = (f32[2,32,512]{2,1,0:T(8,128)}, f32[2,32,512]{2,1,0:T(8,128)S(1)}, u32[]{:S(2)}, u32[]{:S(2)}) collective-permute-start(f32[2,32,512]{2,1,0:T(8,128)} %refs_0_.1), channel_id=1, source_target_pairs={{1,0},{0,1},{3,2},{2,3},{5,4},{4,5},{7,6},{6,7},{9,8},{8,9},{11,10... | collective-permute-start | bytes 393224 | tf_op jit(solution)/shard_map/ppermute | solution.py:493
  6.3 6.9 %build_dense.1.refs_4_.refs_5_ = bf16[2,4,512,1024]{3,2,1,0:T(8,128)(2,1)S(1)} custom-call(s32[2,512]{1,0:T(2,128)} %rows_hbm.1, s32[2,512]{1,0:T(2,128)} %cols_hbm.1, s32[1,2]{1,0:T(1,128)} %bitcast.1, bf16[2,512,4096]{2,1,0:T(8,128)(2,1)} %blocks_ref.1), custom_call_target="tpu_custom_call" | custom-call | tf_op jit(solution)/shard_map/build_dense/pallas_call | solution.py:114
  13.2 2.0 %collective-permute-done.2.refs_3_ = f32[2,32,512]{2,1,0:T(8,128)S(1)} collective-permute-done((f32[2,32,512]{2,1,0:T(8,128)}, f32[2,32,512]{2,1,0:T(8,128)S(1)}, u32[]{:S(2)}, u32[]{:S(2)}) %collective-permute-start.2) | collective-permute-done | bytes 131104 | tf_op jit(solution)/shard_map/ppermute | solution.py:493
  15.3 2.7 %apply_plain.1.refs_0_ = f32[2,32,512]{2,1,0:T(8,128)S(1)} custom-call(f32[2,32,512]{2,1,0:T(8,128)S(1)} %copy-done, f32[2,32,512]{2,1,0:T(8,128)S(1)} %collective-permute-done.refs_1_, f32[2,32,512]{2,1,0:T(8,128)S(1)} %collective-permute-done.1.refs_2_, f32[2,32,512]{2,1,0:T(8,128)S(1)} %collective-permute-done.2.refs_3_, ...), custom_call_target="tpu_custom_call" | custom-call | tf_op jit(solution)/shard_map/apply_plain/pallas_call | solution.py:259
  18.0 2.5 %collective-permute-start.5 = (f32[2,32,512]{2,1,0:T(8,128)S(1)}, f32[2,32,512]{2,1,0:T(8,128)S(1)}, u32[]{:S(2)}, u32[]{:S(2)}) collective-permute-start(f32[2,32,512]{2,1,0:T(8,128)S(1)} %apply_plain.1.refs_0_), channel_id=1, source_target_pairs={{3,0},{2,1},{1,2},{0,3},{7,4},{6,5},{5,6},{4,7},{11,8},{10,9},{9,1... | collective-permute-start | bytes 393224 | tf_op jit(solution)/shard_map/ppermute | solution.py:493
  20.5 1.9 %collective-permute-start.4 = (f32[2,32,512]{2,1,0:T(8,128)S(1)}, f32[2,32,512]{2,1,0:T(8,128)S(1)}, u32[]{:S(2)}, u32[]{:S(2)}) collective-permute-start(f32[2,32,512]{2,1,0:T(8,128)S(1)} %apply_plain.1.refs_0_), channel_id=1, source_target_pairs={{2,0},{3,1},{0,2},{1,3},{6,4},{7,5},{4,6},{5,7},{10,8},{11,9},{8,1... | collective-permute-start | bytes 393224 | tf_op jit(solution)/shard_map/ppermute | solution.py:493
  22.8 2.1 %collective-permute-done.5.refs_3_ = f32[2,32,512]{2,1,0:T(8,128)S(1)} collective-permute-done((f32[2,32,512]{2,1,0:T(8,128)S(1)}, f32[2,32,512]{2,1,0:T(8,128)S(1)}, u32[]{:S(2)}, u32[]{:S(2)}) %collective-permute-start.5) | collective-permute-done | bytes 131104 | tf_op jit(solution)/shard_map/ppermute | solution.py:493
  24.9 8.0 %collective-permute-done.4.refs_2_ = f32[2,32,512]{2,1,0:T(8,128)S(1)} collective-permute-done((f32[2,32,512]{2,1,0:T(8,128)S(1)}, f32[2,32,512]{2,1,0:T(8,128)S(1)}, u32[]{:S(2)}, u32[]{:S(2)}) %collective-permute-start.4) | collective-permute-done | bytes 131104 | tf_op jit(solution)/shard_map/ppermute | solution.py:493
  33.0 5.3 %apply_solved.1 = f32[2,32,512]{2,1,0:T(8,128)S(1)} custom-call(f32[2,32,512]{2,1,0:T(8,128)S(1)} %apply_plain.1.refs_0_, f32[2,32,512]{2,1,0:T(8,128)S(1)} %collective-permute-done.3.refs_1_, f32[2,32,512]{2,1,0:T(8,128)S(1)} %collective-permute-done.4.refs_2_, f32[2,32,512]{2,1,0:T(8,128)S(1)} %collective-permute-done.5.refs_3_, ...), custom_call_target="tpu_custom_call" | custom-call | tf_op jit(solution)/shard_map/apply_solved/pallas_call | solution.py:259
  38.2 7.4 %all_gather.3.all_ref.refs_4_ = f32[8,32,512]{2,1,0:T(8,128)S(1)} all-gather(f32[2,32,512]{2,1,0:T(8,128)S(1)} %apply_solved.1), channel_id=1, replica_groups=mesh['parts'=2,'layer'=4,'node'=4] {'layer'}, dimensions={0}, use_global_device_ids=true | all-gather | bytes 655360 | tf_op jit(solution)/shard_map/all_gather | solution.py:520
  46.2 2.7 %collective-permute-start.8 = (f32[288,128]{1,0:T(8,128)S(1)}, f32[288,128]{1,0:T(8,128)S(1)}, u32[]{:S(2)}, u32[]{:S(2)}) collective-permute-start(f32[288,128]{1,0:T(8,128)S(1)} %cross_gram.1.refs_0_), channel_id=1, source_target_pairs={{3,0},{2,1},{1,2},{0,3},{7,4},{6,5},{5,6},{4,7},{11,8},{10,9},{9,1... | collective-permute-start | bytes 442376 | tf_op jit(solution)/shard_map/ppermute | solution.py:493
  48.9 1.7 %collective-permute-start.6 = (f32[288,128]{1,0:T(8,128)S(1)}, f32[288,128]{1,0:T(8,128)S(1)}, u32[]{:S(2)}, u32[]{:S(2)}) collective-permute-start(f32[288,128]{1,0:T(8,128)S(1)} %cross_gram.1.refs_0_), channel_id=1, source_target_pairs={{1,0},{0,1},{3,2},{2,3},{5,4},{4,5},{7,6},{6,7},{9,8},{8,9},{11,10... | collective-permute-start | bytes 442376 | tf_op jit(solution)/shard_map/ppermute | solution.py:493
  50.7 4.2 %collective-permute-done.8.refs_3_ = f32[288,128]{1,0:T(8,128)S(1)} collective-permute-done((f32[288,128]{1,0:T(8,128)S(1)}, f32[288,128]{1,0:T(8,128)S(1)}, u32[]{:S(2)}, u32[]{:S(2)}) %collective-permute-start.8) | collective-permute-done | bytes 147488 | tf_op jit(solution)/shard_map/ppermute | solution.py:493
  54.9 6.2 %collective-permute-done.7.refs_2_ = f32[288,128]{1,0:T(8,128)S(1)} collective-permute-done((f32[288,128]{1,0:T(8,128)S(1)}, f32[288,128]{1,0:T(8,128)S(1)}, u32[]{:S(2)}, u32[]{:S(2)}) %collective-permute-start.7) | collective-permute-done | bytes 147488 | tf_op jit(solution)/shard_map/ppermute | solution.py:493
  61.1 9.5 %joint_solve.1 = (f32[2,32,512]{2,1,0:T(8,128)}, f32[2,32,512]{2,1,0:T(8,128)S(1)}, bf16[2,32,512]{2,1,0:T(8,128)(2,1)S(1)}) custom-call(f32[288,128]{1,0:T(8,128)S(1)} %cross_gram.1.refs_0_, f32[288,128]{1,0:T(8,128)S(1)} %collective-permute-done.6.refs_1_, f32[288,128]{1,0:T(8,128)S(1)} %collective-permute-done.7.refs_2_, ...), custom_call_target="tpu_custom_call" | custom-call | tf_op jit(solution)/shard_map/joint_solve/pallas_call | solution.py:475
  70.7 2.1 %collective-permute-start.11 = (bf16[2,32,512]{2,1,0:T(8,128)(2,1)S(1)}, bf16[2,32,512]{2,1,0:T(8,128)(2,1)S(1)}, u32[]{:S(2)}, u32[]{:S(2)}) collective-permute-start(bf16[2,32,512]{2,1,0:T(8,128)(2,1)S(1)} %get-tuple-element.6.refs_0_), channel_id=1, source_target_pairs={{3,0},{2,1},{1,2},{0,3},{7,4},{6,5},{5,6},{4,7},{11,8},{10,9},{9,1... | collective-permute-start | bytes 196616 | tf_op jit(solution)/shard_map/ppermute | solution.py:493
  72.7 2.3 %collective-permute-start.9 = (bf16[2,32,512]{2,1,0:T(8,128)(2,1)S(1)}, bf16[2,32,512]{2,1,0:T(8,128)(2,1)S(1)}, u32[]{:S(2)}, u32[]{:S(2)}) collective-permute-start(bf16[2,32,512]{2,1,0:T(8,128)(2,1)S(1)} %get-tuple-element.6.refs_0_), channel_id=1, source_target_pairs={{1,0},{0,1},{3,2},{2,3},{5,4},{4,5},{7,6},{6,7},{9,8},{8,9},{11,10... | collective-permute-start | bytes 196616 | tf_op jit(solution)/shard_map/ppermute | solution.py:493
  75.1 1.9 %collective-permute-done.11.refs_3_ = bf16[2,32,512]{2,1,0:T(8,128)(2,1)S(1)} collective-permute-done((bf16[2,32,512]{2,1,0:T(8,128)(2,1)S(1)}, bf16[2,32,512]{2,1,0:T(8,128)(2,1)S(1)}, u32[]{:S(2)}, u32[]{:S(2)}) %collective-permute-start.11) | collective-permute-done | bytes 65568 | tf_op jit(solution)/shard_map/ppermute | solution.py:493
  76.9 2.0 %collective-permute-done.10.refs_2_ = bf16[2,32,512]{2,1,0:T(8,128)(2,1)S(1)} collective-permute-done((bf16[2,32,512]{2,1,0:T(8,128)(2,1)S(1)}, bf16[2,32,512]{2,1,0:T(8,128)(2,1)S(1)}, u32[]{:S(2)}, u32[]{:S(2)}) %collective-permute-start.10) | collective-permute-done | bytes 65568 | tf_op jit(solution)/shard_map/ppermute | solution.py:493
  78.9 3.1 %apply_score.1 = f32[2,32,32]{2,1,0:T(8,128)S(1)} custom-call(bf16[2,32,512]{2,1,0:T(8,128)(2,1)S(1)} %get-tuple-element.6.refs_0_, bf16[2,32,512]{2,1,0:T(8,128)(2,1)S(1)} %collective-permute-done.9.refs_1_, bf16[2,32,512]{2,1,0:T(8,128)(2,1)S(1)} %collective-permute-done.10.refs_2_, bf16[2,32,512]{2,1,0:T(8,128)(2,1)S(1)} %collective-permute-done.11.refs_3_, ...), custom_call_target="tpu_custom_call" | custom-call | tf_op jit(solution)/shard_map/apply_score/pallas_call | solution.py:259
  82.0 2.5 %collective-permute-start.14 = (f32[2,32,32]{2,1,0:T(8,128)S(1)}, f32[2,32,32]{2,1,0:T(8,128)S(1)}, u32[]{:S(2)}, u32[]{:S(2)}) collective-permute-start(f32[2,32,32]{2,1,0:T(8,128)S(1)} %apply_score.1), channel_id=1, source_target_pairs={{3,0},{2,1},{1,2},{0,3},{7,4},{6,5},{5,6},{4,7},{11,8},{10,9},{9,1... | collective-permute-start | bytes 24584 | tf_op jit(solution)/shard_map/ppermute | solution.py:493
  84.5 2.0 %collective-permute-start.12 = (f32[2,32,32]{2,1,0:T(8,128)S(1)}, f32[2,32,32]{2,1,0:T(8,128)S(1)}, u32[]{:S(2)}, u32[]{:S(2)}) collective-permute-start(f32[2,32,32]{2,1,0:T(8,128)S(1)} %apply_score.1), channel_id=1, source_target_pairs={{1,0},{0,1},{3,2},{2,3},{5,4},{4,5},{7,6},{6,7},{9,8},{8,9},{11,10... | collective-permute-start | bytes 24584 | tf_op jit(solution)/shard_map/ppermute | solution.py:493
  87.7 1.5 %collective-permute-done.13 = f32[2,32,32]{2,1,0:T(8,128)S(1)} collective-permute-done((f32[2,32,32]{2,1,0:T(8,128)S(1)}, f32[2,32,32]{2,1,0:T(8,128)S(1)}, u32[]{:S(2)}, u32[]{:S(2)}) %collective-permute-start.13) | collective-permute-done | bytes 8224 | tf_op jit(solution)/shard_map/ppermute | solution.py:493
  (16 shorter events, 3.1 us)
Async XLA Ops:
  0.6 12.6 %collective-permute-start.1 = (f32[2,32,512]{2,1,0:T(8,128)}, f32[2,32,512]{2,1,0:T(8,128)S(1)}, u32[]{:S(2)}, u32[]{:S(2)}) collective-permute-start(f32[2,32,512]{2,1,0:T(8,128)} %refs_0_.1), channel_id=1, source_target_pairs={{2,0},{3,1},{0,2},{1,3},{6,4},{7,5},{4,6},{5,7},{10,8},{11,9},{8,1... | collective-permute-start | bytes 393224 | tf_op jit(solution)/shard_map/ppermute | solution.py:493
  4.7 8.5 %collective-permute-start = (f32[2,32,512]{2,1,0:T(8,128)}, f32[2,32,512]{2,1,0:T(8,128)S(1)}, u32[]{:S(2)}, u32[]{:S(2)}) collective-permute-start(f32[2,32,512]{2,1,0:T(8,128)} %refs_0_.1), channel_id=1, source_target_pairs={{1,0},{0,1},{3,2},{2,3},{5,4},{4,5},{7,6},{6,7},{9,8},{8,9},{11,10... | collective-permute-start | bytes 393224 | tf_op jit(solution)/shard_map/ppermute | solution.py:493
  6.3 9.0 %collective-permute-start.2 = (f32[2,32,512]{2,1,0:T(8,128)}, f32[2,32,512]{2,1,0:T(8,128)S(1)}, u32[]{:S(2)}, u32[]{:S(2)}) collective-permute-start(f32[2,32,512]{2,1,0:T(8,128)} %refs_0_.1), channel_id=1, source_target_pairs={{3,0},{2,1},{1,2},{0,3},{7,4},{6,5},{5,6},{4,7},{11,8},{10,9},{9,1... | collective-permute-start | bytes 393224 | tf_op jit(solution)/shard_map/ppermute | solution.py:493
  6.3 9.0 %copy-start = (f32[2,32,512]{2,1,0:T(8,128)S(1)}, f32[2,32,512]{2,1,0:T(8,128)}, u32[]{:S(2)}) copy-start(f32[2,32,512]{2,1,0:T(8,128)} %refs_0_.1) | copy-start | bytes 393220
  18.0 6.9 %collective-permute-start.5 = (f32[2,32,512]{2,1,0:T(8,128)S(1)}, f32[2,32,512]{2,1,0:T(8,128)S(1)}, u32[]{:S(2)}, u32[]{:S(2)}) collective-permute-start(f32[2,32,512]{2,1,0:T(8,128)S(1)} %apply_plain.1.refs_0_), channel_id=1, source_target_pairs={{3,0},{2,1},{1,2},{0,3},{7,4},{6,5},{5,6},{4,7},{11,8},{10,9},{9,1... | collective-permute-start | bytes 393224 | tf_op jit(solution)/shard_map/ppermute | solution.py:493
  20.5 12.5 %collective-permute-start.4 = (f32[2,32,512]{2,1,0:T(8,128)S(1)}, f32[2,32,512]{2,1,0:T(8,128)S(1)}, u32[]{:S(2)}, u32[]{:S(2)}) collective-permute-start(f32[2,32,512]{2,1,0:T(8,128)S(1)} %apply_plain.1.refs_0_), channel_id=1, source_target_pairs={{2,0},{3,1},{0,2},{1,3},{6,4},{7,5},{4,6},{5,7},{10,8},{11,9},{8,1... | collective-permute-start | bytes 393224 | tf_op jit(solution)/shard_map/ppermute | solution.py:493
  22.3 10.6 %collective-permute-start.3 = (f32[2,32,512]{2,1,0:T(8,128)S(1)}, f32[2,32,512]{2,1,0:T(8,128)S(1)}, u32[]{:S(2)}, u32[]{:S(2)}) collective-permute-start(f32[2,32,512]{2,1,0:T(8,128)S(1)} %apply_plain.1.refs_0_), channel_id=1, source_target_pairs={{1,0},{0,1},{3,2},{2,3},{5,4},{4,5},{7,6},{6,7},{9,8},{8,9},{11,10... | collective-permute-start | bytes 393224 | tf_op jit(solution)/shard_map/ppermute | solution.py:493
  46.2 8.7 %collective-permute-start.8 = (f32[288,128]{1,0:T(8,128)S(1)}, f32[288,128]{1,0:T(8,128)S(1)}, u32[]{:S(2)}, u32[]{:S(2)}) collective-permute-start(f32[288,128]{1,0:T(8,128)S(1)} %cross_gram.1.refs_0_), channel_id=1, source_target_pairs={{3,0},{2,1},{1,2},{0,3},{7,4},{6,5},{5,6},{4,7},{11,8},{10,9},{9,1... | collective-permute-start | bytes 442376 | tf_op jit(solution)/shard_map/ppermute | solution.py:493
  48.9 12.2 %collective-permute-start.7 = (f32[288,128]{1,0:T(8,128)S(1)}, f32[288,128]{1,0:T(8,128)S(1)}, u32[]{:S(2)}, u32[]{:S(2)}) collective-permute-start(f32[288,128]{1,0:T(8,128)S(1)} %cross_gram.1.refs_0_), channel_id=1, source_target_pairs={{2,0},{3,1},{0,2},{1,3},{6,4},{7,5},{4,6},{5,7},{10,8},{11,9},{8,1... | collective-permute-start | bytes 442376 | tf_op jit(solution)/shard_map/ppermute | solution.py:493
  48.9 12.2 %collective-permute-start.6 = (f32[288,128]{1,0:T(8,128)S(1)}, f32[288,128]{1,0:T(8,128)S(1)}, u32[]{:S(2)}, u32[]{:S(2)}) collective-permute-start(f32[288,128]{1,0:T(8,128)S(1)} %cross_gram.1.refs_0_), channel_id=1, source_target_pairs={{1,0},{0,1},{3,2},{2,3},{5,4},{4,5},{7,6},{6,7},{9,8},{8,9},{11,10... | collective-permute-start | bytes 442376 | tf_op jit(solution)/shard_map/ppermute | solution.py:493
  70.7 6.3 %collective-permute-start.11 = (bf16[2,32,512]{2,1,0:T(8,128)(2,1)S(1)}, bf16[2,32,512]{2,1,0:T(8,128)(2,1)S(1)}, u32[]{:S(2)}, u32[]{:S(2)}) collective-permute-start(bf16[2,32,512]{2,1,0:T(8,128)(2,1)S(1)} %get-tuple-element.6.refs_0_), channel_id=1, source_target_pairs={{3,0},{2,1},{1,2},{0,3},{7,4},{6,5},{5,6},{4,7},{11,8},{10,9},{9,1... | collective-permute-start | bytes 196616 | tf_op jit(solution)/shard_map/ppermute | solution.py:493
  72.7 6.2 %collective-permute-start.10 = (bf16[2,32,512]{2,1,0:T(8,128)(2,1)S(1)}, bf16[2,32,512]{2,1,0:T(8,128)(2,1)S(1)}, u32[]{:S(2)}, u32[]{:S(2)}) collective-permute-start(bf16[2,32,512]{2,1,0:T(8,128)(2,1)S(1)} %get-tuple-element.6.refs_0_), channel_id=1, source_target_pairs={{2,0},{3,1},{0,2},{1,3},{6,4},{7,5},{4,6},{5,7},{10,8},{11,9},{8,1... | collective-permute-start | bytes 196616 | tf_op jit(solution)/shard_map/ppermute | solution.py:493
  72.7 6.2 %collective-permute-start.9 = (bf16[2,32,512]{2,1,0:T(8,128)(2,1)S(1)}, bf16[2,32,512]{2,1,0:T(8,128)(2,1)S(1)}, u32[]{:S(2)}, u32[]{:S(2)}) collective-permute-start(bf16[2,32,512]{2,1,0:T(8,128)(2,1)S(1)} %get-tuple-element.6.refs_0_), channel_id=1, source_target_pairs={{1,0},{0,1},{3,2},{2,3},{5,4},{4,5},{7,6},{6,7},{9,8},{8,9},{11,10... | collective-permute-start | bytes 196616 | tf_op jit(solution)/shard_map/ppermute | solution.py:493
  82.0 5.8 %collective-permute-start.14 = (f32[2,32,32]{2,1,0:T(8,128)S(1)}, f32[2,32,32]{2,1,0:T(8,128)S(1)}, u32[]{:S(2)}, u32[]{:S(2)}) collective-permute-start(f32[2,32,32]{2,1,0:T(8,128)S(1)} %apply_score.1), channel_id=1, source_target_pairs={{3,0},{2,1},{1,2},{0,3},{7,4},{6,5},{5,6},{4,7},{11,8},{10,9},{9,1... | collective-permute-start | bytes 24584 | tf_op jit(solution)/shard_map/ppermute | solution.py:493
  84.5 4.8 %collective-permute-start.13 = (f32[2,32,32]{2,1,0:T(8,128)S(1)}, f32[2,32,32]{2,1,0:T(8,128)S(1)}, u32[]{:S(2)}, u32[]{:S(2)}) collective-permute-start(f32[2,32,32]{2,1,0:T(8,128)S(1)} %apply_score.1), channel_id=1, source_target_pairs={{2,0},{3,1},{0,2},{1,3},{6,4},{7,5},{4,6},{5,7},{10,8},{11,9},{8,1... | collective-permute-start | bytes 24584 | tf_op jit(solution)/shard_map/ppermute | solution.py:493
  84.5 4.8 %collective-permute-start.12 = (f32[2,32,32]{2,1,0:T(8,128)S(1)}, f32[2,32,32]{2,1,0:T(8,128)S(1)}, u32[]{:S(2)}, u32[]{:S(2)}) collective-permute-start(f32[2,32,32]{2,1,0:T(8,128)S(1)} %apply_score.1), channel_id=1, source_target_pairs={{1,0},{0,1},{3,2},{2,3},{5,4},{4,5},{7,6},{6,7},{9,8},{8,9},{11,10... | collective-permute-start | bytes 24584 | tf_op jit(solution)/shard_map/ppermute | solution.py:493

commit v8 on v7

--- a/solution.py
+++ b/solution.py
@@ -29,15 +29,15 @@
     return [pl.BlockSpec(memory_space=pltpu.VMEM)] * count
 
 
-def place(z, chunks, u, dense_ref, layer):
+def place(z, chunks, u, dense_ref):
     for c in range(chunks * CHUNK_COLS):
         piece = z[c * 8 : c * 8 + 8]
         piece = jnp.concatenate([piece[:, :128], piece[:, 128:]], axis=0)
         hi = piece.astype(BF16)
         lo = (piece - hi.astype(F32)).astype(BF16)
         lanes = slice((c % CHUNK_COLS) * 128, (c % CHUNK_COLS) * 128 + 128)
-        dense_ref[layer, c // CHUNK_COLS, pl.ds(pl.multiple_of(u * 16, 16), 16), lanes] = hi
-        dense_ref[layer, c // CHUNK_COLS, pl.ds(pl.multiple_of(u * 16 + TALL, 16), 16), lanes] = lo
+        dense_ref[c // CHUNK_COLS, pl.ds(pl.multiple_of(u * 16, 16), 16), lanes] = hi
+        dense_ref[c // CHUNK_COLS, pl.ds(pl.multiple_of(u * 16 + TALL, 16), 16), lanes] = lo
 
 
 def one_hot(rows_ref, cols_ref, counts_ref, layer, flip, base, positions):
@@ -57,16 +57,15 @@
     def step(u, carry):
         cols = pl.ds(pl.multiple_of(u * 256, 256), 256)
         z = jnp.dot(onehot, blocks_ref[0, :, cols], preferred_element_type=F32)
-        place(z, chunks, u, dense_ref, 0)
+        place(z, chunks, u, dense_ref.at[0])
         return carry
 
     lax.fori_loop(0, BLK * BLK // 256, step, 0)
 
 
-def build_whole_kernel(
-    rows_hbm, cols_hbm, counts_hbm, blocks_ref, dense_ref, held, rows_ref, cols_ref, counts_ref, arrived, index_arrived
-):
-    layers, chunks = dense_ref.shape[:2]
+def build_whole_kernel(rows_hbm, cols_hbm, counts_hbm, blocks_ref, *refs):
+    *dense_refs, held, rows_ref, cols_ref, counts_ref, arrived, index_arrived = refs
+    layers, chunks = len(dense_refs), dense_refs[0].shape[0]
     index_copies = [
         pltpu.make_async_copy(source, target, index_arrived.at[i])
         for i, (source, target) in enumerate(
@@ -99,7 +98,7 @@
             for v in range(inner):
                 cols = pl.ds(pl.multiple_of(piece * width + v * 256, 256), 256)
                 z = jnp.dot(onehot, held[layer, :, cols], preferred_element_type=F32)
-                place(z, chunks, piece * inner + v, dense_ref, layer)
+                place(z, chunks, piece * inner + v, dense_refs[layer])
             return carry
 
         lax.fori_loop(0, pieces, step, 0)
@@ -114,8 +113,8 @@
         return pl.pallas_call(
             build_whole_kernel,
             in_specs=[pl.BlockSpec(memory_space=pltpu.HBM)] * 4,
-            out_specs=pl.BlockSpec(memory_space=pltpu.VMEM),
-            out_shape=dense,
+            out_specs=vmem_specs(layers),
+            out_shape=[jax.ShapeDtypeStruct(dense.shape[1:], BF16)] * layers,
             scratch_shapes=[
                 pltpu.VMEM(blocks.shape, BF16),
                 pltpu.VMEM(block_rows.shape, jnp.int32),
@@ -222,49 +221,72 @@
     return total + (middle[:, k : 2 * k] + (top[:, 2 * k : 3 * k] + bottom[:, :k]))
 
 
-def apply_whole_kernel(mode, piece_count, *refs):
-    pieces, refs = refs[:piece_count], refs[piece_count:]
-    if mode == "score":
-        left_ref, refs = refs[0], refs[1:]
-    dense_ref, out_ref, halves, tall = refs
-    layers, k = pieces[0].shape[:2]
-    if mode == "solved":
-        images = [jnp.concatenate([piece[layer] for piece in pieces], axis=1) for layer in range(layers)]
-        grams = [product(image, image) for image in images]
-        inverses = [inverse_factor(gram) for gram in grams]
-        bases = [
-            jnp.dot(inverse, image, precision=HIGHEST, preferred_element_type=F32)
-            for inverse, image in zip(inverses, images)
-        ]
-        parts = [[basis[:, d * ROWS_DEV : d * ROWS_DEV + ROWS_DEV] for d in range(piece_count)] for basis in bases]
-    else:
-        parts = [[piece[layer] for piece in pieces] for layer in range(layers)]
-    totals = [
-        sum(image_part(part, dense_ref[layer, chunk]) for chunk, part in enumerate(parts[layer]))
-        for layer in range(layers)
+def image_of(parts, dense_ref):
+    return sum(image_part(part, dense_ref[chunk]) for chunk, part in enumerate(parts))
+
+
+def first_kernel(layer, piece_count, *refs):
+    pieces, (dense_ref, out_ref, halves, tall) = refs[:piece_count], refs[piece_count:]
+    total = image_of([piece[layer] for piece in pieces], dense_ref)
+    out_ref[...] = to_wide(total, out_ref.shape[0], halves, tall)
+
+
+def second_kernel(piece_count, *refs):
+    pieces, (dense_ref, out_ref, halves, tall) = refs[:piece_count], refs[piece_count:]
+    image = jnp.concatenate([piece[...] for piece in pieces], axis=1)
+    inverse = inverse_factor(product(image, image))
+    basis = jnp.dot(inverse, image, precision=HIGHEST, preferred_element_type=F32)
+    parts = [basis[:, d * ROWS_DEV : d * ROWS_DEV + ROWS_DEV] for d in range(piece_count)]
+    out_ref[...] = to_wide(image_of(parts, dense_ref), out_ref.shape[0], halves, tall)
+
+
+def score_kernel(layers, piece_count, *refs):
+    pieces, left_ref, refs = refs[:piece_count], refs[piece_count], refs[piece_count + 1 :]
+    dense_refs, (out_ref, halves, tall) = refs[:layers], refs[layers:]
+    totals = [image_of([piece[layer] for piece in pieces], dense_refs[layer]) for layer in range(layers)]
+    wide = [
+        to_wide(totals[layer], left_ref.shape[1], halves.at[layer], tall.at[layer]) for layer in range(layers)
     ]
-    wide = [to_wide(totals[layer], k, halves.at[layer], tall.at[layer]) for layer in range(layers)]
     for layer in range(layers):
-        out_ref[layer] = product(left_ref[layer], wide[layer]) if mode == "score" else wide[layer]
-
-
-def apply_dense(mode, pieces, dense, left=None):
+        out_ref[layer] = product(left_ref[layer], wide[layer])
+
+
+def apply_whole(kernel, name, operands, out_shape, *lead):
+    return pl.pallas_call(
+        kernel,
+        in_specs=vmem_specs(len(operands)),
+        out_specs=pl.BlockSpec(memory_space=pltpu.VMEM),
+        out_shape=jax.ShapeDtypeStruct(out_shape, F32),
+        scratch_shapes=[pltpu.VMEM((*lead, TALL, 128), F32), pltpu.VMEM((*lead, ROWS_DEV, 128), F32)],
+        compiler_params=params(14),
+        cost_estimate=pl.CostEstimate(flops=0, bytes_accessed=4 * MIB, transcendentals=0),
+        name=name,
+    )(*operands)
+
+
+def apply_first(layer, pieces, dense):
+    kernel = functools.partial(first_kernel, layer, len(pieces))
+    return apply_whole(kernel, "apply_first", [*pieces, dense], pieces[0].shape[1:])
+
+
+def apply_second(pieces, dense):
+    kernel = functools.partial(second_kernel, len(pieces))
+    return apply_whole(kernel, "apply_second", [*pieces, dense], pieces[0].shape)
+
+
+def apply_score(pieces, left, dense):
+    kernel = functools.partial(score_kernel, len(dense), len(pieces))
+    layers, k = left.shape[:2]
+    return apply_whole(kernel, "apply_score", [*pieces, left, *dense], (layers, k, k), layers)
+
+
+def apply_dense(mode, basis, dense, left=None):
     layers, chunks = dense.shape[:2]
-    k = pieces[0].shape[-2]
+    k = basis.shape[-2]
     image = jax.ShapeDtypeStruct((layers, k, ROWS_DEV), F32)
     small = jax.ShapeDtypeStruct((layers, k, k), F32)
-    out_shape = {"gram": [image, small], "plain": [image], "solved": [image], "score": [small]}[mode]
-    operands = list(pieces) + ([left] if mode == "score" else []) + [dense]
-    if len(pieces) == chunks:
-        return pl.pallas_call(
-            functools.partial(apply_whole_kernel, mode, chunks),
-            in_specs=vmem_specs(len(operands)),
-            out_specs=vmem_specs(len(out_shape)),
-            out_shape=out_shape,
-            scratch_shapes=[pltpu.VMEM((layers, TALL, 128), F32), pltpu.VMEM((layers, ROWS_DEV, 128), F32)],
-            compiler_params=params(14),
-            name="apply_" + mode,
-        )(*operands)
+    out_shape = {"gram": [image, small], "plain": [image], "score": [small]}[mode]
+    operands = [basis] + ([left] if mode == "score" else []) + [dense]
     dense_spec = pl.BlockSpec((1, 1, 2 * TALL, CHUNK_LANES), lambda l, s: (l, s, 0, 0))
     image_spec = pl.BlockSpec((1, k, ROWS_DEV), lambda l, s: (l, 0, 0))
     small_spec = pl.BlockSpec((1, k, k), lambda l, s: (l, 0, 0))
@@ -396,30 +418,45 @@
     )(gram, image)
 
 
-def cross_kernel(k, all_ref, out_ref):
-    every = all_ref[...].reshape(-1, all_ref.shape[2])
-    gram = lax.dot_general(every, every, TRANS_B, precision=HIGHEST, preferred_element_type=F32)
+def cross_kernel(k, groups, *refs):
+    pieces, (out_ref, stacked, packed) = refs[:-3], refs[-3:]
+    g = lax.axis_index("layer")
+    layers = len(pieces) // groups
+    for i, piece in enumerate(pieces):
+        at = ((g ^ (i % groups)) * layers + i // groups) * k
+        stacked[pl.ds(pl.multiple_of(at, k), k)] = piece[...]
+    gram = lax.dot_general(
+        stacked[...], stacked[...], TRANS_B, precision=HIGHEST, preferred_element_type=F32
+    )
     half = gram.shape[0] // 2
     first, last = gram[:half, :half], gram[half:, half:]
     row = lax.broadcasted_iota(jnp.int32, (half, half), 0) // k
     col = lax.broadcasted_iota(jnp.int32, (half, half), 1) // k
-    out_ref[:half] = gram[:half, half:]
-    out_ref[half : 2 * half] = jnp.where(col >= row, first, last)
+    packed[:half] = gram[:half, half:]
+    packed[half : 2 * half] = jnp.where(col >= row, first, last)
     diagonal = jnp.where(col == row, last, 0.0)
-    out_ref[2 * half :] = sum(diagonal[r * k : r * k + k] for r in range(half // k))
-
-
-def cross(every):
-    _, k, _ = every.shape
-    half = every.shape[0] * k // 2
+    packed[2 * half :] = sum(diagonal[r * k : r * k + k] for r in range(half // k))
+    rows = out_ref.shape[0]
+    out_ref[...] = packed[pl.ds(pl.multiple_of((g & 1) * rows, 16), rows)]
+
+
+def cross(chains):
+    k, width = chains[0][0].shape
+    groups = len(chains[0])
+    size = len(chains) * groups * k
+    pieces = [piece for chain in chains for piece in chain]
     return pl.pallas_call(
-        functools.partial(cross_kernel, k),
-        in_specs=vmem_specs(1),
-        out_specs=pl.BlockSpec(memory_space=pltpu.VMEM),
-        out_shape=jax.ShapeDtypeStruct((2 * half + k, half), F32),
+        functools.partial(cross_kernel, k, groups),
+        in_specs=vmem_specs(len(pieces)),
+        out_specs=vmem_specs(2),
+        out_shape=[
+            jax.ShapeDtypeStruct(((size + k) // 2, size // 2), F32),
+            jax.ShapeDtypeStruct((size, width), F32),
+        ],
+        scratch_shapes=[pltpu.VMEM((size + k, size // 2), F32)],
         compiler_params=params(6),
         name="cross_gram",
-    )(every)
+    )(*pieces)
 
 
 def unpack(packed, k, work):
@@ -435,9 +472,13 @@
     work[half:, half:] = under.T + jnp.where(col == row, diagonal, 0.0)
 
 
-def joint_kernel(piece_count, k, *refs):
-    packed_refs, (images_ref, out_ref, again_ref, rounded_ref, work) = refs[:piece_count], refs[piece_count:]
-    unpack(add_pieces([ref[...] for ref in packed_refs]), k, work)
+def joint_kernel(k, *refs):
+    own_ref, other_ref, images_ref, out_ref, again_ref, rounded_ref, work, packed = refs
+    rows = own_ref.shape[0]
+    odd = lax.axis_index("layer") & 1
+    packed[pl.ds(pl.multiple_of(odd * rows, 16), rows)] = own_ref[...]
+    packed[pl.ds(pl.multiple_of((1 - odd) * rows, 16), rows)] = other_ref[...]
+    unpack(packed[...], k, work)
     size = work.shape[0]
     steps = size // k
     lane = lax.broadcasted_iota(jnp.int32, (k, size), 1)
@@ -460,31 +501,29 @@
                 work[r * k : r * k + k] = jnp.where(here, 0.0, rows) - update(r * k, k)
     rows = out_ref.shape[0] * k
     own = work[pl.ds(pl.multiple_of(lax.axis_index("layer") * rows, rows), rows)] * across
-    images = images_ref[...].reshape(size, -1)
-    joint = jnp.dot(own, images, precision=HIGHEST, preferred_element_type=F32)
+    joint = jnp.dot(own, images_ref[...], precision=HIGHEST, preferred_element_type=F32)
     joint = joint.reshape(out_ref.shape)
     out_ref[...] = joint
     again_ref[...] = joint
     rounded_ref[...] = joint.astype(BF16)
 
 
-def joint_solve(packed, images, layers):
-    _, k, width = images.shape
-    size = images.shape[0] * k
-    shape = (layers, k, width)
+def joint_solve(own, other, images, shape):
+    size = images.shape[0]
+    k = shape[1]
     return pl.pallas_call(
-        functools.partial(joint_kernel, len(packed), k),
-        in_specs=vmem_specs(len(packed) + 1),
+        functools.partial(joint_kernel, k),
+        in_specs=vmem_specs(3),
         out_specs=vmem_specs(3),
         out_shape=[
             jax.ShapeDtypeStruct(shape, F32),
             jax.ShapeDtypeStruct(shape, F32),
             jax.ShapeDtypeStruct(shape, BF16),
         ],
-        scratch_shapes=[pltpu.VMEM((size, size), F32)],
+        scratch_shapes=[pltpu.VMEM((size, size), F32), pltpu.VMEM((size + k, size // 2), F32)],
         compiler_params=params(8),
         name="joint_solve",
-    )(*packed, images)
+    )(own, other, images)
 
 
 def around(x, axis, count):
@@ -500,27 +539,34 @@
     return (pieces[0] + pieces[1]) + (pieces[2] + pieces[3])
 
 
-def per_device(shards, blocks, block_rows, block_cols, counts, start):
+def per_device(shards, groups, blocks, block_rows, block_cols, counts, start):
     few = shards == 4
+    layers = start.shape[0]
 
     def gather(x):
-        return around(x, "node", shards) if few else [lax.all_gather(x, "node")]
-
-    def partials(x):
-        return around(x, "node", shards) if few else [lax.psum(x, "node")]
-
-    first = gather(start if few else start.astype(BF16))
+        return around(x, "node", shards) if few else lax.all_gather(x, "node")
+
+    def total(x):
+        return add_pieces(around(x, "node", shards)) if few else lax.psum(x, "node")
+
+    first = gather(start.astype(BF16))
     dense = build_dense(block_rows, block_cols, counts, blocks, shards * BROWS // CHUNK_COLS)
     if few:
-        (image,) = apply_dense("plain", first, dense)
-        (image,) = apply_dense("solved", gather(image), dense)
+        images = [apply_first(layer, first, dense[layer]) for layer in range(layers)]
+        images = [apply_second(gather(images[layer]), dense[layer]) for layer in range(layers)]
     else:
         image, gram = apply_dense("gram", first, dense)
-        (image,) = apply_dense("plain", gather(solve(lax.psum(gram, "node"), image)), dense)
-    images = lax.all_gather(image, "layer", axis=0, tiled=True)
-    joint_basis, again, rounded = joint_solve(partials(cross(images)), images, start.shape[0])
-    (partial,) = apply_dense("score", gather(rounded), dense, again)
-    return joint_basis, add_pieces(partials(partial))
+        (image,) = apply_dense("plain", gather(solve(total(gram), image)), dense)
+        images = [image[layer] for layer in range(layers)]
+    own, stacked = cross([around(image, "layer", groups) for image in images])
+    own = total(own)
+    other = lax.ppermute(own, "layer", [(m ^ 1, m) for m in range(groups)])
+    joint_basis, again, rounded = joint_solve(own, other, stacked, start.shape)
+    if few:
+        partial = apply_score(gather(rounded), again, dense)
+    else:
+        (partial,) = apply_dense("score", gather(rounded), dense, again)
+    return joint_basis, total(partial)
 
 
 def solution(mesh):
@@ -533,7 +579,7 @@
     )
     out_specs = (P(("parts", "layer"), None, "node"), P(("parts", "layer"), None, None))
     return jax.shard_map(
-        functools.partial(per_device, mesh.shape["node"]),
+        functools.partial(per_device, mesh.shape["node"], mesh.shape["layer"]),
         mesh=mesh,
         in_specs=in_specs,
         out_specs=out_specs,

time: 90.1 us -> 82 us (0.910)
  waiting for transfers between devices: 29.4 us -> 17.8 us
  starting transfers between devices: 23.8 us -> 32 us
  blocking collectives: 7.37 us -> 0 us
  Pallas kernels: 28 us -> 29.8 us
  other arithmetic: 0.63 us -> 1.56 us
    ppermute x15 -> x24, waiting for transfers between devices: 29.4 us -> 16.5 us  [around(): pieces.append(lax.ppermute(x, axis, [(m ^ d, m) for m in range(count)]))]
    ppermute x15 -> x24, starting transfers between devices: 23.8 us -> 31.9 us  [around(): pieces.append(lax.ppermute(x, axis, [(m ^ d, m) for m in range(count)]))]
    all_gather x1 -> x0, blocking collectives: 7.37 us -> none  [per_device(): images = lax.all_gather(image, 'layer', axis=0, tiled=True)]
    pallas_call x5 -> x7, Pallas kernels: 21.2 us -> 23 us  [the longest x5 12.6 us: apply_whole(): pl.pallas_call(kernel, in_specs=vmem_specs(len(operands)), out_specs=pl.B...]
    ppermute x0 -> x1, waiting for transfers between devices: none -> 1.25 us  [per_device(): other = lax.ppermute(own, 'layer', [(m ^ 1, m) for m in range(groups)])]
    convert_element_type x0 -> x1, other arithmetic: none -> 0.92 us  [per_device(): first = gather(start.astype(BF16))]
  transfers between devices with their start and end apart: 15 -> 25, of which waited for: 9 -> 9; matrix products, arithmetic and copies ran while one was open for 0% -> 0% of each run, Pallas kernels for 8% -> 18%
where the time goes in v8:
time: 82 us; the launch traced here: 81.8 us
  starting transfers between devices  32 us (39%)
  Pallas kernels  29.8 us (36%)
  waiting for transfers between devices  17.8 us (22%)
  other arithmetic  1.56 us (2%)
    ppermute x24, starting transfers between devices, around(): pieces.append(lax.ppermute(x, axis, [(m ^ d, m) for m in range(count)]))  31.9 us
    ppermute x24, waiting for transfers between devices, around(): pieces.append(lax.ppermute(x, axis, [(m ^ d, m) for m in range(count)]))  16.5 us
    pallas_call x5, Pallas kernels, apply_whole(): pl.pallas_call(kernel, in_specs=vmem_specs(len(operands)), out_specs=pl.B...  12.6 us
    pallas_call x1, Pallas kernels, joint_solve(): pl.pallas_call(functools.partial(joint_kernel, k), in_specs=vmem_specs(3)...  9.72 us
    pallas_call x1, Pallas kernels, build_dense(): pl.pallas_call(build_whole_kernel, in_specs=[pl.BlockSpec(memory_space=pl...  6.83 us
  transfers between devices with their start and end apart: 25, of which 9 were waited for; matrix products, arithmetic and copies ran while one was open for 0% of the time, Pallas kernels for 18%

profile of v8, /device:TPU:0, one launch (start us, length us, event | category | flops | bytes accessed | tf_op | source)
XLA Modules:
  0.0 81.8 jit_solution(6414637342070685215)
XLA Ops:
  1.5 5.1 %collective-permute-start.2 = (bf16[2,32,512]{2,1,0:T(8,128)(2,1)S(1)}, bf16[2,32,512]{2,1,0:T(8,128)(2,1)S(1)}, u32[]{:S(2)}, u32[]{:S(2)}) collective-permute-start(bf16[2,32,512]{2,1,0:T(8,128)(2,1)S(1)} %convert_element_type.3.refs_0_), channel_id=1, source_target_pairs={{3,0},{2,1},{1,2},{0,3},{7,4},{6,5},{5,6},{4,7},{11,8},{10,9},{9,1... | collective-permute-start | bytes 196616 | tf_op jit(solution)/shard_map/ppermute | solution.py:532
  7.3 6.8 %build_dense.1 = (bf16[4,512,1024]{2,1,0:T(8,128)(2,1)S(1)}, bf16[4,512,1024]{2,1,0:T(8,128)(2,1)S(1)}) custom-call(s32[2,512]{1,0:T(2,128)} %rows_hbm.1, s32[2,512]{1,0:T(2,128)} %cols_hbm.1, s32[1,2]{1,0:T(1,128)} %bitcast.1, bf16[2,512,4096]{2,1,0:T(8,128)(2,1)} %blocks_ref.1), custom_call_target="tpu_custom_call" | custom-call | tf_op jit(solution)/shard_map/build_dense/pallas_call | solution.py:113
  14.2 1.5 %apply_first.3.refs_0_ = f32[32,512]{1,0:T(8,128)S(1)} custom-call(bf16[2,32,512]{2,1,0:T(8,128)(2,1)S(1)} %convert_element_type.3.refs_0_, bf16[2,32,512]{2,1,0:T(8,128)(2,1)S(1)} %collective-permute-done.refs_1_, bf16[2,32,512]{2,1,0:T(8,128)(2,1)S(1)} %collective-permute-done.1.refs_2_, bf16[2,32,512]{2,1,0:T(8,128)(2,1)S(1)} %collective-permute-done.2.refs_3_, ...), custom_call_target="tpu_custom_call" | custom-call | bytes 4194304 | tf_op jit(solution)/shard_map/apply_first/pallas_call | solution.py:255
  15.7 3.8 %collective-permute-start.11 = (f32[32,512]{1,0:T(8,128)S(1)}, f32[32,512]{1,0:T(8,128)S(1)}, u32[]{:S(2)}, u32[]{:S(2)}) collective-permute-start(f32[32,512]{1,0:T(8,128)S(1)} %apply_first.3.refs_0_), channel_id=1, source_target_pairs={{3,0},{2,1},{1,2},{0,3},{7,4},{6,5},{5,6},{4,7},{11,8},{10,9},{9,1... | collective-permute-start | bytes 196616 | tf_op jit(solution)/shard_map/ppermute | solution.py:532
  20.2 1.5 %apply_first.2.refs_0_ = f32[32,512]{1,0:T(8,128)S(1)} custom-call(bf16[2,32,512]{2,1,0:T(8,128)(2,1)S(1)} %convert_element_type.3.refs_0_, bf16[2,32,512]{2,1,0:T(8,128)(2,1)S(1)} %collective-permute-done.refs_1_, bf16[2,32,512]{2,1,0:T(8,128)(2,1)S(1)} %collective-permute-done.1.refs_2_, bf16[2,32,512]{2,1,0:T(8,128)(2,1)S(1)} %collective-permute-done.2.refs_3_, ...), custom_call_target="tpu_custom_call" | custom-call | bytes 4194304 | tf_op jit(solution)/shard_map/apply_first/pallas_call | solution.py:255
  21.7 3.8 %collective-permute-start.5 = (f32[32,512]{1,0:T(8,128)S(1)}, f32[32,512]{1,0:T(8,128)S(1)}, u32[]{:S(2)}, u32[]{:S(2)}) collective-permute-start(f32[32,512]{1,0:T(8,128)S(1)} %apply_first.2.refs_0_), channel_id=1, source_target_pairs={{3,0},{2,1},{1,2},{0,3},{7,4},{6,5},{5,6},{4,7},{11,8},{10,9},{9,1... | collective-permute-start | bytes 196616 | tf_op jit(solution)/shard_map/ppermute | solution.py:532
  26.1 3.2 %apply_second.3.refs_4_ = f32[32,512]{1,0:T(8,128)S(1)} custom-call(f32[32,512]{1,0:T(8,128)S(1)} %apply_first.3.refs_0_, f32[32,512]{1,0:T(8,128)S(1)} %collective-permute-done.9.refs_1_, f32[32,512]{1,0:T(8,128)S(1)} %collective-permute-done.10.refs_2_, f32[32,512]{1,0:T(8,128)S(1)} %collective-permute-done.11.refs_3_, ...), custom_call_target="tpu_custom_call" | custom-call | bytes 4194304 | tf_op jit(solution)/shard_map/apply_second/pallas_call | solution.py:255
  29.4 1.7 %collective-permute-start.13 = (f32[32,512]{1,0:T(8,128)S(1)}, f32[32,512]{1,0:T(8,128)S(1)}, u32[]{:S(2)}, u32[]{:S(2)}) collective-permute-start(f32[32,512]{1,0:T(8,128)S(1)} %apply_second.3.refs_4_), channel_id=1, source_target_pairs={{8,0},{12,4},{0,8},{4,12},{9,1},{13,5},{1,9},{5,13},{10,2},{14,6},... | collective-permute-start | bytes 196616 | tf_op jit(solution)/shard_map/ppermute | solution.py:532
  31.3 3.2 %apply_second.2.refs_0_ = f32[32,512]{1,0:T(8,128)S(1)} custom-call(f32[32,512]{1,0:T(8,128)S(1)} %apply_first.2.refs_0_, f32[32,512]{1,0:T(8,128)S(1)} %collective-permute-done.3.refs_1_, f32[32,512]{1,0:T(8,128)S(1)} %collective-permute-done.4.refs_2_, f32[32,512]{1,0:T(8,128)S(1)} %collective-permute-done.5.refs_3_, ...), custom_call_target="tpu_custom_call" | custom-call | bytes 4194304 | tf_op jit(solution)/shard_map/apply_second/pallas_call | solution.py:255
  34.5 1.3 %collective-permute-start.8 = (f32[32,512]{1,0:T(8,128)S(1)}, f32[32,512]{1,0:T(8,128)S(1)}, u32[]{:S(2)}, u32[]{:S(2)}) collective-permute-start(f32[32,512]{1,0:T(8,128)S(1)} %apply_second.2.refs_0_), channel_id=1, source_target_pairs={{12,0},{8,4},{4,8},{0,12},{13,1},{9,5},{5,9},{1,13},{14,2},{10,6},... | collective-permute-start | bytes 196616 | tf_op jit(solution)/shard_map/ppermute | solution.py:532
  36.6 1.9 %collective-permute-done.8.refs_3_ = f32[32,512]{1,0:T(8,128)S(1)} collective-permute-done((f32[32,512]{1,0:T(8,128)S(1)}, f32[32,512]{1,0:T(8,128)S(1)}, u32[]{:S(2)}, u32[]{:S(2)}) %collective-permute-start.8) | collective-permute-done | bytes 65568 | tf_op jit(solution)/shard_map/ppermute | solution.py:532
  38.5 1.9 %collective-permute-done.7.refs_2_ = f32[32,512]{1,0:T(8,128)S(1)} collective-permute-done((f32[32,512]{1,0:T(8,128)S(1)}, f32[32,512]{1,0:T(8,128)S(1)}, u32[]{:S(2)}, u32[]{:S(2)}) %collective-permute-start.7) | collective-permute-done | bytes 65568 | tf_op jit(solution)/shard_map/ppermute | solution.py:532
  41.1 3.8 %collective-permute-start.17 = (f32[144,128]{1,0:T(8,128)S(1)}, f32[144,128]{1,0:T(8,128)S(1)}, u32[]{:S(2)}, u32[]{:S(2)}) collective-permute-start(f32[144,128]{1,0:T(8,128)S(1)} %get-tuple-element.11), channel_id=1, source_target_pairs={{3,0},{2,1},{1,2},{0,3},{7,4},{6,5},{5,6},{4,7},{11,8},{10,9},{9,1... | collective-permute-start | bytes 221192 | tf_op jit(solution)/shard_map/ppermute | solution.py:532
  45.5 2.7 %collective-permute-done.17 = f32[144,128]{1,0:T(8,128)S(1)} collective-permute-done((f32[144,128]{1,0:T(8,128)S(1)}, f32[144,128]{1,0:T(8,128)S(1)}, u32[]{:S(2)}, u32[]{:S(2)}) %collective-permute-start.17) | collective-permute-done | bytes 73760 | tf_op jit(solution)/shard_map/ppermute | solution.py:532
  48.2 2.8 %collective-permute-done.16 = f32[144,128]{1,0:T(8,128)S(1)} collective-permute-done((f32[144,128]{1,0:T(8,128)S(1)}, f32[144,128]{1,0:T(8,128)S(1)}, u32[]{:S(2)}, u32[]{:S(2)}) %collective-permute-start.16) | collective-permute-done | bytes 73760 | tf_op jit(solution)/shard_map/ppermute | solution.py:532
  52.4 9.7 %joint_solve.1 = (f32[2,32,512]{2,1,0:T(8,128)}, f32[2,32,512]{2,1,0:T(8,128)S(1)}, bf16[2,32,512]{2,1,0:T(8,128)(2,1)S(1)}) custom-call(f32[144,128]{1,0:T(8,128)S(1)} %add_add_fusion.refs_0_, f32[144,128]{1,0:T(8,128)S(1)} %collective-permute-done.18.refs_1_, f32[256,512]{1,0:T(8,128)S(1)} %get-tuple-element.12.refs_2_), custom_call_target="tpu_custom_call" | custom-call | tf_op jit(solution)/shard_map/joint_solve/pallas_call | solution.py:514
  62.2 2.4 %collective-permute-start.21 = (bf16[2,32,512]{2,1,0:T(8,128)(2,1)S(1)}, bf16[2,32,512]{2,1,0:T(8,128)(2,1)S(1)}, u32[]{:S(2)}, u32[]{:S(2)}) collective-permute-start(bf16[2,32,512]{2,1,0:T(8,128)(2,1)S(1)} %get-tuple-element.14.refs_0_), channel_id=1, source_target_pairs={{3,0},{2,1},{1,2},{0,3},{7,4},{6,5},{5,6},{4,7},{11,8},{10,9},{9,1... | collective-permute-start | bytes 196616 | tf_op jit(solution)/shard_map/ppermute | solution.py:532
  64.7 1.9 %collective-permute-start.19 = (bf16[2,32,512]{2,1,0:T(8,128)(2,1)S(1)}, bf16[2,32,512]{2,1,0:T(8,128)(2,1)S(1)}, u32[]{:S(2)}, u32[]{:S(2)}) collective-permute-start(bf16[2,32,512]{2,1,0:T(8,128)(2,1)S(1)} %get-tuple-element.14.refs_0_), channel_id=1, source_target_pairs={{1,0},{0,1},{3,2},{2,3},{5,4},{4,5},{7,6},{6,7},{9,8},{8,9},{11,10... | collective-permute-start | bytes 196616 | tf_op jit(solution)/shard_map/ppermute | solution.py:532
  66.5 2.4 %collective-permute-done.21.refs_3_ = bf16[2,32,512]{2,1,0:T(8,128)(2,1)S(1)} collective-permute-done((bf16[2,32,512]{2,1,0:T(8,128)(2,1)S(1)}, bf16[2,32,512]{2,1,0:T(8,128)(2,1)S(1)}, u32[]{:S(2)}, u32[]{:S(2)}) %collective-permute-start.21) | collective-permute-done | bytes 65568 | tf_op jit(solution)/shard_map/ppermute | solution.py:532
  68.9 2.2 %collective-permute-done.20.refs_2_ = bf16[2,32,512]{2,1,0:T(8,128)(2,1)S(1)} collective-permute-done((bf16[2,32,512]{2,1,0:T(8,128)(2,1)S(1)}, bf16[2,32,512]{2,1,0:T(8,128)(2,1)S(1)}, u32[]{:S(2)}, u32[]{:S(2)}) %collective-permute-start.20) | collective-permute-done | bytes 65568 | tf_op jit(solution)/shard_map/ppermute | solution.py:532
  71.1 3.1 %apply_score.1 = f32[2,32,32]{2,1,0:T(8,128)S(1)} custom-call(bf16[2,32,512]{2,1,0:T(8,128)(2,1)S(1)} %get-tuple-element.14.refs_0_, bf16[2,32,512]{2,1,0:T(8,128)(2,1)S(1)} %collective-permute-done.19.refs_1_, bf16[2,32,512]{2,1,0:T(8,128)(2,1)S(1)} %collective-permute-done.20.refs_2_, bf16[2,32,512]{2,1,0:T(8,128)(2,1)S(1)} %collective-permute-done.21.refs_3_, ...), custom_call_target="tpu_custom_call" | custom-call | bytes 4194304 | tf_op jit(solution)/shard_map/apply_score/pallas_call | solution.py:255
  74.2 2.2 %collective-permute-start.24 = (f32[2,32,32]{2,1,0:T(8,128)S(1)}, f32[2,32,32]{2,1,0:T(8,128)S(1)}, u32[]{:S(2)}, u32[]{:S(2)}) collective-permute-start(f32[2,32,32]{2,1,0:T(8,128)S(1)} %apply_score.1), channel_id=1, source_target_pairs={{3,0},{2,1},{1,2},{0,3},{7,4},{6,5},{5,6},{4,7},{11,8},{10,9},{9,1... | collective-permute-start | bytes 24584 | tf_op jit(solution)/shard_map/ppermute | solution.py:532
  76.4 2.2 %collective-permute-start.22 = (f32[2,32,32]{2,1,0:T(8,128)S(1)}, f32[2,32,32]{2,1,0:T(8,128)S(1)}, u32[]{:S(2)}, u32[]{:S(2)}) collective-permute-start(f32[2,32,32]{2,1,0:T(8,128)S(1)} %apply_score.1), channel_id=1, source_target_pairs={{1,0},{0,1},{3,2},{2,3},{5,4},{4,5},{7,6},{6,7},{9,8},{8,9},{11,10... | collective-permute-start | bytes 24584 | tf_op jit(solution)/shard_map/ppermute | solution.py:532
  78.6 1.4 %collective-permute-done.24 = f32[2,32,32]{2,1,0:T(8,128)S(1)} collective-permute-done((f32[2,32,32]{2,1,0:T(8,128)S(1)}, f32[2,32,32]{2,1,0:T(8,128)S(1)}, u32[]{:S(2)}, u32[]{:S(2)}) %collective-permute-start.24) | collective-permute-done | bytes 8224 | tf_op jit(solution)/shard_map/ppermute | solution.py:532
  (37 shorter events, 8.5 us)
Async XLA Ops:
  1.5 12.6 %collective-permute-start.2 = (bf16[2,32,512]{2,1,0:T(8,128)(2,1)S(1)}, bf16[2,32,512]{2,1,0:T(8,128)(2,1)S(1)}, u32[]{:S(2)}, u32[]{:S(2)}) collective-permute-start(bf16[2,32,512]{2,1,0:T(8,128)(2,1)S(1)} %convert_element_type.3.refs_0_), channel_id=1, source_target_pairs={{3,0},{2,1},{1,2},{0,3},{7,4},{6,5},{5,6},{4,7},{11,8},{10,9},{9,1... | collective-permute-start | bytes 196616 | tf_op jit(solution)/shard_map/ppermute | solution.py:532
  6.7 7.5 %collective-permute-start.1 = (bf16[2,32,512]{2,1,0:T(8,128)(2,1)S(1)}, bf16[2,32,512]{2,1,0:T(8,128)(2,1)S(1)}, u32[]{:S(2)}, u32[]{:S(2)}) collective-permute-start(bf16[2,32,512]{2,1,0:T(8,128)(2,1)S(1)} %convert_element_type.3.refs_0_), channel_id=1, source_target_pairs={{2,0},{3,1},{0,2},{1,3},{6,4},{7,5},{4,6},{5,7},{10,8},{11,9},{8,1... | collective-permute-start | bytes 196616 | tf_op jit(solution)/shard_map/ppermute | solution.py:532
  6.7 7.5 %collective-permute-start = (bf16[2,32,512]{2,1,0:T(8,128)(2,1)S(1)}, bf16[2,32,512]{2,1,0:T(8,128)(2,1)S(1)}, u32[]{:S(2)}, u32[]{:S(2)}) collective-permute-start(bf16[2,32,512]{2,1,0:T(8,128)(2,1)S(1)} %convert_element_type.3.refs_0_), channel_id=1, source_target_pairs={{1,0},{0,1},{3,2},{2,3},{5,4},{4,5},{7,6},{6,7},{9,8},{8,9},{11,10... | collective-permute-start | bytes 196616 | tf_op jit(solution)/shard_map/ppermute | solution.py:532
  15.7 9.8 %collective-permute-start.11 = (f32[32,512]{1,0:T(8,128)S(1)}, f32[32,512]{1,0:T(8,128)S(1)}, u32[]{:S(2)}, u32[]{:S(2)}) collective-permute-start(f32[32,512]{1,0:T(8,128)S(1)} %apply_first.3.refs_0_), channel_id=1, source_target_pairs={{3,0},{2,1},{1,2},{0,3},{7,4},{6,5},{5,6},{4,7},{11,8},{10,9},{9,1... | collective-permute-start | bytes 196616 | tf_op jit(solution)/shard_map/ppermute | solution.py:532
  19.5 6.6 %collective-permute-start.10 = (f32[32,512]{1,0:T(8,128)S(1)}, f32[32,512]{1,0:T(8,128)S(1)}, u32[]{:S(2)}, u32[]{:S(2)}) collective-permute-start(f32[32,512]{1,0:T(8,128)S(1)} %apply_first.3.refs_0_), channel_id=1, source_target_pairs={{2,0},{3,1},{0,2},{1,3},{6,4},{7,5},{4,6},{5,7},{10,8},{11,9},{8,1... | collective-permute-start | bytes 196616 | tf_op jit(solution)/shard_map/ppermute | solution.py:532
  19.5 6.6 %collective-permute-start.9 = (f32[32,512]{1,0:T(8,128)S(1)}, f32[32,512]{1,0:T(8,128)S(1)}, u32[]{:S(2)}, u32[]{:S(2)}) collective-permute-start(f32[32,512]{1,0:T(8,128)S(1)} %apply_first.3.refs_0_), channel_id=1, source_target_pairs={{1,0},{0,1},{3,2},{2,3},{5,4},{4,5},{7,6},{6,7},{9,8},{8,9},{11,10... | collective-permute-start | bytes 196616 | tf_op jit(solution)/shard_map/ppermute | solution.py:532
  21.7 9.5 %collective-permute-start.5 = (f32[32,512]{1,0:T(8,128)S(1)}, f32[32,512]{1,0:T(8,128)S(1)}, u32[]{:S(2)}, u32[]{:S(2)}) collective-permute-start(f32[32,512]{1,0:T(8,128)S(1)} %apply_first.2.refs_0_), channel_id=1, source_target_pairs={{3,0},{2,1},{1,2},{0,3},{7,4},{6,5},{5,6},{4,7},{11,8},{10,9},{9,1... | collective-permute-start | bytes 196616 | tf_op jit(solution)/shard_map/ppermute | solution.py:532
  25.5 5.8 %collective-permute-start.4 = (f32[32,512]{1,0:T(8,128)S(1)}, f32[32,512]{1,0:T(8,128)S(1)}, u32[]{:S(2)}, u32[]{:S(2)}) collective-permute-start(f32[32,512]{1,0:T(8,128)S(1)} %apply_first.2.refs_0_), channel_id=1, source_target_pairs={{2,0},{3,1},{0,2},{1,3},{6,4},{7,5},{4,6},{5,7},{10,8},{11,9},{8,1... | collective-permute-start | bytes 196616 | tf_op jit(solution)/shard_map/ppermute | solution.py:532
  25.5 5.8 %collective-permute-start.3 = (f32[32,512]{1,0:T(8,128)S(1)}, f32[32,512]{1,0:T(8,128)S(1)}, u32[]{:S(2)}, u32[]{:S(2)}) collective-permute-start(f32[32,512]{1,0:T(8,128)S(1)} %apply_first.2.refs_0_), channel_id=1, source_target_pairs={{1,0},{0,1},{3,2},{2,3},{5,4},{4,5},{7,6},{6,7},{9,8},{8,9},{11,10... | collective-permute-start | bytes 196616 | tf_op jit(solution)/shard_map/ppermute | solution.py:532
  29.4 7.2 %collective-permute-start.14 = (f32[32,512]{1,0:T(8,128)S(1)}, f32[32,512]{1,0:T(8,128)S(1)}, u32[]{:S(2)}, u32[]{:S(2)}) collective-permute-start(f32[32,512]{1,0:T(8,128)S(1)} %apply_second.3.refs_4_), channel_id=1, source_target_pairs={{12,0},{8,4},{4,8},{0,12},{13,1},{9,5},{5,9},{1,13},{14,2},{10,6},... | collective-permute-start | bytes 196616 | tf_op jit(solution)/shard_map/ppermute | solution.py:532
  29.4 7.1 %collective-permute-start.13 = (f32[32,512]{1,0:T(8,128)S(1)}, f32[32,512]{1,0:T(8,128)S(1)}, u32[]{:S(2)}, u32[]{:S(2)}) collective-permute-start(f32[32,512]{1,0:T(8,128)S(1)} %apply_second.3.refs_4_), channel_id=1, source_target_pairs={{8,0},{12,4},{0,8},{4,12},{9,1},{13,5},{1,9},{5,13},{10,2},{14,6},... | collective-permute-start | bytes 196616 | tf_op jit(solution)/shard_map/ppermute | solution.py:532
  31.1 5.5 %collective-permute-start.12 = (f32[32,512]{1,0:T(8,128)S(1)}, f32[32,512]{1,0:T(8,128)S(1)}, u32[]{:S(2)}, u32[]{:S(2)}) collective-permute-start(f32[32,512]{1,0:T(8,128)S(1)} %apply_second.3.refs_4_), channel_id=1, source_target_pairs={{4,0},{0,4},{12,8},{8,12},{5,1},{1,5},{13,9},{9,13},{6,2},{2,6},{1... | collective-permute-start | bytes 196616 | tf_op jit(solution)/shard_map/ppermute | solution.py:532
  34.5 4.0 %collective-permute-start.8 = (f32[32,512]{1,0:T(8,128)S(1)}, f32[32,512]{1,0:T(8,128)S(1)}, u32[]{:S(2)}, u32[]{:S(2)}) collective-permute-start(f32[32,512]{1,0:T(8,128)S(1)} %apply_second.2.refs_0_), channel_id=1, source_target_pairs={{12,0},{8,4},{4,8},{0,12},{13,1},{9,5},{5,9},{1,13},{14,2},{10,6},... | collective-permute-start | bytes 196616 | tf_op jit(solution)/shard_map/ppermute | solution.py:532
  35.8 4.6 %collective-permute-start.7 = (f32[32,512]{1,0:T(8,128)S(1)}, f32[32,512]{1,0:T(8,128)S(1)}, u32[]{:S(2)}, u32[]{:S(2)}) collective-permute-start(f32[32,512]{1,0:T(8,128)S(1)} %apply_second.2.refs_0_), channel_id=1, source_target_pairs={{8,0},{12,4},{0,8},{4,12},{9,1},{13,5},{1,9},{5,13},{10,2},{14,6},... | collective-permute-start | bytes 196616 | tf_op jit(solution)/shard_map/ppermute | solution.py:532
  36.6 3.8 %collective-permute-start.6 = (f32[32,512]{1,0:T(8,128)S(1)}, f32[32,512]{1,0:T(8,128)S(1)}, u32[]{:S(2)}, u32[]{:S(2)}) collective-permute-start(f32[32,512]{1,0:T(8,128)S(1)} %apply_second.2.refs_0_), channel_id=1, source_target_pairs={{4,0},{0,4},{12,8},{8,12},{5,1},{1,5},{13,9},{9,13},{6,2},{2,6},{1... | collective-permute-start | bytes 196616 | tf_op jit(solution)/shard_map/ppermute | solution.py:532
  41.1 7.1 %collective-permute-start.17 = (f32[144,128]{1,0:T(8,128)S(1)}, f32[144,128]{1,0:T(8,128)S(1)}, u32[]{:S(2)}, u32[]{:S(2)}) collective-permute-start(f32[144,128]{1,0:T(8,128)S(1)} %get-tuple-element.11), channel_id=1, source_target_pairs={{3,0},{2,1},{1,2},{0,3},{7,4},{6,5},{5,6},{4,7},{11,8},{10,9},{9,1... | collective-permute-start | bytes 221192 | tf_op jit(solution)/shard_map/ppermute | solution.py:532
  44.9 6.2 %collective-permute-start.16 = (f32[144,128]{1,0:T(8,128)S(1)}, f32[144,128]{1,0:T(8,128)S(1)}, u32[]{:S(2)}, u32[]{:S(2)}) collective-permute-start(f32[144,128]{1,0:T(8,128)S(1)} %get-tuple-element.11), channel_id=1, source_target_pairs={{2,0},{3,1},{0,2},{1,3},{6,4},{7,5},{4,6},{5,7},{10,8},{11,9},{8,1... | collective-permute-start | bytes 221192 | tf_op jit(solution)/shard_map/ppermute | solution.py:532
  44.9 6.2 %collective-permute-start.15 = (f32[144,128]{1,0:T(8,128)S(1)}, f32[144,128]{1,0:T(8,128)S(1)}, u32[]{:S(2)}, u32[]{:S(2)}) collective-permute-start(f32[144,128]{1,0:T(8,128)S(1)} %get-tuple-element.11), channel_id=1, source_target_pairs={{1,0},{0,1},{3,2},{2,3},{5,4},{4,5},{7,6},{6,7},{9,8},{8,9},{11,10... | collective-permute-start | bytes 221192 | tf_op jit(solution)/shard_map/ppermute | solution.py:532
  62.2 6.8 %collective-permute-start.21 = (bf16[2,32,512]{2,1,0:T(8,128)(2,1)S(1)}, bf16[2,32,512]{2,1,0:T(8,128)(2,1)S(1)}, u32[]{:S(2)}, u32[]{:S(2)}) collective-permute-start(bf16[2,32,512]{2,1,0:T(8,128)(2,1)S(1)} %get-tuple-element.14.refs_0_), channel_id=1, source_target_pairs={{3,0},{2,1},{1,2},{0,3},{7,4},{6,5},{5,6},{4,7},{11,8},{10,9},{9,1... | collective-permute-start | bytes 196616 | tf_op jit(solution)/shard_map/ppermute | solution.py:532
  64.5 6.6 %collective-permute-start.20 = (bf16[2,32,512]{2,1,0:T(8,128)(2,1)S(1)}, bf16[2,32,512]{2,1,0:T(8,128)(2,1)S(1)}, u32[]{:S(2)}, u32[]{:S(2)}) collective-permute-start(bf16[2,32,512]{2,1,0:T(8,128)(2,1)S(1)} %get-tuple-element.14.refs_0_), channel_id=1, source_target_pairs={{2,0},{3,1},{0,2},{1,3},{6,4},{7,5},{4,6},{5,7},{10,8},{11,9},{8,1... | collective-permute-start | bytes 196616 | tf_op jit(solution)/shard_map/ppermute | solution.py:532
  64.7 6.5 %collective-permute-start.19 = (bf16[2,32,512]{2,1,0:T(8,128)(2,1)S(1)}, bf16[2,32,512]{2,1,0:T(8,128)(2,1)S(1)}, u32[]{:S(2)}, u32[]{:S(2)}) collective-permute-start(bf16[2,32,512]{2,1,0:T(8,128)(2,1)S(1)} %get-tuple-element.14.refs_0_), channel_id=1, source_target_pairs={{1,0},{0,1},{3,2},{2,3},{5,4},{4,5},{7,6},{6,7},{9,8},{8,9},{11,10... | collective-permute-start | bytes 196616 | tf_op jit(solution)/shard_map/ppermute | solution.py:532
  74.2 5.8 %collective-permute-start.24 = (f32[2,32,32]{2,1,0:T(8,128)S(1)}, f32[2,32,32]{2,1,0:T(8,128)S(1)}, u32[]{:S(2)}, u32[]{:S(2)}) collective-permute-start(f32[2,32,32]{2,1,0:T(8,128)S(1)} %apply_score.1), channel_id=1, source_target_pairs={{3,0},{2,1},{1,2},{0,3},{7,4},{6,5},{5,6},{4,7},{11,8},{10,9},{9,1... | collective-permute-start | bytes 24584 | tf_op jit(solution)/shard_map/ppermute | solution.py:532
  76.4 4.8 %collective-permute-start.23 = (f32[2,32,32]{2,1,0:T(8,128)S(1)}, f32[2,32,32]{2,1,0:T(8,128)S(1)}, u32[]{:S(2)}, u32[]{:S(2)}) collective-permute-start(f32[2,32,32]{2,1,0:T(8,128)S(1)} %apply_score.1), channel_id=1, source_target_pairs={{2,0},{3,1},{0,2},{1,3},{6,4},{7,5},{4,6},{5,7},{10,8},{11,9},{8,1... | collective-permute-start | bytes 24584 | tf_op jit(solution)/shard_map/ppermute | solution.py:532
  76.4 4.8 %collective-permute-start.22 = (f32[2,32,32]{2,1,0:T(8,128)S(1)}, f32[2,32,32]{2,1,0:T(8,128)S(1)}, u32[]{:S(2)}, u32[]{:S(2)}) collective-permute-start(f32[2,32,32]{2,1,0:T(8,128)S(1)} %apply_score.1), channel_id=1, source_target_pairs={{1,0},{0,1},{3,2},{2,3},{5,4},{4,5},{7,6},{6,7},{9,8},{8,9},{11,10... | collective-permute-start | bytes 24584 | tf_op jit(solution)/shard_map/ppermute | solution.py:532
  (1 other events, 1.3 us)

commit v9 on v8

--- a/solution.py
+++ b/solution.py
@@ -240,10 +240,20 @@
     out_ref[...] = to_wide(image_of(parts, dense_ref), out_ref.shape[0], halves, tall)
 
 
-def score_kernel(layers, piece_count, *refs):
+def own_kernel(basis_ref, *refs):
+    *dense_refs, out_ref = refs
+    for layer, dense_ref in enumerate(dense_refs):
+        out_ref[layer] = image_part(basis_ref[layer], dense_ref[0])
+
+
+def score_kernel(layers, piece_count, own_ref, *refs):
     pieces, left_ref, refs = refs[:piece_count], refs[piece_count], refs[piece_count + 1 :]
     dense_refs, (out_ref, halves, tall) = refs[:layers], refs[layers:]
-    totals = [image_of([piece[layer] for piece in pieces], dense_refs[layer]) for layer in range(layers)]
+    totals = [
+        own_ref[layer]
+        + sum(image_part(piece[layer], dense_refs[layer][d + 1]) for d, piece in enumerate(pieces))
+        for layer in range(layers)
+    ]
     wide = [
         to_wide(totals[layer], left_ref.shape[1], halves.at[layer], tall.at[layer]) for layer in range(layers)
     ]
@@ -274,10 +284,24 @@
     return apply_whole(kernel, "apply_second", [*pieces, dense], pieces[0].shape)
 
 
+def apply_own(basis, dense):
+    layers, k = basis.shape[:2]
+    return pl.pallas_call(
+        own_kernel,
+        in_specs=vmem_specs(1 + layers),
+        out_specs=pl.BlockSpec(memory_space=pltpu.VMEM),
+        out_shape=jax.ShapeDtypeStruct((layers, 2 * TALL, 2 * k), F32),
+        compiler_params=params(14),
+        cost_estimate=pl.CostEstimate(flops=0, bytes_accessed=2 * MIB, transcendentals=0),
+        name="apply_own",
+    )(basis, *dense)
+
+
 def apply_score(pieces, left, dense):
-    kernel = functools.partial(score_kernel, len(dense), len(pieces))
+    kernel = functools.partial(score_kernel, len(dense), len(pieces) - 1)
     layers, k = left.shape[:2]
-    return apply_whole(kernel, "apply_score", [*pieces, left, *dense], (layers, k, k), layers)
+    operands = [apply_own(pieces[0], dense), *pieces[1:], left, *dense]
+    return apply_whole(kernel, "apply_score", operands, (layers, k, k), layers)
 
 
 def apply_dense(mode, basis, dense, left=None):
@@ -466,10 +490,11 @@
     mixed = packed[half : 2 * half]
     under = jnp.where(col < row, mixed, 0.0)
     diagonal = jnp.concatenate([packed[2 * half :]] * (half // k), axis=0)
-    work[:half, :half] = jnp.where(col >= row, mixed, 0.0)
+    over = jnp.where(col > row, mixed, 0.0)
+    work[:half, :half] = jnp.where(col >= row, mixed, over.T)
     work[:half, half:] = packed[:half]
     work[half:, :half] = jnp.zeros((half, half), F32)
-    work[half:, half:] = under.T + jnp.where(col == row, diagonal, 0.0)
+    work[half:, half:] = under + under.T + jnp.where(col == row, diagonal, 0.0)
 
 
 def joint_kernel(k, *refs):
@@ -480,14 +505,15 @@
     packed[pl.ds(pl.multiple_of((1 - odd) * rows, 16), rows)] = other_ref[...]
     unpack(packed[...], k, work)
     size = work.shape[0]
-    steps = size // k
-    lane = lax.broadcasted_iota(jnp.int32, (k, size), 1)
-    lane_128 = lax.broadcasted_iota(jnp.int32, (k, 128), 1)
-    sub_128 = lax.broadcasted_iota(jnp.int32, (k, 128), 0)
+    band = 2 * k
+    steps = size // band
+    lane = lax.broadcasted_iota(jnp.int32, (band, size), 1)
+    lane_128 = lax.broadcasted_iota(jnp.int32, (band, 128), 1)
+    sub_128 = lax.broadcasted_iota(jnp.int32, (band, 128), 0)
     gram, across = unit_scale(work[...])
     work[...] = gram
     for s in range(steps):
-        lo, hi = s * k, (s + 1) * k
+        lo, hi = s * band, (s + 1) * band
         here = (lane >= lo) & (lane < hi)
         eye = jnp.where(lane_128 == sub_128 + lo % 128, 1.0, 0.0)
         solved = joined(eliminate(tiled(jnp.concatenate([work[lo:hi], eye], axis=1)), lo))
@@ -497,8 +523,8 @@
         if s + 1 < steps:
             update = gram_update(panel, hi // 128 * 128)
             for r in range(s + 1, steps):
-                rows = work[r * k : r * k + k]
-                work[r * k : r * k + k] = jnp.where(here, 0.0, rows) - update(r * k, k)
+                rows = work[r * band : r * band + band]
+                work[r * band : r * band + band] = jnp.where(here, 0.0, rows) - update(r * band, band)
     rows = out_ref.shape[0] * k
     own = work[pl.ds(pl.multiple_of(lax.axis_index("layer") * rows, rows), rows)] * across
     joint = jnp.dot(own, images_ref[...], precision=HIGHEST, preferred_element_type=F32)

time: 82 us -> 82 us (level)
  transfers between devices with their start and end apart: 25 -> 25, of which waited for: 9 -> 9; matrix products, arithmetic and copies ran while one was open for 0% -> 0% of each run, Pallas kernels for 18% -> 19%
where the time goes in v9:
time: 82 us; the launch traced here: 81.9 us
  starting transfers between devices  32 us (39%)
  Pallas kernels  30.6 us (37%)
  waiting for transfers between devices  17 us (21%)
  other arithmetic  1.56 us (2%)
    ppermute x24, starting transfers between devices, around(): pieces.append(lax.ppermute(x, axis, [(m ^ d, m) for m in range(count)]))  31.9 us
    ppermute x24, waiting for transfers between devices, around(): pieces.append(lax.ppermute(x, axis, [(m ^ d, m) for m in range(count)]))  15.7 us
    pallas_call x5, Pallas kernels, apply_whole(): pl.pallas_call(kernel, in_specs=vmem_specs(len(operands)), out_specs=pl.B...  12 us
    pallas_call x1, Pallas kernels, joint_solve(): pl.pallas_call(functools.partial(joint_kernel, k), in_specs=vmem_specs(3)...  10.3 us
    pallas_call x1, Pallas kernels, build_dense(): pl.pallas_call(build_whole_kernel, in_specs=[pl.BlockSpec(memory_space=pl...  6.83 us
  transfers between devices with their start and end apart: 25, of which 9 were waited for; matrix products, arithmetic and copies ran while one was open for 0% of the time, Pallas kernels for 19%

profile of v9, /device:TPU:0, one launch (start us, length us, event | category | flops | bytes accessed | tf_op | source)
XLA Modules:
  0.0 81.9 jit_solution(4189175225562658017)
XLA Ops:
  1.5 5.1 %collective-permute-start.2 = (bf16[2,32,512]{2,1,0:T(8,128)(2,1)S(1)}, bf16[2,32,512]{2,1,0:T(8,128)(2,1)S(1)}, u32[]{:S(2)}, u32[]{:S(2)}) collective-permute-start(bf16[2,32,512]{2,1,0:T(8,128)(2,1)S(1)} %convert_element_type.3.refs_0_), channel_id=1, source_target_pairs={{3,0},{2,1},{1,2},{0,3},{7,4},{6,5},{5,6},{4,7},{11,8},{10,9},{9,1... | collective-permute-start | bytes 196616 | tf_op jit(solution)/shard_map/ppermute | solution.py:558
  7.3 6.8 %build_dense.1 = (bf16[4,512,1024]{2,1,0:T(8,128)(2,1)S(1)}, bf16[4,512,1024]{2,1,0:T(8,128)(2,1)S(1)}) custom-call(s32[2,512]{1,0:T(2,128)} %rows_hbm.1, s32[2,512]{1,0:T(2,128)} %cols_hbm.1, s32[1,2]{1,0:T(1,128)} %bitcast.1, bf16[2,512,4096]{2,1,0:T(8,128)(2,1)} %blocks_ref.1), custom_call_target="tpu_custom_call" | custom-call | tf_op jit(solution)/shard_map/build_dense/pallas_call | solution.py:113
  14.2 1.5 %apply_first.3.refs_0_ = f32[32,512]{1,0:T(8,128)S(1)} custom-call(bf16[2,32,512]{2,1,0:T(8,128)(2,1)S(1)} %convert_element_type.3.refs_0_, bf16[2,32,512]{2,1,0:T(8,128)(2,1)S(1)} %collective-permute-done.refs_1_, bf16[2,32,512]{2,1,0:T(8,128)(2,1)S(1)} %collective-permute-done.1.refs_2_, bf16[2,32,512]{2,1,0:T(8,128)(2,1)S(1)} %collective-permute-done.2.refs_3_, ...), custom_call_target="tpu_custom_call" | custom-call | bytes 4194304 | tf_op jit(solution)/shard_map/apply_first/pallas_call | solution.py:265
  15.7 3.8 %collective-permute-start.11 = (f32[32,512]{1,0:T(8,128)S(1)}, f32[32,512]{1,0:T(8,128)S(1)}, u32[]{:S(2)}, u32[]{:S(2)}) collective-permute-start(f32[32,512]{1,0:T(8,128)S(1)} %apply_first.3.refs_0_), channel_id=1, source_target_pairs={{3,0},{2,1},{1,2},{0,3},{7,4},{6,5},{5,6},{4,7},{11,8},{10,9},{9,1... | collective-permute-start | bytes 196616 | tf_op jit(solution)/shard_map/ppermute | solution.py:558
  20.2 1.5 %apply_first.2.refs_0_ = f32[32,512]{1,0:T(8,128)S(1)} custom-call(bf16[2,32,512]{2,1,0:T(8,128)(2,1)S(1)} %convert_element_type.3.refs_0_, bf16[2,32,512]{2,1,0:T(8,128)(2,1)S(1)} %collective-permute-done.refs_1_, bf16[2,32,512]{2,1,0:T(8,128)(2,1)S(1)} %collective-permute-done.1.refs_2_, bf16[2,32,512]{2,1,0:T(8,128)(2,1)S(1)} %collective-permute-done.2.refs_3_, ...), custom_call_target="tpu_custom_call" | custom-call | bytes 4194304 | tf_op jit(solution)/shard_map/apply_first/pallas_call | solution.py:265
  21.7 3.8 %collective-permute-start.5 = (f32[32,512]{1,0:T(8,128)S(1)}, f32[32,512]{1,0:T(8,128)S(1)}, u32[]{:S(2)}, u32[]{:S(2)}) collective-permute-start(f32[32,512]{1,0:T(8,128)S(1)} %apply_first.2.refs_0_), channel_id=1, source_target_pairs={{3,0},{2,1},{1,2},{0,3},{7,4},{6,5},{5,6},{4,7},{11,8},{10,9},{9,1... | collective-permute-start | bytes 196616 | tf_op jit(solution)/shard_map/ppermute | solution.py:558
  26.1 3.2 %apply_second.3.refs_4_ = f32[32,512]{1,0:T(8,128)S(1)} custom-call(f32[32,512]{1,0:T(8,128)S(1)} %apply_first.3.refs_0_, f32[32,512]{1,0:T(8,128)S(1)} %collective-permute-done.9.refs_1_, f32[32,512]{1,0:T(8,128)S(1)} %collective-permute-done.10.refs_2_, f32[32,512]{1,0:T(8,128)S(1)} %collective-permute-done.11.refs_3_, ...), custom_call_target="tpu_custom_call" | custom-call | bytes 4194304 | tf_op jit(solution)/shard_map/apply_second/pallas_call | solution.py:265
  29.4 1.7 %collective-permute-start.13 = (f32[32,512]{1,0:T(8,128)S(1)}, f32[32,512]{1,0:T(8,128)S(1)}, u32[]{:S(2)}, u32[]{:S(2)}) collective-permute-start(f32[32,512]{1,0:T(8,128)S(1)} %apply_second.3.refs_4_), channel_id=1, source_target_pairs={{8,0},{12,4},{0,8},{4,12},{9,1},{13,5},{1,9},{5,13},{10,2},{14,6},... | collective-permute-start | bytes 196616 | tf_op jit(solution)/shard_map/ppermute | solution.py:558
  31.3 3.2 %apply_second.2.refs_0_ = f32[32,512]{1,0:T(8,128)S(1)} custom-call(f32[32,512]{1,0:T(8,128)S(1)} %apply_first.2.refs_0_, f32[32,512]{1,0:T(8,128)S(1)} %collective-permute-done.3.refs_1_, f32[32,512]{1,0:T(8,128)S(1)} %collective-permute-done.4.refs_2_, f32[32,512]{1,0:T(8,128)S(1)} %collective-permute-done.5.refs_3_, ...), custom_call_target="tpu_custom_call" | custom-call | bytes 4194304 | tf_op jit(solution)/shard_map/apply_second/pallas_call | solution.py:265
  34.5 1.3 %collective-permute-start.8 = (f32[32,512]{1,0:T(8,128)S(1)}, f32[32,512]{1,0:T(8,128)S(1)}, u32[]{:S(2)}, u32[]{:S(2)}) collective-permute-start(f32[32,512]{1,0:T(8,128)S(1)} %apply_second.2.refs_0_), channel_id=1, source_target_pairs={{12,0},{8,4},{4,8},{0,12},{13,1},{9,5},{5,9},{1,13},{14,2},{10,6},... | collective-permute-start | bytes 196616 | tf_op jit(solution)/shard_map/ppermute | solution.py:558
  36.6 1.9 %collective-permute-done.8.refs_3_ = f32[32,512]{1,0:T(8,128)S(1)} collective-permute-done((f32[32,512]{1,0:T(8,128)S(1)}, f32[32,512]{1,0:T(8,128)S(1)}, u32[]{:S(2)}, u32[]{:S(2)}) %collective-permute-start.8) | collective-permute-done | bytes 65568 | tf_op jit(solution)/shard_map/ppermute | solution.py:558
  38.5 1.9 %collective-permute-done.7.refs_2_ = f32[32,512]{1,0:T(8,128)S(1)} collective-permute-done((f32[32,512]{1,0:T(8,128)S(1)}, f32[32,512]{1,0:T(8,128)S(1)}, u32[]{:S(2)}, u32[]{:S(2)}) %collective-permute-start.7) | collective-permute-done | bytes 65568 | tf_op jit(solution)/shard_map/ppermute | solution.py:558
  41.1 3.8 %collective-permute-start.17 = (f32[144,128]{1,0:T(8,128)S(1)}, f32[144,128]{1,0:T(8,128)S(1)}, u32[]{:S(2)}, u32[]{:S(2)}) collective-permute-start(f32[144,128]{1,0:T(8,128)S(1)} %get-tuple-element.11), channel_id=1, source_target_pairs={{3,0},{2,1},{1,2},{0,3},{7,4},{6,5},{5,6},{4,7},{11,8},{10,9},{9,1... | collective-permute-start | bytes 221192 | tf_op jit(solution)/shard_map/ppermute | solution.py:558
  45.5 2.7 %collective-permute-done.17 = f32[144,128]{1,0:T(8,128)S(1)} collective-permute-done((f32[144,128]{1,0:T(8,128)S(1)}, f32[144,128]{1,0:T(8,128)S(1)}, u32[]{:S(2)}, u32[]{:S(2)}) %collective-permute-start.17) | collective-permute-done | bytes 73760 | tf_op jit(solution)/shard_map/ppermute | solution.py:558
  48.2 2.8 %collective-permute-done.16 = f32[144,128]{1,0:T(8,128)S(1)} collective-permute-done((f32[144,128]{1,0:T(8,128)S(1)}, f32[144,128]{1,0:T(8,128)S(1)}, u32[]{:S(2)}, u32[]{:S(2)}) %collective-permute-start.16) | collective-permute-done | bytes 73760 | tf_op jit(solution)/shard_map/ppermute | solution.py:558
  52.4 10.3 %joint_solve.1 = (f32[2,32,512]{2,1,0:T(8,128)}, f32[2,32,512]{2,1,0:T(8,128)S(1)}, bf16[2,32,512]{2,1,0:T(8,128)(2,1)S(1)}) custom-call(f32[144,128]{1,0:T(8,128)S(1)} %add_add_fusion.refs_0_, f32[144,128]{1,0:T(8,128)S(1)} %collective-permute-done.18.refs_1_, f32[256,512]{1,0:T(8,128)S(1)} %get-tuple-element.12.refs_2_), custom_call_target="tpu_custom_call" | custom-call | tf_op jit(solution)/shard_map/joint_solve/pallas_call | solution.py:540
  62.7 2.4 %collective-permute-start.21 = (bf16[2,32,512]{2,1,0:T(8,128)(2,1)S(1)}, bf16[2,32,512]{2,1,0:T(8,128)(2,1)S(1)}, u32[]{:S(2)}, u32[]{:S(2)}) collective-permute-start(bf16[2,32,512]{2,1,0:T(8,128)(2,1)S(1)} %get-tuple-element.14.basis_ref), channel_id=1, source_target_pairs={{3,0},{2,1},{1,2},{0,3},{7,4},{6,5},{5,6},{4,7},{11,8},{10,9},{9,1... | collective-permute-start | bytes 196616 | tf_op jit(solution)/shard_map/ppermute | solution.py:558
  65.2 1.9 %collective-permute-start.19 = (bf16[2,32,512]{2,1,0:T(8,128)(2,1)S(1)}, bf16[2,32,512]{2,1,0:T(8,128)(2,1)S(1)}, u32[]{:S(2)}, u32[]{:S(2)}) collective-permute-start(bf16[2,32,512]{2,1,0:T(8,128)(2,1)S(1)} %get-tuple-element.14.basis_ref), channel_id=1, source_target_pairs={{1,0},{0,1},{3,2},{2,3},{5,4},{4,5},{7,6},{6,7},{9,8},{8,9},{11,10... | collective-permute-start | bytes 196616 | tf_op jit(solution)/shard_map/ppermute | solution.py:558
  67.9 1.6 %collective-permute-done.21.refs_2_ = bf16[2,32,512]{2,1,0:T(8,128)(2,1)S(1)} collective-permute-done((bf16[2,32,512]{2,1,0:T(8,128)(2,1)S(1)}, bf16[2,32,512]{2,1,0:T(8,128)(2,1)S(1)}, u32[]{:S(2)}, u32[]{:S(2)}) %collective-permute-start.21) | collective-permute-done | bytes 65568 | tf_op jit(solution)/shard_map/ppermute | solution.py:558
  69.5 2.2 %collective-permute-done.20.refs_1_ = bf16[2,32,512]{2,1,0:T(8,128)(2,1)S(1)} collective-permute-done((bf16[2,32,512]{2,1,0:T(8,128)(2,1)S(1)}, bf16[2,32,512]{2,1,0:T(8,128)(2,1)S(1)}, u32[]{:S(2)}, u32[]{:S(2)}) %collective-permute-start.20) | collective-permute-done | bytes 65568 | tf_op jit(solution)/shard_map/ppermute | solution.py:558
  71.7 2.5 %apply_score.1 = f32[2,32,32]{2,1,0:T(8,128)S(1)} custom-call(f32[2,512,64]{2,1,0:T(8,128)S(1)} %apply_own.1.own_ref, bf16[2,32,512]{2,1,0:T(8,128)(2,1)S(1)} %collective-permute-done.19.refs_0_, bf16[2,32,512]{2,1,0:T(8,128)(2,1)S(1)} %collective-permute-done.20.refs_1_, bf16[2,32,512]{2,1,0:T(8,128)(2,1)S(1)} %collective-permute-done.21.refs_2_, ...), custom_call_target="tpu_custom_call" | custom-call | bytes 4194304 | tf_op jit(solution)/shard_map/apply_score/pallas_call | solution.py:265
  74.2 2.2 %collective-permute-start.24 = (f32[2,32,32]{2,1,0:T(8,128)S(1)}, f32[2,32,32]{2,1,0:T(8,128)S(1)}, u32[]{:S(2)}, u32[]{:S(2)}) collective-permute-start(f32[2,32,32]{2,1,0:T(8,128)S(1)} %apply_score.1), channel_id=1, source_target_pairs={{3,0},{2,1},{1,2},{0,3},{7,4},{6,5},{5,6},{4,7},{11,8},{10,9},{9,1... | collective-permute-start | bytes 24584 | tf_op jit(solution)/shard_map/ppermute | solution.py:558
  76.4 2.2 %collective-permute-start.22 = (f32[2,32,32]{2,1,0:T(8,128)S(1)}, f32[2,32,32]{2,1,0:T(8,128)S(1)}, u32[]{:S(2)}, u32[]{:S(2)}) collective-permute-start(f32[2,32,32]{2,1,0:T(8,128)S(1)} %apply_score.1), channel_id=1, source_target_pairs={{1,0},{0,1},{3,2},{2,3},{5,4},{4,5},{7,6},{6,7},{9,8},{8,9},{11,10... | collective-permute-start | bytes 24584 | tf_op jit(solution)/shard_map/ppermute | solution.py:558
  78.7 1.4 %collective-permute-done.24 = f32[2,32,32]{2,1,0:T(8,128)S(1)} collective-permute-done((f32[2,32,32]{2,1,0:T(8,128)S(1)}, f32[2,32,32]{2,1,0:T(8,128)S(1)}, u32[]{:S(2)}, u32[]{:S(2)}) %collective-permute-start.24) | collective-permute-done | bytes 8224 | tf_op jit(solution)/shard_map/ppermute | solution.py:558
  (38 shorter events, 9.3 us)
Async XLA Ops:
  1.5 12.6 %collective-permute-start.2 = (bf16[2,32,512]{2,1,0:T(8,128)(2,1)S(1)}, bf16[2,32,512]{2,1,0:T(8,128)(2,1)S(1)}, u32[]{:S(2)}, u32[]{:S(2)}) collective-permute-start(bf16[2,32,512]{2,1,0:T(8,128)(2,1)S(1)} %convert_element_type.3.refs_0_), channel_id=1, source_target_pairs={{3,0},{2,1},{1,2},{0,3},{7,4},{6,5},{5,6},{4,7},{11,8},{10,9},{9,1... | collective-permute-start | bytes 196616 | tf_op jit(solution)/shard_map/ppermute | solution.py:558
  6.7 7.5 %collective-permute-start.1 = (bf16[2,32,512]{2,1,0:T(8,128)(2,1)S(1)}, bf16[2,32,512]{2,1,0:T(8,128)(2,1)S(1)}, u32[]{:S(2)}, u32[]{:S(2)}) collective-permute-start(bf16[2,32,512]{2,1,0:T(8,128)(2,1)S(1)} %convert_element_type.3.refs_0_), channel_id=1, source_target_pairs={{2,0},{3,1},{0,2},{1,3},{6,4},{7,5},{4,6},{5,7},{10,8},{11,9},{8,1... | collective-permute-start | bytes 196616 | tf_op jit(solution)/shard_map/ppermute | solution.py:558
  6.7 7.5 %collective-permute-start = (bf16[2,32,512]{2,1,0:T(8,128)(2,1)S(1)}, bf16[2,32,512]{2,1,0:T(8,128)(2,1)S(1)}, u32[]{:S(2)}, u32[]{:S(2)}) collective-permute-start(bf16[2,32,512]{2,1,0:T(8,128)(2,1)S(1)} %convert_element_type.3.refs_0_), channel_id=1, source_target_pairs={{1,0},{0,1},{3,2},{2,3},{5,4},{4,5},{7,6},{6,7},{9,8},{8,9},{11,10... | collective-permute-start | bytes 196616 | tf_op jit(solution)/shard_map/ppermute | solution.py:558
  15.7 9.8 %collective-permute-start.11 = (f32[32,512]{1,0:T(8,128)S(1)}, f32[32,512]{1,0:T(8,128)S(1)}, u32[]{:S(2)}, u32[]{:S(2)}) collective-permute-start(f32[32,512]{1,0:T(8,128)S(1)} %apply_first.3.refs_0_), channel_id=1, source_target_pairs={{3,0},{2,1},{1,2},{0,3},{7,4},{6,5},{5,6},{4,7},{11,8},{10,9},{9,1... | collective-permute-start | bytes 196616 | tf_op jit(solution)/shard_map/ppermute | solution.py:558
  19.5 6.6 %collective-permute-start.10 = (f32[32,512]{1,0:T(8,128)S(1)}, f32[32,512]{1,0:T(8,128)S(1)}, u32[]{:S(2)}, u32[]{:S(2)}) collective-permute-start(f32[32,512]{1,0:T(8,128)S(1)} %apply_first.3.refs_0_), channel_id=1, source_target_pairs={{2,0},{3,1},{0,2},{1,3},{6,4},{7,5},{4,6},{5,7},{10,8},{11,9},{8,1... | collective-permute-start | bytes 196616 | tf_op jit(solution)/shard_map/ppermute | solution.py:558
  19.5 6.6 %collective-permute-start.9 = (f32[32,512]{1,0:T(8,128)S(1)}, f32[32,512]{1,0:T(8,128)S(1)}, u32[]{:S(2)}, u32[]{:S(2)}) collective-permute-start(f32[32,512]{1,0:T(8,128)S(1)} %apply_first.3.refs_0_), channel_id=1, source_target_pairs={{1,0},{0,1},{3,2},{2,3},{5,4},{4,5},{7,6},{6,7},{9,8},{8,9},{11,10... | collective-permute-start | bytes 196616 | tf_op jit(solution)/shard_map/ppermute | solution.py:558
  21.7 9.5 %collective-permute-start.5 = (f32[32,512]{1,0:T(8,128)S(1)}, f32[32,512]{1,0:T(8,128)S(1)}, u32[]{:S(2)}, u32[]{:S(2)}) collective-permute-start(f32[32,512]{1,0:T(8,128)S(1)} %apply_first.2.refs_0_), channel_id=1, source_target_pairs={{3,0},{2,1},{1,2},{0,3},{7,4},{6,5},{5,6},{4,7},{11,8},{10,9},{9,1... | collective-permute-start | bytes 196616 | tf_op jit(solution)/shard_map/ppermute | solution.py:558
  25.5 5.8 %collective-permute-start.4 = (f32[32,512]{1,0:T(8,128)S(1)}, f32[32,512]{1,0:T(8,128)S(1)}, u32[]{:S(2)}, u32[]{:S(2)}) collective-permute-start(f32[32,512]{1,0:T(8,128)S(1)} %apply_first.2.refs_0_), channel_id=1, source_target_pairs={{2,0},{3,1},{0,2},{1,3},{6,4},{7,5},{4,6},{5,7},{10,8},{11,9},{8,1... | collective-permute-start | bytes 196616 | tf_op jit(solution)/shard_map/ppermute | solution.py:558
  25.5 5.8 %collective-permute-start.3 = (f32[32,512]{1,0:T(8,128)S(1)}, f32[32,512]{1,0:T(8,128)S(1)}, u32[]{:S(2)}, u32[]{:S(2)}) collective-permute-start(f32[32,512]{1,0:T(8,128)S(1)} %apply_first.2.refs_0_), channel_id=1, source_target_pairs={{1,0},{0,1},{3,2},{2,3},{5,4},{4,5},{7,6},{6,7},{9,8},{8,9},{11,10... | collective-permute-start | bytes 196616 | tf_op jit(solution)/shard_map/ppermute | solution.py:558
  29.4 7.2 %collective-permute-start.14 = (f32[32,512]{1,0:T(8,128)S(1)}, f32[32,512]{1,0:T(8,128)S(1)}, u32[]{:S(2)}, u32[]{:S(2)}) collective-permute-start(f32[32,512]{1,0:T(8,128)S(1)} %apply_second.3.refs_4_), channel_id=1, source_target_pairs={{12,0},{8,4},{4,8},{0,12},{13,1},{9,5},{5,9},{1,13},{14,2},{10,6},... | collective-permute-start | bytes 196616 | tf_op jit(solution)/shard_map/ppermute | solution.py:558
  29.4 7.1 %collective-permute-start.13 = (f32[32,512]{1,0:T(8,128)S(1)}, f32[32,512]{1,0:T(8,128)S(1)}, u32[]{:S(2)}, u32[]{:S(2)}) collective-permute-start(f32[32,512]{1,0:T(8,128)S(1)} %apply_second.3.refs_4_), channel_id=1, source_target_pairs={{8,0},{12,4},{0,8},{4,12},{9,1},{13,5},{1,9},{5,13},{10,2},{14,6},... | collective-permute-start | bytes 196616 | tf_op jit(solution)/shard_map/ppermute | solution.py:558
  31.1 5.5 %collective-permute-start.12 = (f32[32,512]{1,0:T(8,128)S(1)}, f32[32,512]{1,0:T(8,128)S(1)}, u32[]{:S(2)}, u32[]{:S(2)}) collective-permute-start(f32[32,512]{1,0:T(8,128)S(1)} %apply_second.3.refs_4_), channel_id=1, source_target_pairs={{4,0},{0,4},{12,8},{8,12},{5,1},{1,5},{13,9},{9,13},{6,2},{2,6},{1... | collective-permute-start | bytes 196616 | tf_op jit(solution)/shard_map/ppermute | solution.py:558
  34.5 4.0 %collective-permute-start.8 = (f32[32,512]{1,0:T(8,128)S(1)}, f32[32,512]{1,0:T(8,128)S(1)}, u32[]{:S(2)}, u32[]{:S(2)}) collective-permute-start(f32[32,512]{1,0:T(8,128)S(1)} %apply_second.2.refs_0_), channel_id=1, source_target_pairs={{12,0},{8,4},{4,8},{0,12},{13,1},{9,5},{5,9},{1,13},{14,2},{10,6},... | collective-permute-start | bytes 196616 | tf_op jit(solution)/shard_map/ppermute | solution.py:558
  35.8 4.6 %collective-permute-start.7 = (f32[32,512]{1,0:T(8,128)S(1)}, f32[32,512]{1,0:T(8,128)S(1)}, u32[]{:S(2)}, u32[]{:S(2)}) collective-permute-start(f32[32,512]{1,0:T(8,128)S(1)} %apply_second.2.refs_0_), channel_id=1, source_target_pairs={{8,0},{12,4},{0,8},{4,12},{9,1},{13,5},{1,9},{5,13},{10,2},{14,6},... | collective-permute-start | bytes 196616 | tf_op jit(solution)/shard_map/ppermute | solution.py:558
  36.6 3.8 %collective-permute-start.6 = (f32[32,512]{1,0:T(8,128)S(1)}, f32[32,512]{1,0:T(8,128)S(1)}, u32[]{:S(2)}, u32[]{:S(2)}) collective-permute-start(f32[32,512]{1,0:T(8,128)S(1)} %apply_second.2.refs_0_), channel_id=1, source_target_pairs={{4,0},{0,4},{12,8},{8,12},{5,1},{1,5},{13,9},{9,13},{6,2},{2,6},{1... | collective-permute-start | bytes 196616 | tf_op jit(solution)/shard_map/ppermute | solution.py:558
  41.1 7.1 %collective-permute-start.17 = (f32[144,128]{1,0:T(8,128)S(1)}, f32[144,128]{1,0:T(8,128)S(1)}, u32[]{:S(2)}, u32[]{:S(2)}) collective-permute-start(f32[144,128]{1,0:T(8,128)S(1)} %get-tuple-element.11), channel_id=1, source_target_pairs={{3,0},{2,1},{1,2},{0,3},{7,4},{6,5},{5,6},{4,7},{11,8},{10,9},{9,1... | collective-permute-start | bytes 221192 | tf_op jit(solution)/shard_map/ppermute | solution.py:558
  44.9 6.2 %collective-permute-start.16 = (f32[144,128]{1,0:T(8,128)S(1)}, f32[144,128]{1,0:T(8,128)S(1)}, u32[]{:S(2)}, u32[]{:S(2)}) collective-permute-start(f32[144,128]{1,0:T(8,128)S(1)} %get-tuple-element.11), channel_id=1, source_target_pairs={{2,0},{3,1},{0,2},{1,3},{6,4},{7,5},{4,6},{5,7},{10,8},{11,9},{8,1... | collective-permute-start | bytes 221192 | tf_op jit(solution)/shard_map/ppermute | solution.py:558
  44.9 6.2 %collective-permute-start.15 = (f32[144,128]{1,0:T(8,128)S(1)}, f32[144,128]{1,0:T(8,128)S(1)}, u32[]{:S(2)}, u32[]{:S(2)}) collective-permute-start(f32[144,128]{1,0:T(8,128)S(1)} %get-tuple-element.11), channel_id=1, source_target_pairs={{1,0},{0,1},{3,2},{2,3},{5,4},{4,5},{7,6},{6,7},{9,8},{8,9},{11,10... | collective-permute-start | bytes 221192 | tf_op jit(solution)/shard_map/ppermute | solution.py:558
  62.7 6.8 %collective-permute-start.21 = (bf16[2,32,512]{2,1,0:T(8,128)(2,1)S(1)}, bf16[2,32,512]{2,1,0:T(8,128)(2,1)S(1)}, u32[]{:S(2)}, u32[]{:S(2)}) collective-permute-start(bf16[2,32,512]{2,1,0:T(8,128)(2,1)S(1)} %get-tuple-element.14.basis_ref), channel_id=1, source_target_pairs={{3,0},{2,1},{1,2},{0,3},{7,4},{6,5},{5,6},{4,7},{11,8},{10,9},{9,1... | collective-permute-start | bytes 196616 | tf_op jit(solution)/shard_map/ppermute | solution.py:558
  65.1 6.6 %collective-permute-start.20 = (bf16[2,32,512]{2,1,0:T(8,128)(2,1)S(1)}, bf16[2,32,512]{2,1,0:T(8,128)(2,1)S(1)}, u32[]{:S(2)}, u32[]{:S(2)}) collective-permute-start(bf16[2,32,512]{2,1,0:T(8,128)(2,1)S(1)} %get-tuple-element.14.basis_ref), channel_id=1, source_target_pairs={{2,0},{3,1},{0,2},{1,3},{6,4},{7,5},{4,6},{5,7},{10,8},{11,9},{8,1... | collective-permute-start | bytes 196616 | tf_op jit(solution)/shard_map/ppermute | solution.py:558
  65.2 6.5 %collective-permute-start.19 = (bf16[2,32,512]{2,1,0:T(8,128)(2,1)S(1)}, bf16[2,32,512]{2,1,0:T(8,128)(2,1)S(1)}, u32[]{:S(2)}, u32[]{:S(2)}) collective-permute-start(bf16[2,32,512]{2,1,0:T(8,128)(2,1)S(1)} %get-tuple-element.14.basis_ref), channel_id=1, source_target_pairs={{1,0},{0,1},{3,2},{2,3},{5,4},{4,5},{7,6},{6,7},{9,8},{8,9},{11,10... | collective-permute-start | bytes 196616 | tf_op jit(solution)/shard_map/ppermute | solution.py:558
  74.2 5.8 %collective-permute-start.24 = (f32[2,32,32]{2,1,0:T(8,128)S(1)}, f32[2,32,32]{2,1,0:T(8,128)S(1)}, u32[]{:S(2)}, u32[]{:S(2)}) collective-permute-start(f32[2,32,32]{2,1,0:T(8,128)S(1)} %apply_score.1), channel_id=1, source_target_pairs={{3,0},{2,1},{1,2},{0,3},{7,4},{6,5},{5,6},{4,7},{11,8},{10,9},{9,1... | collective-permute-start | bytes 24584 | tf_op jit(solution)/shard_map/ppermute | solution.py:558
  76.4 4.8 %collective-permute-start.23 = (f32[2,32,32]{2,1,0:T(8,128)S(1)}, f32[2,32,32]{2,1,0:T(8,128)S(1)}, u32[]{:S(2)}, u32[]{:S(2)}) collective-permute-start(f32[2,32,32]{2,1,0:T(8,128)S(1)} %apply_score.1), channel_id=1, source_target_pairs={{2,0},{3,1},{0,2},{1,3},{6,4},{7,5},{4,6},{5,7},{10,8},{11,9},{8,1... | collective-permute-start | bytes 24584 | tf_op jit(solution)/shard_map/ppermute | solution.py:558
  76.4 4.8 %collective-permute-start.22 = (f32[2,32,32]{2,1,0:T(8,128)S(1)}, f32[2,32,32]{2,1,0:T(8,128)S(1)}, u32[]{:S(2)}, u32[]{:S(2)}) collective-permute-start(f32[2,32,32]{2,1,0:T(8,128)S(1)} %apply_score.1), channel_id=1, source_target_pairs={{1,0},{0,1},{3,2},{2,3},{5,4},{4,5},{7,6},{6,7},{9,8},{8,9},{11,10... | collective-permute-start | bytes 24584 | tf_op jit(solution)/shard_map/ppermute | solution.py:558
  (1 other events, 1.3 us)

commit v10 on v9

--- a/solution.py
+++ b/solution.py
@@ -234,8 +234,7 @@
 def second_kernel(piece_count, *refs):
     pieces, (dense_ref, out_ref, halves, tall) = refs[:piece_count], refs[piece_count:]
     image = jnp.concatenate([piece[...] for piece in pieces], axis=1)
-    inverse = inverse_factor(product(image, image))
-    basis = jnp.dot(inverse, image, precision=HIGHEST, preferred_element_type=F32)
+    basis = solve_rows(product(image, image), image)
     parts = [basis[:, d * ROWS_DEV : d * ROWS_DEV + ROWS_DEV] for d in range(piece_count)]
     out_ref[...] = to_wide(image_of(parts, dense_ref), out_ref.shape[0], halves, tall)
 
@@ -334,18 +333,19 @@
     return jnp.broadcast_to(x, (8, 128))
 
 
-def eliminate(rows, offset):
-    groups, tiles = len(rows), len(rows[0])
-    rows = [list(row) for row in rows]
-    home, at = offset // 128, offset % 128
+def inverse_factor(block):
+    k = block.shape[0]
+    lane = lax.broadcasted_iota(jnp.int32, (k, 128), 1)
+    row = lax.broadcasted_iota(jnp.int32, (k, 128), 0)
+    start = jnp.where(lane < k, block, jnp.where(lane % k == row, 1.0, 0.0))
+    rows = [start[g * 8 : g * 8 + 8] for g in range(k // 8)]
     sub = lax.broadcasted_iota(jnp.int32, (8, 128), 0)
     solved = []
-    for h in range(groups):
-        below = range(h + 1, groups)
-        lane = at + 8 * h
-        col = [{g: spread(rows[g][home][:, lane + q : lane + q + 1]) for g in range(h, groups)} for q in range(8)]
+    for h in range(k // 8):
+        below = range(h + 1, k // 8)
+        col = [{g: spread(rows[g][:, 8 * h + q : 8 * h + q + 1]) for g in range(h, k // 8)} for q in range(8)]
         cell = {(p, q): spread(col[p][h][q : q + 1]) for q in range(8) for p in range(q + 1)}
-        row = [[spread(rows[h][t][q : q + 1]) for t in range(tiles)] for q in range(8)]
+        row = [spread(rows[h][q : q + 1]) for q in range(8)]
         done = []
         for m in range(0, 8, 2):
             n = m + 1
@@ -361,36 +361,31 @@
             for q in later:
                 for g in below:
                     col[q][g] = col[q][g] - r * (col[m][g] * u[q] + col[n][g] * v[q])
-            for t in range(tiles):
-                x = r * (c * row[m][t] - b * row[n][t])
-                y = r * (a * row[n][t] - b * row[m][t])
-                for q in later:
-                    row[q][t] = row[q][t] - (cell[m, q] * x + cell[n, q] * y)
-                for g in below:
-                    rows[g][t] = rows[g][t] - (col[m][g] * x + col[n][g] * y)
+            x = r * (c * row[m] - b * row[n])
+            y = r * (a * row[n] - b * row[m])
+            for q in later:
+                row[q] = row[q] - (cell[m, q] * x + cell[n, q] * y)
+            for g in below:
+                rows[g] = rows[g] - (col[m][g] * x + col[n][g] * y)
             over = pl.reciprocal(a, approx=True)
-            done.append([lax.rsqrt(a) * x for x in row[m]])
-            scale = lax.rsqrt(det * over)
-            done.append([scale * (x - (b * over) * w) for x, w in zip(row[n], row[m])])
-        finished = []
-        for t in range(tiles):
-            x = done[7][t]
-            for q in range(7):
-                x = jnp.where(sub == q, done[q][t], x)
-            finished.append(x)
+            done.append(lax.rsqrt(a) * row[m])
+            done.append(lax.rsqrt(det * over) * (row[n] - (b * over) * row[m]))
+        finished = done[7]
+        for q in range(7):
+            finished = jnp.where(sub == q, done[q], finished)
         solved.append(finished)
-    return solved
-
-
-def tiled(x):
-    return [
-        [x[g * 8 : g * 8 + 8, t * 128 : t * 128 + 128] for t in range(x.shape[1] // 128)]
-        for g in range(x.shape[0] // 8)
-    ]
-
-
-def joined(tiles):
-    return jnp.concatenate([jnp.concatenate(row, axis=1) for row in tiles], axis=0)
+    return jnp.concatenate(solved, axis=0)
+
+
+def times(inverse, right):
+    k = right.shape[0]
+    a, b, c = [piece.astype(F32) for piece in split3(inverse)]
+    lane = lax.broadcasted_iota(jnp.int32, inverse.shape, 1)
+    major = jnp.where(lane < k, 0.0, jnp.where(lane < 3 * k, a, b)).astype(BF16)
+    minor = jnp.where(lane < k, 0.0, jnp.where(lane < 2 * k, b, jnp.where(lane < 3 * k, a, c))).astype(BF16)
+    p, q, r = split3(right)
+    total = jnp.dot(major, jnp.concatenate([p, p, q, p], axis=0), preferred_element_type=F32)
+    return total + jnp.dot(minor, jnp.concatenate([p, q, r, p], axis=0), preferred_element_type=F32)
 
 
 def unit_scale(gram):
@@ -400,7 +395,13 @@
     down = 1.0 / jnp.sqrt(jnp.sum(kept, axis=1, keepdims=True))
     across = jnp.sum(kept, axis=0, keepdims=True)
     across = 1.0 / jnp.sqrt(jnp.where(across == 0.0, 1.0, across))
-    return gram * down * across, across
+    return gram * down * across, down, across
+
+
+def solve_rows(gram, image):
+    k = gram.shape[0]
+    block, down, _ = unit_scale(jnp.concatenate([gram, jnp.zeros((k, 128 - k), F32)], axis=1))
+    return times(inverse_factor(block), image * down)
 
 
 def gram_update(panel, first):
@@ -414,21 +415,9 @@
     return lambda at, count: parts[at // 128 * 128][at % 128 : at % 128 + count]
 
 
-def inverse_factor(gram):
-    k = gram.shape[0]
-    lane = lax.broadcasted_iota(jnp.int32, (k, 128), 1)
-    sub = lax.broadcasted_iota(jnp.int32, (k, 128), 0)
-    eye = jnp.where(lane == sub, 1.0, 0.0)
-    gram, across = unit_scale(jnp.concatenate([gram, jnp.zeros((k, 128 - k), F32)], axis=1))
-    solved = eliminate(tiled(jnp.concatenate([gram, eye], axis=1)), 0)
-    return (joined(solved)[:, 128:] * across)[:, :k]
-
-
 def solve_kernel(gram_ref, image_ref, out_ref):
     for layer in range(image_ref.shape[0]):
-        inverse = inverse_factor(gram_ref[layer])
-        solved = jnp.dot(inverse, image_ref[layer], precision=HIGHEST, preferred_element_type=F32)
-        out_ref[layer] = solved.astype(BF16)
+        out_ref[layer] = solve_rows(gram_ref[layer], image_ref[layer]).astype(BF16)
 
 
 def solve(gram, image):
@@ -490,11 +479,10 @@
     mixed = packed[half : 2 * half]
     under = jnp.where(col < row, mixed, 0.0)
     diagonal = jnp.concatenate([packed[2 * half :]] * (half // k), axis=0)
-    over = jnp.where(col > row, mixed, 0.0)
-    work[:half, :half] = jnp.where(col >= row, mixed, over.T)
+    work[:half, :half] = jnp.where(col >= row, mixed, 0.0)
     work[:half, half:] = packed[:half]
     work[half:, :half] = jnp.zeros((half, half), F32)
-    work[half:, half:] = under + under.T + jnp.where(col == row, diagonal, 0.0)
+    work[half:, half:] = under.T + jnp.where(col == row, diagonal, 0.0)
 
 
 def joint_kernel(k, *refs):
@@ -505,26 +493,25 @@
     packed[pl.ds(pl.multiple_of((1 - odd) * rows, 16), rows)] = other_ref[...]
     unpack(packed[...], k, work)
     size = work.shape[0]
-    band = 2 * k
-    steps = size // band
-    lane = lax.broadcasted_iota(jnp.int32, (band, size), 1)
-    lane_128 = lax.broadcasted_iota(jnp.int32, (band, 128), 1)
-    sub_128 = lax.broadcasted_iota(jnp.int32, (band, 128), 0)
-    gram, across = unit_scale(work[...])
+    steps = size // k
+    lane = lax.broadcasted_iota(jnp.int32, (k, size), 1)
+    sub = lax.broadcasted_iota(jnp.int32, (k, size), 0)
+    gram, _, across = unit_scale(work[...])
     work[...] = gram
     for s in range(steps):
-        lo, hi = s * band, (s + 1) * band
+        lo, hi = s * k, (s + 1) * k
         here = (lane >= lo) & (lane < hi)
-        eye = jnp.where(lane_128 == sub_128 + lo % 128, 1.0, 0.0)
-        solved = joined(eliminate(tiled(jnp.concatenate([work[lo:hi], eye], axis=1)), lo))
-        panel, tail = solved[:, :size], solved[:, size:]
-        panel = jnp.where(here, jnp.concatenate([tail] * (size // 128), axis=1), panel)
+        panel = work[lo:hi]
+        tile = lo // 128 * 128
+        block = pltpu.roll(panel[:, tile : tile + 128], (tile - lo) % 128, 1)
+        eye = jnp.where(lane == sub + lo, 1.0, 0.0)
+        panel = times(inverse_factor(block), jnp.where(here, eye, panel))
         work[lo:hi] = jnp.where(lane < hi, panel, 0.0)
         if s + 1 < steps:
             update = gram_update(panel, hi // 128 * 128)
             for r in range(s + 1, steps):
-                rows = work[r * band : r * band + band]
-                work[r * band : r * band + band] = jnp.where(here, 0.0, rows) - update(r * band, band)
+                rows = work[r * k : r * k + k]
+                work[r * k : r * k + k] = jnp.where(here, 0.0, rows) - update(r * k, k)
     rows = out_ref.shape[0] * k
     own = work[pl.ds(pl.multiple_of(lax.axis_index("layer") * rows, rows), rows)] * across
     joint = jnp.dot(own, images_ref[...], precision=HIGHEST, preferred_element_type=F32)

time: 82 us -> 82.4 us (level)
  no operation moved by 1% of the time
where the time goes in v10:
time: 82.4 us; the launch traced here: 82.3 us
  starting transfers between devices  31.9 us (39%)
  Pallas kernels  31 us (38%)
  waiting for transfers between devices  17 us (21%)
  other arithmetic  1.56 us (2%)
    ppermute x24, starting transfers between devices, around(): pieces.append(lax.ppermute(x, axis, [(m ^ d, m) for m in range(count)]))  31.9 us
    ppermute x24, waiting for transfers between devices, around(): pieces.append(lax.ppermute(x, axis, [(m ^ d, m) for m in range(count)]))  15.8 us
    pallas_call x5, Pallas kernels, apply_whole(): pl.pallas_call(kernel, in_specs=vmem_specs(len(operands)), out_specs=pl.B...  12.1 us
    pallas_call x1, Pallas kernels, joint_solve(): pl.pallas_call(functools.partial(joint_kernel, k), in_specs=vmem_specs(3)...  10.7 us
    pallas_call x1, Pallas kernels, build_dense(): pl.pallas_call(build_whole_kernel, in_specs=[pl.BlockSpec(memory_space=pl...  6.83 us
  transfers between devices with their start and end apart: 25, of which 9 were waited for; matrix products, arithmetic and copies ran while one was open for 0% of the time, Pallas kernels for 19%

profile of v10, /device:TPU:0, one launch (start us, length us, event | category | flops | bytes accessed | tf_op | source)
XLA Modules:
  0.0 82.3 jit_solution(10100705198289575461)
XLA Ops:
  1.5 5.1 %collective-permute-start.2 = (bf16[2,32,512]{2,1,0:T(8,128)(2,1)S(1)}, bf16[2,32,512]{2,1,0:T(8,128)(2,1)S(1)}, u32[]{:S(2)}, u32[]{:S(2)}) collective-permute-start(bf16[2,32,512]{2,1,0:T(8,128)(2,1)S(1)} %convert_element_type.3.refs_0_), channel_id=1, source_target_pairs={{3,0},{2,1},{1,2},{0,3},{7,4},{6,5},{5,6},{4,7},{11,8},{10,9},{9,1... | collective-permute-start | bytes 196616 | tf_op jit(solution)/shard_map/ppermute | solution.py:545
  7.3 6.8 %build_dense.1 = (bf16[4,512,1024]{2,1,0:T(8,128)(2,1)S(1)}, bf16[4,512,1024]{2,1,0:T(8,128)(2,1)S(1)}) custom-call(s32[2,512]{1,0:T(2,128)} %rows_hbm.1, s32[2,512]{1,0:T(2,128)} %cols_hbm.1, s32[1,2]{1,0:T(1,128)} %bitcast.1, bf16[2,512,4096]{2,1,0:T(8,128)(2,1)} %blocks_ref.1), custom_call_target="tpu_custom_call" | custom-call | tf_op jit(solution)/shard_map/build_dense/pallas_call | solution.py:113
  14.2 1.5 %apply_first.3.refs_0_ = f32[32,512]{1,0:T(8,128)S(1)} custom-call(bf16[2,32,512]{2,1,0:T(8,128)(2,1)S(1)} %convert_element_type.3.refs_0_, bf16[2,32,512]{2,1,0:T(8,128)(2,1)S(1)} %collective-permute-done.refs_1_, bf16[2,32,512]{2,1,0:T(8,128)(2,1)S(1)} %collective-permute-done.1.refs_2_, bf16[2,32,512]{2,1,0:T(8,128)(2,1)S(1)} %collective-permute-done.2.refs_3_, ...), custom_call_target="tpu_custom_call" | custom-call | bytes 4194304 | tf_op jit(solution)/shard_map/apply_first/pallas_call | solution.py:264
  15.7 3.8 %collective-permute-start.11 = (f32[32,512]{1,0:T(8,128)S(1)}, f32[32,512]{1,0:T(8,128)S(1)}, u32[]{:S(2)}, u32[]{:S(2)}) collective-permute-start(f32[32,512]{1,0:T(8,128)S(1)} %apply_first.3.refs_0_), channel_id=1, source_target_pairs={{3,0},{2,1},{1,2},{0,3},{7,4},{6,5},{5,6},{4,7},{11,8},{10,9},{9,1... | collective-permute-start | bytes 196616 | tf_op jit(solution)/shard_map/ppermute | solution.py:545
  20.2 1.5 %apply_first.2.refs_0_ = f32[32,512]{1,0:T(8,128)S(1)} custom-call(bf16[2,32,512]{2,1,0:T(8,128)(2,1)S(1)} %convert_element_type.3.refs_0_, bf16[2,32,512]{2,1,0:T(8,128)(2,1)S(1)} %collective-permute-done.refs_1_, bf16[2,32,512]{2,1,0:T(8,128)(2,1)S(1)} %collective-permute-done.1.refs_2_, bf16[2,32,512]{2,1,0:T(8,128)(2,1)S(1)} %collective-permute-done.2.refs_3_, ...), custom_call_target="tpu_custom_call" | custom-call | bytes 4194304 | tf_op jit(solution)/shard_map/apply_first/pallas_call | solution.py:264
  21.7 3.8 %collective-permute-start.5 = (f32[32,512]{1,0:T(8,128)S(1)}, f32[32,512]{1,0:T(8,128)S(1)}, u32[]{:S(2)}, u32[]{:S(2)}) collective-permute-start(f32[32,512]{1,0:T(8,128)S(1)} %apply_first.2.refs_0_), channel_id=1, source_target_pairs={{3,0},{2,1},{1,2},{0,3},{7,4},{6,5},{5,6},{4,7},{11,8},{10,9},{9,1... | collective-permute-start | bytes 196616 | tf_op jit(solution)/shard_map/ppermute | solution.py:545
  26.1 3.2 %apply_second.3.refs_4_ = f32[32,512]{1,0:T(8,128)S(1)} custom-call(f32[32,512]{1,0:T(8,128)S(1)} %apply_first.3.refs_0_, f32[32,512]{1,0:T(8,128)S(1)} %collective-permute-done.9.refs_1_, f32[32,512]{1,0:T(8,128)S(1)} %collective-permute-done.10.refs_2_, f32[32,512]{1,0:T(8,128)S(1)} %collective-permute-done.11.refs_3_, ...), custom_call_target="tpu_custom_call" | custom-call | bytes 4194304 | tf_op jit(solution)/shard_map/apply_second/pallas_call | solution.py:264
  29.5 1.7 %collective-permute-start.13 = (f32[32,512]{1,0:T(8,128)S(1)}, f32[32,512]{1,0:T(8,128)S(1)}, u32[]{:S(2)}, u32[]{:S(2)}) collective-permute-start(f32[32,512]{1,0:T(8,128)S(1)} %apply_second.3.refs_4_), channel_id=1, source_target_pairs={{8,0},{12,4},{0,8},{4,12},{9,1},{13,5},{1,9},{5,13},{10,2},{14,6},... | collective-permute-start | bytes 196616 | tf_op jit(solution)/shard_map/ppermute | solution.py:545
  31.3 3.2 %apply_second.2.refs_0_ = f32[32,512]{1,0:T(8,128)S(1)} custom-call(f32[32,512]{1,0:T(8,128)S(1)} %apply_first.2.refs_0_, f32[32,512]{1,0:T(8,128)S(1)} %collective-permute-done.3.refs_1_, f32[32,512]{1,0:T(8,128)S(1)} %collective-permute-done.4.refs_2_, f32[32,512]{1,0:T(8,128)S(1)} %collective-permute-done.5.refs_3_, ...), custom_call_target="tpu_custom_call" | custom-call | bytes 4194304 | tf_op jit(solution)/shard_map/apply_second/pallas_call | solution.py:264
  34.6 1.3 %collective-permute-start.8 = (f32[32,512]{1,0:T(8,128)S(1)}, f32[32,512]{1,0:T(8,128)S(1)}, u32[]{:S(2)}, u32[]{:S(2)}) collective-permute-start(f32[32,512]{1,0:T(8,128)S(1)} %apply_second.2.refs_0_), channel_id=1, source_target_pairs={{12,0},{8,4},{4,8},{0,12},{13,1},{9,5},{5,9},{1,13},{14,2},{10,6},... | collective-permute-start | bytes 196616 | tf_op jit(solution)/shard_map/ppermute | solution.py:545
  36.6 2.0 %collective-permute-done.8.refs_3_ = f32[32,512]{1,0:T(8,128)S(1)} collective-permute-done((f32[32,512]{1,0:T(8,128)S(1)}, f32[32,512]{1,0:T(8,128)S(1)}, u32[]{:S(2)}, u32[]{:S(2)}) %collective-permute-start.8) | collective-permute-done | bytes 65568 | tf_op jit(solution)/shard_map/ppermute | solution.py:545
  38.6 1.8 %collective-permute-done.7.refs_2_ = f32[32,512]{1,0:T(8,128)S(1)} collective-permute-done((f32[32,512]{1,0:T(8,128)S(1)}, f32[32,512]{1,0:T(8,128)S(1)}, u32[]{:S(2)}, u32[]{:S(2)}) %collective-permute-start.7) | collective-permute-done | bytes 65568 | tf_op jit(solution)/shard_map/ppermute | solution.py:545
  41.1 3.8 %collective-permute-start.17 = (f32[144,128]{1,0:T(8,128)S(1)}, f32[144,128]{1,0:T(8,128)S(1)}, u32[]{:S(2)}, u32[]{:S(2)}) collective-permute-start(f32[144,128]{1,0:T(8,128)S(1)} %get-tuple-element.11), channel_id=1, source_target_pairs={{3,0},{2,1},{1,2},{0,3},{7,4},{6,5},{5,6},{4,7},{11,8},{10,9},{9,1... | collective-permute-start | bytes 221192 | tf_op jit(solution)/shard_map/ppermute | solution.py:545
  45.6 2.7 %collective-permute-done.17 = f32[144,128]{1,0:T(8,128)S(1)} collective-permute-done((f32[144,128]{1,0:T(8,128)S(1)}, f32[144,128]{1,0:T(8,128)S(1)}, u32[]{:S(2)}, u32[]{:S(2)}) %collective-permute-start.17) | collective-permute-done | bytes 73760 | tf_op jit(solution)/shard_map/ppermute | solution.py:545
  48.2 2.8 %collective-permute-done.16 = f32[144,128]{1,0:T(8,128)S(1)} collective-permute-done((f32[144,128]{1,0:T(8,128)S(1)}, f32[144,128]{1,0:T(8,128)S(1)}, u32[]{:S(2)}, u32[]{:S(2)}) %collective-permute-start.16) | collective-permute-done | bytes 73760 | tf_op jit(solution)/shard_map/ppermute | solution.py:545
  52.4 10.7 %joint_solve.1 = (f32[2,32,512]{2,1,0:T(8,128)}, f32[2,32,512]{2,1,0:T(8,128)S(1)}, bf16[2,32,512]{2,1,0:T(8,128)(2,1)S(1)}) custom-call(f32[144,128]{1,0:T(8,128)S(1)} %add_add_fusion.refs_0_, f32[144,128]{1,0:T(8,128)S(1)} %collective-permute-done.18.refs_1_, f32[256,512]{1,0:T(8,128)S(1)} %get-tuple-element.12.refs_2_), custom_call_target="tpu_custom_call" | custom-call | tf_op jit(solution)/shard_map/joint_solve/pallas_call | solution.py:527
  63.1 2.4 %collective-permute-start.21 = (bf16[2,32,512]{2,1,0:T(8,128)(2,1)S(1)}, bf16[2,32,512]{2,1,0:T(8,128)(2,1)S(1)}, u32[]{:S(2)}, u32[]{:S(2)}) collective-permute-start(bf16[2,32,512]{2,1,0:T(8,128)(2,1)S(1)} %get-tuple-element.14.basis_ref), channel_id=1, source_target_pairs={{3,0},{2,1},{1,2},{0,3},{7,4},{6,5},{5,6},{4,7},{11,8},{10,9},{9,1... | collective-permute-start | bytes 196616 | tf_op jit(solution)/shard_map/ppermute | solution.py:545
  65.6 1.9 %collective-permute-start.19 = (bf16[2,32,512]{2,1,0:T(8,128)(2,1)S(1)}, bf16[2,32,512]{2,1,0:T(8,128)(2,1)S(1)}, u32[]{:S(2)}, u32[]{:S(2)}) collective-permute-start(bf16[2,32,512]{2,1,0:T(8,128)(2,1)S(1)} %get-tuple-element.14.basis_ref), channel_id=1, source_target_pairs={{1,0},{0,1},{3,2},{2,3},{5,4},{4,5},{7,6},{6,7},{9,8},{8,9},{11,10... | collective-permute-start | bytes 196616 | tf_op jit(solution)/shard_map/ppermute | solution.py:545
  68.3 1.6 %collective-permute-done.21.refs_2_ = bf16[2,32,512]{2,1,0:T(8,128)(2,1)S(1)} collective-permute-done((bf16[2,32,512]{2,1,0:T(8,128)(2,1)S(1)}, bf16[2,32,512]{2,1,0:T(8,128)(2,1)S(1)}, u32[]{:S(2)}, u32[]{:S(2)}) %collective-permute-start.21) | collective-permute-done | bytes 65568 | tf_op jit(solution)/shard_map/ppermute | solution.py:545
  69.9 2.2 %collective-permute-done.20.refs_1_ = bf16[2,32,512]{2,1,0:T(8,128)(2,1)S(1)} collective-permute-done((bf16[2,32,512]{2,1,0:T(8,128)(2,1)S(1)}, bf16[2,32,512]{2,1,0:T(8,128)(2,1)S(1)}, u32[]{:S(2)}, u32[]{:S(2)}) %collective-permute-start.20) | collective-permute-done | bytes 65568 | tf_op jit(solution)/shard_map/ppermute | solution.py:545
  72.1 2.5 %apply_score.1 = f32[2,32,32]{2,1,0:T(8,128)S(1)} custom-call(f32[2,512,64]{2,1,0:T(8,128)S(1)} %apply_own.1.own_ref, bf16[2,32,512]{2,1,0:T(8,128)(2,1)S(1)} %collective-permute-done.19.refs_0_, bf16[2,32,512]{2,1,0:T(8,128)(2,1)S(1)} %collective-permute-done.20.refs_1_, bf16[2,32,512]{2,1,0:T(8,128)(2,1)S(1)} %collective-permute-done.21.refs_2_, ...), custom_call_target="tpu_custom_call" | custom-call | bytes 4194304 | tf_op jit(solution)/shard_map/apply_score/pallas_call | solution.py:264
  74.6 2.2 %collective-permute-start.24 = (f32[2,32,32]{2,1,0:T(8,128)S(1)}, f32[2,32,32]{2,1,0:T(8,128)S(1)}, u32[]{:S(2)}, u32[]{:S(2)}) collective-permute-start(f32[2,32,32]{2,1,0:T(8,128)S(1)} %apply_score.1), channel_id=1, source_target_pairs={{3,0},{2,1},{1,2},{0,3},{7,4},{6,5},{5,6},{4,7},{11,8},{10,9},{9,1... | collective-permute-start | bytes 24584 | tf_op jit(solution)/shard_map/ppermute | solution.py:545
  76.8 2.2 %collective-permute-start.22 = (f32[2,32,32]{2,1,0:T(8,128)S(1)}, f32[2,32,32]{2,1,0:T(8,128)S(1)}, u32[]{:S(2)}, u32[]{:S(2)}) collective-permute-start(f32[2,32,32]{2,1,0:T(8,128)S(1)} %apply_score.1), channel_id=1, source_target_pairs={{1,0},{0,1},{3,2},{2,3},{5,4},{4,5},{7,6},{6,7},{9,8},{8,9},{11,10... | collective-permute-start | bytes 24584 | tf_op jit(solution)/shard_map/ppermute | solution.py:545
  79.0 1.4 %collective-permute-done.24 = f32[2,32,32]{2,1,0:T(8,128)S(1)} collective-permute-done((f32[2,32,32]{2,1,0:T(8,128)S(1)}, f32[2,32,32]{2,1,0:T(8,128)S(1)}, u32[]{:S(2)}, u32[]{:S(2)}) %collective-permute-start.24) | collective-permute-done | bytes 8224 | tf_op jit(solution)/shard_map/ppermute | solution.py:545
  (38 shorter events, 9.3 us)
Async XLA Ops:
  1.5 12.6 %collective-permute-start.2 = (bf16[2,32,512]{2,1,0:T(8,128)(2,1)S(1)}, bf16[2,32,512]{2,1,0:T(8,128)(2,1)S(1)}, u32[]{:S(2)}, u32[]{:S(2)}) collective-permute-start(bf16[2,32,512]{2,1,0:T(8,128)(2,1)S(1)} %convert_element_type.3.refs_0_), channel_id=1, source_target_pairs={{3,0},{2,1},{1,2},{0,3},{7,4},{6,5},{5,6},{4,7},{11,8},{10,9},{9,1... | collective-permute-start | bytes 196616 | tf_op jit(solution)/shard_map/ppermute | solution.py:545
  6.7 7.5 %collective-permute-start.1 = (bf16[2,32,512]{2,1,0:T(8,128)(2,1)S(1)}, bf16[2,32,512]{2,1,0:T(8,128)(2,1)S(1)}, u32[]{:S(2)}, u32[]{:S(2)}) collective-permute-start(bf16[2,32,512]{2,1,0:T(8,128)(2,1)S(1)} %convert_element_type.3.refs_0_), channel_id=1, source_target_pairs={{2,0},{3,1},{0,2},{1,3},{6,4},{7,5},{4,6},{5,7},{10,8},{11,9},{8,1... | collective-permute-start | bytes 196616 | tf_op jit(solution)/shard_map/ppermute | solution.py:545
  6.7 7.5 %collective-permute-start = (bf16[2,32,512]{2,1,0:T(8,128)(2,1)S(1)}, bf16[2,32,512]{2,1,0:T(8,128)(2,1)S(1)}, u32[]{:S(2)}, u32[]{:S(2)}) collective-permute-start(bf16[2,32,512]{2,1,0:T(8,128)(2,1)S(1)} %convert_element_type.3.refs_0_), channel_id=1, source_target_pairs={{1,0},{0,1},{3,2},{2,3},{5,4},{4,5},{7,6},{6,7},{9,8},{8,9},{11,10... | collective-permute-start | bytes 196616 | tf_op jit(solution)/shard_map/ppermute | solution.py:545
  15.7 9.8 %collective-permute-start.11 = (f32[32,512]{1,0:T(8,128)S(1)}, f32[32,512]{1,0:T(8,128)S(1)}, u32[]{:S(2)}, u32[]{:S(2)}) collective-permute-start(f32[32,512]{1,0:T(8,128)S(1)} %apply_first.3.refs_0_), channel_id=1, source_target_pairs={{3,0},{2,1},{1,2},{0,3},{7,4},{6,5},{5,6},{4,7},{11,8},{10,9},{9,1... | collective-permute-start | bytes 196616 | tf_op jit(solution)/shard_map/ppermute | solution.py:545
  19.5 6.6 %collective-permute-start.10 = (f32[32,512]{1,0:T(8,128)S(1)}, f32[32,512]{1,0:T(8,128)S(1)}, u32[]{:S(2)}, u32[]{:S(2)}) collective-permute-start(f32[32,512]{1,0:T(8,128)S(1)} %apply_first.3.refs_0_), channel_id=1, source_target_pairs={{2,0},{3,1},{0,2},{1,3},{6,4},{7,5},{4,6},{5,7},{10,8},{11,9},{8,1... | collective-permute-start | bytes 196616 | tf_op jit(solution)/shard_map/ppermute | solution.py:545
  19.5 6.6 %collective-permute-start.9 = (f32[32,512]{1,0:T(8,128)S(1)}, f32[32,512]{1,0:T(8,128)S(1)}, u32[]{:S(2)}, u32[]{:S(2)}) collective-permute-start(f32[32,512]{1,0:T(8,128)S(1)} %apply_first.3.refs_0_), channel_id=1, source_target_pairs={{1,0},{0,1},{3,2},{2,3},{5,4},{4,5},{7,6},{6,7},{9,8},{8,9},{11,10... | collective-permute-start | bytes 196616 | tf_op jit(solution)/shard_map/ppermute | solution.py:545
  21.7 9.5 %collective-permute-start.5 = (f32[32,512]{1,0:T(8,128)S(1)}, f32[32,512]{1,0:T(8,128)S(1)}, u32[]{:S(2)}, u32[]{:S(2)}) collective-permute-start(f32[32,512]{1,0:T(8,128)S(1)} %apply_first.2.refs_0_), channel_id=1, source_target_pairs={{3,0},{2,1},{1,2},{0,3},{7,4},{6,5},{5,6},{4,7},{11,8},{10,9},{9,1... | collective-permute-start | bytes 196616 | tf_op jit(solution)/shard_map/ppermute | solution.py:545
  25.5 5.8 %collective-permute-start.4 = (f32[32,512]{1,0:T(8,128)S(1)}, f32[32,512]{1,0:T(8,128)S(1)}, u32[]{:S(2)}, u32[]{:S(2)}) collective-permute-start(f32[32,512]{1,0:T(8,128)S(1)} %apply_first.2.refs_0_), channel_id=1, source_target_pairs={{2,0},{3,1},{0,2},{1,3},{6,4},{7,5},{4,6},{5,7},{10,8},{11,9},{8,1... | collective-permute-start | bytes 196616 | tf_op jit(solution)/shard_map/ppermute | solution.py:545
  25.5 5.8 %collective-permute-start.3 = (f32[32,512]{1,0:T(8,128)S(1)}, f32[32,512]{1,0:T(8,128)S(1)}, u32[]{:S(2)}, u32[]{:S(2)}) collective-permute-start(f32[32,512]{1,0:T(8,128)S(1)} %apply_first.2.refs_0_), channel_id=1, source_target_pairs={{1,0},{0,1},{3,2},{2,3},{5,4},{4,5},{7,6},{6,7},{9,8},{8,9},{11,10... | collective-permute-start | bytes 196616 | tf_op jit(solution)/shard_map/ppermute | solution.py:545
  29.4 7.2 %collective-permute-start.14 = (f32[32,512]{1,0:T(8,128)S(1)}, f32[32,512]{1,0:T(8,128)S(1)}, u32[]{:S(2)}, u32[]{:S(2)}) collective-permute-start(f32[32,512]{1,0:T(8,128)S(1)} %apply_second.3.refs_4_), channel_id=1, source_target_pairs={{12,0},{8,4},{4,8},{0,12},{13,1},{9,5},{5,9},{1,13},{14,2},{10,6},... | collective-permute-start | bytes 196616 | tf_op jit(solution)/shard_map/ppermute | solution.py:545
  29.5 7.1 %collective-permute-start.13 = (f32[32,512]{1,0:T(8,128)S(1)}, f32[32,512]{1,0:T(8,128)S(1)}, u32[]{:S(2)}, u32[]{:S(2)}) collective-permute-start(f32[32,512]{1,0:T(8,128)S(1)} %apply_second.3.refs_4_), channel_id=1, source_target_pairs={{8,0},{12,4},{0,8},{4,12},{9,1},{13,5},{1,9},{5,13},{10,2},{14,6},... | collective-permute-start | bytes 196616 | tf_op jit(solution)/shard_map/ppermute | solution.py:545
  31.1 5.5 %collective-permute-start.12 = (f32[32,512]{1,0:T(8,128)S(1)}, f32[32,512]{1,0:T(8,128)S(1)}, u32[]{:S(2)}, u32[]{:S(2)}) collective-permute-start(f32[32,512]{1,0:T(8,128)S(1)} %apply_second.3.refs_4_), channel_id=1, source_target_pairs={{4,0},{0,4},{12,8},{8,12},{5,1},{1,5},{13,9},{9,13},{6,2},{2,6},{1... | collective-permute-start | bytes 196616 | tf_op jit(solution)/shard_map/ppermute | solution.py:545
  34.6 4.0 %collective-permute-start.8 = (f32[32,512]{1,0:T(8,128)S(1)}, f32[32,512]{1,0:T(8,128)S(1)}, u32[]{:S(2)}, u32[]{:S(2)}) collective-permute-start(f32[32,512]{1,0:T(8,128)S(1)} %apply_second.2.refs_0_), channel_id=1, source_target_pairs={{12,0},{8,4},{4,8},{0,12},{13,1},{9,5},{5,9},{1,13},{14,2},{10,6},... | collective-permute-start | bytes 196616 | tf_op jit(solution)/shard_map/ppermute | solution.py:545
  35.9 4.6 %collective-permute-start.7 = (f32[32,512]{1,0:T(8,128)S(1)}, f32[32,512]{1,0:T(8,128)S(1)}, u32[]{:S(2)}, u32[]{:S(2)}) collective-permute-start(f32[32,512]{1,0:T(8,128)S(1)} %apply_second.2.refs_0_), channel_id=1, source_target_pairs={{8,0},{12,4},{0,8},{4,12},{9,1},{13,5},{1,9},{5,13},{10,2},{14,6},... | collective-permute-start | bytes 196616 | tf_op jit(solution)/shard_map/ppermute | solution.py:545
  36.6 3.8 %collective-permute-start.6 = (f32[32,512]{1,0:T(8,128)S(1)}, f32[32,512]{1,0:T(8,128)S(1)}, u32[]{:S(2)}, u32[]{:S(2)}) collective-permute-start(f32[32,512]{1,0:T(8,128)S(1)} %apply_second.2.refs_0_), channel_id=1, source_target_pairs={{4,0},{0,4},{12,8},{8,12},{5,1},{1,5},{13,9},{9,13},{6,2},{2,6},{1... | collective-permute-start | bytes 196616 | tf_op jit(solution)/shard_map/ppermute | solution.py:545
  41.1 7.1 %collective-permute-start.17 = (f32[144,128]{1,0:T(8,128)S(1)}, f32[144,128]{1,0:T(8,128)S(1)}, u32[]{:S(2)}, u32[]{:S(2)}) collective-permute-start(f32[144,128]{1,0:T(8,128)S(1)} %get-tuple-element.11), channel_id=1, source_target_pairs={{3,0},{2,1},{1,2},{0,3},{7,4},{6,5},{5,6},{4,7},{11,8},{10,9},{9,1... | collective-permute-start | bytes 221192 | tf_op jit(solution)/shard_map/ppermute | solution.py:545
  44.9 6.2 %collective-permute-start.16 = (f32[144,128]{1,0:T(8,128)S(1)}, f32[144,128]{1,0:T(8,128)S(1)}, u32[]{:S(2)}, u32[]{:S(2)}) collective-permute-start(f32[144,128]{1,0:T(8,128)S(1)} %get-tuple-element.11), channel_id=1, source_target_pairs={{2,0},{3,1},{0,2},{1,3},{6,4},{7,5},{4,6},{5,7},{10,8},{11,9},{8,1... | collective-permute-start | bytes 221192 | tf_op jit(solution)/shard_map/ppermute | solution.py:545
  44.9 6.2 %collective-permute-start.15 = (f32[144,128]{1,0:T(8,128)S(1)}, f32[144,128]{1,0:T(8,128)S(1)}, u32[]{:S(2)}, u32[]{:S(2)}) collective-permute-start(f32[144,128]{1,0:T(8,128)S(1)} %get-tuple-element.11), channel_id=1, source_target_pairs={{1,0},{0,1},{3,2},{2,3},{5,4},{4,5},{7,6},{6,7},{9,8},{8,9},{11,10... | collective-permute-start | bytes 221192 | tf_op jit(solution)/shard_map/ppermute | solution.py:545
  63.1 6.8 %collective-permute-start.21 = (bf16[2,32,512]{2,1,0:T(8,128)(2,1)S(1)}, bf16[2,32,512]{2,1,0:T(8,128)(2,1)S(1)}, u32[]{:S(2)}, u32[]{:S(2)}) collective-permute-start(bf16[2,32,512]{2,1,0:T(8,128)(2,1)S(1)} %get-tuple-element.14.basis_ref), channel_id=1, source_target_pairs={{3,0},{2,1},{1,2},{0,3},{7,4},{6,5},{5,6},{4,7},{11,8},{10,9},{9,1... | collective-permute-start | bytes 196616 | tf_op jit(solution)/shard_map/ppermute | solution.py:545
  65.5 6.6 %collective-permute-start.20 = (bf16[2,32,512]{2,1,0:T(8,128)(2,1)S(1)}, bf16[2,32,512]{2,1,0:T(8,128)(2,1)S(1)}, u32[]{:S(2)}, u32[]{:S(2)}) collective-permute-start(bf16[2,32,512]{2,1,0:T(8,128)(2,1)S(1)} %get-tuple-element.14.basis_ref), channel_id=1, source_target_pairs={{2,0},{3,1},{0,2},{1,3},{6,4},{7,5},{4,6},{5,7},{10,8},{11,9},{8,1... | collective-permute-start | bytes 196616 | tf_op jit(solution)/shard_map/ppermute | solution.py:545
  65.6 6.5 %collective-permute-start.19 = (bf16[2,32,512]{2,1,0:T(8,128)(2,1)S(1)}, bf16[2,32,512]{2,1,0:T(8,128)(2,1)S(1)}, u32[]{:S(2)}, u32[]{:S(2)}) collective-permute-start(bf16[2,32,512]{2,1,0:T(8,128)(2,1)S(1)} %get-tuple-element.14.basis_ref), channel_id=1, source_target_pairs={{1,0},{0,1},{3,2},{2,3},{5,4},{4,5},{7,6},{6,7},{9,8},{8,9},{11,10... | collective-permute-start | bytes 196616 | tf_op jit(solution)/shard_map/ppermute | solution.py:545
  74.6 5.8 %collective-permute-start.24 = (f32[2,32,32]{2,1,0:T(8,128)S(1)}, f32[2,32,32]{2,1,0:T(8,128)S(1)}, u32[]{:S(2)}, u32[]{:S(2)}) collective-permute-start(f32[2,32,32]{2,1,0:T(8,128)S(1)} %apply_score.1), channel_id=1, source_target_pairs={{3,0},{2,1},{1,2},{0,3},{7,4},{6,5},{5,6},{4,7},{11,8},{10,9},{9,1... | collective-permute-start | bytes 24584 | tf_op jit(solution)/shard_map/ppermute | solution.py:545
  76.8 4.8 %collective-permute-start.23 = (f32[2,32,32]{2,1,0:T(8,128)S(1)}, f32[2,32,32]{2,1,0:T(8,128)S(1)}, u32[]{:S(2)}, u32[]{:S(2)}) collective-permute-start(f32[2,32,32]{2,1,0:T(8,128)S(1)} %apply_score.1), channel_id=1, source_target_pairs={{2,0},{3,1},{0,2},{1,3},{6,4},{7,5},{4,6},{5,7},{10,8},{11,9},{8,1... | collective-permute-start | bytes 24584 | tf_op jit(solution)/shard_map/ppermute | solution.py:545
  76.8 4.8 %collective-permute-start.22 = (f32[2,32,32]{2,1,0:T(8,128)S(1)}, f32[2,32,32]{2,1,0:T(8,128)S(1)}, u32[]{:S(2)}, u32[]{:S(2)}) collective-permute-start(f32[2,32,32]{2,1,0:T(8,128)S(1)} %apply_score.1), channel_id=1, source_target_pairs={{1,0},{0,1},{3,2},{2,3},{5,4},{4,5},{7,6},{6,7},{9,8},{8,9},{11,10... | collective-permute-start | bytes 24584 | tf_op jit(solution)/shard_map/ppermute | solution.py:545
  (1 other events, 1.3 us)

commit v11 on v9

--- a/solution.py
+++ b/solution.py
@@ -351,13 +351,21 @@
             n = m + 1
             a, b, c = cell[m, m], cell[m, n], cell[n, n]
             det = a * c - b * b
-            r = pl.reciprocal(det, approx=True)
+            if m % 4 == 0:
+                r = pl.reciprocal(det, approx=True)
+            else:
+                r = square * pl.reciprocal(whole, approx=True)
             later = range(m + 2, 8)
             u = {q: c * cell[m, q] - b * cell[n, q] for q in later}
             v = {q: a * cell[n, q] - b * cell[m, q] for q in later}
-            for q in later:
-                for p in range(m + 2, q + 1):
-                    cell[p, q] = cell[p, q] - r * (cell[m, p] * u[q] + cell[n, p] * v[q])
+            taken = {(p, q): cell[m, p] * u[q] + cell[n, p] * v[q] for q in later for p in range(m + 2, q + 1)}
+            if m % 4 == 0:
+                i, j = m + 2, m + 3
+                first, cross, last = (det * cell[pq] - taken[pq] for pq in ((i, i), (i, j), (j, j)))
+                whole = first * last - cross * cross
+                square = det * det
+            for pq in taken:
+                cell[pq] = cell[pq] - r * taken[pq]
             for q in later:
                 for g in below:
                     col[q][g] = col[q][g] - r * (col[m][g] * u[q] + col[n][g] * v[q])
@@ -490,11 +498,10 @@
     mixed = packed[half : 2 * half]
     under = jnp.where(col < row, mixed, 0.0)
     diagonal = jnp.concatenate([packed[2 * half :]] * (half // k), axis=0)
-    over = jnp.where(col > row, mixed, 0.0)
-    work[:half, :half] = jnp.where(col >= row, mixed, over.T)
+    work[:half, :half] = jnp.where(col >= row, mixed, 0.0)
     work[:half, half:] = packed[:half]
     work[half:, :half] = jnp.zeros((half, half), F32)
-    work[half:, half:] = under + under.T + jnp.where(col == row, diagonal, 0.0)
+    work[half:, half:] = under.T + jnp.where(col == row, diagonal, 0.0)
 
 
 def joint_kernel(k, *refs):
@@ -505,15 +512,14 @@
     packed[pl.ds(pl.multiple_of((1 - odd) * rows, 16), rows)] = other_ref[...]
     unpack(packed[...], k, work)
     size = work.shape[0]
-    band = 2 * k
-    steps = size // band
-    lane = lax.broadcasted_iota(jnp.int32, (band, size), 1)
-    lane_128 = lax.broadcasted_iota(jnp.int32, (band, 128), 1)
-    sub_128 = lax.broadcasted_iota(jnp.int32, (band, 128), 0)
+    steps = size // k
+    lane = lax.broadcasted_iota(jnp.int32, (k, size), 1)
+    lane_128 = lax.broadcasted_iota(jnp.int32, (k, 128), 1)
+    sub_128 = lax.broadcasted_iota(jnp.int32, (k, 128), 0)
     gram, across = unit_scale(work[...])
     work[...] = gram
     for s in range(steps):
-        lo, hi = s * band, (s + 1) * band
+        lo, hi = s * k, (s + 1) * k
         here = (lane >= lo) & (lane < hi)
         eye = jnp.where(lane_128 == sub_128 + lo % 128, 1.0, 0.0)
         solved = joined(eliminate(tiled(jnp.concatenate([work[lo:hi], eye], axis=1)), lo))
@@ -523,8 +529,8 @@
         if s + 1 < steps:
             update = gram_update(panel, hi // 128 * 128)
             for r in range(s + 1, steps):
-                rows = work[r * band : r * band + band]
-                work[r * band : r * band + band] = jnp.where(here, 0.0, rows) - update(r * band, band)
+                rows = work[r * k : r * k + k]
+                work[r * k : r * k + k] = jnp.where(here, 0.0, rows) - update(r * k, k)
     rows = out_ref.shape[0] * k
     own = work[pl.ds(pl.multiple_of(lax.axis_index("layer") * rows, rows), rows)] * across
     joint = jnp.dot(own, images_ref[...], precision=HIGHEST, preferred_element_type=F32)

time: 82 us -> 81.3 us (level)
  no operation moved by 1% of the time
where the time goes in v11:
time: 81.3 us; the launch traced here: 81.2 us
  starting transfers between devices  32 us (39%)
  Pallas kernels  29.9 us (37%)
  waiting for transfers between devices  17 us (21%)
  other arithmetic  1.56 us (2%)
    ppermute x24, starting transfers between devices, around(): pieces.append(lax.ppermute(x, axis, [(m ^ d, m) for m in range(count)]))  31.9 us
    ppermute x24, waiting for transfers between devices, around(): pieces.append(lax.ppermute(x, axis, [(m ^ d, m) for m in range(count)]))  15.8 us
    pallas_call x5, Pallas kernels, apply_whole(): pl.pallas_call(kernel, in_specs=vmem_specs(len(operands)), out_specs=pl.B...  12 us
    pallas_call x1, Pallas kernels, joint_solve(): pl.pallas_call(functools.partial(joint_kernel, k), in_specs=vmem_specs(3)...  9.62 us
    pallas_call x1, Pallas kernels, build_dense(): pl.pallas_call(build_whole_kernel, in_specs=[pl.BlockSpec(memory_space=pl...  6.83 us
  transfers between devices with their start and end apart: 25, of which 9 were waited for; matrix products, arithmetic and copies ran while one was open for 0% of the time, Pallas kernels for 19%

profile of v11, /device:TPU:0, one launch (start us, length us, event | category | flops | bytes accessed | tf_op | source)
XLA Modules:
  0.0 81.2 jit_solution(1492417231507972660)
XLA Ops:
  1.5 5.1 %collective-permute-start.2 = (bf16[2,32,512]{2,1,0:T(8,128)(2,1)S(1)}, bf16[2,32,512]{2,1,0:T(8,128)(2,1)S(1)}, u32[]{:S(2)}, u32[]{:S(2)}) collective-permute-start(bf16[2,32,512]{2,1,0:T(8,128)(2,1)S(1)} %convert_element_type.3.refs_0_), channel_id=1, source_target_pairs={{3,0},{2,1},{1,2},{0,3},{7,4},{6,5},{5,6},{4,7},{11,8},{10,9},{9,1... | collective-permute-start | bytes 196616 | tf_op jit(solution)/shard_map/ppermute | solution.py:564
  7.3 6.8 %build_dense.1 = (bf16[4,512,1024]{2,1,0:T(8,128)(2,1)S(1)}, bf16[4,512,1024]{2,1,0:T(8,128)(2,1)S(1)}) custom-call(s32[2,512]{1,0:T(2,128)} %rows_hbm.1, s32[2,512]{1,0:T(2,128)} %cols_hbm.1, s32[1,2]{1,0:T(1,128)} %bitcast.1, bf16[2,512,4096]{2,1,0:T(8,128)(2,1)} %blocks_ref.1), custom_call_target="tpu_custom_call" | custom-call | tf_op jit(solution)/shard_map/build_dense/pallas_call | solution.py:113
  14.2 1.5 %apply_first.3.refs_0_ = f32[32,512]{1,0:T(8,128)S(1)} custom-call(bf16[2,32,512]{2,1,0:T(8,128)(2,1)S(1)} %convert_element_type.3.refs_0_, bf16[2,32,512]{2,1,0:T(8,128)(2,1)S(1)} %collective-permute-done.refs_1_, bf16[2,32,512]{2,1,0:T(8,128)(2,1)S(1)} %collective-permute-done.1.refs_2_, bf16[2,32,512]{2,1,0:T(8,128)(2,1)S(1)} %collective-permute-done.2.refs_3_, ...), custom_call_target="tpu_custom_call" | custom-call | bytes 4194304 | tf_op jit(solution)/shard_map/apply_first/pallas_call | solution.py:265
  15.7 3.8 %collective-permute-start.11 = (f32[32,512]{1,0:T(8,128)S(1)}, f32[32,512]{1,0:T(8,128)S(1)}, u32[]{:S(2)}, u32[]{:S(2)}) collective-permute-start(f32[32,512]{1,0:T(8,128)S(1)} %apply_first.3.refs_0_), channel_id=1, source_target_pairs={{3,0},{2,1},{1,2},{0,3},{7,4},{6,5},{5,6},{4,7},{11,8},{10,9},{9,1... | collective-permute-start | bytes 196616 | tf_op jit(solution)/shard_map/ppermute | solution.py:564
  20.2 1.5 %apply_first.2.refs_0_ = f32[32,512]{1,0:T(8,128)S(1)} custom-call(bf16[2,32,512]{2,1,0:T(8,128)(2,1)S(1)} %convert_element_type.3.refs_0_, bf16[2,32,512]{2,1,0:T(8,128)(2,1)S(1)} %collective-permute-done.refs_1_, bf16[2,32,512]{2,1,0:T(8,128)(2,1)S(1)} %collective-permute-done.1.refs_2_, bf16[2,32,512]{2,1,0:T(8,128)(2,1)S(1)} %collective-permute-done.2.refs_3_, ...), custom_call_target="tpu_custom_call" | custom-call | bytes 4194304 | tf_op jit(solution)/shard_map/apply_first/pallas_call | solution.py:265
  21.7 3.8 %collective-permute-start.5 = (f32[32,512]{1,0:T(8,128)S(1)}, f32[32,512]{1,0:T(8,128)S(1)}, u32[]{:S(2)}, u32[]{:S(2)}) collective-permute-start(f32[32,512]{1,0:T(8,128)S(1)} %apply_first.2.refs_0_), channel_id=1, source_target_pairs={{3,0},{2,1},{1,2},{0,3},{7,4},{6,5},{5,6},{4,7},{11,8},{10,9},{9,1... | collective-permute-start | bytes 196616 | tf_op jit(solution)/shard_map/ppermute | solution.py:564
  26.1 3.2 %apply_second.3.refs_4_ = f32[32,512]{1,0:T(8,128)S(1)} custom-call(f32[32,512]{1,0:T(8,128)S(1)} %apply_first.3.refs_0_, f32[32,512]{1,0:T(8,128)S(1)} %collective-permute-done.9.refs_1_, f32[32,512]{1,0:T(8,128)S(1)} %collective-permute-done.10.refs_2_, f32[32,512]{1,0:T(8,128)S(1)} %collective-permute-done.11.refs_3_, ...), custom_call_target="tpu_custom_call" | custom-call | bytes 4194304 | tf_op jit(solution)/shard_map/apply_second/pallas_call | solution.py:265
  29.4 1.7 %collective-permute-start.13 = (f32[32,512]{1,0:T(8,128)S(1)}, f32[32,512]{1,0:T(8,128)S(1)}, u32[]{:S(2)}, u32[]{:S(2)}) collective-permute-start(f32[32,512]{1,0:T(8,128)S(1)} %apply_second.3.refs_4_), channel_id=1, source_target_pairs={{8,0},{12,4},{0,8},{4,12},{9,1},{13,5},{1,9},{5,13},{10,2},{14,6},... | collective-permute-start | bytes 196616 | tf_op jit(solution)/shard_map/ppermute | solution.py:564
  31.3 3.2 %apply_second.2.refs_0_ = f32[32,512]{1,0:T(8,128)S(1)} custom-call(f32[32,512]{1,0:T(8,128)S(1)} %apply_first.2.refs_0_, f32[32,512]{1,0:T(8,128)S(1)} %collective-permute-done.3.refs_1_, f32[32,512]{1,0:T(8,128)S(1)} %collective-permute-done.4.refs_2_, f32[32,512]{1,0:T(8,128)S(1)} %collective-permute-done.5.refs_3_, ...), custom_call_target="tpu_custom_call" | custom-call | bytes 4194304 | tf_op jit(solution)/shard_map/apply_second/pallas_call | solution.py:265
  34.5 1.3 %collective-permute-start.8 = (f32[32,512]{1,0:T(8,128)S(1)}, f32[32,512]{1,0:T(8,128)S(1)}, u32[]{:S(2)}, u32[]{:S(2)}) collective-permute-start(f32[32,512]{1,0:T(8,128)S(1)} %apply_second.2.refs_0_), channel_id=1, source_target_pairs={{12,0},{8,4},{4,8},{0,12},{13,1},{9,5},{5,9},{1,13},{14,2},{10,6},... | collective-permute-start | bytes 196616 | tf_op jit(solution)/shard_map/ppermute | solution.py:564
  36.6 1.9 %collective-permute-done.8.refs_3_ = f32[32,512]{1,0:T(8,128)S(1)} collective-permute-done((f32[32,512]{1,0:T(8,128)S(1)}, f32[32,512]{1,0:T(8,128)S(1)}, u32[]{:S(2)}, u32[]{:S(2)}) %collective-permute-start.8) | collective-permute-done | bytes 65568 | tf_op jit(solution)/shard_map/ppermute | solution.py:564
  38.5 1.9 %collective-permute-done.7.refs_2_ = f32[32,512]{1,0:T(8,128)S(1)} collective-permute-done((f32[32,512]{1,0:T(8,128)S(1)}, f32[32,512]{1,0:T(8,128)S(1)}, u32[]{:S(2)}, u32[]{:S(2)}) %collective-permute-start.7) | collective-permute-done | bytes 65568 | tf_op jit(solution)/shard_map/ppermute | solution.py:564
  41.1 3.8 %collective-permute-start.17 = (f32[144,128]{1,0:T(8,128)S(1)}, f32[144,128]{1,0:T(8,128)S(1)}, u32[]{:S(2)}, u32[]{:S(2)}) collective-permute-start(f32[144,128]{1,0:T(8,128)S(1)} %get-tuple-element.11), channel_id=1, source_target_pairs={{3,0},{2,1},{1,2},{0,3},{7,4},{6,5},{5,6},{4,7},{11,8},{10,9},{9,1... | collective-permute-start | bytes 221192 | tf_op jit(solution)/shard_map/ppermute | solution.py:564
  45.5 2.7 %collective-permute-done.17 = f32[144,128]{1,0:T(8,128)S(1)} collective-permute-done((f32[144,128]{1,0:T(8,128)S(1)}, f32[144,128]{1,0:T(8,128)S(1)}, u32[]{:S(2)}, u32[]{:S(2)}) %collective-permute-start.17) | collective-permute-done | bytes 73760 | tf_op jit(solution)/shard_map/ppermute | solution.py:564
  48.2 2.8 %collective-permute-done.16 = f32[144,128]{1,0:T(8,128)S(1)} collective-permute-done((f32[144,128]{1,0:T(8,128)S(1)}, f32[144,128]{1,0:T(8,128)S(1)}, u32[]{:S(2)}, u32[]{:S(2)}) %collective-permute-start.16) | collective-permute-done | bytes 73760 | tf_op jit(solution)/shard_map/ppermute | solution.py:564
  52.4 9.6 %joint_solve.1 = (f32[2,32,512]{2,1,0:T(8,128)}, f32[2,32,512]{2,1,0:T(8,128)S(1)}, bf16[2,32,512]{2,1,0:T(8,128)(2,1)S(1)}) custom-call(f32[144,128]{1,0:T(8,128)S(1)} %add_add_fusion.refs_0_, f32[144,128]{1,0:T(8,128)S(1)} %collective-permute-done.18.refs_1_, f32[256,512]{1,0:T(8,128)S(1)} %get-tuple-element.12.refs_2_), custom_call_target="tpu_custom_call" | custom-call | tf_op jit(solution)/shard_map/joint_solve/pallas_call | solution.py:546
  62.0 2.4 %collective-permute-start.21 = (bf16[2,32,512]{2,1,0:T(8,128)(2,1)S(1)}, bf16[2,32,512]{2,1,0:T(8,128)(2,1)S(1)}, u32[]{:S(2)}, u32[]{:S(2)}) collective-permute-start(bf16[2,32,512]{2,1,0:T(8,128)(2,1)S(1)} %get-tuple-element.14.basis_ref), channel_id=1, source_target_pairs={{3,0},{2,1},{1,2},{0,3},{7,4},{6,5},{5,6},{4,7},{11,8},{10,9},{9,1... | collective-permute-start | bytes 196616 | tf_op jit(solution)/shard_map/ppermute | solution.py:564
  64.5 1.9 %collective-permute-start.19 = (bf16[2,32,512]{2,1,0:T(8,128)(2,1)S(1)}, bf16[2,32,512]{2,1,0:T(8,128)(2,1)S(1)}, u32[]{:S(2)}, u32[]{:S(2)}) collective-permute-start(bf16[2,32,512]{2,1,0:T(8,128)(2,1)S(1)} %get-tuple-element.14.basis_ref), channel_id=1, source_target_pairs={{1,0},{0,1},{3,2},{2,3},{5,4},{4,5},{7,6},{6,7},{9,8},{8,9},{11,10... | collective-permute-start | bytes 196616 | tf_op jit(solution)/shard_map/ppermute | solution.py:564
  67.2 1.6 %collective-permute-done.21.refs_2_ = bf16[2,32,512]{2,1,0:T(8,128)(2,1)S(1)} collective-permute-done((bf16[2,32,512]{2,1,0:T(8,128)(2,1)S(1)}, bf16[2,32,512]{2,1,0:T(8,128)(2,1)S(1)}, u32[]{:S(2)}, u32[]{:S(2)}) %collective-permute-start.21) | collective-permute-done | bytes 65568 | tf_op jit(solution)/shard_map/ppermute | solution.py:564
  68.8 2.2 %collective-permute-done.20.refs_1_ = bf16[2,32,512]{2,1,0:T(8,128)(2,1)S(1)} collective-permute-done((bf16[2,32,512]{2,1,0:T(8,128)(2,1)S(1)}, bf16[2,32,512]{2,1,0:T(8,128)(2,1)S(1)}, u32[]{:S(2)}, u32[]{:S(2)}) %collective-permute-start.20) | collective-permute-done | bytes 65568 | tf_op jit(solution)/shard_map/ppermute | solution.py:564
  71.0 2.5 %apply_score.1 = f32[2,32,32]{2,1,0:T(8,128)S(1)} custom-call(f32[2,512,64]{2,1,0:T(8,128)S(1)} %apply_own.1.own_ref, bf16[2,32,512]{2,1,0:T(8,128)(2,1)S(1)} %collective-permute-done.19.refs_0_, bf16[2,32,512]{2,1,0:T(8,128)(2,1)S(1)} %collective-permute-done.20.refs_1_, bf16[2,32,512]{2,1,0:T(8,128)(2,1)S(1)} %collective-permute-done.21.refs_2_, ...), custom_call_target="tpu_custom_call" | custom-call | bytes 4194304 | tf_op jit(solution)/shard_map/apply_score/pallas_call | solution.py:265
  73.5 2.2 %collective-permute-start.24 = (f32[2,32,32]{2,1,0:T(8,128)S(1)}, f32[2,32,32]{2,1,0:T(8,128)S(1)}, u32[]{:S(2)}, u32[]{:S(2)}) collective-permute-start(f32[2,32,32]{2,1,0:T(8,128)S(1)} %apply_score.1), channel_id=1, source_target_pairs={{3,0},{2,1},{1,2},{0,3},{7,4},{6,5},{5,6},{4,7},{11,8},{10,9},{9,1... | collective-permute-start | bytes 24584 | tf_op jit(solution)/shard_map/ppermute | solution.py:564
  75.7 2.2 %collective-permute-start.22 = (f32[2,32,32]{2,1,0:T(8,128)S(1)}, f32[2,32,32]{2,1,0:T(8,128)S(1)}, u32[]{:S(2)}, u32[]{:S(2)}) collective-permute-start(f32[2,32,32]{2,1,0:T(8,128)S(1)} %apply_score.1), channel_id=1, source_target_pairs={{1,0},{0,1},{3,2},{2,3},{5,4},{4,5},{7,6},{6,7},{9,8},{8,9},{11,10... | collective-permute-start | bytes 24584 | tf_op jit(solution)/shard_map/ppermute | solution.py:564
  77.9 1.4 %collective-permute-done.24 = f32[2,32,32]{2,1,0:T(8,128)S(1)} collective-permute-done((f32[2,32,32]{2,1,0:T(8,128)S(1)}, f32[2,32,32]{2,1,0:T(8,128)S(1)}, u32[]{:S(2)}, u32[]{:S(2)}) %collective-permute-start.24) | collective-permute-done | bytes 8224 | tf_op jit(solution)/shard_map/ppermute | solution.py:564
  (38 shorter events, 9.3 us)
Async XLA Ops:
  1.5 12.6 %collective-permute-start.2 = (bf16[2,32,512]{2,1,0:T(8,128)(2,1)S(1)}, bf16[2,32,512]{2,1,0:T(8,128)(2,1)S(1)}, u32[]{:S(2)}, u32[]{:S(2)}) collective-permute-start(bf16[2,32,512]{2,1,0:T(8,128)(2,1)S(1)} %convert_element_type.3.refs_0_), channel_id=1, source_target_pairs={{3,0},{2,1},{1,2},{0,3},{7,4},{6,5},{5,6},{4,7},{11,8},{10,9},{9,1... | collective-permute-start | bytes 196616 | tf_op jit(solution)/shard_map/ppermute | solution.py:564
  6.7 7.5 %collective-permute-start.1 = (bf16[2,32,512]{2,1,0:T(8,128)(2,1)S(1)}, bf16[2,32,512]{2,1,0:T(8,128)(2,1)S(1)}, u32[]{:S(2)}, u32[]{:S(2)}) collective-permute-start(bf16[2,32,512]{2,1,0:T(8,128)(2,1)S(1)} %convert_element_type.3.refs_0_), channel_id=1, source_target_pairs={{2,0},{3,1},{0,2},{1,3},{6,4},{7,5},{4,6},{5,7},{10,8},{11,9},{8,1... | collective-permute-start | bytes 196616 | tf_op jit(solution)/shard_map/ppermute | solution.py:564
  6.7 7.5 %collective-permute-start = (bf16[2,32,512]{2,1,0:T(8,128)(2,1)S(1)}, bf16[2,32,512]{2,1,0:T(8,128)(2,1)S(1)}, u32[]{:S(2)}, u32[]{:S(2)}) collective-permute-start(bf16[2,32,512]{2,1,0:T(8,128)(2,1)S(1)} %convert_element_type.3.refs_0_), channel_id=1, source_target_pairs={{1,0},{0,1},{3,2},{2,3},{5,4},{4,5},{7,6},{6,7},{9,8},{8,9},{11,10... | collective-permute-start | bytes 196616 | tf_op jit(solution)/shard_map/ppermute | solution.py:564
  15.7 9.8 %collective-permute-start.11 = (f32[32,512]{1,0:T(8,128)S(1)}, f32[32,512]{1,0:T(8,128)S(1)}, u32[]{:S(2)}, u32[]{:S(2)}) collective-permute-start(f32[32,512]{1,0:T(8,128)S(1)} %apply_first.3.refs_0_), channel_id=1, source_target_pairs={{3,0},{2,1},{1,2},{0,3},{7,4},{6,5},{5,6},{4,7},{11,8},{10,9},{9,1... | collective-permute-start | bytes 196616 | tf_op jit(solution)/shard_map/ppermute | solution.py:564
  19.5 6.6 %collective-permute-start.10 = (f32[32,512]{1,0:T(8,128)S(1)}, f32[32,512]{1,0:T(8,128)S(1)}, u32[]{:S(2)}, u32[]{:S(2)}) collective-permute-start(f32[32,512]{1,0:T(8,128)S(1)} %apply_first.3.refs_0_), channel_id=1, source_target_pairs={{2,0},{3,1},{0,2},{1,3},{6,4},{7,5},{4,6},{5,7},{10,8},{11,9},{8,1... | collective-permute-start | bytes 196616 | tf_op jit(solution)/shard_map/ppermute | solution.py:564
  19.5 6.6 %collective-permute-start.9 = (f32[32,512]{1,0:T(8,128)S(1)}, f32[32,512]{1,0:T(8,128)S(1)}, u32[]{:S(2)}, u32[]{:S(2)}) collective-permute-start(f32[32,512]{1,0:T(8,128)S(1)} %apply_first.3.refs_0_), channel_id=1, source_target_pairs={{1,0},{0,1},{3,2},{2,3},{5,4},{4,5},{7,6},{6,7},{9,8},{8,9},{11,10... | collective-permute-start | bytes 196616 | tf_op jit(solution)/shard_map/ppermute | solution.py:564
  21.7 9.4 %collective-permute-start.5 = (f32[32,512]{1,0:T(8,128)S(1)}, f32[32,512]{1,0:T(8,128)S(1)}, u32[]{:S(2)}, u32[]{:S(2)}) collective-permute-start(f32[32,512]{1,0:T(8,128)S(1)} %apply_first.2.refs_0_), channel_id=1, source_target_pairs={{3,0},{2,1},{1,2},{0,3},{7,4},{6,5},{5,6},{4,7},{11,8},{10,9},{9,1... | collective-permute-start | bytes 196616 | tf_op jit(solution)/shard_map/ppermute | solution.py:564
  25.5 5.8 %collective-permute-start.4 = (f32[32,512]{1,0:T(8,128)S(1)}, f32[32,512]{1,0:T(8,128)S(1)}, u32[]{:S(2)}, u32[]{:S(2)}) collective-permute-start(f32[32,512]{1,0:T(8,128)S(1)} %apply_first.2.refs_0_), channel_id=1, source_target_pairs={{2,0},{3,1},{0,2},{1,3},{6,4},{7,5},{4,6},{5,7},{10,8},{11,9},{8,1... | collective-permute-start | bytes 196616 | tf_op jit(solution)/shard_map/ppermute | solution.py:564
  25.5 5.8 %collective-permute-start.3 = (f32[32,512]{1,0:T(8,128)S(1)}, f32[32,512]{1,0:T(8,128)S(1)}, u32[]{:S(2)}, u32[]{:S(2)}) collective-permute-start(f32[32,512]{1,0:T(8,128)S(1)} %apply_first.2.refs_0_), channel_id=1, source_target_pairs={{1,0},{0,1},{3,2},{2,3},{5,4},{4,5},{7,6},{6,7},{9,8},{8,9},{11,10... | collective-permute-start | bytes 196616 | tf_op jit(solution)/shard_map/ppermute | solution.py:564
  29.4 7.2 %collective-permute-start.14 = (f32[32,512]{1,0:T(8,128)S(1)}, f32[32,512]{1,0:T(8,128)S(1)}, u32[]{:S(2)}, u32[]{:S(2)}) collective-permute-start(f32[32,512]{1,0:T(8,128)S(1)} %apply_second.3.refs_4_), channel_id=1, source_target_pairs={{12,0},{8,4},{4,8},{0,12},{13,1},{9,5},{5,9},{1,13},{14,2},{10,6},... | collective-permute-start | bytes 196616 | tf_op jit(solution)/shard_map/ppermute | solution.py:564
  29.4 7.1 %collective-permute-start.13 = (f32[32,512]{1,0:T(8,128)S(1)}, f32[32,512]{1,0:T(8,128)S(1)}, u32[]{:S(2)}, u32[]{:S(2)}) collective-permute-start(f32[32,512]{1,0:T(8,128)S(1)} %apply_second.3.refs_4_), channel_id=1, source_target_pairs={{8,0},{12,4},{0,8},{4,12},{9,1},{13,5},{1,9},{5,13},{10,2},{14,6},... | collective-permute-start | bytes 196616 | tf_op jit(solution)/shard_map/ppermute | solution.py:564
  31.1 5.4 %collective-permute-start.12 = (f32[32,512]{1,0:T(8,128)S(1)}, f32[32,512]{1,0:T(8,128)S(1)}, u32[]{:S(2)}, u32[]{:S(2)}) collective-permute-start(f32[32,512]{1,0:T(8,128)S(1)} %apply_second.3.refs_4_), channel_id=1, source_target_pairs={{4,0},{0,4},{12,8},{8,12},{5,1},{1,5},{13,9},{9,13},{6,2},{2,6},{1... | collective-permute-start | bytes 196616 | tf_op jit(solution)/shard_map/ppermute | solution.py:564
  34.5 4.0 %collective-permute-start.8 = (f32[32,512]{1,0:T(8,128)S(1)}, f32[32,512]{1,0:T(8,128)S(1)}, u32[]{:S(2)}, u32[]{:S(2)}) collective-permute-start(f32[32,512]{1,0:T(8,128)S(1)} %apply_second.2.refs_0_), channel_id=1, source_target_pairs={{12,0},{8,4},{4,8},{0,12},{13,1},{9,5},{5,9},{1,13},{14,2},{10,6},... | collective-permute-start | bytes 196616 | tf_op jit(solution)/shard_map/ppermute | solution.py:564
  35.8 4.6 %collective-permute-start.7 = (f32[32,512]{1,0:T(8,128)S(1)}, f32[32,512]{1,0:T(8,128)S(1)}, u32[]{:S(2)}, u32[]{:S(2)}) collective-permute-start(f32[32,512]{1,0:T(8,128)S(1)} %apply_second.2.refs_0_), channel_id=1, source_target_pairs={{8,0},{12,4},{0,8},{4,12},{9,1},{13,5},{1,9},{5,13},{10,2},{14,6},... | collective-permute-start | bytes 196616 | tf_op jit(solution)/shard_map/ppermute | solution.py:564
  36.6 3.8 %collective-permute-start.6 = (f32[32,512]{1,0:T(8,128)S(1)}, f32[32,512]{1,0:T(8,128)S(1)}, u32[]{:S(2)}, u32[]{:S(2)}) collective-permute-start(f32[32,512]{1,0:T(8,128)S(1)} %apply_second.2.refs_0_), channel_id=1, source_target_pairs={{4,0},{0,4},{12,8},{8,12},{5,1},{1,5},{13,9},{9,13},{6,2},{2,6},{1... | collective-permute-start | bytes 196616 | tf_op jit(solution)/shard_map/ppermute | solution.py:564
  41.1 7.1 %collective-permute-start.17 = (f32[144,128]{1,0:T(8,128)S(1)}, f32[144,128]{1,0:T(8,128)S(1)}, u32[]{:S(2)}, u32[]{:S(2)}) collective-permute-start(f32[144,128]{1,0:T(8,128)S(1)} %get-tuple-element.11), channel_id=1, source_target_pairs={{3,0},{2,1},{1,2},{0,3},{7,4},{6,5},{5,6},{4,7},{11,8},{10,9},{9,1... | collective-permute-start | bytes 221192 | tf_op jit(solution)/shard_map/ppermute | solution.py:564
  44.9 6.2 %collective-permute-start.16 = (f32[144,128]{1,0:T(8,128)S(1)}, f32[144,128]{1,0:T(8,128)S(1)}, u32[]{:S(2)}, u32[]{:S(2)}) collective-permute-start(f32[144,128]{1,0:T(8,128)S(1)} %get-tuple-element.11), channel_id=1, source_target_pairs={{2,0},{3,1},{0,2},{1,3},{6,4},{7,5},{4,6},{5,7},{10,8},{11,9},{8,1... | collective-permute-start | bytes 221192 | tf_op jit(solution)/shard_map/ppermute | solution.py:564
  44.9 6.2 %collective-permute-start.15 = (f32[144,128]{1,0:T(8,128)S(1)}, f32[144,128]{1,0:T(8,128)S(1)}, u32[]{:S(2)}, u32[]{:S(2)}) collective-permute-start(f32[144,128]{1,0:T(8,128)S(1)} %get-tuple-element.11), channel_id=1, source_target_pairs={{1,0},{0,1},{3,2},{2,3},{5,4},{4,5},{7,6},{6,7},{9,8},{8,9},{11,10... | collective-permute-start | bytes 221192 | tf_op jit(solution)/shard_map/ppermute | solution.py:564
  62.0 6.8 %collective-permute-start.21 = (bf16[2,32,512]{2,1,0:T(8,128)(2,1)S(1)}, bf16[2,32,512]{2,1,0:T(8,128)(2,1)S(1)}, u32[]{:S(2)}, u32[]{:S(2)}) collective-permute-start(bf16[2,32,512]{2,1,0:T(8,128)(2,1)S(1)} %get-tuple-element.14.basis_ref), channel_id=1, source_target_pairs={{3,0},{2,1},{1,2},{0,3},{7,4},{6,5},{5,6},{4,7},{11,8},{10,9},{9,1... | collective-permute-start | bytes 196616 | tf_op jit(solution)/shard_map/ppermute | solution.py:564
  64.4 6.6 %collective-permute-start.20 = (bf16[2,32,512]{2,1,0:T(8,128)(2,1)S(1)}, bf16[2,32,512]{2,1,0:T(8,128)(2,1)S(1)}, u32[]{:S(2)}, u32[]{:S(2)}) collective-permute-start(bf16[2,32,512]{2,1,0:T(8,128)(2,1)S(1)} %get-tuple-element.14.basis_ref), channel_id=1, source_target_pairs={{2,0},{3,1},{0,2},{1,3},{6,4},{7,5},{4,6},{5,7},{10,8},{11,9},{8,1... | collective-permute-start | bytes 196616 | tf_op jit(solution)/shard_map/ppermute | solution.py:564
  64.5 6.5 %collective-permute-start.19 = (bf16[2,32,512]{2,1,0:T(8,128)(2,1)S(1)}, bf16[2,32,512]{2,1,0:T(8,128)(2,1)S(1)}, u32[]{:S(2)}, u32[]{:S(2)}) collective-permute-start(bf16[2,32,512]{2,1,0:T(8,128)(2,1)S(1)} %get-tuple-element.14.basis_ref), channel_id=1, source_target_pairs={{1,0},{0,1},{3,2},{2,3},{5,4},{4,5},{7,6},{6,7},{9,8},{8,9},{11,10... | collective-permute-start | bytes 196616 | tf_op jit(solution)/shard_map/ppermute | solution.py:564
  73.5 5.8 %collective-permute-start.24 = (f32[2,32,32]{2,1,0:T(8,128)S(1)}, f32[2,32,32]{2,1,0:T(8,128)S(1)}, u32[]{:S(2)}, u32[]{:S(2)}) collective-permute-start(f32[2,32,32]{2,1,0:T(8,128)S(1)} %apply_score.1), channel_id=1, source_target_pairs={{3,0},{2,1},{1,2},{0,3},{7,4},{6,5},{5,6},{4,7},{11,8},{10,9},{9,1... | collective-permute-start | bytes 24584 | tf_op jit(solution)/shard_map/ppermute | solution.py:564
  75.7 4.8 %collective-permute-start.23 = (f32[2,32,32]{2,1,0:T(8,128)S(1)}, f32[2,32,32]{2,1,0:T(8,128)S(1)}, u32[]{:S(2)}, u32[]{:S(2)}) collective-permute-start(f32[2,32,32]{2,1,0:T(8,128)S(1)} %apply_score.1), channel_id=1, source_target_pairs={{2,0},{3,1},{0,2},{1,3},{6,4},{7,5},{4,6},{5,7},{10,8},{11,9},{8,1... | collective-permute-start | bytes 24584 | tf_op jit(solution)/shard_map/ppermute | solution.py:564
  75.7 4.8 %collective-permute-start.22 = (f32[2,32,32]{2,1,0:T(8,128)S(1)}, f32[2,32,32]{2,1,0:T(8,128)S(1)}, u32[]{:S(2)}, u32[]{:S(2)}) collective-permute-start(f32[2,32,32]{2,1,0:T(8,128)S(1)} %apply_score.1), channel_id=1, source_target_pairs={{1,0},{0,1},{3,2},{2,3},{5,4},{4,5},{7,6},{6,7},{9,8},{8,9},{11,10... | collective-permute-start | bytes 24584 | tf_op jit(solution)/shard_map/ppermute | solution.py:564
  (1 other events, 1.3 us)

commit v12 on v11

--- a/solution.py
+++ b/solution.py
@@ -19,6 +19,7 @@
 HIGHEST = lax.Precision.HIGHEST
 TRANS_B = (((1,), (1,)), ((), ()))
 TRANS_A = (((0,), (0,)), ((), ()))
+SPREAD = (2, 88, 128)
 
 
 def params(mib):
@@ -231,13 +232,17 @@
     out_ref[...] = to_wide(total, out_ref.shape[0], halves, tall)
 
 
-def second_kernel(piece_count, *refs):
-    pieces, (dense_ref, out_ref, halves, tall) = refs[:piece_count], refs[piece_count:]
+def second_kernel(piece_count, earlier_count, *refs):
+    pieces, dense_ref, refs = refs[:piece_count], refs[piece_count], refs[piece_count + 1 :]
+    earlier, (out_ref, halves, tall, scratch) = refs[:earlier_count], refs[earlier_count:]
     image = jnp.concatenate([piece[...] for piece in pieces], axis=1)
-    inverse = inverse_factor(product(image, image))
+    inverse = inverse_factor(product(image, image), scratch)
     basis = jnp.dot(inverse, image, precision=HIGHEST, preferred_element_type=F32)
     parts = [basis[:, d * ROWS_DEV : d * ROWS_DEV + ROWS_DEV] for d in range(piece_count)]
-    out_ref[...] = to_wide(image_of(parts, dense_ref), out_ref.shape[0], halves, tall)
+    before = out_ref.shape[0] - 1
+    for ref in earlier:
+        out_ref[:before] = ref[...]
+    out_ref[before] = to_wide(image_of(parts, dense_ref), out_ref.shape[1], halves, tall)
 
 
 def own_kernel(basis_ref, *refs):
@@ -261,13 +266,13 @@
         out_ref[layer] = product(left_ref[layer], wide[layer])
 
 
-def apply_whole(kernel, name, operands, out_shape, *lead):
+def apply_whole(kernel, name, operands, out_shape, *lead, scratch=()):
     return pl.pallas_call(
         kernel,
         in_specs=vmem_specs(len(operands)),
         out_specs=pl.BlockSpec(memory_space=pltpu.VMEM),
         out_shape=jax.ShapeDtypeStruct(out_shape, F32),
-        scratch_shapes=[pltpu.VMEM((*lead, TALL, 128), F32), pltpu.VMEM((*lead, ROWS_DEV, 128), F32)],
+        scratch_shapes=[pltpu.VMEM((*lead, TALL, 128), F32), pltpu.VMEM((*lead, ROWS_DEV, 128), F32), *scratch],
         compiler_params=params(14),
         cost_estimate=pl.CostEstimate(flops=0, bytes_accessed=4 * MIB, transcendentals=0),
         name=name,
@@ -279,9 +284,12 @@
     return apply_whole(kernel, "apply_first", [*pieces, dense], pieces[0].shape[1:])
 
 
-def apply_second(pieces, dense):
-    kernel = functools.partial(second_kernel, len(pieces))
-    return apply_whole(kernel, "apply_second", [*pieces, dense], pieces[0].shape)
+def apply_second(pieces, dense, earlier):
+    kernel = functools.partial(second_kernel, len(pieces), len(earlier))
+    before = sum(array.shape[0] for array in earlier)
+    shape = (before + 1, *pieces[0].shape)
+    operands = [*pieces, dense, *earlier]
+    return apply_whole(kernel, "apply_second", operands, shape, scratch=[pltpu.VMEM(SPREAD, F32)])
 
 
 def apply_own(basis, dense):
@@ -334,7 +342,7 @@
     return jnp.broadcast_to(x, (8, 128))
 
 
-def eliminate(rows, offset):
+def eliminate(rows, offset, scratch):
     groups, tiles = len(rows), len(rows[0])
     rows = [list(row) for row in rows]
     home, at = offset // 128, offset % 128
@@ -344,8 +352,13 @@
         below = range(h + 1, groups)
         lane = at + 8 * h
         col = [{g: spread(rows[g][home][:, lane + q : lane + q + 1]) for g in range(h, groups)} for q in range(8)]
-        cell = {(p, q): spread(col[p][h][q : q + 1]) for q in range(8) for p in range(q + 1)}
-        row = [[spread(rows[h][t][q : q + 1]) for t in range(tiles)] for q in range(8)]
+        held = scratch.at[h % 2]
+        for q in range(8):
+            held[q * 8 : q * 8 + 8] = col[q][h]
+        for t in range(tiles):
+            held[64 + t * 8 : 72 + t * 8] = rows[h][t]
+        cell = {(p, q): spread(held[p * 8 + q : p * 8 + q + 1]) for q in range(8) for p in range(q + 1)}
+        row = [[spread(held[64 + t * 8 + q : 65 + t * 8 + q]) for t in range(tiles)] for q in range(8)]
         done = []
         for m in range(0, 8, 2):
             n = m + 1
@@ -422,19 +435,19 @@
     return lambda at, count: parts[at // 128 * 128][at % 128 : at % 128 + count]
 
 
-def inverse_factor(gram):
+def inverse_factor(gram, scratch):
     k = gram.shape[0]
     lane = lax.broadcasted_iota(jnp.int32, (k, 128), 1)
     sub = lax.broadcasted_iota(jnp.int32, (k, 128), 0)
     eye = jnp.where(lane == sub, 1.0, 0.0)
     gram, across = unit_scale(jnp.concatenate([gram, jnp.zeros((k, 128 - k), F32)], axis=1))
-    solved = eliminate(tiled(jnp.concatenate([gram, eye], axis=1)), 0)
+    solved = eliminate(tiled(jnp.concatenate([gram, eye], axis=1)), 0, scratch)
     return (joined(solved)[:, 128:] * across)[:, :k]
 
 
-def solve_kernel(gram_ref, image_ref, out_ref):
+def solve_kernel(gram_ref, image_ref, out_ref, scratch):
     for layer in range(image_ref.shape[0]):
-        inverse = inverse_factor(gram_ref[layer])
+        inverse = inverse_factor(gram_ref[layer], scratch.at[layer])
         solved = jnp.dot(inverse, image_ref[layer], precision=HIGHEST, preferred_element_type=F32)
         out_ref[layer] = solved.astype(BF16)
 
@@ -445,21 +458,16 @@
         in_specs=vmem_specs(2),
         out_specs=pl.BlockSpec(memory_space=pltpu.VMEM),
         out_shape=jax.ShapeDtypeStruct(image.shape, BF16),
+        scratch_shapes=[pltpu.VMEM((image.shape[0], *SPREAD), F32)],
         compiler_params=params(4),
         name="solve_layers",
     )(gram, image)
 
 
-def cross_kernel(k, groups, *refs):
-    pieces, (out_ref, stacked, packed) = refs[:-3], refs[-3:]
+def cross_kernel(k, images_ref, out_ref, packed):
     g = lax.axis_index("layer")
-    layers = len(pieces) // groups
-    for i, piece in enumerate(pieces):
-        at = ((g ^ (i % groups)) * layers + i // groups) * k
-        stacked[pl.ds(pl.multiple_of(at, k), k)] = piece[...]
-    gram = lax.dot_general(
-        stacked[...], stacked[...], TRANS_B, precision=HIGHEST, preferred_element_type=F32
-    )
+    every = images_ref[...].reshape(-1, images_ref.shape[2])
+    gram = lax.dot_general(every, every, TRANS_B, precision=HIGHEST, preferred_element_type=F32)
     half = gram.shape[0] // 2
     first, last = gram[:half, :half], gram[half:, half:]
     row = lax.broadcasted_iota(jnp.int32, (half, half), 0) // k
@@ -472,23 +480,18 @@
     out_ref[...] = packed[pl.ds(pl.multiple_of((g & 1) * rows, 16), rows)]
 
 
-def cross(chains):
-    k, width = chains[0][0].shape
-    groups = len(chains[0])
-    size = len(chains) * groups * k
-    pieces = [piece for chain in chains for piece in chain]
+def cross(images):
+    layers, k, _ = images.shape
+    size = layers * k
     return pl.pallas_call(
-        functools.partial(cross_kernel, k, groups),
-        in_specs=vmem_specs(len(pieces)),
-        out_specs=vmem_specs(2),
-        out_shape=[
-            jax.ShapeDtypeStruct(((size + k) // 2, size // 2), F32),
-            jax.ShapeDtypeStruct((size, width), F32),
-        ],
+        functools.partial(cross_kernel, k),
+        in_specs=vmem_specs(1),
+        out_specs=pl.BlockSpec(memory_space=pltpu.VMEM),
+        out_shape=jax.ShapeDtypeStruct(((size + k) // 2, size // 2), F32),
         scratch_shapes=[pltpu.VMEM((size + k, size // 2), F32)],
         compiler_params=params(6),
         name="cross_gram",
-    )(*pieces)
+    )(images)
 
 
 def unpack(packed, k, work):
@@ -505,7 +508,7 @@
 
 
 def joint_kernel(k, *refs):
-    own_ref, other_ref, images_ref, out_ref, again_ref, rounded_ref, work, packed = refs
+    own_ref, other_ref, images_ref, out_ref, again_ref, rounded_ref, work, packed, scratch = refs
     rows = own_ref.shape[0]
     odd = lax.axis_index("layer") & 1
     packed[pl.ds(pl.multiple_of(odd * rows, 16), rows)] = own_ref[...]
@@ -522,7 +525,7 @@
         lo, hi = s * k, (s + 1) * k
         here = (lane >= lo) & (lane < hi)
         eye = jnp.where(lane_128 == sub_128 + lo % 128, 1.0, 0.0)
-        solved = joined(eliminate(tiled(jnp.concatenate([work[lo:hi], eye], axis=1)), lo))
+        solved = joined(eliminate(tiled(jnp.concatenate([work[lo:hi], eye], axis=1)), lo, scratch.at[s % 2]))
         panel, tail = solved[:, :size], solved[:, size:]
         panel = jnp.where(here, jnp.concatenate([tail] * (size // 128), axis=1), panel)
         work[lo:hi] = jnp.where(lane < hi, panel, 0.0)
@@ -533,7 +536,7 @@
                 work[r * k : r * k + k] = jnp.where(here, 0.0, rows) - update(r * k, k)
     rows = out_ref.shape[0] * k
     own = work[pl.ds(pl.multiple_of(lax.axis_index("layer") * rows, rows), rows)] * across
-    joint = jnp.dot(own, images_ref[...], precision=HIGHEST, preferred_element_type=F32)
+    joint = jnp.dot(own, images_ref[...].reshape(size, -1), precision=HIGHEST, preferred_element_type=F32)
     joint = joint.reshape(out_ref.shape)
     out_ref[...] = joint
     again_ref[...] = joint
@@ -541,8 +544,8 @@
 
 
 def joint_solve(own, other, images, shape):
-    size = images.shape[0]
     k = shape[1]
+    size = images.shape[0] * k
     return pl.pallas_call(
         functools.partial(joint_kernel, k),
         in_specs=vmem_specs(3),
@@ -552,7 +555,11 @@
             jax.ShapeDtypeStruct(shape, F32),
             jax.ShapeDtypeStruct(shape, BF16),
         ],
-        scratch_shapes=[pltpu.VMEM((size, size), F32), pltpu.VMEM((size + k, size // 2), F32)],
+        scratch_shapes=[
+            pltpu.VMEM((size, size), F32),
+            pltpu.VMEM((size + k, size // 2), F32),
+            pltpu.VMEM((2, *SPREAD), F32),
+        ],
         compiler_params=params(8),
         name="joint_solve",
     )(own, other, images)
@@ -585,15 +592,17 @@
     dense = build_dense(block_rows, block_cols, counts, blocks, shards * BROWS // CHUNK_COLS)
     if few:
         images = [apply_first(layer, first, dense[layer]) for layer in range(layers)]
-        images = [apply_second(gather(images[layer]), dense[layer]) for layer in range(layers)]
+        image = None
+        for layer in range(layers):
+            image = apply_second(gather(images[layer]), dense[layer], [] if image is None else [image])
     else:
         image, gram = apply_dense("gram", first, dense)
         (image,) = apply_dense("plain", gather(solve(total(gram), image)), dense)
-        images = [image[layer] for layer in range(layers)]
-    own, stacked = cross([around(image, "layer", groups) for image in images])
+    images = lax.all_gather(image, "layer", axis=0, tiled=True)
+    own = cross(images)
     own = total(own)
     other = lax.ppermute(own, "layer", [(m ^ 1, m) for m in range(groups)])
-    joint_basis, again, rounded = joint_solve(own, other, stacked, start.shape)
+    joint_basis, again, rounded = joint_solve(own, other, images, start.shape)
     if few:
         partial = apply_score(gather(rounded), again, dense)
     else:

time: 81.3 us -> 80.1 us (0.985)
  blocking collectives: 0 us -> 7.36 us
  starting transfers between devices: 32 us -> 28.1 us
  waiting for transfers between devices: 17 us -> 14.5 us
  Pallas kernels: 29.9 us -> 27.8 us
    all_gather x0 -> x1, blocking collectives: none -> 7.36 us  [per_device(): images = lax.all_gather(image, 'layer', axis=0, tiled=True)]
    ppermute x24 -> x18, starting transfers between devices: 31.9 us -> 27.9 us  [around(): pieces.append(lax.ppermute(x, axis, [(m ^ d, m) for m in range(count)]))]
    ppermute x24 -> x18, waiting for transfers between devices: 15.8 us -> 13.3 us  [around(): pieces.append(lax.ppermute(x, axis, [(m ^ d, m) for m in range(count)]))]
    pallas_call x1, Pallas kernels: 9.62 us -> 7.92 us  [joint_solve(): pl.pallas_call(functools.partial(joint_kernel, k), in_specs=vmem_specs(3)...]
  transfers between devices with their start and end apart: 25 -> 19, of which waited for: 9 -> 8; matrix products, arithmetic and copies ran while one was open for 0% -> 0% of each run, Pallas kernels for 19% -> 15%
where the time goes in v12:
time: 80.1 us; the launch traced here: 80 us
  starting transfers between devices  28.1 us (35%)
  Pallas kernels  27.8 us (35%)
  waiting for transfers between devices  14.5 us (18%)
  blocking collectives  7.36 us (9%)
  other arithmetic  1.56 us (2%)
    ppermute x18, starting transfers between devices, around(): pieces.append(lax.ppermute(x, axis, [(m ^ d, m) for m in range(count)]))  27.9 us
    ppermute x18, waiting for transfers between devices, around(): pieces.append(lax.ppermute(x, axis, [(m ^ d, m) for m in range(count)]))  13.3 us
    pallas_call x5, Pallas kernels, apply_whole(): pl.pallas_call(kernel, in_specs=vmem_specs(len(operands)), out_specs=pl.B...  11.6 us
    pallas_call x1, Pallas kernels, joint_solve(): pl.pallas_call(functools.partial(joint_kernel, k), in_specs=vmem_specs(3)...  7.92 us
    all_gather x1, blocking collectives, per_device(): images = lax.all_gather(image, 'layer', axis=0, tiled=True)  7.36 us
    pallas_call x1, Pallas kernels, build_dense(): pl.pallas_call(build_whole_kernel, in_specs=[pl.BlockSpec(memory_space=pl...  6.83 us
  transfers between devices with their start and end apart: 19, of which 8 were waited for; matrix products, arithmetic and copies ran while one was open for 0% of the time, Pallas kernels for 15%

profile of v12, /device:TPU:0, one launch (start us, length us, event | category | flops | bytes accessed | tf_op | source)
XLA Modules:
  0.0 80.0 jit_solution(11263349449853361042)
XLA Ops:
  1.5 5.1 %collective-permute-start.2 = (bf16[2,32,512]{2,1,0:T(8,128)(2,1)S(1)}, bf16[2,32,512]{2,1,0:T(8,128)(2,1)S(1)}, u32[]{:S(2)}, u32[]{:S(2)}) collective-permute-start(bf16[2,32,512]{2,1,0:T(8,128)(2,1)S(1)} %convert_element_type.3.refs_0_), channel_id=1, source_target_pairs={{3,0},{2,1},{1,2},{0,3},{7,4},{6,5},{5,6},{4,7},{11,8},{10,9},{9,1... | collective-permute-start | bytes 196616 | tf_op jit(solution)/shard_map/ppermute | solution.py:571
  7.3 6.8 %build_dense.1 = (bf16[4,512,1024]{2,1,0:T(8,128)(2,1)S(1)}, bf16[4,512,1024]{2,1,0:T(8,128)(2,1)S(1)}) custom-call(s32[2,512]{1,0:T(2,128)} %rows_hbm.1, s32[2,512]{1,0:T(2,128)} %cols_hbm.1, s32[1,2]{1,0:T(1,128)} %bitcast.1, bf16[2,512,4096]{2,1,0:T(8,128)(2,1)} %blocks_ref.1), custom_call_target="tpu_custom_call" | custom-call | tf_op jit(solution)/shard_map/build_dense/pallas_call | solution.py:114
  14.2 1.5 %apply_first.3.refs_0_ = f32[32,512]{1,0:T(8,128)S(1)} custom-call(bf16[2,32,512]{2,1,0:T(8,128)(2,1)S(1)} %convert_element_type.3.refs_0_, bf16[2,32,512]{2,1,0:T(8,128)(2,1)S(1)} %collective-permute-done.refs_1_, bf16[2,32,512]{2,1,0:T(8,128)(2,1)S(1)} %collective-permute-done.1.refs_2_, bf16[2,32,512]{2,1,0:T(8,128)(2,1)S(1)} %collective-permute-done.2.refs_3_, ...), custom_call_target="tpu_custom_call" | custom-call | bytes 4194304 | tf_op jit(solution)/shard_map/apply_first/pallas_call | solution.py:270
  15.7 3.8 %collective-permute-start.8 = (f32[32,512]{1,0:T(8,128)S(1)}, f32[32,512]{1,0:T(8,128)S(1)}, u32[]{:S(2)}, u32[]{:S(2)}) collective-permute-start(f32[32,512]{1,0:T(8,128)S(1)} %apply_first.3.refs_0_), channel_id=1, source_target_pairs={{3,0},{2,1},{1,2},{0,3},{7,4},{6,5},{5,6},{4,7},{11,8},{10,9},{9,1... | collective-permute-start | bytes 196616 | tf_op jit(solution)/shard_map/ppermute | solution.py:571
  20.2 1.5 %apply_first.2.refs_0_ = f32[32,512]{1,0:T(8,128)S(1)} custom-call(bf16[2,32,512]{2,1,0:T(8,128)(2,1)S(1)} %convert_element_type.3.refs_0_, bf16[2,32,512]{2,1,0:T(8,128)(2,1)S(1)} %collective-permute-done.refs_1_, bf16[2,32,512]{2,1,0:T(8,128)(2,1)S(1)} %collective-permute-done.1.refs_2_, bf16[2,32,512]{2,1,0:T(8,128)(2,1)S(1)} %collective-permute-done.2.refs_3_, ...), custom_call_target="tpu_custom_call" | custom-call | bytes 4194304 | tf_op jit(solution)/shard_map/apply_first/pallas_call | solution.py:270
  21.7 3.8 %collective-permute-start.5 = (f32[32,512]{1,0:T(8,128)S(1)}, f32[32,512]{1,0:T(8,128)S(1)}, u32[]{:S(2)}, u32[]{:S(2)}) collective-permute-start(f32[32,512]{1,0:T(8,128)S(1)} %apply_first.2.refs_0_), channel_id=1, source_target_pairs={{3,0},{2,1},{1,2},{0,3},{7,4},{6,5},{5,6},{4,7},{11,8},{10,9},{9,1... | collective-permute-start | bytes 196616 | tf_op jit(solution)/shard_map/ppermute | solution.py:571
  26.1 3.0 %apply_second.2.refs_5_ = f32[1,32,512]{2,1,0:T(8,128)S(1)} custom-call(f32[32,512]{1,0:T(8,128)S(1)} %apply_first.3.refs_0_, f32[32,512]{1,0:T(8,128)S(1)} %collective-permute-done.6.refs_1_, f32[32,512]{1,0:T(8,128)S(1)} %collective-permute-done.7.refs_2_, f32[32,512]{1,0:T(8,128)S(1)} %collective-permute-done.8.refs_3_, ...), custom_call_target="tpu_custom_call" | custom-call | bytes 4194304 | tf_op jit(solution)/shard_map/apply_second/pallas_call | solution.py:270
  29.2 1.5 %collective-permute-done.4.refs_2_ = f32[32,512]{1,0:T(8,128)S(1)} collective-permute-done((f32[32,512]{1,0:T(8,128)S(1)}, f32[32,512]{1,0:T(8,128)S(1)}, u32[]{:S(2)}, u32[]{:S(2)}) %collective-permute-start.4) | collective-permute-done | bytes 65568 | tf_op jit(solution)/shard_map/ppermute | solution.py:571
  30.6 3.0 %apply_second.3 = f32[2,32,512]{2,1,0:T(8,128)S(1)} custom-call(f32[32,512]{1,0:T(8,128)S(1)} %apply_first.2.refs_0_, f32[32,512]{1,0:T(8,128)S(1)} %collective-permute-done.3.refs_1_, f32[32,512]{1,0:T(8,128)S(1)} %collective-permute-done.4.refs_2_, f32[32,512]{1,0:T(8,128)S(1)} %collective-permute-done.5.refs_3_, ...), custom_call_target="tpu_custom_call" | custom-call | bytes 4194304 | tf_op jit(solution)/shard_map/apply_second/pallas_call | solution.py:270
  33.7 7.4 %all_gather.3.images_ref.refs_2_ = f32[8,32,512]{2,1,0:T(8,128)S(1)} all-gather(f32[2,32,512]{2,1,0:T(8,128)S(1)} %apply_second.3), channel_id=1, replica_groups=mesh['parts'=2,'layer'=4,'node'=4] {'layer'}, dimensions={0}, use_global_device_ids=true | all-gather | bytes 655360 | tf_op jit(solution)/shard_map/all_gather | solution.py:601
  41.7 2.4 %collective-permute-start.11 = (f32[144,128]{1,0:T(8,128)S(1)}, f32[144,128]{1,0:T(8,128)S(1)}, u32[]{:S(2)}, u32[]{:S(2)}) collective-permute-start(f32[144,128]{1,0:T(8,128)S(1)} %cross_gram.1), channel_id=1, source_target_pairs={{3,0},{2,1},{1,2},{0,3},{7,4},{6,5},{5,6},{4,7},{11,8},{10,9},{9,1... | collective-permute-start | bytes 221192 | tf_op jit(solution)/shard_map/ppermute | solution.py:571
  44.0 2.1 %collective-permute-start.9 = (f32[144,128]{1,0:T(8,128)S(1)}, f32[144,128]{1,0:T(8,128)S(1)}, u32[]{:S(2)}, u32[]{:S(2)}) collective-permute-start(f32[144,128]{1,0:T(8,128)S(1)} %cross_gram.1), channel_id=1, source_target_pairs={{1,0},{0,1},{3,2},{2,3},{5,4},{4,5},{7,6},{6,7},{9,8},{8,9},{11,10... | collective-permute-start | bytes 221192 | tf_op jit(solution)/shard_map/ppermute | solution.py:571
  46.1 2.6 %collective-permute-done.11 = f32[144,128]{1,0:T(8,128)S(1)} collective-permute-done((f32[144,128]{1,0:T(8,128)S(1)}, f32[144,128]{1,0:T(8,128)S(1)}, u32[]{:S(2)}, u32[]{:S(2)}) %collective-permute-start.11) | collective-permute-done | bytes 73760 | tf_op jit(solution)/shard_map/ppermute | solution.py:571
  48.7 2.6 %collective-permute-done.10 = f32[144,128]{1,0:T(8,128)S(1)} collective-permute-done((f32[144,128]{1,0:T(8,128)S(1)}, f32[144,128]{1,0:T(8,128)S(1)}, u32[]{:S(2)}, u32[]{:S(2)}) %collective-permute-start.10) | collective-permute-done | bytes 73760 | tf_op jit(solution)/shard_map/ppermute | solution.py:571
  52.6 7.9 %joint_solve.1 = (f32[2,32,512]{2,1,0:T(8,128)}, f32[2,32,512]{2,1,0:T(8,128)S(1)}, bf16[2,32,512]{2,1,0:T(8,128)(2,1)S(1)}) custom-call(f32[144,128]{1,0:T(8,128)S(1)} %add_add_fusion.refs_0_, f32[144,128]{1,0:T(8,128)S(1)} %collective-permute-done.12.refs_1_, f32[8,32,512]{2,1,0:T(8,128)S(1)} %all_gather.3.images_ref.refs_2_), custom_call_target="tpu_custom_call" | custom-call | tf_op jit(solution)/shard_map/joint_solve/pallas_call | solution.py:549
  60.6 2.6 %collective-permute-start.15 = (bf16[2,32,512]{2,1,0:T(8,128)(2,1)S(1)}, bf16[2,32,512]{2,1,0:T(8,128)(2,1)S(1)}, u32[]{:S(2)}, u32[]{:S(2)}) collective-permute-start(bf16[2,32,512]{2,1,0:T(8,128)(2,1)S(1)} %get-tuple-element.10.basis_ref), channel_id=1, source_target_pairs={{3,0},{2,1},{1,2},{0,3},{7,4},{6,5},{5,6},{4,7},{11,8},{10,9},{9,1... | collective-permute-start | bytes 196616 | tf_op jit(solution)/shard_map/ppermute | solution.py:571
  63.2 1.7 %collective-permute-start.13 = (bf16[2,32,512]{2,1,0:T(8,128)(2,1)S(1)}, bf16[2,32,512]{2,1,0:T(8,128)(2,1)S(1)}, u32[]{:S(2)}, u32[]{:S(2)}) collective-permute-start(bf16[2,32,512]{2,1,0:T(8,128)(2,1)S(1)} %get-tuple-element.10.basis_ref), channel_id=1, source_target_pairs={{1,0},{0,1},{3,2},{2,3},{5,4},{4,5},{7,6},{6,7},{9,8},{8,9},{11,10... | collective-permute-start | bytes 196616 | tf_op jit(solution)/shard_map/ppermute | solution.py:571
  65.7 1.6 %collective-permute-done.15.refs_2_ = bf16[2,32,512]{2,1,0:T(8,128)(2,1)S(1)} collective-permute-done((bf16[2,32,512]{2,1,0:T(8,128)(2,1)S(1)}, bf16[2,32,512]{2,1,0:T(8,128)(2,1)S(1)}, u32[]{:S(2)}, u32[]{:S(2)}) %collective-permute-start.15) | collective-permute-done | bytes 65568 | tf_op jit(solution)/shard_map/ppermute | solution.py:571
  67.3 2.0 %collective-permute-done.14.refs_1_ = bf16[2,32,512]{2,1,0:T(8,128)(2,1)S(1)} collective-permute-done((bf16[2,32,512]{2,1,0:T(8,128)(2,1)S(1)}, bf16[2,32,512]{2,1,0:T(8,128)(2,1)S(1)}, u32[]{:S(2)}, u32[]{:S(2)}) %collective-permute-start.14) | collective-permute-done | bytes 65568 | tf_op jit(solution)/shard_map/ppermute | solution.py:571
  69.3 2.5 %apply_score.1 = f32[2,32,32]{2,1,0:T(8,128)S(1)} custom-call(f32[2,512,64]{2,1,0:T(8,128)S(1)} %apply_own.1.own_ref, bf16[2,32,512]{2,1,0:T(8,128)(2,1)S(1)} %collective-permute-done.13.refs_0_, bf16[2,32,512]{2,1,0:T(8,128)(2,1)S(1)} %collective-permute-done.14.refs_1_, bf16[2,32,512]{2,1,0:T(8,128)(2,1)S(1)} %collective-permute-done.15.refs_2_, ...), custom_call_target="tpu_custom_call" | custom-call | bytes 4194304 | tf_op jit(solution)/shard_map/apply_score/pallas_call | solution.py:270
  71.8 2.7 %collective-permute-start.18 = (f32[2,32,32]{2,1,0:T(8,128)S(1)}, f32[2,32,32]{2,1,0:T(8,128)S(1)}, u32[]{:S(2)}, u32[]{:S(2)}) collective-permute-start(f32[2,32,32]{2,1,0:T(8,128)S(1)} %apply_score.1), channel_id=1, source_target_pairs={{3,0},{2,1},{1,2},{0,3},{7,4},{6,5},{5,6},{4,7},{11,8},{10,9},{9,1... | collective-permute-start | bytes 24584 | tf_op jit(solution)/shard_map/ppermute | solution.py:571
  74.5 1.7 %collective-permute-start.16 = (f32[2,32,32]{2,1,0:T(8,128)S(1)}, f32[2,32,32]{2,1,0:T(8,128)S(1)}, u32[]{:S(2)}, u32[]{:S(2)}) collective-permute-start(f32[2,32,32]{2,1,0:T(8,128)S(1)} %apply_score.1), channel_id=1, source_target_pairs={{1,0},{0,1},{3,2},{2,3},{5,4},{4,5},{7,6},{6,7},{9,8},{8,9},{11,10... | collective-permute-start | bytes 24584 | tf_op jit(solution)/shard_map/ppermute | solution.py:571
  76.3 1.3 %collective-permute-done.18 = f32[2,32,32]{2,1,0:T(8,128)S(1)} collective-permute-done((f32[2,32,32]{2,1,0:T(8,128)S(1)}, f32[2,32,32]{2,1,0:T(8,128)S(1)}, u32[]{:S(2)}, u32[]{:S(2)}) %collective-permute-start.18) | collective-permute-done | bytes 8224 | tf_op jit(solution)/shard_map/ppermute | solution.py:571
  77.6 1.7 %collective-permute-done.17 = f32[2,32,32]{2,1,0:T(8,128)S(1)} collective-permute-done((f32[2,32,32]{2,1,0:T(8,128)S(1)}, f32[2,32,32]{2,1,0:T(8,128)S(1)}, u32[]{:S(2)}, u32[]{:S(2)}) %collective-permute-start.17) | collective-permute-done | bytes 8224 | tf_op jit(solution)/shard_map/ppermute | solution.py:571
  (27 shorter events, 6.3 us)
Async XLA Ops:
  1.5 12.6 %collective-permute-start.2 = (bf16[2,32,512]{2,1,0:T(8,128)(2,1)S(1)}, bf16[2,32,512]{2,1,0:T(8,128)(2,1)S(1)}, u32[]{:S(2)}, u32[]{:S(2)}) collective-permute-start(bf16[2,32,512]{2,1,0:T(8,128)(2,1)S(1)} %convert_element_type.3.refs_0_), channel_id=1, source_target_pairs={{3,0},{2,1},{1,2},{0,3},{7,4},{6,5},{5,6},{4,7},{11,8},{10,9},{9,1... | collective-permute-start | bytes 196616 | tf_op jit(solution)/shard_map/ppermute | solution.py:571
  6.7 7.5 %collective-permute-start.1 = (bf16[2,32,512]{2,1,0:T(8,128)(2,1)S(1)}, bf16[2,32,512]{2,1,0:T(8,128)(2,1)S(1)}, u32[]{:S(2)}, u32[]{:S(2)}) collective-permute-start(bf16[2,32,512]{2,1,0:T(8,128)(2,1)S(1)} %convert_element_type.3.refs_0_), channel_id=1, source_target_pairs={{2,0},{3,1},{0,2},{1,3},{6,4},{7,5},{4,6},{5,7},{10,8},{11,9},{8,1... | collective-permute-start | bytes 196616 | tf_op jit(solution)/shard_map/ppermute | solution.py:571
  6.7 7.5 %collective-permute-start = (bf16[2,32,512]{2,1,0:T(8,128)(2,1)S(1)}, bf16[2,32,512]{2,1,0:T(8,128)(2,1)S(1)}, u32[]{:S(2)}, u32[]{:S(2)}) collective-permute-start(bf16[2,32,512]{2,1,0:T(8,128)(2,1)S(1)} %convert_element_type.3.refs_0_), channel_id=1, source_target_pairs={{1,0},{0,1},{3,2},{2,3},{5,4},{4,5},{7,6},{6,7},{9,8},{8,9},{11,10... | collective-permute-start | bytes 196616 | tf_op jit(solution)/shard_map/ppermute | solution.py:571
  15.7 9.8 %collective-permute-start.8 = (f32[32,512]{1,0:T(8,128)S(1)}, f32[32,512]{1,0:T(8,128)S(1)}, u32[]{:S(2)}, u32[]{:S(2)}) collective-permute-start(f32[32,512]{1,0:T(8,128)S(1)} %apply_first.3.refs_0_), channel_id=1, source_target_pairs={{3,0},{2,1},{1,2},{0,3},{7,4},{6,5},{5,6},{4,7},{11,8},{10,9},{9,1... | collective-permute-start | bytes 196616 | tf_op jit(solution)/shard_map/ppermute | solution.py:571
  19.5 6.6 %collective-permute-start.7 = (f32[32,512]{1,0:T(8,128)S(1)}, f32[32,512]{1,0:T(8,128)S(1)}, u32[]{:S(2)}, u32[]{:S(2)}) collective-permute-start(f32[32,512]{1,0:T(8,128)S(1)} %apply_first.3.refs_0_), channel_id=1, source_target_pairs={{2,0},{3,1},{0,2},{1,3},{6,4},{7,5},{4,6},{5,7},{10,8},{11,9},{8,1... | collective-permute-start | bytes 196616 | tf_op jit(solution)/shard_map/ppermute | solution.py:571
  19.5 6.6 %collective-permute-start.6 = (f32[32,512]{1,0:T(8,128)S(1)}, f32[32,512]{1,0:T(8,128)S(1)}, u32[]{:S(2)}, u32[]{:S(2)}) collective-permute-start(f32[32,512]{1,0:T(8,128)S(1)} %apply_first.3.refs_0_), channel_id=1, source_target_pairs={{1,0},{0,1},{3,2},{2,3},{5,4},{4,5},{7,6},{6,7},{9,8},{8,9},{11,10... | collective-permute-start | bytes 196616 | tf_op jit(solution)/shard_map/ppermute | solution.py:571
  21.7 7.5 %collective-permute-start.5 = (f32[32,512]{1,0:T(8,128)S(1)}, f32[32,512]{1,0:T(8,128)S(1)}, u32[]{:S(2)}, u32[]{:S(2)}) collective-permute-start(f32[32,512]{1,0:T(8,128)S(1)} %apply_first.2.refs_0_), channel_id=1, source_target_pairs={{3,0},{2,1},{1,2},{0,3},{7,4},{6,5},{5,6},{4,7},{11,8},{10,9},{9,1... | collective-permute-start | bytes 196616 | tf_op jit(solution)/shard_map/ppermute | solution.py:571
  25.5 5.2 %collective-permute-start.4 = (f32[32,512]{1,0:T(8,128)S(1)}, f32[32,512]{1,0:T(8,128)S(1)}, u32[]{:S(2)}, u32[]{:S(2)}) collective-permute-start(f32[32,512]{1,0:T(8,128)S(1)} %apply_first.2.refs_0_), channel_id=1, source_target_pairs={{2,0},{3,1},{0,2},{1,3},{6,4},{7,5},{4,6},{5,7},{10,8},{11,9},{8,1... | collective-permute-start | bytes 196616 | tf_op jit(solution)/shard_map/ppermute | solution.py:571
  25.5 5.2 %collective-permute-start.3 = (f32[32,512]{1,0:T(8,128)S(1)}, f32[32,512]{1,0:T(8,128)S(1)}, u32[]{:S(2)}, u32[]{:S(2)}) collective-permute-start(f32[32,512]{1,0:T(8,128)S(1)} %apply_first.2.refs_0_), channel_id=1, source_target_pairs={{1,0},{0,1},{3,2},{2,3},{5,4},{4,5},{7,6},{6,7},{9,8},{8,9},{11,10... | collective-permute-start | bytes 196616 | tf_op jit(solution)/shard_map/ppermute | solution.py:571
  41.7 7.0 %collective-permute-start.11 = (f32[144,128]{1,0:T(8,128)S(1)}, f32[144,128]{1,0:T(8,128)S(1)}, u32[]{:S(2)}, u32[]{:S(2)}) collective-permute-start(f32[144,128]{1,0:T(8,128)S(1)} %cross_gram.1), channel_id=1, source_target_pairs={{3,0},{2,1},{1,2},{0,3},{7,4},{6,5},{5,6},{4,7},{11,8},{10,9},{9,1... | collective-permute-start | bytes 221192 | tf_op jit(solution)/shard_map/ppermute | solution.py:571
  44.0 7.3 %collective-permute-start.10 = (f32[144,128]{1,0:T(8,128)S(1)}, f32[144,128]{1,0:T(8,128)S(1)}, u32[]{:S(2)}, u32[]{:S(2)}) collective-permute-start(f32[144,128]{1,0:T(8,128)S(1)} %cross_gram.1), channel_id=1, source_target_pairs={{2,0},{3,1},{0,2},{1,3},{6,4},{7,5},{4,6},{5,7},{10,8},{11,9},{8,1... | collective-permute-start | bytes 221192 | tf_op jit(solution)/shard_map/ppermute | solution.py:571
  44.0 7.3 %collective-permute-start.9 = (f32[144,128]{1,0:T(8,128)S(1)}, f32[144,128]{1,0:T(8,128)S(1)}, u32[]{:S(2)}, u32[]{:S(2)}) collective-permute-start(f32[144,128]{1,0:T(8,128)S(1)} %cross_gram.1), channel_id=1, source_target_pairs={{1,0},{0,1},{3,2},{2,3},{5,4},{4,5},{7,6},{6,7},{9,8},{8,9},{11,10... | collective-permute-start | bytes 221192 | tf_op jit(solution)/shard_map/ppermute | solution.py:571
  51.3 1.3 %collective-permute-start.12 = (f32[144,128]{1,0:T(8,128)S(1)}, f32[144,128]{1,0:T(8,128)S(1)}, u32[]{:S(2)}, u32[]{:S(2)}) collective-permute-start(f32[144,128]{1,0:T(8,128)S(1)} %add_add_fusion.refs_0_), channel_id=1, source_target_pairs={{4,0},{0,4},{12,8},{8,12},{5,1},{1,5},{13,9},{9,13},{6,2},{2,6},{1... | collective-permute-start | bytes 221192 | tf_op jit(solution)/shard_map/ppermute | solution.py:604
  60.6 6.7 %collective-permute-start.15 = (bf16[2,32,512]{2,1,0:T(8,128)(2,1)S(1)}, bf16[2,32,512]{2,1,0:T(8,128)(2,1)S(1)}, u32[]{:S(2)}, u32[]{:S(2)}) collective-permute-start(bf16[2,32,512]{2,1,0:T(8,128)(2,1)S(1)} %get-tuple-element.10.basis_ref), channel_id=1, source_target_pairs={{3,0},{2,1},{1,2},{0,3},{7,4},{6,5},{5,6},{4,7},{11,8},{10,9},{9,1... | collective-permute-start | bytes 196616 | tf_op jit(solution)/shard_map/ppermute | solution.py:571
  63.2 6.1 %collective-permute-start.14 = (bf16[2,32,512]{2,1,0:T(8,128)(2,1)S(1)}, bf16[2,32,512]{2,1,0:T(8,128)(2,1)S(1)}, u32[]{:S(2)}, u32[]{:S(2)}) collective-permute-start(bf16[2,32,512]{2,1,0:T(8,128)(2,1)S(1)} %get-tuple-element.10.basis_ref), channel_id=1, source_target_pairs={{2,0},{3,1},{0,2},{1,3},{6,4},{7,5},{4,6},{5,7},{10,8},{11,9},{8,1... | collective-permute-start | bytes 196616 | tf_op jit(solution)/shard_map/ppermute | solution.py:571
  63.2 6.1 %collective-permute-start.13 = (bf16[2,32,512]{2,1,0:T(8,128)(2,1)S(1)}, bf16[2,32,512]{2,1,0:T(8,128)(2,1)S(1)}, u32[]{:S(2)}, u32[]{:S(2)}) collective-permute-start(bf16[2,32,512]{2,1,0:T(8,128)(2,1)S(1)} %get-tuple-element.10.basis_ref), channel_id=1, source_target_pairs={{1,0},{0,1},{3,2},{2,3},{5,4},{4,5},{7,6},{6,7},{9,8},{8,9},{11,10... | collective-permute-start | bytes 196616 | tf_op jit(solution)/shard_map/ppermute | solution.py:571
  71.8 5.8 %collective-permute-start.18 = (f32[2,32,32]{2,1,0:T(8,128)S(1)}, f32[2,32,32]{2,1,0:T(8,128)S(1)}, u32[]{:S(2)}, u32[]{:S(2)}) collective-permute-start(f32[2,32,32]{2,1,0:T(8,128)S(1)} %apply_score.1), channel_id=1, source_target_pairs={{3,0},{2,1},{1,2},{0,3},{7,4},{6,5},{5,6},{4,7},{11,8},{10,9},{9,1... | collective-permute-start | bytes 24584 | tf_op jit(solution)/shard_map/ppermute | solution.py:571
  74.5 4.8 %collective-permute-start.17 = (f32[2,32,32]{2,1,0:T(8,128)S(1)}, f32[2,32,32]{2,1,0:T(8,128)S(1)}, u32[]{:S(2)}, u32[]{:S(2)}) collective-permute-start(f32[2,32,32]{2,1,0:T(8,128)S(1)} %apply_score.1), channel_id=1, source_target_pairs={{2,0},{3,1},{0,2},{1,3},{6,4},{7,5},{4,6},{5,7},{10,8},{11,9},{8,1... | collective-permute-start | bytes 24584 | tf_op jit(solution)/shard_map/ppermute | solution.py:571
  74.5 4.8 %collective-permute-start.16 = (f32[2,32,32]{2,1,0:T(8,128)S(1)}, f32[2,32,32]{2,1,0:T(8,128)S(1)}, u32[]{:S(2)}, u32[]{:S(2)}) collective-permute-start(f32[2,32,32]{2,1,0:T(8,128)S(1)} %apply_score.1), channel_id=1, source_target_pairs={{1,0},{0,1},{3,2},{2,3},{5,4},{4,5},{7,6},{6,7},{9,8},{8,9},{11,10... | collective-permute-start | bytes 24584 | tf_op jit(solution)/shard_map/ppermute | solution.py:571

commit v13 on v12

--- a/solution.py
+++ b/solution.py
@@ -64,9 +64,16 @@
     lax.fori_loop(0, BLK * BLK // 256, step, 0)
 
 
-def build_whole_kernel(rows_hbm, cols_hbm, counts_hbm, blocks_ref, *refs):
-    *dense_refs, held, rows_ref, cols_ref, counts_ref, arrived, index_arrived = refs
-    layers, chunks = len(dense_refs), dense_refs[0].shape[0]
+def fill(onehot, held, dense_ref, piece, width):
+    for v in range(width // 256):
+        cols = pl.ds(pl.multiple_of(piece * width + v * 256, 256), 256)
+        z = jnp.dot(onehot, held[:, cols], preferred_element_type=F32)
+        place(z, dense_ref.shape[0], piece * (width // 256) + v, dense_ref)
+
+
+def build_first_kernel(rows_hbm, cols_hbm, counts_hbm, blocks_ref, dense_ref, *refs):
+    *refs, held, rows_ref, cols_ref, counts_ref, arrived, index_arrived = refs
+    others, onehots = refs[: len(refs) // 2], refs[len(refs) // 2 :]
     index_copies = [
         pltpu.make_async_copy(source, target, index_arrived.at[i])
         for i, (source, target) in enumerate(
@@ -75,58 +82,107 @@
     ]
     for copy in index_copies:
         copy.start()
-    pieces = arrived.shape[1]
-    width = held.shape[2] // pieces
-    inner = width // 256
-
-    def fetch(layer, piece):
+    pieces = arrived.shape[0] - len(others)
+    width = held.shape[1] // pieces
+
+    def fetch(piece):
         cols = pl.ds(pl.multiple_of(piece * width, width), width)
-        return pltpu.make_async_copy(
-            blocks_ref.at[layer, :, cols], held.at[layer, :, cols], arrived.at[layer, piece]
-        )
-
-    for layer in range(layers):
-        for piece in range(pieces):
-            fetch(layer, piece).start()
-    flip = lax.axis_index("node") * CHUNK_COLS
+        return pltpu.make_async_copy(blocks_ref.at[0, :, cols], held.at[:, cols], arrived.at[piece])
+
+    for piece in range(pieces):
+        fetch(piece).start()
+    whole = [
+        pltpu.make_async_copy(blocks_ref.at[i + 1], other, arrived.at[pieces + i]) for i, other in enumerate(others)
+    ]
+    for copy in whole:
+        copy.start()
     for copy in index_copies:
         copy.wait()
-    for layer in range(layers):
-        onehot = one_hot(rows_ref, cols_ref, counts_ref, layer, flip, 0, chunks * CHUNK_COLS * BROWS)
-
-        def step(piece, carry):
-            fetch(layer, piece).wait()
-            for v in range(inner):
-                cols = pl.ds(pl.multiple_of(piece * width + v * 256, 256), 256)
-                z = jnp.dot(onehot, held[layer, :, cols], preferred_element_type=F32)
-                place(z, chunks, piece * inner + v, dense_refs[layer])
-            return carry
-
-        lax.fori_loop(0, pieces, step, 0)
+    flip = lax.axis_index("node") * CHUNK_COLS
+    positions = dense_ref.shape[0] * CHUNK_COLS * BROWS
+    onehot = one_hot(rows_ref, cols_ref, counts_ref, 0, flip, 0, positions)
+    for i, ref in enumerate(onehots):
+        ref[...] = one_hot(rows_ref, cols_ref, counts_ref, i + 1, flip, 0, positions)
+
+    def step(piece, carry):
+        fetch(piece).wait()
+        fill(onehot, held, dense_ref, piece, width)
+        return carry
+
+    lax.fori_loop(0, pieces, step, 0)
+    for copy in whole:
+        copy.wait()
+
+
+def build_next_kernel(onehot_ref, blocks_ref, dense_ref):
+    onehot = onehot_ref[...]
+    width = blocks_ref.shape[1] // 4
+
+    def step(piece, carry):
+        fill(onehot, blocks_ref, dense_ref, piece, width)
+        return carry
+
+    lax.fori_loop(0, 4, step, 0)
+
+
+def relay_kernel(x_ref, _, out_ref):
+    out_ref[...] = x_ref[...]
+
+
+def relay(x, after):
+    return pl.pallas_call(
+        relay_kernel,
+        in_specs=vmem_specs(1) + [pl.BlockSpec(memory_space=pl.ANY)],
+        out_specs=pl.BlockSpec(memory_space=pltpu.VMEM),
+        out_shape=jax.ShapeDtypeStruct(x.shape, x.dtype),
+        compiler_params=params(2),
+        name="relay",
+    )(x, after)
+
+
+def build_first(block_rows, block_cols, counts, blocks, chunk_total):
+    layers, slots, width = blocks.shape
+    dense = jax.ShapeDtypeStruct((chunk_total, 2 * TALL, CHUNK_LANES), BF16)
+    positions = chunk_total * CHUNK_COLS * BROWS
+    operands = (block_rows, block_cols, counts.T, blocks)
+    outs = pl.pallas_call(
+        build_first_kernel,
+        in_specs=[pl.BlockSpec(memory_space=pltpu.HBM)] * 4,
+        out_specs=vmem_specs(2 * layers - 1),
+        out_shape=[dense]
+        + [jax.ShapeDtypeStruct((slots, width), BF16)] * (layers - 1)
+        + [jax.ShapeDtypeStruct((positions, slots), BF16)] * (layers - 1),
+        scratch_shapes=[
+            pltpu.VMEM((slots, width), BF16),
+            pltpu.VMEM(block_rows.shape, jnp.int32),
+            pltpu.VMEM(block_cols.shape, jnp.int32),
+            pltpu.SMEM((1, layers), jnp.int32),
+            pltpu.SemaphoreType.DMA((4 + layers - 1,)),
+            pltpu.SemaphoreType.DMA((3,)),
+        ],
+        compiler_params=params(28),
+        cost_estimate=pl.CostEstimate(flops=0, bytes_accessed=12 * MIB, transcendentals=0),
+        name="build_first",
+    )(*[pltpu.with_memory_space_constraint(x, pltpu.HBM) for x in operands])
+    return outs[0], list(zip(outs[layers:], outs[1:layers]))
+
+
+def build_next(onehot, blocks, chunk_total):
+    return pl.pallas_call(
+        build_next_kernel,
+        in_specs=vmem_specs(2),
+        out_specs=pl.BlockSpec(memory_space=pltpu.VMEM),
+        out_shape=jax.ShapeDtypeStruct((chunk_total, 2 * TALL, CHUNK_LANES), BF16),
+        compiler_params=params(20),
+        cost_estimate=pl.CostEstimate(flops=0, bytes_accessed=12 * MIB, transcendentals=0),
+        name="build_next",
+    )(onehot, blocks)
 
 
 def build_dense(block_rows, block_cols, counts, blocks, chunk_total):
     layers, slots, width = blocks.shape
     dense = jax.ShapeDtypeStruct((layers, chunk_total, 2 * TALL, CHUNK_LANES), BF16)
     operands = (block_rows, block_cols, counts.T, blocks)
-    if chunk_total <= 4:
-        pieces = 4
-        return pl.pallas_call(
-            build_whole_kernel,
-            in_specs=[pl.BlockSpec(memory_space=pltpu.HBM)] * 4,
-            out_specs=vmem_specs(layers),
-            out_shape=[jax.ShapeDtypeStruct(dense.shape[1:], BF16)] * layers,
-            scratch_shapes=[
-                pltpu.VMEM(blocks.shape, BF16),
-                pltpu.VMEM(block_rows.shape, jnp.int32),
-                pltpu.VMEM(block_cols.shape, jnp.int32),
-                pltpu.SMEM((1, layers), jnp.int32),
-                pltpu.SemaphoreType.DMA((layers, pieces)),
-                pltpu.SemaphoreType.DMA((3,)),
-            ],
-            compiler_params=params(28),
-            name="build_dense",
-        )(*[pltpu.with_memory_space_constraint(x, pltpu.HBM) for x in operands])
     return pl.pallas_call(
         build_kernel,
         grid=(layers, chunk_total // 4),
@@ -227,7 +283,7 @@
 
 
 def first_kernel(layer, piece_count, *refs):
-    pieces, (dense_ref, out_ref, halves, tall) = refs[:piece_count], refs[piece_count:]
+    pieces, (dense_ref, _, out_ref, halves, tall) = refs[:piece_count], refs[piece_count:]
     total = image_of([piece[layer] for piece in pieces], dense_ref)
     out_ref[...] = to_wide(total, out_ref.shape[0], halves, tall)
 
@@ -245,18 +301,19 @@
     out_ref[before] = to_wide(image_of(parts, dense_ref), out_ref.shape[1], halves, tall)
 
 
-def own_kernel(basis_ref, *refs):
-    *dense_refs, out_ref = refs
+def some_kernel(chunk, layers, basis_ref, *refs):
+    dense_refs, (*so_far, out_ref) = refs[:layers], refs[layers:]
     for layer, dense_ref in enumerate(dense_refs):
-        out_ref[layer] = image_part(basis_ref[layer], dense_ref[0])
-
-
-def score_kernel(layers, piece_count, own_ref, *refs):
-    pieces, left_ref, refs = refs[:piece_count], refs[piece_count], refs[piece_count + 1 :]
+        part = image_part(basis_ref[layer], dense_ref[chunk])
+        out_ref[layer] = sum((ref[layer] for ref in so_far), part)
+
+
+def score_kernel(layers, chunks, so_far_ref, *refs):
+    pieces, left_ref, refs = refs[: len(chunks)], refs[len(chunks)], refs[len(chunks) + 1 :]
     dense_refs, (out_ref, halves, tall) = refs[:layers], refs[layers:]
     totals = [
-        own_ref[layer]
-        + sum(image_part(piece[layer], dense_refs[layer][d + 1]) for d, piece in enumerate(pieces))
+        so_far_ref[layer]
+        + sum(image_part(piece[layer], dense_refs[layer][chunk]) for chunk, piece in zip(chunks, pieces))
         for layer in range(layers)
     ]
     wide = [
@@ -266,22 +323,22 @@
         out_ref[layer] = product(left_ref[layer], wide[layer])
 
 
-def apply_whole(kernel, name, operands, out_shape, *lead, scratch=()):
+def apply_whole(kernel, name, operands, out_shape, *lead, scratch=(), after=()):
     return pl.pallas_call(
         kernel,
-        in_specs=vmem_specs(len(operands)),
+        in_specs=vmem_specs(len(operands)) + [pl.BlockSpec(memory_space=pl.ANY)] * len(after),
         out_specs=pl.BlockSpec(memory_space=pltpu.VMEM),
         out_shape=jax.ShapeDtypeStruct(out_shape, F32),
         scratch_shapes=[pltpu.VMEM((*lead, TALL, 128), F32), pltpu.VMEM((*lead, ROWS_DEV, 128), F32), *scratch],
         compiler_params=params(14),
         cost_estimate=pl.CostEstimate(flops=0, bytes_accessed=4 * MIB, transcendentals=0),
         name=name,
-    )(*operands)
-
-
-def apply_first(layer, pieces, dense):
+    )(*operands, *after)
+
+
+def apply_first(layer, pieces, dense, after):
     kernel = functools.partial(first_kernel, layer, len(pieces))
-    return apply_whole(kernel, "apply_first", [*pieces, dense], pieces[0].shape[1:])
+    return apply_whole(kernel, "apply_first", [*pieces, dense], pieces[0].shape[1:], after=[after])
 
 
 def apply_second(pieces, dense, earlier):
@@ -292,23 +349,26 @@
     return apply_whole(kernel, "apply_second", operands, shape, scratch=[pltpu.VMEM(SPREAD, F32)])
 
 
-def apply_own(basis, dense):
+def apply_some(chunk, basis, dense, *so_far):
     layers, k = basis.shape[:2]
     return pl.pallas_call(
-        own_kernel,
-        in_specs=vmem_specs(1 + layers),
+        functools.partial(some_kernel, chunk, layers),
+        in_specs=vmem_specs(1 + layers + len(so_far)),
         out_specs=pl.BlockSpec(memory_space=pltpu.VMEM),
         out_shape=jax.ShapeDtypeStruct((layers, 2 * TALL, 2 * k), F32),
         compiler_params=params(14),
         cost_estimate=pl.CostEstimate(flops=0, bytes_accessed=2 * MIB, transcendentals=0),
-        name="apply_own",
-    )(basis, *dense)
+        name=f"apply_some_{chunk}",
+    )(basis, *dense, *so_far)
 
 
 def apply_score(pieces, left, dense):
-    kernel = functools.partial(score_kernel, len(dense), len(pieces) - 1)
+    last = len(pieces) - 1
+    so_far = apply_some(last, pieces[last], dense, apply_some(0, pieces[0], dense))
+    chunks = range(1, last)
+    kernel = functools.partial(score_kernel, len(dense), chunks)
     layers, k = left.shape[:2]
-    operands = [apply_own(pieces[0], dense), *pieces[1:], left, *dense]
+    operands = [so_far, *pieces[1:last], left, *dense]
     return apply_whole(kernel, "apply_score", operands, (layers, k, k), layers)
 
 
@@ -565,11 +625,12 @@
     )(own, other, images)
 
 
+def swap(x, axis, d, count):
+    return lax.ppermute(x, axis, [(m ^ d, m) for m in range(count)])
+
+
 def around(x, axis, count):
-    pieces = [x]
-    for d in range(1, count):
-        pieces.append(lax.ppermute(x, axis, [(m ^ d, m) for m in range(count)]))
-    return pieces
+    return [x] + [swap(x, axis, d, count) for d in range(1, count)]
 
 
 def add_pieces(pieces):
@@ -588,20 +649,26 @@
     def total(x):
         return add_pieces(around(x, "node", shards)) if few else lax.psum(x, "node")
 
-    first = gather(start.astype(BF16))
-    dense = build_dense(block_rows, block_cols, counts, blocks, shards * BROWS // CHUNK_COLS)
+    rounded = start.astype(BF16)
+    chunk_total = shards * BROWS // CHUNK_COLS
     if few:
-        images = [apply_first(layer, first, dense[layer]) for layer in range(layers)]
+        near, far = swap(rounded, "node", 1, shards), swap(rounded, "node", 2, shards)
+        dense_first, rest = build_first(block_rows, block_cols, counts, blocks, chunk_total)
+        far = relay(far, dense_first)
+        dense = [dense_first] + [build_next(*one, chunk_total) for one in rest]
+        first = [rounded, near, far, swap(far, "node", 1, shards)]
+        images = [apply_first(layer, first, dense[layer], dense[-1]) for layer in range(layers)]
         image = None
         for layer in range(layers):
             image = apply_second(gather(images[layer]), dense[layer], [] if image is None else [image])
     else:
-        image, gram = apply_dense("gram", first, dense)
+        dense = build_dense(block_rows, block_cols, counts, blocks, chunk_total)
+        image, gram = apply_dense("gram", gather(rounded), dense)
         (image,) = apply_dense("plain", gather(solve(total(gram), image)), dense)
     images = lax.all_gather(image, "layer", axis=0, tiled=True)
     own = cross(images)
     own = total(own)
-    other = lax.ppermute(own, "layer", [(m ^ 1, m) for m in range(groups)])
+    other = swap(own, "layer", 1, groups)
     joint_basis, again, rounded = joint_solve(own, other, images, start.shape)
     if few:
         partial = apply_score(gather(rounded), again, dense)

time: 80.1 us -> 79 us (0.986)
  waiting for transfers between devices: 14.5 us -> 13.6 us
    ppermute x19, waiting for transfers between devices: 14.5 us -> 13.6 us  [swap(): return lax.ppermute(x, axis, [(m ^ d, m) for m in range(count)])]
    pallas_call x7 -> x10, Pallas kernels: 19.2 us -> 18.6 us  [the longest x5 11.1 us: apply_whole(): pl.pallas_call(kernel, in_specs=vmem_specs(len(operands)) + [pl.BlockSpec...]
  transfers between devices with their start and end apart: 19 -> 19, of which waited for: 8 -> 9; matrix products, arithmetic and copies ran while one was open for 0% -> 0% of each run, Pallas kernels for 15% -> 15%
where the time goes in v13:
time: 79 us; the launch traced here: 78.8 us
  starting transfers between devices  28.4 us (36%)
  Pallas kernels  27.1 us (34%)
  waiting for transfers between devices  13.6 us (17%)
  blocking collectives  7.36 us (9%)
  other arithmetic  1.56 us (2%)
    ppermute x19, starting transfers between devices, swap(): return lax.ppermute(x, axis, [(m ^ d, m) for m in range(count)])  28.4 us
    ppermute x19, waiting for transfers between devices, swap(): return lax.ppermute(x, axis, [(m ^ d, m) for m in range(count)])  13.6 us
    pallas_call x5, Pallas kernels, apply_whole(): pl.pallas_call(kernel, in_specs=vmem_specs(len(operands)) + [pl.BlockSpec...  11.1 us
    pallas_call x1, Pallas kernels, joint_solve(): pl.pallas_call(functools.partial(joint_kernel, k), in_specs=vmem_specs(3)...  7.92 us
    all_gather x1, blocking collectives, per_device(): images = lax.all_gather(image, 'layer', axis=0, tiled=True)  7.36 us
    pallas_call x1, Pallas kernels, build_first(): pl.pallas_call(build_first_kernel, in_specs=[pl.BlockSpec(memory_space=pl...  3.92 us
    pallas_call x1, Pallas kernels, build_next(): pl.pallas_call(build_next_kernel, in_specs=vmem_specs(2), out_specs=pl.Bl...  2.02 us
  transfers between devices with their start and end apart: 19, of which 9 were waited for; matrix products, arithmetic and copies ran while one was open for 0% of the time, Pallas kernels for 15%

profile of v13, /device:TPU:0, one launch (start us, length us, event | category | flops | bytes accessed | tf_op | source)
XLA Modules:
  0.0 78.8 jit_solution(15968496151720127600)
XLA Ops:
  1.5 4.1 %collective-permute-start.1 = (bf16[2,32,512]{2,1,0:T(8,128)(2,1)S(1)}, bf16[2,32,512]{2,1,0:T(8,128)(2,1)S(1)}, u32[]{:S(2)}, u32[]{:S(2)}) collective-permute-start(bf16[2,32,512]{2,1,0:T(8,128)(2,1)S(1)} %convert_element_type.3.refs_0_), channel_id=1, source_target_pairs={{2,0},{3,1},{0,2},{1,3},{6,4},{7,5},{4,6},{5,7},{10,8},{11,9},{8,1... | collective-permute-start | bytes 196616 | tf_op jit(solution)/shard_map/ppermute | solution.py:629
  5.6 1.6 %collective-permute-start = (bf16[2,32,512]{2,1,0:T(8,128)(2,1)S(1)}, bf16[2,32,512]{2,1,0:T(8,128)(2,1)S(1)}, u32[]{:S(2)}, u32[]{:S(2)}) collective-permute-start(bf16[2,32,512]{2,1,0:T(8,128)(2,1)S(1)} %convert_element_type.3.refs_0_), channel_id=1, source_target_pairs={{1,0},{0,1},{3,2},{2,3},{5,4},{4,5},{7,6},{6,7},{9,8},{8,9},{11,10... | collective-permute-start | bytes 196616 | tf_op jit(solution)/shard_map/ppermute | solution.py:629
  7.2 3.9 %build_first.1 = (bf16[4,512,1024]{2,1,0:T(8,128)(2,1)S(1)}, bf16[512,4096]{1,0:T(8,128)(2,1)S(1)}, bf16[256,512]{1,0:T(8,128)(2,1)S(1)}) custom-call(s32[2,512]{1,0:T(2,128)} %rows_hbm.1, s32[2,512]{1,0:T(2,128)} %cols_hbm.1, s32[1,2]{1,0:T(1,128)} %bitcast.1, bf16[2,512,4096]{2,1,0:T(8,128)(2,1)} %blocks_ref.1), custom_call_target="tpu_custom_call" | custom-call | bytes 12582912 | tf_op jit(solution)/shard_map/build_first/pallas_call | solution.py:148
  11.7 2.0 %build_next.1.refs_4_.refs_5_.refs_1_ = bf16[4,512,1024]{2,1,0:T(8,128)(2,1)S(1)} custom-call(bf16[256,512]{1,0:T(8,128)(2,1)S(1)} %get-tuple-element.9.onehot_ref, bf16[512,4096]{1,0:T(8,128)(2,1)S(1)} %get-tuple-element.10.blocks_ref), custom_call_target="tpu_custom_call" | custom-call | bytes 12582912 | tf_op jit(solution)/shard_map/build_next/pallas_call | solution.py:171
  13.7 1.8 %collective-permute-done.2.refs_3_ = bf16[2,32,512]{2,1,0:T(8,128)(2,1)S(1)} collective-permute-done((bf16[2,32,512]{2,1,0:T(8,128)(2,1)S(1)}, bf16[2,32,512]{2,1,0:T(8,128)(2,1)S(1)}, u32[]{:S(2)}, u32[]{:S(2)}) %collective-permute-start.2) | collective-permute-done | bytes 65568 | tf_op jit(solution)/shard_map/ppermute | solution.py:629
  15.5 1.5 %apply_first.3.refs_0_ = f32[32,512]{1,0:T(8,128)S(1)} custom-call(bf16[2,32,512]{2,1,0:T(8,128)(2,1)S(1)} %convert_element_type.3.refs_0_, bf16[2,32,512]{2,1,0:T(8,128)(2,1)S(1)} %collective-permute-done.refs_1_, bf16[2,32,512]{2,1,0:T(8,128)(2,1)S(1)} %relay.1.refs_2_, bf16[2,32,512]{2,1,0:T(8,128)(2,1)S(1)} %collective-permute-done.2.refs_3_, ...), custom_call_target="tpu_custom_call" | custom-call | bytes 4194304 | tf_op jit(solution)/shard_map/apply_first/pallas_call | solution.py:327
  17.0 1.5 %collective-permute-start.8 = (f32[32,512]{1,0:T(8,128)S(1)}, f32[32,512]{1,0:T(8,128)S(1)}, u32[]{:S(2)}, u32[]{:S(2)}) collective-permute-start(f32[32,512]{1,0:T(8,128)S(1)} %apply_first.3.refs_0_), channel_id=1, source_target_pairs={{3,0},{2,1},{1,2},{0,3},{7,4},{6,5},{5,6},{4,7},{11,8},{10,9},{9,1... | collective-permute-start | bytes 196616 | tf_op jit(solution)/shard_map/ppermute | solution.py:629
  19.0 2.5 %collective-permute-start.6 = (f32[32,512]{1,0:T(8,128)S(1)}, f32[32,512]{1,0:T(8,128)S(1)}, u32[]{:S(2)}, u32[]{:S(2)}) collective-permute-start(f32[32,512]{1,0:T(8,128)S(1)} %apply_first.3.refs_0_), channel_id=1, source_target_pairs={{1,0},{0,1},{3,2},{2,3},{5,4},{4,5},{7,6},{6,7},{9,8},{8,9},{11,10... | collective-permute-start | bytes 196616 | tf_op jit(solution)/shard_map/ppermute | solution.py:629
  21.5 1.5 %apply_first.2.refs_0_ = f32[32,512]{1,0:T(8,128)S(1)} custom-call(bf16[2,32,512]{2,1,0:T(8,128)(2,1)S(1)} %convert_element_type.3.refs_0_, bf16[2,32,512]{2,1,0:T(8,128)(2,1)S(1)} %collective-permute-done.refs_1_, bf16[2,32,512]{2,1,0:T(8,128)(2,1)S(1)} %relay.1.refs_2_, bf16[2,32,512]{2,1,0:T(8,128)(2,1)S(1)} %collective-permute-done.2.refs_3_, ...), custom_call_target="tpu_custom_call" | custom-call | bytes 4194304 | tf_op jit(solution)/shard_map/apply_first/pallas_call | solution.py:327
  23.0 1.5 %collective-permute-start.5 = (f32[32,512]{1,0:T(8,128)S(1)}, f32[32,512]{1,0:T(8,128)S(1)}, u32[]{:S(2)}, u32[]{:S(2)}) collective-permute-start(f32[32,512]{1,0:T(8,128)S(1)} %apply_first.2.refs_0_), channel_id=1, source_target_pairs={{3,0},{2,1},{1,2},{0,3},{7,4},{6,5},{5,6},{4,7},{11,8},{10,9},{9,1... | collective-permute-start | bytes 196616 | tf_op jit(solution)/shard_map/ppermute | solution.py:629
  24.5 2.9 %collective-permute-start.3 = (f32[32,512]{1,0:T(8,128)S(1)}, f32[32,512]{1,0:T(8,128)S(1)}, u32[]{:S(2)}, u32[]{:S(2)}) collective-permute-start(f32[32,512]{1,0:T(8,128)S(1)} %apply_first.2.refs_0_), channel_id=1, source_target_pairs={{1,0},{0,1},{3,2},{2,3},{5,4},{4,5},{7,6},{6,7},{9,8},{8,9},{11,10... | collective-permute-start | bytes 196616 | tf_op jit(solution)/shard_map/ppermute | solution.py:629
  27.5 3.0 %apply_second.2.refs_5_ = f32[1,32,512]{2,1,0:T(8,128)S(1)} custom-call(f32[32,512]{1,0:T(8,128)S(1)} %apply_first.3.refs_0_, f32[32,512]{1,0:T(8,128)S(1)} %collective-permute-done.6.refs_1_, f32[32,512]{1,0:T(8,128)S(1)} %collective-permute-done.7.refs_2_, f32[32,512]{1,0:T(8,128)S(1)} %collective-permute-done.8.refs_3_, ...), custom_call_target="tpu_custom_call" | custom-call | bytes 4194304 | tf_op jit(solution)/shard_map/apply_second/pallas_call | solution.py:327
  30.5 3.0 %apply_second.3 = f32[2,32,512]{2,1,0:T(8,128)S(1)} custom-call(f32[32,512]{1,0:T(8,128)S(1)} %apply_first.2.refs_0_, f32[32,512]{1,0:T(8,128)S(1)} %collective-permute-done.3.refs_1_, f32[32,512]{1,0:T(8,128)S(1)} %collective-permute-done.4.refs_2_, f32[32,512]{1,0:T(8,128)S(1)} %collective-permute-done.5.refs_3_, ...), custom_call_target="tpu_custom_call" | custom-call | bytes 4194304 | tf_op jit(solution)/shard_map/apply_second/pallas_call | solution.py:327
  33.5 7.4 %all_gather.3.images_ref.refs_2_ = f32[8,32,512]{2,1,0:T(8,128)S(1)} all-gather(f32[2,32,512]{2,1,0:T(8,128)S(1)} %apply_second.3), channel_id=1, replica_groups=mesh['parts'=2,'layer'=4,'node'=4] {'layer'}, dimensions={0}, use_global_device_ids=true | all-gather | bytes 655360 | tf_op jit(solution)/shard_map/all_gather | solution.py:668
  41.5 1.6 %collective-permute-start.11 = (f32[144,128]{1,0:T(8,128)S(1)}, f32[144,128]{1,0:T(8,128)S(1)}, u32[]{:S(2)}, u32[]{:S(2)}) collective-permute-start(f32[144,128]{1,0:T(8,128)S(1)} %cross_gram.1), channel_id=1, source_target_pairs={{3,0},{2,1},{1,2},{0,3},{7,4},{6,5},{5,6},{4,7},{11,8},{10,9},{9,1... | collective-permute-start | bytes 221192 | tf_op jit(solution)/shard_map/ppermute | solution.py:629
  44.3 1.7 %collective-permute-start.9 = (f32[144,128]{1,0:T(8,128)S(1)}, f32[144,128]{1,0:T(8,128)S(1)}, u32[]{:S(2)}, u32[]{:S(2)}) collective-permute-start(f32[144,128]{1,0:T(8,128)S(1)} %cross_gram.1), channel_id=1, source_target_pairs={{1,0},{0,1},{3,2},{2,3},{5,4},{4,5},{7,6},{6,7},{9,8},{8,9},{11,10... | collective-permute-start | bytes 221192 | tf_op jit(solution)/shard_map/ppermute | solution.py:629
  46.0 2.6 %collective-permute-done.11 = f32[144,128]{1,0:T(8,128)S(1)} collective-permute-done((f32[144,128]{1,0:T(8,128)S(1)}, f32[144,128]{1,0:T(8,128)S(1)}, u32[]{:S(2)}, u32[]{:S(2)}) %collective-permute-start.11) | collective-permute-done | bytes 73760 | tf_op jit(solution)/shard_map/ppermute | solution.py:629
  48.6 2.9 %collective-permute-done.10 = f32[144,128]{1,0:T(8,128)S(1)} collective-permute-done((f32[144,128]{1,0:T(8,128)S(1)}, f32[144,128]{1,0:T(8,128)S(1)}, u32[]{:S(2)}, u32[]{:S(2)}) %collective-permute-start.10) | collective-permute-done | bytes 73760 | tf_op jit(solution)/shard_map/ppermute | solution.py:629
  52.8 7.9 %joint_solve.1 = (f32[2,32,512]{2,1,0:T(8,128)}, f32[2,32,512]{2,1,0:T(8,128)S(1)}, bf16[2,32,512]{2,1,0:T(8,128)(2,1)S(1)}) custom-call(f32[144,128]{1,0:T(8,128)S(1)} %add_add_fusion.refs_0_, f32[144,128]{1,0:T(8,128)S(1)} %collective-permute-done.12.refs_1_, f32[8,32,512]{2,1,0:T(8,128)S(1)} %all_gather.3.images_ref.refs_2_), custom_call_target="tpu_custom_call" | custom-call | tf_op jit(solution)/shard_map/joint_solve/pallas_call | solution.py:609
  62.2 2.9 %collective-permute-start.14 = (bf16[2,32,512]{2,1,0:T(8,128)(2,1)S(1)}, bf16[2,32,512]{2,1,0:T(8,128)(2,1)S(1)}, u32[]{:S(2)}, u32[]{:S(2)}) collective-permute-start(bf16[2,32,512]{2,1,0:T(8,128)(2,1)S(1)} %get-tuple-element.12.basis_ref), channel_id=1, source_target_pairs={{1,0},{0,1},{3,2},{2,3},{5,4},{4,5},{7,6},{6,7},{9,8},{8,9},{11,10... | collective-permute-start | bytes 196616 | tf_op jit(solution)/shard_map/ppermute | solution.py:629
  65.9 1.6 %collective-permute-done.13.basis_ref = bf16[2,32,512]{2,1,0:T(8,128)(2,1)S(1)} collective-permute-done((bf16[2,32,512]{2,1,0:T(8,128)(2,1)S(1)}, bf16[2,32,512]{2,1,0:T(8,128)(2,1)S(1)}, u32[]{:S(2)}, u32[]{:S(2)}) %collective-permute-start.13) | collective-permute-done | bytes 65568 | tf_op jit(solution)/shard_map/ppermute | solution.py:629
  69.5 2.0 %apply_score.1 = f32[2,32,32]{2,1,0:T(8,128)S(1)} custom-call(f32[2,512,64]{2,1,0:T(8,128)S(1)} %apply_some_3.1.so_far_ref, bf16[2,32,512]{2,1,0:T(8,128)(2,1)S(1)} %collective-permute-done.14.refs_0_, bf16[2,32,512]{2,1,0:T(8,128)(2,1)S(1)} %collective-permute-done.15.refs_1_, f32[2,32,512]{2,1,0:T(8,128)S(1)} %get-tuple-element.13.refs_2_, ...), custom_call_target="tpu_custom_call" | custom-call | bytes 4194304 | tf_op jit(solution)/shard_map/apply_score/pallas_call | solution.py:327
  71.5 1.5 %collective-permute-start.18 = (f32[2,32,32]{2,1,0:T(8,128)S(1)}, f32[2,32,32]{2,1,0:T(8,128)S(1)}, u32[]{:S(2)}, u32[]{:S(2)}) collective-permute-start(f32[2,32,32]{2,1,0:T(8,128)S(1)} %apply_score.1), channel_id=1, source_target_pairs={{3,0},{2,1},{1,2},{0,3},{7,4},{6,5},{5,6},{4,7},{11,8},{10,9},{9,1... | collective-permute-start | bytes 24584 | tf_op jit(solution)/shard_map/ppermute | solution.py:629
  73.0 2.9 %collective-permute-start.16 = (f32[2,32,32]{2,1,0:T(8,128)S(1)}, f32[2,32,32]{2,1,0:T(8,128)S(1)}, u32[]{:S(2)}, u32[]{:S(2)}) collective-permute-start(f32[2,32,32]{2,1,0:T(8,128)S(1)} %apply_score.1), channel_id=1, source_target_pairs={{1,0},{0,1},{3,2},{2,3},{5,4},{4,5},{7,6},{6,7},{9,8},{8,9},{11,10... | collective-permute-start | bytes 24584 | tf_op jit(solution)/shard_map/ppermute | solution.py:629
  (30 shorter events, 12.2 us)
Async XLA Ops:
  1.5 9.6 %collective-permute-start.1 = (bf16[2,32,512]{2,1,0:T(8,128)(2,1)S(1)}, bf16[2,32,512]{2,1,0:T(8,128)(2,1)S(1)}, u32[]{:S(2)}, u32[]{:S(2)}) collective-permute-start(bf16[2,32,512]{2,1,0:T(8,128)(2,1)S(1)} %convert_element_type.3.refs_0_), channel_id=1, source_target_pairs={{2,0},{3,1},{0,2},{1,3},{6,4},{7,5},{4,6},{5,7},{10,8},{11,9},{8,1... | collective-permute-start | bytes 196616 | tf_op jit(solution)/shard_map/ppermute | solution.py:629
  5.6 8.1 %collective-permute-start = (bf16[2,32,512]{2,1,0:T(8,128)(2,1)S(1)}, bf16[2,32,512]{2,1,0:T(8,128)(2,1)S(1)}, u32[]{:S(2)}, u32[]{:S(2)}) collective-permute-start(bf16[2,32,512]{2,1,0:T(8,128)(2,1)S(1)} %convert_element_type.3.refs_0_), channel_id=1, source_target_pairs={{1,0},{0,1},{3,2},{2,3},{5,4},{4,5},{7,6},{6,7},{9,8},{8,9},{11,10... | collective-permute-start | bytes 196616 | tf_op jit(solution)/shard_map/ppermute | solution.py:629
  11.2 4.3 %collective-permute-start.2 = (bf16[2,32,512]{2,1,0:T(8,128)(2,1)S(1)}, bf16[2,32,512]{2,1,0:T(8,128)(2,1)S(1)}, u32[]{:S(2)}, u32[]{:S(2)}) collective-permute-start(bf16[2,32,512]{2,1,0:T(8,128)(2,1)S(1)} %relay.1.refs_2_), channel_id=1, source_target_pairs={{1,0},{0,1},{3,2},{2,3},{5,4},{4,5},{7,6},{6,7},{9,8},{8,9},{11,10... | collective-permute-start | bytes 196616 | tf_op jit(solution)/shard_map/ppermute | solution.py:629
  17.0 7.5 %collective-permute-start.8 = (f32[32,512]{1,0:T(8,128)S(1)}, f32[32,512]{1,0:T(8,128)S(1)}, u32[]{:S(2)}, u32[]{:S(2)}) collective-permute-start(f32[32,512]{1,0:T(8,128)S(1)} %apply_first.3.refs_0_), channel_id=1, source_target_pairs={{3,0},{2,1},{1,2},{0,3},{7,4},{6,5},{5,6},{4,7},{11,8},{10,9},{9,1... | collective-permute-start | bytes 196616 | tf_op jit(solution)/shard_map/ppermute | solution.py:629
  18.5 8.9 %collective-permute-start.7 = (f32[32,512]{1,0:T(8,128)S(1)}, f32[32,512]{1,0:T(8,128)S(1)}, u32[]{:S(2)}, u32[]{:S(2)}) collective-permute-start(f32[32,512]{1,0:T(8,128)S(1)} %apply_first.3.refs_0_), channel_id=1, source_target_pairs={{2,0},{3,1},{0,2},{1,3},{6,4},{7,5},{4,6},{5,7},{10,8},{11,9},{8,1... | collective-permute-start | bytes 196616 | tf_op jit(solution)/shard_map/ppermute | solution.py:629
  19.0 8.5 %collective-permute-start.6 = (f32[32,512]{1,0:T(8,128)S(1)}, f32[32,512]{1,0:T(8,128)S(1)}, u32[]{:S(2)}, u32[]{:S(2)}) collective-permute-start(f32[32,512]{1,0:T(8,128)S(1)} %apply_first.3.refs_0_), channel_id=1, source_target_pairs={{1,0},{0,1},{3,2},{2,3},{5,4},{4,5},{7,6},{6,7},{9,8},{8,9},{11,10... | collective-permute-start | bytes 196616 | tf_op jit(solution)/shard_map/ppermute | solution.py:629
  23.0 7.5 %collective-permute-start.5 = (f32[32,512]{1,0:T(8,128)S(1)}, f32[32,512]{1,0:T(8,128)S(1)}, u32[]{:S(2)}, u32[]{:S(2)}) collective-permute-start(f32[32,512]{1,0:T(8,128)S(1)} %apply_first.2.refs_0_), channel_id=1, source_target_pairs={{3,0},{2,1},{1,2},{0,3},{7,4},{6,5},{5,6},{4,7},{11,8},{10,9},{9,1... | collective-permute-start | bytes 196616 | tf_op jit(solution)/shard_map/ppermute | solution.py:629
  24.5 6.0 %collective-permute-start.4 = (f32[32,512]{1,0:T(8,128)S(1)}, f32[32,512]{1,0:T(8,128)S(1)}, u32[]{:S(2)}, u32[]{:S(2)}) collective-permute-start(f32[32,512]{1,0:T(8,128)S(1)} %apply_first.2.refs_0_), channel_id=1, source_target_pairs={{2,0},{3,1},{0,2},{1,3},{6,4},{7,5},{4,6},{5,7},{10,8},{11,9},{8,1... | collective-permute-start | bytes 196616 | tf_op jit(solution)/shard_map/ppermute | solution.py:629
  24.5 6.0 %collective-permute-start.3 = (f32[32,512]{1,0:T(8,128)S(1)}, f32[32,512]{1,0:T(8,128)S(1)}, u32[]{:S(2)}, u32[]{:S(2)}) collective-permute-start(f32[32,512]{1,0:T(8,128)S(1)} %apply_first.2.refs_0_), channel_id=1, source_target_pairs={{1,0},{0,1},{3,2},{2,3},{5,4},{4,5},{7,6},{6,7},{9,8},{8,9},{11,10... | collective-permute-start | bytes 196616 | tf_op jit(solution)/shard_map/ppermute | solution.py:629
  41.5 7.0 %collective-permute-start.11 = (f32[144,128]{1,0:T(8,128)S(1)}, f32[144,128]{1,0:T(8,128)S(1)}, u32[]{:S(2)}, u32[]{:S(2)}) collective-permute-start(f32[144,128]{1,0:T(8,128)S(1)} %cross_gram.1), channel_id=1, source_target_pairs={{3,0},{2,1},{1,2},{0,3},{7,4},{6,5},{5,6},{4,7},{11,8},{10,9},{9,1... | collective-permute-start | bytes 221192 | tf_op jit(solution)/shard_map/ppermute | solution.py:629
  43.1 8.4 %collective-permute-start.10 = (f32[144,128]{1,0:T(8,128)S(1)}, f32[144,128]{1,0:T(8,128)S(1)}, u32[]{:S(2)}, u32[]{:S(2)}) collective-permute-start(f32[144,128]{1,0:T(8,128)S(1)} %cross_gram.1), channel_id=1, source_target_pairs={{2,0},{3,1},{0,2},{1,3},{6,4},{7,5},{4,6},{5,7},{10,8},{11,9},{8,1... | collective-permute-start | bytes 221192 | tf_op jit(solution)/shard_map/ppermute | solution.py:629
  44.3 7.2 %collective-permute-start.9 = (f32[144,128]{1,0:T(8,128)S(1)}, f32[144,128]{1,0:T(8,128)S(1)}, u32[]{:S(2)}, u32[]{:S(2)}) collective-permute-start(f32[144,128]{1,0:T(8,128)S(1)} %cross_gram.1), channel_id=1, source_target_pairs={{1,0},{0,1},{3,2},{2,3},{5,4},{4,5},{7,6},{6,7},{9,8},{8,9},{11,10... | collective-permute-start | bytes 221192 | tf_op jit(solution)/shard_map/ppermute | solution.py:629
  51.5 1.3 %collective-permute-start.12 = (f32[144,128]{1,0:T(8,128)S(1)}, f32[144,128]{1,0:T(8,128)S(1)}, u32[]{:S(2)}, u32[]{:S(2)}) collective-permute-start(f32[144,128]{1,0:T(8,128)S(1)} %add_add_fusion.refs_0_), channel_id=1, source_target_pairs={{4,0},{0,4},{12,8},{8,12},{5,1},{1,5},{13,9},{9,13},{6,2},{2,6},{1... | collective-permute-start | bytes 221192 | tf_op jit(solution)/shard_map/ppermute | solution.py:629
  60.8 6.8 %collective-permute-start.13 = (bf16[2,32,512]{2,1,0:T(8,128)(2,1)S(1)}, bf16[2,32,512]{2,1,0:T(8,128)(2,1)S(1)}, u32[]{:S(2)}, u32[]{:S(2)}) collective-permute-start(bf16[2,32,512]{2,1,0:T(8,128)(2,1)S(1)} %get-tuple-element.12.basis_ref), channel_id=1, source_target_pairs={{3,0},{2,1},{1,2},{0,3},{7,4},{6,5},{5,6},{4,7},{11,8},{10,9},{9,1... | collective-permute-start | bytes 196616 | tf_op jit(solution)/shard_map/ppermute | solution.py:629
  62.2 7.3 %collective-permute-start.15 = (bf16[2,32,512]{2,1,0:T(8,128)(2,1)S(1)}, bf16[2,32,512]{2,1,0:T(8,128)(2,1)S(1)}, u32[]{:S(2)}, u32[]{:S(2)}) collective-permute-start(bf16[2,32,512]{2,1,0:T(8,128)(2,1)S(1)} %get-tuple-element.12.basis_ref), channel_id=1, source_target_pairs={{2,0},{3,1},{0,2},{1,3},{6,4},{7,5},{4,6},{5,7},{10,8},{11,9},{8,1... | collective-permute-start | bytes 196616 | tf_op jit(solution)/shard_map/ppermute | solution.py:629
  62.2 7.3 %collective-permute-start.14 = (bf16[2,32,512]{2,1,0:T(8,128)(2,1)S(1)}, bf16[2,32,512]{2,1,0:T(8,128)(2,1)S(1)}, u32[]{:S(2)}, u32[]{:S(2)}) collective-permute-start(bf16[2,32,512]{2,1,0:T(8,128)(2,1)S(1)} %get-tuple-element.12.basis_ref), channel_id=1, source_target_pairs={{1,0},{0,1},{3,2},{2,3},{5,4},{4,5},{7,6},{6,7},{9,8},{8,9},{11,10... | collective-permute-start | bytes 196616 | tf_op jit(solution)/shard_map/ppermute | solution.py:629
  71.5 5.8 %collective-permute-start.18 = (f32[2,32,32]{2,1,0:T(8,128)S(1)}, f32[2,32,32]{2,1,0:T(8,128)S(1)}, u32[]{:S(2)}, u32[]{:S(2)}) collective-permute-start(f32[2,32,32]{2,1,0:T(8,128)S(1)} %apply_score.1), channel_id=1, source_target_pairs={{3,0},{2,1},{1,2},{0,3},{7,4},{6,5},{5,6},{4,7},{11,8},{10,9},{9,1... | collective-permute-start | bytes 24584 | tf_op jit(solution)/shard_map/ppermute | solution.py:629
  73.0 5.1 %collective-permute-start.17 = (f32[2,32,32]{2,1,0:T(8,128)S(1)}, f32[2,32,32]{2,1,0:T(8,128)S(1)}, u32[]{:S(2)}, u32[]{:S(2)}) collective-permute-start(f32[2,32,32]{2,1,0:T(8,128)S(1)} %apply_score.1), channel_id=1, source_target_pairs={{2,0},{3,1},{0,2},{1,3},{6,4},{7,5},{4,6},{5,7},{10,8},{11,9},{8,1... | collective-permute-start | bytes 24584 | tf_op jit(solution)/shard_map/ppermute | solution.py:629
  73.0 5.2 %collective-permute-start.16 = (f32[2,32,32]{2,1,0:T(8,128)S(1)}, f32[2,32,32]{2,1,0:T(8,128)S(1)}, u32[]{:S(2)}, u32[]{:S(2)}) collective-permute-start(f32[2,32,32]{2,1,0:T(8,128)S(1)} %apply_score.1), channel_id=1, source_target_pairs={{1,0},{0,1},{3,2},{2,3},{5,4},{4,5},{7,6},{6,7},{9,8},{8,9},{11,10... | collective-permute-start | bytes 24584 | tf_op jit(solution)/shard_map/ppermute | solution.py:629

commit v14 on v13

--- a/solution.py
+++ b/solution.py
@@ -71,9 +71,18 @@
         place(z, dense_ref.shape[0], piece * (width // 256) + v, dense_ref)
 
 
-def build_first_kernel(rows_hbm, cols_hbm, counts_hbm, blocks_ref, dense_ref, *refs):
-    *refs, held, rows_ref, cols_ref, counts_ref, arrived, index_arrived = refs
-    others, onehots = refs[: len(refs) // 2], refs[len(refs) // 2 :]
+def build_whole_kernel(rows_hbm, cols_hbm, counts_hbm, blocks_ref, *refs):
+    *dense_refs, held, rows_ref, cols_ref, counts_ref, arrived, index_arrived = refs
+    layers, pieces = arrived.shape
+    width = held.shape[2] // pieces
+    ahead = 3
+
+    def fetch(layer, piece):
+        cols = pl.ds(pl.multiple_of(piece * width, width), width)
+        return pltpu.make_async_copy(
+            blocks_ref.at[layer, :, cols], held.at[layer, :, cols], arrived.at[layer, piece]
+        )
+
     index_copies = [
         pltpu.make_async_copy(source, target, index_arrived.at[i])
         for i, (source, target) in enumerate(
@@ -82,101 +91,54 @@
     ]
     for copy in index_copies:
         copy.start()
-    pieces = arrived.shape[0] - len(others)
-    width = held.shape[1] // pieces
-
-    def fetch(piece):
-        cols = pl.ds(pl.multiple_of(piece * width, width), width)
-        return pltpu.make_async_copy(blocks_ref.at[0, :, cols], held.at[:, cols], arrived.at[piece])
-
-    for piece in range(pieces):
-        fetch(piece).start()
-    whole = [
-        pltpu.make_async_copy(blocks_ref.at[i + 1], other, arrived.at[pieces + i]) for i, other in enumerate(others)
-    ]
-    for copy in whole:
-        copy.start()
+    for piece in range(ahead):
+        fetch(0, piece).start()
     for copy in index_copies:
         copy.wait()
     flip = lax.axis_index("node") * CHUNK_COLS
-    positions = dense_ref.shape[0] * CHUNK_COLS * BROWS
-    onehot = one_hot(rows_ref, cols_ref, counts_ref, 0, flip, 0, positions)
-    for i, ref in enumerate(onehots):
-        ref[...] = one_hot(rows_ref, cols_ref, counts_ref, i + 1, flip, 0, positions)
-
-    def step(piece, carry):
-        fetch(piece).wait()
-        fill(onehot, held, dense_ref, piece, width)
-        return carry
-
-    lax.fori_loop(0, pieces, step, 0)
-    for copy in whole:
-        copy.wait()
-
-
-def build_next_kernel(onehot_ref, blocks_ref, dense_ref):
-    onehot = onehot_ref[...]
-    width = blocks_ref.shape[1] // 4
-
-    def step(piece, carry):
-        fill(onehot, blocks_ref, dense_ref, piece, width)
-        return carry
-
-    lax.fori_loop(0, 4, step, 0)
-
-
-def relay_kernel(x_ref, _, out_ref):
-    out_ref[...] = x_ref[...]
-
-
-def relay(x, after):
-    return pl.pallas_call(
-        relay_kernel,
-        in_specs=vmem_specs(1) + [pl.BlockSpec(memory_space=pl.ANY)],
-        out_specs=pl.BlockSpec(memory_space=pltpu.VMEM),
-        out_shape=jax.ShapeDtypeStruct(x.shape, x.dtype),
-        compiler_params=params(2),
-        name="relay",
-    )(x, after)
-
-
-def build_first(block_rows, block_cols, counts, blocks, chunk_total):
-    layers, slots, width = blocks.shape
+    for layer, dense_ref in enumerate(dense_refs):
+        onehot = one_hot(rows_ref, cols_ref, counts_ref, layer, flip, 0, dense_ref.shape[0] * CHUNK_COLS * BROWS)
+
+        def step(piece, carry):
+            fetch(layer, piece).wait()
+
+            @pl.when(piece + ahead < pieces)
+            def _():
+                fetch(layer, piece + ahead).start()
+
+            if layer + 1 < layers:
+
+                @pl.when(piece + ahead >= pieces)
+                def _():
+                    fetch(layer + 1, piece + ahead - pieces).start()
+
+            fill(onehot, held.at[layer], dense_ref, piece, width)
+            return carry
+
+        lax.fori_loop(0, pieces, step, 0)
+
+
+def build_whole(block_rows, block_cols, counts, blocks, chunk_total):
+    layers = blocks.shape[0]
     dense = jax.ShapeDtypeStruct((chunk_total, 2 * TALL, CHUNK_LANES), BF16)
-    positions = chunk_total * CHUNK_COLS * BROWS
     operands = (block_rows, block_cols, counts.T, blocks)
-    outs = pl.pallas_call(
-        build_first_kernel,
+    return pl.pallas_call(
+        build_whole_kernel,
         in_specs=[pl.BlockSpec(memory_space=pltpu.HBM)] * 4,
-        out_specs=vmem_specs(2 * layers - 1),
-        out_shape=[dense]
-        + [jax.ShapeDtypeStruct((slots, width), BF16)] * (layers - 1)
-        + [jax.ShapeDtypeStruct((positions, slots), BF16)] * (layers - 1),
+        out_specs=vmem_specs(layers),
+        out_shape=[dense] * layers,
         scratch_shapes=[
-            pltpu.VMEM((slots, width), BF16),
+            pltpu.VMEM(blocks.shape, BF16),
             pltpu.VMEM(block_rows.shape, jnp.int32),
             pltpu.VMEM(block_cols.shape, jnp.int32),
             pltpu.SMEM((1, layers), jnp.int32),
-            pltpu.SemaphoreType.DMA((4 + layers - 1,)),
+            pltpu.SemaphoreType.DMA((layers, 4)),
             pltpu.SemaphoreType.DMA((3,)),
         ],
         compiler_params=params(28),
-        cost_estimate=pl.CostEstimate(flops=0, bytes_accessed=12 * MIB, transcendentals=0),
-        name="build_first",
+        cost_estimate=pl.CostEstimate(flops=0, bytes_accessed=20 * MIB, transcendentals=0),
+        name="build_whole",
     )(*[pltpu.with_memory_space_constraint(x, pltpu.HBM) for x in operands])
-    return outs[0], list(zip(outs[layers:], outs[1:layers]))
-
-
-def build_next(onehot, blocks, chunk_total):
-    return pl.pallas_call(
-        build_next_kernel,
-        in_specs=vmem_specs(2),
-        out_specs=pl.BlockSpec(memory_space=pltpu.VMEM),
-        out_shape=jax.ShapeDtypeStruct((chunk_total, 2 * TALL, CHUNK_LANES), BF16),
-        compiler_params=params(20),
-        cost_estimate=pl.CostEstimate(flops=0, bytes_accessed=12 * MIB, transcendentals=0),
-        name="build_next",
-    )(onehot, blocks)
 
 
 def build_dense(block_rows, block_cols, counts, blocks, chunk_total):
@@ -278,13 +240,9 @@
     return total + (middle[:, k : 2 * k] + (top[:, 2 * k : 3 * k] + bottom[:, :k]))
 
 
-def image_of(parts, dense_ref):
-    return sum(image_part(part, dense_ref[chunk]) for chunk, part in enumerate(parts))
-
-
-def first_kernel(layer, piece_count, *refs):
-    pieces, (dense_ref, _, out_ref, halves, tall) = refs[:piece_count], refs[piece_count:]
-    total = image_of([piece[layer] for piece in pieces], dense_ref)
+def first_kernel(layer, chunks, *refs):
+    pieces, (dense_ref, out_ref, halves, tall) = refs[: len(chunks)], refs[len(chunks) :]
+    total = sum(image_part(piece[layer], dense_ref[chunk]) for chunk, piece in zip(chunks, pieces))
     out_ref[...] = to_wide(total, out_ref.shape[0], halves, tall)
 
 
@@ -298,7 +256,7 @@
     before = out_ref.shape[0] - 1
     for ref in earlier:
         out_ref[:before] = ref[...]
-    out_ref[before] = to_wide(image_of(parts, dense_ref), out_ref.shape[1], halves, tall)
+    out_ref[before] = to_wide(sum(image_part(part, dense_ref[chunk]) for chunk, part in zip(ORDER, parts)), out_ref.shape[1], halves, tall)
 
 
 def some_kernel(chunk, layers, basis_ref, *refs):
@@ -323,22 +281,22 @@
         out_ref[layer] = product(left_ref[layer], wide[layer])
 
 
-def apply_whole(kernel, name, operands, out_shape, *lead, scratch=(), after=()):
+def apply_whole(kernel, name, operands, out_shape, *lead, scratch=()):
     return pl.pallas_call(
         kernel,
-        in_specs=vmem_specs(len(operands)) + [pl.BlockSpec(memory_space=pl.ANY)] * len(after),
+        in_specs=vmem_specs(len(operands)),
         out_specs=pl.BlockSpec(memory_space=pltpu.VMEM),
         out_shape=jax.ShapeDtypeStruct(out_shape, F32),
         scratch_shapes=[pltpu.VMEM((*lead, TALL, 128), F32), pltpu.VMEM((*lead, ROWS_DEV, 128), F32), *scratch],
         compiler_params=params(14),
         cost_estimate=pl.CostEstimate(flops=0, bytes_accessed=4 * MIB, transcendentals=0),
         name=name,
-    )(*operands, *after)
-
-
-def apply_first(layer, pieces, dense, after):
-    kernel = functools.partial(first_kernel, layer, len(pieces))
-    return apply_whole(kernel, "apply_first", [*pieces, dense], pieces[0].shape[1:], after=[after])
+    )(*operands)
+
+
+def apply_first(layer, chunks, pieces, dense):
+    kernel = functools.partial(first_kernel, layer, chunks)
+    return apply_whole(kernel, "apply_first", [*pieces, dense], pieces[0].shape[1:])
 
 
 def apply_second(pieces, dense, earlier):
@@ -363,12 +321,10 @@
 
 
 def apply_score(pieces, left, dense):
-    last = len(pieces) - 1
-    so_far = apply_some(last, pieces[last], dense, apply_some(0, pieces[0], dense))
-    chunks = range(1, last)
-    kernel = functools.partial(score_kernel, len(dense), chunks)
+    so_far = apply_some(ORDER[1], pieces[1], dense, apply_some(0, pieces[0], dense))
+    kernel = functools.partial(score_kernel, len(dense), ORDER[2:])
     layers, k = left.shape[:2]
-    operands = [so_far, *pieces[1:last], left, *dense]
+    operands = [so_far, *pieces[2:], left, *dense]
     return apply_whole(kernel, "apply_score", operands, (layers, k, k), layers)
 
 
@@ -629,14 +585,17 @@
     return lax.ppermute(x, axis, [(m ^ d, m) for m in range(count)])
 
 
+ORDER = (0, 3, 2, 1)
+
+
 def around(x, axis, count):
-    return [x] + [swap(x, axis, d, count) for d in range(1, count)]
-
-
-def add_pieces(pieces):
-    if len(pieces) == 1:
-        return pieces[0]
-    return (pieces[0] + pieces[1]) + (pieces[2] + pieces[3])
+    return [x] + [swap(x, axis, d, count) for d in ORDER[1:]]
+
+
+def add_pieces(pieces, flip):
+    own, near, far, across = (pieces[ORDER.index(d)] for d in range(4))
+    low, high = own + near, across + far
+    return high + low if flip else low + high
 
 
 def per_device(shards, groups, blocks, block_rows, block_cols, counts, start):
@@ -646,18 +605,16 @@
     def gather(x):
         return around(x, "node", shards) if few else lax.all_gather(x, "node")
 
-    def total(x):
-        return add_pieces(around(x, "node", shards)) if few else lax.psum(x, "node")
+    def total(x, flip=False):
+        return add_pieces(around(x, "node", shards), flip) if few else lax.psum(x, "node")
 
     rounded = start.astype(BF16)
     chunk_total = shards * BROWS // CHUNK_COLS
     if few:
-        near, far = swap(rounded, "node", 1, shards), swap(rounded, "node", 2, shards)
-        dense_first, rest = build_first(block_rows, block_cols, counts, blocks, chunk_total)
-        far = relay(far, dense_first)
-        dense = [dense_first] + [build_next(*one, chunk_total) for one in rest]
-        first = [rounded, near, far, swap(far, "node", 1, shards)]
-        images = [apply_first(layer, first, dense[layer], dense[-1]) for layer in range(layers)]
+        chunks = (0, 1, 3, 2)
+        first = [rounded] + [swap(rounded, "node", d, shards) for d in chunks[1:]]
+        dense = build_whole(block_rows, block_cols, counts, blocks, chunk_total)
+        images = [apply_first(layer, chunks, first, dense[layer]) for layer in range(layers)]
         image = None
         for layer in range(layers):
             image = apply_second(gather(images[layer]), dense[layer], [] if image is None else [image])
@@ -674,7 +631,7 @@
         partial = apply_score(gather(rounded), again, dense)
     else:
         (partial,) = apply_dense("score", gather(rounded), dense, again)
-    return joint_basis, total(partial)
+    return joint_basis, total(partial, True)
 
 
 def solution(mesh):

time: 79 us -> 77.8 us (0.985)
    pallas_call x8 -> x6, Pallas kernels: 17 us -> 16.5 us  [the longest x5 11 us: apply_whole(): pl.pallas_call(kernel, in_specs=vmem_specs(len(operands)), out_specs=pl.B...]
where the time goes in v14:
time: 77.8 us; the launch traced here: 77.6 us
  starting transfers between devices  27.9 us (36%)
  Pallas kernels  26.6 us (34%)
  waiting for transfers between devices  13.4 us (17%)
  blocking collectives  7.37 us (9%)
  other arithmetic  1.56 us (2%)
    ppermute x19, starting transfers between devices, swap(): return lax.ppermute(x, axis, [(m ^ d, m) for m in range(count)])  27.9 us
    ppermute x19, waiting for transfers between devices, swap(): return lax.ppermute(x, axis, [(m ^ d, m) for m in range(count)])  13.4 us
    pallas_call x5, Pallas kernels, apply_whole(): pl.pallas_call(kernel, in_specs=vmem_specs(len(operands)), out_specs=pl.B...  11 us
    pallas_call x1, Pallas kernels, joint_solve(): pl.pallas_call(functools.partial(joint_kernel, k), in_specs=vmem_specs(3)...  7.92 us
    all_gather x1, blocking collectives, per_device(): images = lax.all_gather(image, 'layer', axis=0, tiled=True)  7.37 us
    pallas_call x1, Pallas kernels, build_whole(): pl.pallas_call(build_whole_kernel, in_specs=[pl.BlockSpec(memory_space=pl...  5.44 us
    pallas_call x2, Pallas kernels, apply_some(): pl.pallas_call(functools.partial(some_kernel, chunk, layers), in_specs=vm...  1.57 us
  transfers between devices with their start and end apart: 19, of which 9 were waited for; matrix products, arithmetic and copies ran while one was open for 0% of the time, Pallas kernels for 15%

profile of v14, /device:TPU:0, one launch (start us, length us, event | category | flops | bytes accessed | tf_op | source)
XLA Modules:
  0.0 77.6 jit_solution(7332875385489465483)
XLA Ops:
  1.5 3.1 %collective-permute-start = (bf16[2,32,512]{2,1,0:T(8,128)(2,1)S(1)}, bf16[2,32,512]{2,1,0:T(8,128)(2,1)S(1)}, u32[]{:S(2)}, u32[]{:S(2)}) collective-permute-start(bf16[2,32,512]{2,1,0:T(8,128)(2,1)S(1)} %convert_element_type.3.refs_0_), channel_id=1, source_target_pairs={{1,0},{0,1},{3,2},{2,3},{5,4},{4,5},{7,6},{6,7},{9,8},{8,9},{11,10... | collective-permute-start | bytes 196616 | tf_op jit(solution)/shard_map/ppermute | solution.py:585
  4.6 2.5 %collective-permute-start.1 = (bf16[2,32,512]{2,1,0:T(8,128)(2,1)S(1)}, bf16[2,32,512]{2,1,0:T(8,128)(2,1)S(1)}, u32[]{:S(2)}, u32[]{:S(2)}) collective-permute-start(bf16[2,32,512]{2,1,0:T(8,128)(2,1)S(1)} %convert_element_type.3.refs_0_), channel_id=1, source_target_pairs={{3,0},{2,1},{1,2},{0,3},{7,4},{6,5},{5,6},{4,7},{11,8},{10,9},{9,1... | collective-permute-start | bytes 196616 | tf_op jit(solution)/shard_map/ppermute | solution.py:585
  7.2 5.4 %build_whole.1 = (bf16[4,512,1024]{2,1,0:T(8,128)(2,1)S(1)}, bf16[4,512,1024]{2,1,0:T(8,128)(2,1)S(1)}) custom-call(s32[2,512]{1,0:T(2,128)} %rows_hbm.1, s32[2,512]{1,0:T(2,128)} %cols_hbm.1, s32[1,2]{1,0:T(1,128)} %bitcast.1, bf16[2,512,4096]{2,1,0:T(8,128)(2,1)} %blocks_ref.1), custom_call_target="tpu_custom_call" | custom-call | bytes 20971520 | tf_op jit(solution)/shard_map/build_whole/pallas_call | solution.py:125
  13.6 1.5 %apply_first.3.refs_0_ = f32[32,512]{1,0:T(8,128)S(1)} custom-call(bf16[2,32,512]{2,1,0:T(8,128)(2,1)S(1)} %convert_element_type.3.refs_0_, bf16[2,32,512]{2,1,0:T(8,128)(2,1)S(1)} %collective-permute-done.refs_1_, bf16[2,32,512]{2,1,0:T(8,128)(2,1)S(1)} %collective-permute-done.1.refs_2_, bf16[2,32,512]{2,1,0:T(8,128)(2,1)S(1)} %collective-permute-done.2.refs_3_, ...), custom_call_target="tpu_custom_call" | custom-call | bytes 4194304 | tf_op jit(solution)/shard_map/apply_first/pallas_call | solution.py:285
  15.1 2.5 %collective-permute-start.6 = (f32[32,512]{1,0:T(8,128)S(1)}, f32[32,512]{1,0:T(8,128)S(1)}, u32[]{:S(2)}, u32[]{:S(2)}) collective-permute-start(f32[32,512]{1,0:T(8,128)S(1)} %apply_first.3.refs_0_), channel_id=1, source_target_pairs={{3,0},{2,1},{1,2},{0,3},{7,4},{6,5},{5,6},{4,7},{11,8},{10,9},{9,1... | collective-permute-start | bytes 196616 | tf_op jit(solution)/shard_map/ppermute | solution.py:585
  17.6 2.0 %collective-permute-start.8 = (f32[32,512]{1,0:T(8,128)S(1)}, f32[32,512]{1,0:T(8,128)S(1)}, u32[]{:S(2)}, u32[]{:S(2)}) collective-permute-start(f32[32,512]{1,0:T(8,128)S(1)} %apply_first.3.refs_0_), channel_id=1, source_target_pairs={{1,0},{0,1},{3,2},{2,3},{5,4},{4,5},{7,6},{6,7},{9,8},{8,9},{11,10... | collective-permute-start | bytes 196616 | tf_op jit(solution)/shard_map/ppermute | solution.py:585
  19.5 1.5 %apply_first.2.refs_0_ = f32[32,512]{1,0:T(8,128)S(1)} custom-call(bf16[2,32,512]{2,1,0:T(8,128)(2,1)S(1)} %convert_element_type.3.refs_0_, bf16[2,32,512]{2,1,0:T(8,128)(2,1)S(1)} %collective-permute-done.refs_1_, bf16[2,32,512]{2,1,0:T(8,128)(2,1)S(1)} %collective-permute-done.1.refs_2_, bf16[2,32,512]{2,1,0:T(8,128)(2,1)S(1)} %collective-permute-done.2.refs_3_, ...), custom_call_target="tpu_custom_call" | custom-call | bytes 4194304 | tf_op jit(solution)/shard_map/apply_first/pallas_call | solution.py:285
  21.0 2.5 %collective-permute-start.3 = (f32[32,512]{1,0:T(8,128)S(1)}, f32[32,512]{1,0:T(8,128)S(1)}, u32[]{:S(2)}, u32[]{:S(2)}) collective-permute-start(f32[32,512]{1,0:T(8,128)S(1)} %apply_first.2.refs_0_), channel_id=1, source_target_pairs={{3,0},{2,1},{1,2},{0,3},{7,4},{6,5},{5,6},{4,7},{11,8},{10,9},{9,1... | collective-permute-start | bytes 196616 | tf_op jit(solution)/shard_map/ppermute | solution.py:585
  23.5 2.0 %collective-permute-start.5 = (f32[32,512]{1,0:T(8,128)S(1)}, f32[32,512]{1,0:T(8,128)S(1)}, u32[]{:S(2)}, u32[]{:S(2)}) collective-permute-start(f32[32,512]{1,0:T(8,128)S(1)} %apply_first.2.refs_0_), channel_id=1, source_target_pairs={{1,0},{0,1},{3,2},{2,3},{5,4},{4,5},{7,6},{6,7},{9,8},{8,9},{11,10... | collective-permute-start | bytes 196616 | tf_op jit(solution)/shard_map/ppermute | solution.py:585
  25.5 3.0 %apply_second.2.refs_5_ = f32[1,32,512]{2,1,0:T(8,128)S(1)} custom-call(f32[32,512]{1,0:T(8,128)S(1)} %apply_first.3.refs_0_, f32[32,512]{1,0:T(8,128)S(1)} %collective-permute-done.6.refs_1_, f32[32,512]{1,0:T(8,128)S(1)} %collective-permute-done.7.refs_2_, f32[32,512]{1,0:T(8,128)S(1)} %collective-permute-done.8.refs_3_, ...), custom_call_target="tpu_custom_call" | custom-call | bytes 4194304 | tf_op jit(solution)/shard_map/apply_second/pallas_call | solution.py:285
  29.6 3.0 %apply_second.3 = f32[2,32,512]{2,1,0:T(8,128)S(1)} custom-call(f32[32,512]{1,0:T(8,128)S(1)} %apply_first.2.refs_0_, f32[32,512]{1,0:T(8,128)S(1)} %collective-permute-done.3.refs_1_, f32[32,512]{1,0:T(8,128)S(1)} %collective-permute-done.4.refs_2_, f32[32,512]{1,0:T(8,128)S(1)} %collective-permute-done.5.refs_3_, ...), custom_call_target="tpu_custom_call" | custom-call | bytes 4194304 | tf_op jit(solution)/shard_map/apply_second/pallas_call | solution.py:285
  32.6 7.4 %all_gather.3.images_ref.refs_2_ = f32[8,32,512]{2,1,0:T(8,128)S(1)} all-gather(f32[2,32,512]{2,1,0:T(8,128)S(1)} %apply_second.3), channel_id=1, replica_groups=mesh['parts'=2,'layer'=4,'node'=4] {'layer'}, dimensions={0}, use_global_device_ids=true | all-gather | bytes 655360 | tf_op jit(solution)/shard_map/all_gather | solution.py:625
  40.6 2.0 %collective-permute-start.10 = (f32[144,128]{1,0:T(8,128)S(1)}, f32[144,128]{1,0:T(8,128)S(1)}, u32[]{:S(2)}, u32[]{:S(2)}) collective-permute-start(f32[144,128]{1,0:T(8,128)S(1)} %cross_gram.1), channel_id=1, source_target_pairs={{3,0},{2,1},{1,2},{0,3},{7,4},{6,5},{5,6},{4,7},{11,8},{10,9},{9,1... | collective-permute-start | bytes 221192 | tf_op jit(solution)/shard_map/ppermute | solution.py:585
  42.6 2.5 %collective-permute-start.9 = (f32[144,128]{1,0:T(8,128)S(1)}, f32[144,128]{1,0:T(8,128)S(1)}, u32[]{:S(2)}, u32[]{:S(2)}) collective-permute-start(f32[144,128]{1,0:T(8,128)S(1)} %cross_gram.1), channel_id=1, source_target_pairs={{1,0},{0,1},{3,2},{2,3},{5,4},{4,5},{7,6},{6,7},{9,8},{8,9},{11,10... | collective-permute-start | bytes 221192 | tf_op jit(solution)/shard_map/ppermute | solution.py:585
  45.1 2.6 %collective-permute-done.10 = f32[144,128]{1,0:T(8,128)S(1)} collective-permute-done((f32[144,128]{1,0:T(8,128)S(1)}, f32[144,128]{1,0:T(8,128)S(1)}, u32[]{:S(2)}, u32[]{:S(2)}) %collective-permute-start.10) | collective-permute-done | bytes 73760 | tf_op jit(solution)/shard_map/ppermute | solution.py:585
  47.7 2.5 %collective-permute-done.11 = f32[144,128]{1,0:T(8,128)S(1)} collective-permute-done((f32[144,128]{1,0:T(8,128)S(1)}, f32[144,128]{1,0:T(8,128)S(1)}, u32[]{:S(2)}, u32[]{:S(2)}) %collective-permute-start.11) | collective-permute-done | bytes 73760 | tf_op jit(solution)/shard_map/ppermute | solution.py:585
  51.6 7.9 %joint_solve.1 = (f32[2,32,512]{2,1,0:T(8,128)}, f32[2,32,512]{2,1,0:T(8,128)S(1)}, bf16[2,32,512]{2,1,0:T(8,128)(2,1)S(1)}) custom-call(f32[144,128]{1,0:T(8,128)S(1)} %add_add_fusion.refs_0_, f32[144,128]{1,0:T(8,128)S(1)} %collective-permute-done.12.refs_1_, f32[8,32,512]{2,1,0:T(8,128)S(1)} %all_gather.3.images_ref.refs_2_), custom_call_target="tpu_custom_call" | custom-call | tf_op jit(solution)/shard_map/joint_solve/pallas_call | solution.py:565
  59.5 1.9 %collective-permute-start.13 = (bf16[2,32,512]{2,1,0:T(8,128)(2,1)S(1)}, bf16[2,32,512]{2,1,0:T(8,128)(2,1)S(1)}, u32[]{:S(2)}, u32[]{:S(2)}) collective-permute-start(bf16[2,32,512]{2,1,0:T(8,128)(2,1)S(1)} %get-tuple-element.10.basis_ref), channel_id=1, source_target_pairs={{3,0},{2,1},{1,2},{0,3},{7,4},{6,5},{5,6},{4,7},{11,8},{10,9},{9,1... | collective-permute-start | bytes 196616 | tf_op jit(solution)/shard_map/ppermute | solution.py:585
  61.4 2.5 %collective-permute-start.15 = (bf16[2,32,512]{2,1,0:T(8,128)(2,1)S(1)}, bf16[2,32,512]{2,1,0:T(8,128)(2,1)S(1)}, u32[]{:S(2)}, u32[]{:S(2)}) collective-permute-start(bf16[2,32,512]{2,1,0:T(8,128)(2,1)S(1)} %get-tuple-element.10.basis_ref), channel_id=1, source_target_pairs={{1,0},{0,1},{3,2},{2,3},{5,4},{4,5},{7,6},{6,7},{9,8},{8,9},{11,10... | collective-permute-start | bytes 196616 | tf_op jit(solution)/shard_map/ppermute | solution.py:585
  64.6 1.6 %collective-permute-done.13.basis_ref = bf16[2,32,512]{2,1,0:T(8,128)(2,1)S(1)} collective-permute-done((bf16[2,32,512]{2,1,0:T(8,128)(2,1)S(1)}, bf16[2,32,512]{2,1,0:T(8,128)(2,1)S(1)}, u32[]{:S(2)}, u32[]{:S(2)}) %collective-permute-start.13) | collective-permute-done | bytes 65568 | tf_op jit(solution)/shard_map/ppermute | solution.py:585
  68.2 2.0 %apply_score.1 = f32[2,32,32]{2,1,0:T(8,128)S(1)} custom-call(f32[2,512,64]{2,1,0:T(8,128)S(1)} %apply_some_3.1.so_far_ref, bf16[2,32,512]{2,1,0:T(8,128)(2,1)S(1)} %collective-permute-done.14.refs_0_, bf16[2,32,512]{2,1,0:T(8,128)(2,1)S(1)} %collective-permute-done.15.refs_1_, f32[2,32,512]{2,1,0:T(8,128)S(1)} %get-tuple-element.11.refs_2_, ...), custom_call_target="tpu_custom_call" | custom-call | bytes 4194304 | tf_op jit(solution)/shard_map/apply_score/pallas_call | solution.py:285
  70.2 2.0 %collective-permute-start.16 = (f32[2,32,32]{2,1,0:T(8,128)S(1)}, f32[2,32,32]{2,1,0:T(8,128)S(1)}, u32[]{:S(2)}, u32[]{:S(2)}) collective-permute-start(f32[2,32,32]{2,1,0:T(8,128)S(1)} %apply_score.1), channel_id=1, source_target_pairs={{3,0},{2,1},{1,2},{0,3},{7,4},{6,5},{5,6},{4,7},{11,8},{10,9},{9,1... | collective-permute-start | bytes 24584 | tf_op jit(solution)/shard_map/ppermute | solution.py:585
  72.2 2.5 %collective-permute-start.18 = (f32[2,32,32]{2,1,0:T(8,128)S(1)}, f32[2,32,32]{2,1,0:T(8,128)S(1)}, u32[]{:S(2)}, u32[]{:S(2)}) collective-permute-start(f32[2,32,32]{2,1,0:T(8,128)S(1)} %apply_score.1), channel_id=1, source_target_pairs={{1,0},{0,1},{3,2},{2,3},{5,4},{4,5},{7,6},{6,7},{9,8},{8,9},{11,10... | collective-permute-start | bytes 24584 | tf_op jit(solution)/shard_map/ppermute | solution.py:585
  74.7 1.4 %collective-permute-done.16 = f32[2,32,32]{2,1,0:T(8,128)S(1)} collective-permute-done((f32[2,32,32]{2,1,0:T(8,128)S(1)}, f32[2,32,32]{2,1,0:T(8,128)S(1)}, u32[]{:S(2)}, u32[]{:S(2)}) %collective-permute-start.16) | collective-permute-done | bytes 8224 | tf_op jit(solution)/shard_map/ppermute | solution.py:585
  (28 shorter events, 9.3 us)
Async XLA Ops:
  1.5 11.1 %collective-permute-start = (bf16[2,32,512]{2,1,0:T(8,128)(2,1)S(1)}, bf16[2,32,512]{2,1,0:T(8,128)(2,1)S(1)}, u32[]{:S(2)}, u32[]{:S(2)}) collective-permute-start(bf16[2,32,512]{2,1,0:T(8,128)(2,1)S(1)} %convert_element_type.3.refs_0_), channel_id=1, source_target_pairs={{1,0},{0,1},{3,2},{2,3},{5,4},{4,5},{7,6},{6,7},{9,8},{8,9},{11,10... | collective-permute-start | bytes 196616 | tf_op jit(solution)/shard_map/ppermute | solution.py:585
  4.6 8.1 %collective-permute-start.1 = (bf16[2,32,512]{2,1,0:T(8,128)(2,1)S(1)}, bf16[2,32,512]{2,1,0:T(8,128)(2,1)S(1)}, u32[]{:S(2)}, u32[]{:S(2)}) collective-permute-start(bf16[2,32,512]{2,1,0:T(8,128)(2,1)S(1)} %convert_element_type.3.refs_0_), channel_id=1, source_target_pairs={{3,0},{2,1},{1,2},{0,3},{7,4},{6,5},{5,6},{4,7},{11,8},{10,9},{9,1... | collective-permute-start | bytes 196616 | tf_op jit(solution)/shard_map/ppermute | solution.py:585
  7.1 6.4 %collective-permute-start.2 = (bf16[2,32,512]{2,1,0:T(8,128)(2,1)S(1)}, bf16[2,32,512]{2,1,0:T(8,128)(2,1)S(1)}, u32[]{:S(2)}, u32[]{:S(2)}) collective-permute-start(bf16[2,32,512]{2,1,0:T(8,128)(2,1)S(1)} %convert_element_type.3.refs_0_), channel_id=1, source_target_pairs={{2,0},{3,1},{0,2},{1,3},{6,4},{7,5},{4,6},{5,7},{10,8},{11,9},{8,1... | collective-permute-start | bytes 196616 | tf_op jit(solution)/shard_map/ppermute | solution.py:585
  15.1 8.4 %collective-permute-start.6 = (f32[32,512]{1,0:T(8,128)S(1)}, f32[32,512]{1,0:T(8,128)S(1)}, u32[]{:S(2)}, u32[]{:S(2)}) collective-permute-start(f32[32,512]{1,0:T(8,128)S(1)} %apply_first.3.refs_0_), channel_id=1, source_target_pairs={{3,0},{2,1},{1,2},{0,3},{7,4},{6,5},{5,6},{4,7},{11,8},{10,9},{9,1... | collective-permute-start | bytes 196616 | tf_op jit(solution)/shard_map/ppermute | solution.py:585
  17.6 7.9 %collective-permute-start.7 = (f32[32,512]{1,0:T(8,128)S(1)}, f32[32,512]{1,0:T(8,128)S(1)}, u32[]{:S(2)}, u32[]{:S(2)}) collective-permute-start(f32[32,512]{1,0:T(8,128)S(1)} %apply_first.3.refs_0_), channel_id=1, source_target_pairs={{2,0},{3,1},{0,2},{1,3},{6,4},{7,5},{4,6},{5,7},{10,8},{11,9},{8,1... | collective-permute-start | bytes 196616 | tf_op jit(solution)/shard_map/ppermute | solution.py:585
  17.6 7.9 %collective-permute-start.8 = (f32[32,512]{1,0:T(8,128)S(1)}, f32[32,512]{1,0:T(8,128)S(1)}, u32[]{:S(2)}, u32[]{:S(2)}) collective-permute-start(f32[32,512]{1,0:T(8,128)S(1)} %apply_first.3.refs_0_), channel_id=1, source_target_pairs={{1,0},{0,1},{3,2},{2,3},{5,4},{4,5},{7,6},{6,7},{9,8},{8,9},{11,10... | collective-permute-start | bytes 196616 | tf_op jit(solution)/shard_map/ppermute | solution.py:585
  21.0 7.5 %collective-permute-start.3 = (f32[32,512]{1,0:T(8,128)S(1)}, f32[32,512]{1,0:T(8,128)S(1)}, u32[]{:S(2)}, u32[]{:S(2)}) collective-permute-start(f32[32,512]{1,0:T(8,128)S(1)} %apply_first.2.refs_0_), channel_id=1, source_target_pairs={{3,0},{2,1},{1,2},{0,3},{7,4},{6,5},{5,6},{4,7},{11,8},{10,9},{9,1... | collective-permute-start | bytes 196616 | tf_op jit(solution)/shard_map/ppermute | solution.py:585
  23.5 6.1 %collective-permute-start.4 = (f32[32,512]{1,0:T(8,128)S(1)}, f32[32,512]{1,0:T(8,128)S(1)}, u32[]{:S(2)}, u32[]{:S(2)}) collective-permute-start(f32[32,512]{1,0:T(8,128)S(1)} %apply_first.2.refs_0_), channel_id=1, source_target_pairs={{2,0},{3,1},{0,2},{1,3},{6,4},{7,5},{4,6},{5,7},{10,8},{11,9},{8,1... | collective-permute-start | bytes 196616 | tf_op jit(solution)/shard_map/ppermute | solution.py:585
  23.5 6.1 %collective-permute-start.5 = (f32[32,512]{1,0:T(8,128)S(1)}, f32[32,512]{1,0:T(8,128)S(1)}, u32[]{:S(2)}, u32[]{:S(2)}) collective-permute-start(f32[32,512]{1,0:T(8,128)S(1)} %apply_first.2.refs_0_), channel_id=1, source_target_pairs={{1,0},{0,1},{3,2},{2,3},{5,4},{4,5},{7,6},{6,7},{9,8},{8,9},{11,10... | collective-permute-start | bytes 196616 | tf_op jit(solution)/shard_map/ppermute | solution.py:585
  40.6 7.1 %collective-permute-start.10 = (f32[144,128]{1,0:T(8,128)S(1)}, f32[144,128]{1,0:T(8,128)S(1)}, u32[]{:S(2)}, u32[]{:S(2)}) collective-permute-start(f32[144,128]{1,0:T(8,128)S(1)} %cross_gram.1), channel_id=1, source_target_pairs={{3,0},{2,1},{1,2},{0,3},{7,4},{6,5},{5,6},{4,7},{11,8},{10,9},{9,1... | collective-permute-start | bytes 221192 | tf_op jit(solution)/shard_map/ppermute | solution.py:585
  42.6 7.6 %collective-permute-start.11 = (f32[144,128]{1,0:T(8,128)S(1)}, f32[144,128]{1,0:T(8,128)S(1)}, u32[]{:S(2)}, u32[]{:S(2)}) collective-permute-start(f32[144,128]{1,0:T(8,128)S(1)} %cross_gram.1), channel_id=1, source_target_pairs={{2,0},{3,1},{0,2},{1,3},{6,4},{7,5},{4,6},{5,7},{10,8},{11,9},{8,1... | collective-permute-start | bytes 221192 | tf_op jit(solution)/shard_map/ppermute | solution.py:585
  42.6 7.6 %collective-permute-start.9 = (f32[144,128]{1,0:T(8,128)S(1)}, f32[144,128]{1,0:T(8,128)S(1)}, u32[]{:S(2)}, u32[]{:S(2)}) collective-permute-start(f32[144,128]{1,0:T(8,128)S(1)} %cross_gram.1), channel_id=1, source_target_pairs={{1,0},{0,1},{3,2},{2,3},{5,4},{4,5},{7,6},{6,7},{9,8},{8,9},{11,10... | collective-permute-start | bytes 221192 | tf_op jit(solution)/shard_map/ppermute | solution.py:585
  50.2 1.3 %collective-permute-start.12 = (f32[144,128]{1,0:T(8,128)S(1)}, f32[144,128]{1,0:T(8,128)S(1)}, u32[]{:S(2)}, u32[]{:S(2)}) collective-permute-start(f32[144,128]{1,0:T(8,128)S(1)} %add_add_fusion.refs_0_), channel_id=1, source_target_pairs={{4,0},{0,4},{12,8},{8,12},{5,1},{1,5},{13,9},{9,13},{6,2},{2,6},{1... | collective-permute-start | bytes 221192 | tf_op jit(solution)/shard_map/ppermute | solution.py:585
  59.5 6.8 %collective-permute-start.13 = (bf16[2,32,512]{2,1,0:T(8,128)(2,1)S(1)}, bf16[2,32,512]{2,1,0:T(8,128)(2,1)S(1)}, u32[]{:S(2)}, u32[]{:S(2)}) collective-permute-start(bf16[2,32,512]{2,1,0:T(8,128)(2,1)S(1)} %get-tuple-element.10.basis_ref), channel_id=1, source_target_pairs={{3,0},{2,1},{1,2},{0,3},{7,4},{6,5},{5,6},{4,7},{11,8},{10,9},{9,1... | collective-permute-start | bytes 196616 | tf_op jit(solution)/shard_map/ppermute | solution.py:585
  61.4 6.8 %collective-permute-start.14 = (bf16[2,32,512]{2,1,0:T(8,128)(2,1)S(1)}, bf16[2,32,512]{2,1,0:T(8,128)(2,1)S(1)}, u32[]{:S(2)}, u32[]{:S(2)}) collective-permute-start(bf16[2,32,512]{2,1,0:T(8,128)(2,1)S(1)} %get-tuple-element.10.basis_ref), channel_id=1, source_target_pairs={{2,0},{3,1},{0,2},{1,3},{6,4},{7,5},{4,6},{5,7},{10,8},{11,9},{8,1... | collective-permute-start | bytes 196616 | tf_op jit(solution)/shard_map/ppermute | solution.py:585
  61.4 6.8 %collective-permute-start.15 = (bf16[2,32,512]{2,1,0:T(8,128)(2,1)S(1)}, bf16[2,32,512]{2,1,0:T(8,128)(2,1)S(1)}, u32[]{:S(2)}, u32[]{:S(2)}) collective-permute-start(bf16[2,32,512]{2,1,0:T(8,128)(2,1)S(1)} %get-tuple-element.10.basis_ref), channel_id=1, source_target_pairs={{1,0},{0,1},{3,2},{2,3},{5,4},{4,5},{7,6},{6,7},{9,8},{8,9},{11,10... | collective-permute-start | bytes 196616 | tf_op jit(solution)/shard_map/ppermute | solution.py:585
  70.2 5.9 %collective-permute-start.16 = (f32[2,32,32]{2,1,0:T(8,128)S(1)}, f32[2,32,32]{2,1,0:T(8,128)S(1)}, u32[]{:S(2)}, u32[]{:S(2)}) collective-permute-start(f32[2,32,32]{2,1,0:T(8,128)S(1)} %apply_score.1), channel_id=1, source_target_pairs={{3,0},{2,1},{1,2},{0,3},{7,4},{6,5},{5,6},{4,7},{11,8},{10,9},{9,1... | collective-permute-start | bytes 24584 | tf_op jit(solution)/shard_map/ppermute | solution.py:585
  72.2 4.8 %collective-permute-start.17 = (f32[2,32,32]{2,1,0:T(8,128)S(1)}, f32[2,32,32]{2,1,0:T(8,128)S(1)}, u32[]{:S(2)}, u32[]{:S(2)}) collective-permute-start(f32[2,32,32]{2,1,0:T(8,128)S(1)} %apply_score.1), channel_id=1, source_target_pairs={{2,0},{3,1},{0,2},{1,3},{6,4},{7,5},{4,6},{5,7},{10,8},{11,9},{8,1... | collective-permute-start | bytes 24584 | tf_op jit(solution)/shard_map/ppermute | solution.py:585
  72.2 4.8 %collective-permute-start.18 = (f32[2,32,32]{2,1,0:T(8,128)S(1)}, f32[2,32,32]{2,1,0:T(8,128)S(1)}, u32[]{:S(2)}, u32[]{:S(2)}) collective-permute-start(f32[2,32,32]{2,1,0:T(8,128)S(1)} %apply_score.1), channel_id=1, source_target_pairs={{1,0},{0,1},{3,2},{2,3},{5,4},{4,5},{7,6},{6,7},{9,8},{8,9},{11,10... | collective-permute-start | bytes 24584 | tf_op jit(solution)/shard_map/ppermute | solution.py:585

commit v15 on v14

--- a/solution.py
+++ b/solution.py
@@ -230,6 +230,18 @@
             out_ref[0] = against(left_ref[0], tall[...])
 
 
+def split_dot(left, right, dims=(((1,), (0,)), ((), ()))):
+    m = left.shape[0]
+    a, b, c = split3(left)
+    p, q, r = split3(right)
+
+    def dot(rows, piece):
+        return lax.dot_general(jnp.concatenate(rows, axis=0), piece, dims, preferred_element_type=F32)
+
+    x, y, z = dot([a, b, c], p), dot([a, b], q), dot([a], r)
+    return x[:m] + ((x[m : 2 * m] + y[:m]) + (y[m : 2 * m] + (x[2 * m :] + z)))
+
+
 def product(a, b):
     k = a.shape[0]
     left = jnp.concatenate(split3(a), axis=0)
@@ -251,7 +263,7 @@
     earlier, (out_ref, halves, tall, scratch) = refs[:earlier_count], refs[earlier_count:]
     image = jnp.concatenate([piece[...] for piece in pieces], axis=1)
     inverse = inverse_factor(product(image, image), scratch)
-    basis = jnp.dot(inverse, image, precision=HIGHEST, preferred_element_type=F32)
+    basis = split_dot(inverse, image)
     parts = [basis[:, d * ROWS_DEV : d * ROWS_DEV + ROWS_DEV] for d in range(piece_count)]
     before = out_ref.shape[0] - 1
     for ref in earlier:
@@ -483,7 +495,7 @@
 def cross_kernel(k, images_ref, out_ref, packed):
     g = lax.axis_index("layer")
     every = images_ref[...].reshape(-1, images_ref.shape[2])
-    gram = lax.dot_general(every, every, TRANS_B, precision=HIGHEST, preferred_element_type=F32)
+    gram = split_dot(every, every, TRANS_B)
     half = gram.shape[0] // 2
     first, last = gram[:half, :half], gram[half:, half:]
     row = lax.broadcasted_iota(jnp.int32, (half, half), 0) // k
@@ -552,7 +564,7 @@
                 work[r * k : r * k + k] = jnp.where(here, 0.0, rows) - update(r * k, k)
     rows = out_ref.shape[0] * k
     own = work[pl.ds(pl.multiple_of(lax.axis_index("layer") * rows, rows), rows)] * across
-    joint = jnp.dot(own, images_ref[...].reshape(size, -1), precision=HIGHEST, preferred_element_type=F32)
+    joint = split_dot(own, images_ref[...].reshape(size, -1))
     joint = joint.reshape(out_ref.shape)
     out_ref[...] = joint
     again_ref[...] = joint

time: 77.8 us -> 78.1 us (level)
  no operation moved by 1% of the time
where the time goes in v15:
time: 78.1 us; the launch traced here: 77.9 us
  starting transfers between devices  27.9 us (36%)
  Pallas kernels  27.2 us (35%)
  waiting for transfers between devices  13.1 us (17%)
  blocking collectives  7.37 us (9%)
  other arithmetic  1.56 us (2%)
    ppermute x19, starting transfers between devices, swap(): return lax.ppermute(x, axis, [(m ^ d, m) for m in range(count)])  27.9 us
    ppermute x19, waiting for transfers between devices, swap(): return lax.ppermute(x, axis, [(m ^ d, m) for m in range(count)])  13.1 us
    pallas_call x5, Pallas kernels, apply_whole(): pl.pallas_call(kernel, in_specs=vmem_specs(len(operands)), out_specs=pl.B...  11.8 us
    pallas_call x1, Pallas kernels, joint_solve(): pl.pallas_call(functools.partial(joint_kernel, k), in_specs=vmem_specs(3)...  7.8 us
    all_gather x1, blocking collectives, per_device(): images = lax.all_gather(image, 'layer', axis=0, tiled=True)  7.37 us
    pallas_call x1, Pallas kernels, build_whole(): pl.pallas_call(build_whole_kernel, in_specs=[pl.BlockSpec(memory_space=pl...  5.44 us
    pallas_call x2, Pallas kernels, apply_some(): pl.pallas_call(functools.partial(some_kernel, chunk, layers), in_specs=vm...  1.57 us
  transfers between devices with their start and end apart: 19, of which 9 were waited for; matrix products, arithmetic and copies ran while one was open for 0% of the time, Pallas kernels for 15%

profile of v15, /device:TPU:0, one launch (start us, length us, event | category | flops | bytes accessed | tf_op | source)
XLA Modules:
  0.0 77.9 jit_solution(4301337380118424237)
XLA Ops:
  1.5 3.1 %collective-permute-start = (bf16[2,32,512]{2,1,0:T(8,128)(2,1)S(1)}, bf16[2,32,512]{2,1,0:T(8,128)(2,1)S(1)}, u32[]{:S(2)}, u32[]{:S(2)}) collective-permute-start(bf16[2,32,512]{2,1,0:T(8,128)(2,1)S(1)} %convert_element_type.3.refs_0_), channel_id=1, source_target_pairs={{1,0},{0,1},{3,2},{2,3},{5,4},{4,5},{7,6},{6,7},{9,8},{8,9},{11,10... | collective-permute-start | bytes 196616 | tf_op jit(solution)/shard_map/ppermute | solution.py:597
  4.6 2.5 %collective-permute-start.1 = (bf16[2,32,512]{2,1,0:T(8,128)(2,1)S(1)}, bf16[2,32,512]{2,1,0:T(8,128)(2,1)S(1)}, u32[]{:S(2)}, u32[]{:S(2)}) collective-permute-start(bf16[2,32,512]{2,1,0:T(8,128)(2,1)S(1)} %convert_element_type.3.refs_0_), channel_id=1, source_target_pairs={{3,0},{2,1},{1,2},{0,3},{7,4},{6,5},{5,6},{4,7},{11,8},{10,9},{9,1... | collective-permute-start | bytes 196616 | tf_op jit(solution)/shard_map/ppermute | solution.py:597
  7.2 5.4 %build_whole.1 = (bf16[4,512,1024]{2,1,0:T(8,128)(2,1)S(1)}, bf16[4,512,1024]{2,1,0:T(8,128)(2,1)S(1)}) custom-call(s32[2,512]{1,0:T(2,128)} %rows_hbm.1, s32[2,512]{1,0:T(2,128)} %cols_hbm.1, s32[1,2]{1,0:T(1,128)} %bitcast.1, bf16[2,512,4096]{2,1,0:T(8,128)(2,1)} %blocks_ref.1), custom_call_target="tpu_custom_call" | custom-call | bytes 20971520 | tf_op jit(solution)/shard_map/build_whole/pallas_call | solution.py:125
  13.6 1.5 %apply_first.3.refs_0_ = f32[32,512]{1,0:T(8,128)S(1)} custom-call(bf16[2,32,512]{2,1,0:T(8,128)(2,1)S(1)} %convert_element_type.3.refs_0_, bf16[2,32,512]{2,1,0:T(8,128)(2,1)S(1)} %collective-permute-done.refs_1_, bf16[2,32,512]{2,1,0:T(8,128)(2,1)S(1)} %collective-permute-done.1.refs_2_, bf16[2,32,512]{2,1,0:T(8,128)(2,1)S(1)} %collective-permute-done.2.refs_3_, ...), custom_call_target="tpu_custom_call" | custom-call | bytes 4194304 | tf_op jit(solution)/shard_map/apply_first/pallas_call | solution.py:297
  15.1 2.5 %collective-permute-start.6 = (f32[32,512]{1,0:T(8,128)S(1)}, f32[32,512]{1,0:T(8,128)S(1)}, u32[]{:S(2)}, u32[]{:S(2)}) collective-permute-start(f32[32,512]{1,0:T(8,128)S(1)} %apply_first.3.refs_0_), channel_id=1, source_target_pairs={{3,0},{2,1},{1,2},{0,3},{7,4},{6,5},{5,6},{4,7},{11,8},{10,9},{9,1... | collective-permute-start | bytes 196616 | tf_op jit(solution)/shard_map/ppermute | solution.py:597
  17.6 2.0 %collective-permute-start.8 = (f32[32,512]{1,0:T(8,128)S(1)}, f32[32,512]{1,0:T(8,128)S(1)}, u32[]{:S(2)}, u32[]{:S(2)}) collective-permute-start(f32[32,512]{1,0:T(8,128)S(1)} %apply_first.3.refs_0_), channel_id=1, source_target_pairs={{1,0},{0,1},{3,2},{2,3},{5,4},{4,5},{7,6},{6,7},{9,8},{8,9},{11,10... | collective-permute-start | bytes 196616 | tf_op jit(solution)/shard_map/ppermute | solution.py:597
  19.5 1.5 %apply_first.2.refs_0_ = f32[32,512]{1,0:T(8,128)S(1)} custom-call(bf16[2,32,512]{2,1,0:T(8,128)(2,1)S(1)} %convert_element_type.3.refs_0_, bf16[2,32,512]{2,1,0:T(8,128)(2,1)S(1)} %collective-permute-done.refs_1_, bf16[2,32,512]{2,1,0:T(8,128)(2,1)S(1)} %collective-permute-done.1.refs_2_, bf16[2,32,512]{2,1,0:T(8,128)(2,1)S(1)} %collective-permute-done.2.refs_3_, ...), custom_call_target="tpu_custom_call" | custom-call | bytes 4194304 | tf_op jit(solution)/shard_map/apply_first/pallas_call | solution.py:297
  21.0 2.5 %collective-permute-start.3 = (f32[32,512]{1,0:T(8,128)S(1)}, f32[32,512]{1,0:T(8,128)S(1)}, u32[]{:S(2)}, u32[]{:S(2)}) collective-permute-start(f32[32,512]{1,0:T(8,128)S(1)} %apply_first.2.refs_0_), channel_id=1, source_target_pairs={{3,0},{2,1},{1,2},{0,3},{7,4},{6,5},{5,6},{4,7},{11,8},{10,9},{9,1... | collective-permute-start | bytes 196616 | tf_op jit(solution)/shard_map/ppermute | solution.py:597
  23.5 2.0 %collective-permute-start.5 = (f32[32,512]{1,0:T(8,128)S(1)}, f32[32,512]{1,0:T(8,128)S(1)}, u32[]{:S(2)}, u32[]{:S(2)}) collective-permute-start(f32[32,512]{1,0:T(8,128)S(1)} %apply_first.2.refs_0_), channel_id=1, source_target_pairs={{1,0},{0,1},{3,2},{2,3},{5,4},{4,5},{7,6},{6,7},{9,8},{8,9},{11,10... | collective-permute-start | bytes 196616 | tf_op jit(solution)/shard_map/ppermute | solution.py:597
  25.5 3.4 %apply_second.2.refs_5_ = f32[1,32,512]{2,1,0:T(8,128)S(1)} custom-call(f32[32,512]{1,0:T(8,128)S(1)} %apply_first.3.refs_0_, f32[32,512]{1,0:T(8,128)S(1)} %collective-permute-done.6.refs_1_, f32[32,512]{1,0:T(8,128)S(1)} %collective-permute-done.7.refs_2_, f32[32,512]{1,0:T(8,128)S(1)} %collective-permute-done.8.refs_3_, ...), custom_call_target="tpu_custom_call" | custom-call | bytes 4194304 | tf_op jit(solution)/shard_map/apply_second/pallas_call | solution.py:297
  29.6 3.4 %apply_second.3 = f32[2,32,512]{2,1,0:T(8,128)S(1)} custom-call(f32[32,512]{1,0:T(8,128)S(1)} %apply_first.2.refs_0_, f32[32,512]{1,0:T(8,128)S(1)} %collective-permute-done.3.refs_1_, f32[32,512]{1,0:T(8,128)S(1)} %collective-permute-done.4.refs_2_, f32[32,512]{1,0:T(8,128)S(1)} %collective-permute-done.5.refs_3_, ...), custom_call_target="tpu_custom_call" | custom-call | bytes 4194304 | tf_op jit(solution)/shard_map/apply_second/pallas_call | solution.py:297
  33.0 7.4 %all_gather.3.images_ref.refs_2_ = f32[8,32,512]{2,1,0:T(8,128)S(1)} all-gather(f32[2,32,512]{2,1,0:T(8,128)S(1)} %apply_second.3), channel_id=1, replica_groups=mesh['parts'=2,'layer'=4,'node'=4] {'layer'}, dimensions={0}, use_global_device_ids=true | all-gather | bytes 655360 | tf_op jit(solution)/shard_map/all_gather | solution.py:637
  41.0 2.0 %collective-permute-start.10 = (f32[144,128]{1,0:T(8,128)S(1)}, f32[144,128]{1,0:T(8,128)S(1)}, u32[]{:S(2)}, u32[]{:S(2)}) collective-permute-start(f32[144,128]{1,0:T(8,128)S(1)} %cross_gram.1), channel_id=1, source_target_pairs={{3,0},{2,1},{1,2},{0,3},{7,4},{6,5},{5,6},{4,7},{11,8},{10,9},{9,1... | collective-permute-start | bytes 221192 | tf_op jit(solution)/shard_map/ppermute | solution.py:597
  43.0 2.5 %collective-permute-start.9 = (f32[144,128]{1,0:T(8,128)S(1)}, f32[144,128]{1,0:T(8,128)S(1)}, u32[]{:S(2)}, u32[]{:S(2)}) collective-permute-start(f32[144,128]{1,0:T(8,128)S(1)} %cross_gram.1), channel_id=1, source_target_pairs={{1,0},{0,1},{3,2},{2,3},{5,4},{4,5},{7,6},{6,7},{9,8},{8,9},{11,10... | collective-permute-start | bytes 221192 | tf_op jit(solution)/shard_map/ppermute | solution.py:597
  45.5 2.6 %collective-permute-done.10 = f32[144,128]{1,0:T(8,128)S(1)} collective-permute-done((f32[144,128]{1,0:T(8,128)S(1)}, f32[144,128]{1,0:T(8,128)S(1)}, u32[]{:S(2)}, u32[]{:S(2)}) %collective-permute-start.10) | collective-permute-done | bytes 73760 | tf_op jit(solution)/shard_map/ppermute | solution.py:597
  48.1 2.5 %collective-permute-done.11 = f32[144,128]{1,0:T(8,128)S(1)} collective-permute-done((f32[144,128]{1,0:T(8,128)S(1)}, f32[144,128]{1,0:T(8,128)S(1)}, u32[]{:S(2)}, u32[]{:S(2)}) %collective-permute-start.11) | collective-permute-done | bytes 73760 | tf_op jit(solution)/shard_map/ppermute | solution.py:597
  51.9 7.8 %joint_solve.1 = (f32[2,32,512]{2,1,0:T(8,128)}, f32[2,32,512]{2,1,0:T(8,128)S(1)}, bf16[2,32,512]{2,1,0:T(8,128)(2,1)S(1)}) custom-call(f32[144,128]{1,0:T(8,128)S(1)} %add_add_fusion.refs_0_, f32[144,128]{1,0:T(8,128)S(1)} %collective-permute-done.12.refs_1_, f32[8,32,512]{2,1,0:T(8,128)S(1)} %all_gather.3.images_ref.refs_2_), custom_call_target="tpu_custom_call" | custom-call | tf_op jit(solution)/shard_map/joint_solve/pallas_call | solution.py:577
  59.7 1.9 %collective-permute-start.13 = (bf16[2,32,512]{2,1,0:T(8,128)(2,1)S(1)}, bf16[2,32,512]{2,1,0:T(8,128)(2,1)S(1)}, u32[]{:S(2)}, u32[]{:S(2)}) collective-permute-start(bf16[2,32,512]{2,1,0:T(8,128)(2,1)S(1)} %get-tuple-element.10.basis_ref), channel_id=1, source_target_pairs={{3,0},{2,1},{1,2},{0,3},{7,4},{6,5},{5,6},{4,7},{11,8},{10,9},{9,1... | collective-permute-start | bytes 196616 | tf_op jit(solution)/shard_map/ppermute | solution.py:597
  61.6 2.5 %collective-permute-start.15 = (bf16[2,32,512]{2,1,0:T(8,128)(2,1)S(1)}, bf16[2,32,512]{2,1,0:T(8,128)(2,1)S(1)}, u32[]{:S(2)}, u32[]{:S(2)}) collective-permute-start(bf16[2,32,512]{2,1,0:T(8,128)(2,1)S(1)} %get-tuple-element.10.basis_ref), channel_id=1, source_target_pairs={{1,0},{0,1},{3,2},{2,3},{5,4},{4,5},{7,6},{6,7},{9,8},{8,9},{11,10... | collective-permute-start | bytes 196616 | tf_op jit(solution)/shard_map/ppermute | solution.py:597
  64.9 1.6 %collective-permute-done.13.basis_ref = bf16[2,32,512]{2,1,0:T(8,128)(2,1)S(1)} collective-permute-done((bf16[2,32,512]{2,1,0:T(8,128)(2,1)S(1)}, bf16[2,32,512]{2,1,0:T(8,128)(2,1)S(1)}, u32[]{:S(2)}, u32[]{:S(2)}) %collective-permute-start.13) | collective-permute-done | bytes 65568 | tf_op jit(solution)/shard_map/ppermute | solution.py:597
  68.5 2.0 %apply_score.1 = f32[2,32,32]{2,1,0:T(8,128)S(1)} custom-call(f32[2,512,64]{2,1,0:T(8,128)S(1)} %apply_some_3.1.so_far_ref, bf16[2,32,512]{2,1,0:T(8,128)(2,1)S(1)} %collective-permute-done.14.refs_0_, bf16[2,32,512]{2,1,0:T(8,128)(2,1)S(1)} %collective-permute-done.15.refs_1_, f32[2,32,512]{2,1,0:T(8,128)S(1)} %get-tuple-element.11.refs_2_, ...), custom_call_target="tpu_custom_call" | custom-call | bytes 4194304 | tf_op jit(solution)/shard_map/apply_score/pallas_call | solution.py:297
  70.4 2.0 %collective-permute-start.16 = (f32[2,32,32]{2,1,0:T(8,128)S(1)}, f32[2,32,32]{2,1,0:T(8,128)S(1)}, u32[]{:S(2)}, u32[]{:S(2)}) collective-permute-start(f32[2,32,32]{2,1,0:T(8,128)S(1)} %apply_score.1), channel_id=1, source_target_pairs={{3,0},{2,1},{1,2},{0,3},{7,4},{6,5},{5,6},{4,7},{11,8},{10,9},{9,1... | collective-permute-start | bytes 24584 | tf_op jit(solution)/shard_map/ppermute | solution.py:597
  72.4 2.5 %collective-permute-start.18 = (f32[2,32,32]{2,1,0:T(8,128)S(1)}, f32[2,32,32]{2,1,0:T(8,128)S(1)}, u32[]{:S(2)}, u32[]{:S(2)}) collective-permute-start(f32[2,32,32]{2,1,0:T(8,128)S(1)} %apply_score.1), channel_id=1, source_target_pairs={{1,0},{0,1},{3,2},{2,3},{5,4},{4,5},{7,6},{6,7},{9,8},{8,9},{11,10... | collective-permute-start | bytes 24584 | tf_op jit(solution)/shard_map/ppermute | solution.py:597
  74.9 1.4 %collective-permute-done.16 = f32[2,32,32]{2,1,0:T(8,128)S(1)} collective-permute-done((f32[2,32,32]{2,1,0:T(8,128)S(1)}, f32[2,32,32]{2,1,0:T(8,128)S(1)}, u32[]{:S(2)}, u32[]{:S(2)}) %collective-permute-start.16) | collective-permute-done | bytes 8224 | tf_op jit(solution)/shard_map/ppermute | solution.py:597
  (28 shorter events, 9.0 us)
Async XLA Ops:
  1.5 11.1 %collective-permute-start = (bf16[2,32,512]{2,1,0:T(8,128)(2,1)S(1)}, bf16[2,32,512]{2,1,0:T(8,128)(2,1)S(1)}, u32[]{:S(2)}, u32[]{:S(2)}) collective-permute-start(bf16[2,32,512]{2,1,0:T(8,128)(2,1)S(1)} %convert_element_type.3.refs_0_), channel_id=1, source_target_pairs={{1,0},{0,1},{3,2},{2,3},{5,4},{4,5},{7,6},{6,7},{9,8},{8,9},{11,10... | collective-permute-start | bytes 196616 | tf_op jit(solution)/shard_map/ppermute | solution.py:597
  4.6 8.1 %collective-permute-start.1 = (bf16[2,32,512]{2,1,0:T(8,128)(2,1)S(1)}, bf16[2,32,512]{2,1,0:T(8,128)(2,1)S(1)}, u32[]{:S(2)}, u32[]{:S(2)}) collective-permute-start(bf16[2,32,512]{2,1,0:T(8,128)(2,1)S(1)} %convert_element_type.3.refs_0_), channel_id=1, source_target_pairs={{3,0},{2,1},{1,2},{0,3},{7,4},{6,5},{5,6},{4,7},{11,8},{10,9},{9,1... | collective-permute-start | bytes 196616 | tf_op jit(solution)/shard_map/ppermute | solution.py:597
  7.1 6.4 %collective-permute-start.2 = (bf16[2,32,512]{2,1,0:T(8,128)(2,1)S(1)}, bf16[2,32,512]{2,1,0:T(8,128)(2,1)S(1)}, u32[]{:S(2)}, u32[]{:S(2)}) collective-permute-start(bf16[2,32,512]{2,1,0:T(8,128)(2,1)S(1)} %convert_element_type.3.refs_0_), channel_id=1, source_target_pairs={{2,0},{3,1},{0,2},{1,3},{6,4},{7,5},{4,6},{5,7},{10,8},{11,9},{8,1... | collective-permute-start | bytes 196616 | tf_op jit(solution)/shard_map/ppermute | solution.py:597
  15.1 8.4 %collective-permute-start.6 = (f32[32,512]{1,0:T(8,128)S(1)}, f32[32,512]{1,0:T(8,128)S(1)}, u32[]{:S(2)}, u32[]{:S(2)}) collective-permute-start(f32[32,512]{1,0:T(8,128)S(1)} %apply_first.3.refs_0_), channel_id=1, source_target_pairs={{3,0},{2,1},{1,2},{0,3},{7,4},{6,5},{5,6},{4,7},{11,8},{10,9},{9,1... | collective-permute-start | bytes 196616 | tf_op jit(solution)/shard_map/ppermute | solution.py:597
  17.6 7.9 %collective-permute-start.7 = (f32[32,512]{1,0:T(8,128)S(1)}, f32[32,512]{1,0:T(8,128)S(1)}, u32[]{:S(2)}, u32[]{:S(2)}) collective-permute-start(f32[32,512]{1,0:T(8,128)S(1)} %apply_first.3.refs_0_), channel_id=1, source_target_pairs={{2,0},{3,1},{0,2},{1,3},{6,4},{7,5},{4,6},{5,7},{10,8},{11,9},{8,1... | collective-permute-start | bytes 196616 | tf_op jit(solution)/shard_map/ppermute | solution.py:597
  17.6 7.9 %collective-permute-start.8 = (f32[32,512]{1,0:T(8,128)S(1)}, f32[32,512]{1,0:T(8,128)S(1)}, u32[]{:S(2)}, u32[]{:S(2)}) collective-permute-start(f32[32,512]{1,0:T(8,128)S(1)} %apply_first.3.refs_0_), channel_id=1, source_target_pairs={{1,0},{0,1},{3,2},{2,3},{5,4},{4,5},{7,6},{6,7},{9,8},{8,9},{11,10... | collective-permute-start | bytes 196616 | tf_op jit(solution)/shard_map/ppermute | solution.py:597
  21.0 7.8 %collective-permute-start.3 = (f32[32,512]{1,0:T(8,128)S(1)}, f32[32,512]{1,0:T(8,128)S(1)}, u32[]{:S(2)}, u32[]{:S(2)}) collective-permute-start(f32[32,512]{1,0:T(8,128)S(1)} %apply_first.2.refs_0_), channel_id=1, source_target_pairs={{3,0},{2,1},{1,2},{0,3},{7,4},{6,5},{5,6},{4,7},{11,8},{10,9},{9,1... | collective-permute-start | bytes 196616 | tf_op jit(solution)/shard_map/ppermute | solution.py:597
  23.5 6.1 %collective-permute-start.4 = (f32[32,512]{1,0:T(8,128)S(1)}, f32[32,512]{1,0:T(8,128)S(1)}, u32[]{:S(2)}, u32[]{:S(2)}) collective-permute-start(f32[32,512]{1,0:T(8,128)S(1)} %apply_first.2.refs_0_), channel_id=1, source_target_pairs={{2,0},{3,1},{0,2},{1,3},{6,4},{7,5},{4,6},{5,7},{10,8},{11,9},{8,1... | collective-permute-start | bytes 196616 | tf_op jit(solution)/shard_map/ppermute | solution.py:597
  23.5 6.1 %collective-permute-start.5 = (f32[32,512]{1,0:T(8,128)S(1)}, f32[32,512]{1,0:T(8,128)S(1)}, u32[]{:S(2)}, u32[]{:S(2)}) collective-permute-start(f32[32,512]{1,0:T(8,128)S(1)} %apply_first.2.refs_0_), channel_id=1, source_target_pairs={{1,0},{0,1},{3,2},{2,3},{5,4},{4,5},{7,6},{6,7},{9,8},{8,9},{11,10... | collective-permute-start | bytes 196616 | tf_op jit(solution)/shard_map/ppermute | solution.py:597
  41.0 7.0 %collective-permute-start.10 = (f32[144,128]{1,0:T(8,128)S(1)}, f32[144,128]{1,0:T(8,128)S(1)}, u32[]{:S(2)}, u32[]{:S(2)}) collective-permute-start(f32[144,128]{1,0:T(8,128)S(1)} %cross_gram.1), channel_id=1, source_target_pairs={{3,0},{2,1},{1,2},{0,3},{7,4},{6,5},{5,6},{4,7},{11,8},{10,9},{9,1... | collective-permute-start | bytes 221192 | tf_op jit(solution)/shard_map/ppermute | solution.py:597
  43.0 7.5 %collective-permute-start.11 = (f32[144,128]{1,0:T(8,128)S(1)}, f32[144,128]{1,0:T(8,128)S(1)}, u32[]{:S(2)}, u32[]{:S(2)}) collective-permute-start(f32[144,128]{1,0:T(8,128)S(1)} %cross_gram.1), channel_id=1, source_target_pairs={{2,0},{3,1},{0,2},{1,3},{6,4},{7,5},{4,6},{5,7},{10,8},{11,9},{8,1... | collective-permute-start | bytes 221192 | tf_op jit(solution)/shard_map/ppermute | solution.py:597
  43.0 7.5 %collective-permute-start.9 = (f32[144,128]{1,0:T(8,128)S(1)}, f32[144,128]{1,0:T(8,128)S(1)}, u32[]{:S(2)}, u32[]{:S(2)}) collective-permute-start(f32[144,128]{1,0:T(8,128)S(1)} %cross_gram.1), channel_id=1, source_target_pairs={{1,0},{0,1},{3,2},{2,3},{5,4},{4,5},{7,6},{6,7},{9,8},{8,9},{11,10... | collective-permute-start | bytes 221192 | tf_op jit(solution)/shard_map/ppermute | solution.py:597
  50.6 1.3 %collective-permute-start.12 = (f32[144,128]{1,0:T(8,128)S(1)}, f32[144,128]{1,0:T(8,128)S(1)}, u32[]{:S(2)}, u32[]{:S(2)}) collective-permute-start(f32[144,128]{1,0:T(8,128)S(1)} %add_add_fusion.refs_0_), channel_id=1, source_target_pairs={{4,0},{0,4},{12,8},{8,12},{5,1},{1,5},{13,9},{9,13},{6,2},{2,6},{1... | collective-permute-start | bytes 221192 | tf_op jit(solution)/shard_map/ppermute | solution.py:597
  59.7 6.8 %collective-permute-start.13 = (bf16[2,32,512]{2,1,0:T(8,128)(2,1)S(1)}, bf16[2,32,512]{2,1,0:T(8,128)(2,1)S(1)}, u32[]{:S(2)}, u32[]{:S(2)}) collective-permute-start(bf16[2,32,512]{2,1,0:T(8,128)(2,1)S(1)} %get-tuple-element.10.basis_ref), channel_id=1, source_target_pairs={{3,0},{2,1},{1,2},{0,3},{7,4},{6,5},{5,6},{4,7},{11,8},{10,9},{9,1... | collective-permute-start | bytes 196616 | tf_op jit(solution)/shard_map/ppermute | solution.py:597
  61.6 6.8 %collective-permute-start.14 = (bf16[2,32,512]{2,1,0:T(8,128)(2,1)S(1)}, bf16[2,32,512]{2,1,0:T(8,128)(2,1)S(1)}, u32[]{:S(2)}, u32[]{:S(2)}) collective-permute-start(bf16[2,32,512]{2,1,0:T(8,128)(2,1)S(1)} %get-tuple-element.10.basis_ref), channel_id=1, source_target_pairs={{2,0},{3,1},{0,2},{1,3},{6,4},{7,5},{4,6},{5,7},{10,8},{11,9},{8,1... | collective-permute-start | bytes 196616 | tf_op jit(solution)/shard_map/ppermute | solution.py:597
  61.6 6.8 %collective-permute-start.15 = (bf16[2,32,512]{2,1,0:T(8,128)(2,1)S(1)}, bf16[2,32,512]{2,1,0:T(8,128)(2,1)S(1)}, u32[]{:S(2)}, u32[]{:S(2)}) collective-permute-start(bf16[2,32,512]{2,1,0:T(8,128)(2,1)S(1)} %get-tuple-element.10.basis_ref), channel_id=1, source_target_pairs={{1,0},{0,1},{3,2},{2,3},{5,4},{4,5},{7,6},{6,7},{9,8},{8,9},{11,10... | collective-permute-start | bytes 196616 | tf_op jit(solution)/shard_map/ppermute | solution.py:597
  70.4 5.9 %collective-permute-start.16 = (f32[2,32,32]{2,1,0:T(8,128)S(1)}, f32[2,32,32]{2,1,0:T(8,128)S(1)}, u32[]{:S(2)}, u32[]{:S(2)}) collective-permute-start(f32[2,32,32]{2,1,0:T(8,128)S(1)} %apply_score.1), channel_id=1, source_target_pairs={{3,0},{2,1},{1,2},{0,3},{7,4},{6,5},{5,6},{4,7},{11,8},{10,9},{9,1... | collective-permute-start | bytes 24584 | tf_op jit(solution)/shard_map/ppermute | solution.py:597
  72.4 4.8 %collective-permute-start.17 = (f32[2,32,32]{2,1,0:T(8,128)S(1)}, f32[2,32,32]{2,1,0:T(8,128)S(1)}, u32[]{:S(2)}, u32[]{:S(2)}) collective-permute-start(f32[2,32,32]{2,1,0:T(8,128)S(1)} %apply_score.1), channel_id=1, source_target_pairs={{2,0},{3,1},{0,2},{1,3},{6,4},{7,5},{4,6},{5,7},{10,8},{11,9},{8,1... | collective-permute-start | bytes 24584 | tf_op jit(solution)/shard_map/ppermute | solution.py:597
  72.4 4.8 %collective-permute-start.18 = (f32[2,32,32]{2,1,0:T(8,128)S(1)}, f32[2,32,32]{2,1,0:T(8,128)S(1)}, u32[]{:S(2)}, u32[]{:S(2)}) collective-permute-start(f32[2,32,32]{2,1,0:T(8,128)S(1)} %apply_score.1), channel_id=1, source_target_pairs={{1,0},{0,1},{3,2},{2,3},{5,4},{4,5},{7,6},{6,7},{9,8},{8,9},{11,10... | collective-permute-start | bytes 24584 | tf_op jit(solution)/shard_map/ppermute | solution.py:597

commit v16 on v15

--- a/solution.py
+++ b/solution.py
@@ -263,7 +263,7 @@
     earlier, (out_ref, halves, tall, scratch) = refs[:earlier_count], refs[earlier_count:]
     image = jnp.concatenate([piece[...] for piece in pieces], axis=1)
     inverse = inverse_factor(product(image, image), scratch)
-    basis = split_dot(inverse, image)
+    basis = jnp.dot(inverse, image, precision=HIGHEST, preferred_element_type=F32)
     parts = [basis[:, d * ROWS_DEV : d * ROWS_DEV + ROWS_DEV] for d in range(piece_count)]
     before = out_ref.shape[0] - 1
     for ref in earlier:
@@ -271,26 +271,43 @@
     out_ref[before] = to_wide(sum(image_part(part, dense_ref[chunk]) for chunk, part in zip(ORDER, parts)), out_ref.shape[1], halves, tall)
 
 
+def turn(left, tall, halves):
+    k, nodes = left.shape
+    tall[...] = jnp.concatenate([left, jnp.zeros((128 - k, nodes), F32)], axis=0).T
+    for b in range(BROWS):
+        even = tall[pl.ds(BLK * b, BLK // 2, stride=2), :]
+        odd = tall[pl.ds(BLK * b + 1, BLK // 2, stride=2), :]
+        halves[pl.ds(b, BLK // 2, stride=BROWS), :] = even + pltpu.roll(odd, k, 1)
+    return halves[...].T[: 2 * k]
+
+
+def own_kernel(layers, basis_ref, left_ref, *refs):
+    dense_refs, (out_ref, turned_ref, tall, halves) = refs[:layers], refs[layers:]
+    for layer, dense_ref in enumerate(dense_refs):
+        out_ref[layer] = image_part(basis_ref[layer], dense_ref[0])
+    for layer in range(layers):
+        turned_ref[layer] = turn(left_ref[layer], tall.at[layer], halves.at[layer])
+
+
 def some_kernel(chunk, layers, basis_ref, *refs):
-    dense_refs, (*so_far, out_ref) = refs[:layers], refs[layers:]
+    dense_refs, (so_far_ref, out_ref) = refs[:layers], refs[layers:]
     for layer, dense_ref in enumerate(dense_refs):
-        part = image_part(basis_ref[layer], dense_ref[chunk])
-        out_ref[layer] = sum((ref[layer] for ref in so_far), part)
+        out_ref[layer] = so_far_ref[layer] + image_part(basis_ref[layer], dense_ref[chunk])
 
 
 def score_kernel(layers, chunks, so_far_ref, *refs):
-    pieces, left_ref, refs = refs[: len(chunks)], refs[len(chunks)], refs[len(chunks) + 1 :]
-    dense_refs, (out_ref, halves, tall) = refs[:layers], refs[layers:]
+    pieces, turned_ref, refs = refs[: len(chunks)], refs[len(chunks)], refs[len(chunks) + 1 :]
+    dense_refs, out_ref = refs[:layers], refs[layers]
+    k = out_ref.shape[1]
     totals = [
         so_far_ref[layer]
         + sum(image_part(piece[layer], dense_refs[layer][chunk]) for chunk, piece in zip(chunks, pieces))
         for layer in range(layers)
     ]
-    wide = [
-        to_wide(totals[layer], left_ref.shape[1], halves.at[layer], tall.at[layer]) for layer in range(layers)
-    ]
+    halves = [total[:TALL] + total[TALL:] for total in totals]
     for layer in range(layers):
-        out_ref[layer] = product(left_ref[layer], wide[layer])
+        pairs = split_dot(turned_ref[layer], halves[layer])
+        out_ref[layer] = pairs[:k, :k] + pairs[k : 2 * k, k : 2 * k]
 
 
 def apply_whole(kernel, name, operands, out_shape, *lead, scratch=()):
@@ -319,25 +336,53 @@
     return apply_whole(kernel, "apply_second", operands, shape, scratch=[pltpu.VMEM(SPREAD, F32)])
 
 
-def apply_some(chunk, basis, dense, *so_far):
-    layers, k = basis.shape[:2]
-    return pl.pallas_call(
-        functools.partial(some_kernel, chunk, layers),
-        in_specs=vmem_specs(1 + layers + len(so_far)),
+def part_cost():
+    return pl.CostEstimate(flops=0, bytes_accessed=2 * MIB, transcendentals=0)
+
+
+def apply_own(basis, left, dense):
+    layers, k, _ = basis.shape
+    return pl.pallas_call(
+        functools.partial(own_kernel, layers),
+        in_specs=vmem_specs(2 + layers),
+        out_specs=vmem_specs(2),
+        out_shape=[
+            jax.ShapeDtypeStruct((layers, 2 * TALL, 2 * k), F32),
+            jax.ShapeDtypeStruct((layers, 2 * k, TALL), F32),
+        ],
+        scratch_shapes=[pltpu.VMEM((layers, ROWS_DEV, 128), F32), pltpu.VMEM((layers, TALL, 128), F32)],
+        compiler_params=params(14),
+        cost_estimate=part_cost(),
+        name="apply_own",
+    )(basis, left, *dense)
+
+
+def apply_some(chunk, basis, dense, so_far):
+    return pl.pallas_call(
+        functools.partial(some_kernel, chunk, len(dense)),
+        in_specs=vmem_specs(2 + len(dense)),
         out_specs=pl.BlockSpec(memory_space=pltpu.VMEM),
-        out_shape=jax.ShapeDtypeStruct((layers, 2 * TALL, 2 * k), F32),
+        out_shape=jax.ShapeDtypeStruct(so_far.shape, F32),
         compiler_params=params(14),
-        cost_estimate=pl.CostEstimate(flops=0, bytes_accessed=2 * MIB, transcendentals=0),
+        cost_estimate=part_cost(),
         name=f"apply_some_{chunk}",
-    )(basis, *dense, *so_far)
+    )(basis, *dense, so_far)
 
 
 def apply_score(pieces, left, dense):
-    so_far = apply_some(ORDER[1], pieces[1], dense, apply_some(0, pieces[0], dense))
-    kernel = functools.partial(score_kernel, len(dense), ORDER[2:])
-    layers, k = left.shape[:2]
-    operands = [so_far, *pieces[2:], left, *dense]
-    return apply_whole(kernel, "apply_score", operands, (layers, k, k), layers)
+    layers, k, _ = left.shape
+    so_far, turned = apply_own(pieces[0], left, dense)
+    so_far = apply_some(ORDER[1], pieces[1], dense, so_far)
+    operands = [so_far, *pieces[2:], turned, *dense]
+    return pl.pallas_call(
+        functools.partial(score_kernel, len(dense), ORDER[2:]),
+        in_specs=vmem_specs(len(operands)),
+        out_specs=pl.BlockSpec(memory_space=pltpu.VMEM),
+        out_shape=jax.ShapeDtypeStruct((layers, k, k), F32),
+        compiler_params=params(14),
+        cost_estimate=part_cost(),
+        name="apply_score",
+    )(*operands)
 
 
 def apply_dense(mode, basis, dense, left=None):
@@ -604,10 +649,9 @@
     return [x] + [swap(x, axis, d, count) for d in ORDER[1:]]
 
 
-def add_pieces(pieces, flip):
+def add_pieces(pieces):
     own, near, far, across = (pieces[ORDER.index(d)] for d in range(4))
-    low, high = own + near, across + far
-    return high + low if flip else low + high
+    return (own + near) + (across + far)
 
 
 def per_device(shards, groups, blocks, block_rows, block_cols, counts, start):
@@ -617,8 +661,8 @@
     def gather(x):
         return around(x, "node", shards) if few else lax.all_gather(x, "node")
 
-    def total(x, flip=False):
-        return add_pieces(around(x, "node", shards), flip) if few else lax.psum(x, "node")
+    def total(x):
+        return add_pieces(around(x, "node", shards)) if few else lax.psum(x, "node")
 
     rounded = start.astype(BF16)
     chunk_total = shards * BROWS // CHUNK_COLS
@@ -643,7 +687,7 @@
         partial = apply_score(gather(rounded), again, dense)
     else:
         (partial,) = apply_dense("score", gather(rounded), dense, again)
-    return joint_basis, total(partial, True)
+    return joint_basis, total(partial)
 
 
 def solution(mesh):

time: 78.1 us -> 77.3 us (0.990)
  Pallas kernels: 27.2 us -> 26.2 us
    pallas_call x5 -> x4, Pallas kernels: 11.8 us -> 9.07 us  [apply_whole(): pl.pallas_call(kernel, in_specs=vmem_specs(len(operands)), out_specs=pl.B...]
    pallas_call x2 -> x3, Pallas kernels: 1.57 us -> 3.26 us  [the longest x1 1.64 us: apply_score(): pl.pallas_call(functools.partial(score_kernel, len(dense), ORDER[2:]), in...]
where the time goes in v16:
time: 77.3 us; the launch traced here: 77.2 us
  starting transfers between devices  27.9 us (36%)
  Pallas kernels  26.2 us (34%)
  waiting for transfers between devices  13.4 us (17%)
  blocking collectives  7.37 us (10%)
  other arithmetic  1.56 us (2%)
    ppermute x19, starting transfers between devices, swap(): return lax.ppermute(x, axis, [(m ^ d, m) for m in range(count)])  27.9 us
    ppermute x19, waiting for transfers between devices, swap(): return lax.ppermute(x, axis, [(m ^ d, m) for m in range(count)])  13.4 us
    pallas_call x4, Pallas kernels, apply_whole(): pl.pallas_call(kernel, in_specs=vmem_specs(len(operands)), out_specs=pl.B...  9.07 us
    pallas_call x1, Pallas kernels, joint_solve(): pl.pallas_call(functools.partial(joint_kernel, k), in_specs=vmem_specs(3)...  7.8 us
    all_gather x1, blocking collectives, per_device(): images = lax.all_gather(image, 'layer', axis=0, tiled=True)  7.37 us
    pallas_call x1, Pallas kernels, build_whole(): pl.pallas_call(build_whole_kernel, in_specs=[pl.BlockSpec(memory_space=pl...  5.44 us
    pallas_call x1, Pallas kernels, apply_score(): pl.pallas_call(functools.partial(score_kernel, len(dense), ORDER[2:]), in...  1.64 us
  transfers between devices with their start and end apart: 19, of which 9 were waited for; matrix products, arithmetic and copies ran while one was open for 0% of the time, Pallas kernels for 15%

profile of v16, /device:TPU:0, one launch (start us, length us, event | category | flops | bytes accessed | tf_op | source)
XLA Modules:
  0.0 77.2 jit_solution(3428081481570955113)
XLA Ops:
  1.5 3.1 %collective-permute-start = (bf16[2,32,512]{2,1,0:T(8,128)(2,1)S(1)}, bf16[2,32,512]{2,1,0:T(8,128)(2,1)S(1)}, u32[]{:S(2)}, u32[]{:S(2)}) collective-permute-start(bf16[2,32,512]{2,1,0:T(8,128)(2,1)S(1)} %convert_element_type.3.refs_0_), channel_id=1, source_target_pairs={{1,0},{0,1},{3,2},{2,3},{5,4},{4,5},{7,6},{6,7},{9,8},{8,9},{11,10... | collective-permute-start | bytes 196616 | tf_op jit(solution)/shard_map/ppermute | solution.py:642
  4.6 2.5 %collective-permute-start.1 = (bf16[2,32,512]{2,1,0:T(8,128)(2,1)S(1)}, bf16[2,32,512]{2,1,0:T(8,128)(2,1)S(1)}, u32[]{:S(2)}, u32[]{:S(2)}) collective-permute-start(bf16[2,32,512]{2,1,0:T(8,128)(2,1)S(1)} %convert_element_type.3.refs_0_), channel_id=1, source_target_pairs={{3,0},{2,1},{1,2},{0,3},{7,4},{6,5},{5,6},{4,7},{11,8},{10,9},{9,1... | collective-permute-start | bytes 196616 | tf_op jit(solution)/shard_map/ppermute | solution.py:642
  7.2 5.4 %build_whole.1 = (bf16[4,512,1024]{2,1,0:T(8,128)(2,1)S(1)}, bf16[4,512,1024]{2,1,0:T(8,128)(2,1)S(1)}) custom-call(s32[2,512]{1,0:T(2,128)} %rows_hbm.1, s32[2,512]{1,0:T(2,128)} %cols_hbm.1, s32[1,2]{1,0:T(1,128)} %bitcast.1, bf16[2,512,4096]{2,1,0:T(8,128)(2,1)} %blocks_ref.1), custom_call_target="tpu_custom_call" | custom-call | bytes 20971520 | tf_op jit(solution)/shard_map/build_whole/pallas_call | solution.py:125
  13.6 1.5 %apply_first.3.refs_0_ = f32[32,512]{1,0:T(8,128)S(1)} custom-call(bf16[2,32,512]{2,1,0:T(8,128)(2,1)S(1)} %convert_element_type.3.refs_0_, bf16[2,32,512]{2,1,0:T(8,128)(2,1)S(1)} %collective-permute-done.refs_1_, bf16[2,32,512]{2,1,0:T(8,128)(2,1)S(1)} %collective-permute-done.1.refs_2_, bf16[2,32,512]{2,1,0:T(8,128)(2,1)S(1)} %collective-permute-done.2.refs_3_, ...), custom_call_target="tpu_custom_call" | custom-call | bytes 4194304 | tf_op jit(solution)/shard_map/apply_first/pallas_call | solution.py:314
  15.1 2.5 %collective-permute-start.6 = (f32[32,512]{1,0:T(8,128)S(1)}, f32[32,512]{1,0:T(8,128)S(1)}, u32[]{:S(2)}, u32[]{:S(2)}) collective-permute-start(f32[32,512]{1,0:T(8,128)S(1)} %apply_first.3.refs_0_), channel_id=1, source_target_pairs={{3,0},{2,1},{1,2},{0,3},{7,4},{6,5},{5,6},{4,7},{11,8},{10,9},{9,1... | collective-permute-start | bytes 196616 | tf_op jit(solution)/shard_map/ppermute | solution.py:642
  17.6 2.0 %collective-permute-start.8 = (f32[32,512]{1,0:T(8,128)S(1)}, f32[32,512]{1,0:T(8,128)S(1)}, u32[]{:S(2)}, u32[]{:S(2)}) collective-permute-start(f32[32,512]{1,0:T(8,128)S(1)} %apply_first.3.refs_0_), channel_id=1, source_target_pairs={{1,0},{0,1},{3,2},{2,3},{5,4},{4,5},{7,6},{6,7},{9,8},{8,9},{11,10... | collective-permute-start | bytes 196616 | tf_op jit(solution)/shard_map/ppermute | solution.py:642
  19.5 1.5 %apply_first.2.refs_0_ = f32[32,512]{1,0:T(8,128)S(1)} custom-call(bf16[2,32,512]{2,1,0:T(8,128)(2,1)S(1)} %convert_element_type.3.refs_0_, bf16[2,32,512]{2,1,0:T(8,128)(2,1)S(1)} %collective-permute-done.refs_1_, bf16[2,32,512]{2,1,0:T(8,128)(2,1)S(1)} %collective-permute-done.1.refs_2_, bf16[2,32,512]{2,1,0:T(8,128)(2,1)S(1)} %collective-permute-done.2.refs_3_, ...), custom_call_target="tpu_custom_call" | custom-call | bytes 4194304 | tf_op jit(solution)/shard_map/apply_first/pallas_call | solution.py:314
  21.0 2.5 %collective-permute-start.3 = (f32[32,512]{1,0:T(8,128)S(1)}, f32[32,512]{1,0:T(8,128)S(1)}, u32[]{:S(2)}, u32[]{:S(2)}) collective-permute-start(f32[32,512]{1,0:T(8,128)S(1)} %apply_first.2.refs_0_), channel_id=1, source_target_pairs={{3,0},{2,1},{1,2},{0,3},{7,4},{6,5},{5,6},{4,7},{11,8},{10,9},{9,1... | collective-permute-start | bytes 196616 | tf_op jit(solution)/shard_map/ppermute | solution.py:642
  23.5 2.0 %collective-permute-start.5 = (f32[32,512]{1,0:T(8,128)S(1)}, f32[32,512]{1,0:T(8,128)S(1)}, u32[]{:S(2)}, u32[]{:S(2)}) collective-permute-start(f32[32,512]{1,0:T(8,128)S(1)} %apply_first.2.refs_0_), channel_id=1, source_target_pairs={{1,0},{0,1},{3,2},{2,3},{5,4},{4,5},{7,6},{6,7},{9,8},{8,9},{11,10... | collective-permute-start | bytes 196616 | tf_op jit(solution)/shard_map/ppermute | solution.py:642
  25.5 3.0 %apply_second.2.refs_5_ = f32[1,32,512]{2,1,0:T(8,128)S(1)} custom-call(f32[32,512]{1,0:T(8,128)S(1)} %apply_first.3.refs_0_, f32[32,512]{1,0:T(8,128)S(1)} %collective-permute-done.6.refs_1_, f32[32,512]{1,0:T(8,128)S(1)} %collective-permute-done.7.refs_2_, f32[32,512]{1,0:T(8,128)S(1)} %collective-permute-done.8.refs_3_, ...), custom_call_target="tpu_custom_call" | custom-call | bytes 4194304 | tf_op jit(solution)/shard_map/apply_second/pallas_call | solution.py:314
  29.6 3.0 %apply_second.3 = f32[2,32,512]{2,1,0:T(8,128)S(1)} custom-call(f32[32,512]{1,0:T(8,128)S(1)} %apply_first.2.refs_0_, f32[32,512]{1,0:T(8,128)S(1)} %collective-permute-done.3.refs_1_, f32[32,512]{1,0:T(8,128)S(1)} %collective-permute-done.4.refs_2_, f32[32,512]{1,0:T(8,128)S(1)} %collective-permute-done.5.refs_3_, ...), custom_call_target="tpu_custom_call" | custom-call | bytes 4194304 | tf_op jit(solution)/shard_map/apply_second/pallas_call | solution.py:314
  32.6 7.4 %all_gather.3.images_ref.refs_2_ = f32[8,32,512]{2,1,0:T(8,128)S(1)} all-gather(f32[2,32,512]{2,1,0:T(8,128)S(1)} %apply_second.3), channel_id=1, replica_groups=mesh['parts'=2,'layer'=4,'node'=4] {'layer'}, dimensions={0}, use_global_device_ids=true | all-gather | bytes 655360 | tf_op jit(solution)/shard_map/all_gather | solution.py:681
  40.6 2.0 %collective-permute-start.10 = (f32[144,128]{1,0:T(8,128)S(1)}, f32[144,128]{1,0:T(8,128)S(1)}, u32[]{:S(2)}, u32[]{:S(2)}) collective-permute-start(f32[144,128]{1,0:T(8,128)S(1)} %cross_gram.1), channel_id=1, source_target_pairs={{3,0},{2,1},{1,2},{0,3},{7,4},{6,5},{5,6},{4,7},{11,8},{10,9},{9,1... | collective-permute-start | bytes 221192 | tf_op jit(solution)/shard_map/ppermute | solution.py:642
  42.6 2.5 %collective-permute-start.9 = (f32[144,128]{1,0:T(8,128)S(1)}, f32[144,128]{1,0:T(8,128)S(1)}, u32[]{:S(2)}, u32[]{:S(2)}) collective-permute-start(f32[144,128]{1,0:T(8,128)S(1)} %cross_gram.1), channel_id=1, source_target_pairs={{1,0},{0,1},{3,2},{2,3},{5,4},{4,5},{7,6},{6,7},{9,8},{8,9},{11,10... | collective-permute-start | bytes 221192 | tf_op jit(solution)/shard_map/ppermute | solution.py:642
  45.1 2.6 %collective-permute-done.10 = f32[144,128]{1,0:T(8,128)S(1)} collective-permute-done((f32[144,128]{1,0:T(8,128)S(1)}, f32[144,128]{1,0:T(8,128)S(1)}, u32[]{:S(2)}, u32[]{:S(2)}) %collective-permute-start.10) | collective-permute-done | bytes 73760 | tf_op jit(solution)/shard_map/ppermute | solution.py:642
  47.7 2.5 %collective-permute-done.11 = f32[144,128]{1,0:T(8,128)S(1)} collective-permute-done((f32[144,128]{1,0:T(8,128)S(1)}, f32[144,128]{1,0:T(8,128)S(1)}, u32[]{:S(2)}, u32[]{:S(2)}) %collective-permute-start.11) | collective-permute-done | bytes 73760 | tf_op jit(solution)/shard_map/ppermute | solution.py:642
  51.5 7.8 %joint_solve.1 = (f32[2,32,512]{2,1,0:T(8,128)}, f32[2,32,512]{2,1,0:T(8,128)S(1)}, bf16[2,32,512]{2,1,0:T(8,128)(2,1)S(1)}) custom-call(f32[144,128]{1,0:T(8,128)S(1)} %add_add_fusion.refs_0_, f32[144,128]{1,0:T(8,128)S(1)} %collective-permute-done.12.refs_1_, f32[8,32,512]{2,1,0:T(8,128)S(1)} %all_gather.3.images_ref.refs_2_), custom_call_target="tpu_custom_call" | custom-call | tf_op jit(solution)/shard_map/joint_solve/pallas_call | solution.py:622
  59.4 1.9 %collective-permute-start.13 = (bf16[2,32,512]{2,1,0:T(8,128)(2,1)S(1)}, bf16[2,32,512]{2,1,0:T(8,128)(2,1)S(1)}, u32[]{:S(2)}, u32[]{:S(2)}) collective-permute-start(bf16[2,32,512]{2,1,0:T(8,128)(2,1)S(1)} %get-tuple-element.12.basis_ref), channel_id=1, source_target_pairs={{3,0},{2,1},{1,2},{0,3},{7,4},{6,5},{5,6},{4,7},{11,8},{10,9},{9,1... | collective-permute-start | bytes 196616 | tf_op jit(solution)/shard_map/ppermute | solution.py:642
  61.3 2.5 %collective-permute-start.15 = (bf16[2,32,512]{2,1,0:T(8,128)(2,1)S(1)}, bf16[2,32,512]{2,1,0:T(8,128)(2,1)S(1)}, u32[]{:S(2)}, u32[]{:S(2)}) collective-permute-start(bf16[2,32,512]{2,1,0:T(8,128)(2,1)S(1)} %get-tuple-element.12.basis_ref), channel_id=1, source_target_pairs={{1,0},{0,1},{3,2},{2,3},{5,4},{4,5},{7,6},{6,7},{9,8},{8,9},{11,10... | collective-permute-start | bytes 196616 | tf_op jit(solution)/shard_map/ppermute | solution.py:642
  64.6 1.5 %collective-permute-done.13.basis_ref = bf16[2,32,512]{2,1,0:T(8,128)(2,1)S(1)} collective-permute-done((bf16[2,32,512]{2,1,0:T(8,128)(2,1)S(1)}, bf16[2,32,512]{2,1,0:T(8,128)(2,1)S(1)}, u32[]{:S(2)}, u32[]{:S(2)}) %collective-permute-start.13) | collective-permute-done | bytes 65568 | tf_op jit(solution)/shard_map/ppermute | solution.py:642
  68.1 1.6 %apply_score.1 = f32[2,32,32]{2,1,0:T(8,128)S(1)} custom-call(f32[2,512,64]{2,1,0:T(8,128)S(1)} %apply_some_3.1.so_far_ref, bf16[2,32,512]{2,1,0:T(8,128)(2,1)S(1)} %collective-permute-done.14.refs_0_, bf16[2,32,512]{2,1,0:T(8,128)(2,1)S(1)} %collective-permute-done.15.refs_1_, f32[2,64,256]{2,1,0:T(8,128)S(1)} %get-tuple-element.15.refs_2_, ...), custom_call_target="tpu_custom_call" | custom-call | bytes 2097152 | tf_op jit(solution)/shard_map/apply_score/pallas_call | solution.py:377
  69.8 2.0 %collective-permute-start.17 = (f32[2,32,32]{2,1,0:T(8,128)S(1)}, f32[2,32,32]{2,1,0:T(8,128)S(1)}, u32[]{:S(2)}, u32[]{:S(2)}) collective-permute-start(f32[2,32,32]{2,1,0:T(8,128)S(1)} %apply_score.1), channel_id=1, source_target_pairs={{3,0},{2,1},{1,2},{0,3},{7,4},{6,5},{5,6},{4,7},{11,8},{10,9},{9,1... | collective-permute-start | bytes 24584 | tf_op jit(solution)/shard_map/ppermute | solution.py:642
  71.7 2.5 %collective-permute-start.16 = (f32[2,32,32]{2,1,0:T(8,128)S(1)}, f32[2,32,32]{2,1,0:T(8,128)S(1)}, u32[]{:S(2)}, u32[]{:S(2)}) collective-permute-start(f32[2,32,32]{2,1,0:T(8,128)S(1)} %apply_score.1), channel_id=1, source_target_pairs={{1,0},{0,1},{3,2},{2,3},{5,4},{4,5},{7,6},{6,7},{9,8},{8,9},{11,10... | collective-permute-start | bytes 24584 | tf_op jit(solution)/shard_map/ppermute | solution.py:642
  74.2 1.4 %collective-permute-done.17 = f32[2,32,32]{2,1,0:T(8,128)S(1)} collective-permute-done((f32[2,32,32]{2,1,0:T(8,128)S(1)}, f32[2,32,32]{2,1,0:T(8,128)S(1)}, u32[]{:S(2)}, u32[]{:S(2)}) %collective-permute-start.17) | collective-permute-done | bytes 8224 | tf_op jit(solution)/shard_map/ppermute | solution.py:642
  (28 shorter events, 9.4 us)
Async XLA Ops:
  1.5 11.1 %collective-permute-start = (bf16[2,32,512]{2,1,0:T(8,128)(2,1)S(1)}, bf16[2,32,512]{2,1,0:T(8,128)(2,1)S(1)}, u32[]{:S(2)}, u32[]{:S(2)}) collective-permute-start(bf16[2,32,512]{2,1,0:T(8,128)(2,1)S(1)} %convert_element_type.3.refs_0_), channel_id=1, source_target_pairs={{1,0},{0,1},{3,2},{2,3},{5,4},{4,5},{7,6},{6,7},{9,8},{8,9},{11,10... | collective-permute-start | bytes 196616 | tf_op jit(solution)/shard_map/ppermute | solution.py:642
  4.6 8.1 %collective-permute-start.1 = (bf16[2,32,512]{2,1,0:T(8,128)(2,1)S(1)}, bf16[2,32,512]{2,1,0:T(8,128)(2,1)S(1)}, u32[]{:S(2)}, u32[]{:S(2)}) collective-permute-start(bf16[2,32,512]{2,1,0:T(8,128)(2,1)S(1)} %convert_element_type.3.refs_0_), channel_id=1, source_target_pairs={{3,0},{2,1},{1,2},{0,3},{7,4},{6,5},{5,6},{4,7},{11,8},{10,9},{9,1... | collective-permute-start | bytes 196616 | tf_op jit(solution)/shard_map/ppermute | solution.py:642
  7.1 6.4 %collective-permute-start.2 = (bf16[2,32,512]{2,1,0:T(8,128)(2,1)S(1)}, bf16[2,32,512]{2,1,0:T(8,128)(2,1)S(1)}, u32[]{:S(2)}, u32[]{:S(2)}) collective-permute-start(bf16[2,32,512]{2,1,0:T(8,128)(2,1)S(1)} %convert_element_type.3.refs_0_), channel_id=1, source_target_pairs={{2,0},{3,1},{0,2},{1,3},{6,4},{7,5},{4,6},{5,7},{10,8},{11,9},{8,1... | collective-permute-start | bytes 196616 | tf_op jit(solution)/shard_map/ppermute | solution.py:642
  15.1 8.4 %collective-permute-start.6 = (f32[32,512]{1,0:T(8,128)S(1)}, f32[32,512]{1,0:T(8,128)S(1)}, u32[]{:S(2)}, u32[]{:S(2)}) collective-permute-start(f32[32,512]{1,0:T(8,128)S(1)} %apply_first.3.refs_0_), channel_id=1, source_target_pairs={{3,0},{2,1},{1,2},{0,3},{7,4},{6,5},{5,6},{4,7},{11,8},{10,9},{9,1... | collective-permute-start | bytes 196616 | tf_op jit(solution)/shard_map/ppermute | solution.py:642
  17.6 7.9 %collective-permute-start.7 = (f32[32,512]{1,0:T(8,128)S(1)}, f32[32,512]{1,0:T(8,128)S(1)}, u32[]{:S(2)}, u32[]{:S(2)}) collective-permute-start(f32[32,512]{1,0:T(8,128)S(1)} %apply_first.3.refs_0_), channel_id=1, source_target_pairs={{2,0},{3,1},{0,2},{1,3},{6,4},{7,5},{4,6},{5,7},{10,8},{11,9},{8,1... | collective-permute-start | bytes 196616 | tf_op jit(solution)/shard_map/ppermute | solution.py:642
  17.6 7.9 %collective-permute-start.8 = (f32[32,512]{1,0:T(8,128)S(1)}, f32[32,512]{1,0:T(8,128)S(1)}, u32[]{:S(2)}, u32[]{:S(2)}) collective-permute-start(f32[32,512]{1,0:T(8,128)S(1)} %apply_first.3.refs_0_), channel_id=1, source_target_pairs={{1,0},{0,1},{3,2},{2,3},{5,4},{4,5},{7,6},{6,7},{9,8},{8,9},{11,10... | collective-permute-start | bytes 196616 | tf_op jit(solution)/shard_map/ppermute | solution.py:642
  21.0 7.5 %collective-permute-start.3 = (f32[32,512]{1,0:T(8,128)S(1)}, f32[32,512]{1,0:T(8,128)S(1)}, u32[]{:S(2)}, u32[]{:S(2)}) collective-permute-start(f32[32,512]{1,0:T(8,128)S(1)} %apply_first.2.refs_0_), channel_id=1, source_target_pairs={{3,0},{2,1},{1,2},{0,3},{7,4},{6,5},{5,6},{4,7},{11,8},{10,9},{9,1... | collective-permute-start | bytes 196616 | tf_op jit(solution)/shard_map/ppermute | solution.py:642
  23.5 6.1 %collective-permute-start.4 = (f32[32,512]{1,0:T(8,128)S(1)}, f32[32,512]{1,0:T(8,128)S(1)}, u32[]{:S(2)}, u32[]{:S(2)}) collective-permute-start(f32[32,512]{1,0:T(8,128)S(1)} %apply_first.2.refs_0_), channel_id=1, source_target_pairs={{2,0},{3,1},{0,2},{1,3},{6,4},{7,5},{4,6},{5,7},{10,8},{11,9},{8,1... | collective-permute-start | bytes 196616 | tf_op jit(solution)/shard_map/ppermute | solution.py:642
  23.5 6.1 %collective-permute-start.5 = (f32[32,512]{1,0:T(8,128)S(1)}, f32[32,512]{1,0:T(8,128)S(1)}, u32[]{:S(2)}, u32[]{:S(2)}) collective-permute-start(f32[32,512]{1,0:T(8,128)S(1)} %apply_first.2.refs_0_), channel_id=1, source_target_pairs={{1,0},{0,1},{3,2},{2,3},{5,4},{4,5},{7,6},{6,7},{9,8},{8,9},{11,10... | collective-permute-start | bytes 196616 | tf_op jit(solution)/shard_map/ppermute | solution.py:642
  40.6 7.0 %collective-permute-start.10 = (f32[144,128]{1,0:T(8,128)S(1)}, f32[144,128]{1,0:T(8,128)S(1)}, u32[]{:S(2)}, u32[]{:S(2)}) collective-permute-start(f32[144,128]{1,0:T(8,128)S(1)} %cross_gram.1), channel_id=1, source_target_pairs={{3,0},{2,1},{1,2},{0,3},{7,4},{6,5},{5,6},{4,7},{11,8},{10,9},{9,1... | collective-permute-start | bytes 221192 | tf_op jit(solution)/shard_map/ppermute | solution.py:642
  42.6 7.5 %collective-permute-start.11 = (f32[144,128]{1,0:T(8,128)S(1)}, f32[144,128]{1,0:T(8,128)S(1)}, u32[]{:S(2)}, u32[]{:S(2)}) collective-permute-start(f32[144,128]{1,0:T(8,128)S(1)} %cross_gram.1), channel_id=1, source_target_pairs={{2,0},{3,1},{0,2},{1,3},{6,4},{7,5},{4,6},{5,7},{10,8},{11,9},{8,1... | collective-permute-start | bytes 221192 | tf_op jit(solution)/shard_map/ppermute | solution.py:642
  42.6 7.5 %collective-permute-start.9 = (f32[144,128]{1,0:T(8,128)S(1)}, f32[144,128]{1,0:T(8,128)S(1)}, u32[]{:S(2)}, u32[]{:S(2)}) collective-permute-start(f32[144,128]{1,0:T(8,128)S(1)} %cross_gram.1), channel_id=1, source_target_pairs={{1,0},{0,1},{3,2},{2,3},{5,4},{4,5},{7,6},{6,7},{9,8},{8,9},{11,10... | collective-permute-start | bytes 221192 | tf_op jit(solution)/shard_map/ppermute | solution.py:642
  50.2 1.3 %collective-permute-start.12 = (f32[144,128]{1,0:T(8,128)S(1)}, f32[144,128]{1,0:T(8,128)S(1)}, u32[]{:S(2)}, u32[]{:S(2)}) collective-permute-start(f32[144,128]{1,0:T(8,128)S(1)} %add_add_fusion.refs_0_), channel_id=1, source_target_pairs={{4,0},{0,4},{12,8},{8,12},{5,1},{1,5},{13,9},{9,13},{6,2},{2,6},{1... | collective-permute-start | bytes 221192 | tf_op jit(solution)/shard_map/ppermute | solution.py:642
  59.4 6.8 %collective-permute-start.13 = (bf16[2,32,512]{2,1,0:T(8,128)(2,1)S(1)}, bf16[2,32,512]{2,1,0:T(8,128)(2,1)S(1)}, u32[]{:S(2)}, u32[]{:S(2)}) collective-permute-start(bf16[2,32,512]{2,1,0:T(8,128)(2,1)S(1)} %get-tuple-element.12.basis_ref), channel_id=1, source_target_pairs={{3,0},{2,1},{1,2},{0,3},{7,4},{6,5},{5,6},{4,7},{11,8},{10,9},{9,1... | collective-permute-start | bytes 196616 | tf_op jit(solution)/shard_map/ppermute | solution.py:642
  61.3 6.8 %collective-permute-start.14 = (bf16[2,32,512]{2,1,0:T(8,128)(2,1)S(1)}, bf16[2,32,512]{2,1,0:T(8,128)(2,1)S(1)}, u32[]{:S(2)}, u32[]{:S(2)}) collective-permute-start(bf16[2,32,512]{2,1,0:T(8,128)(2,1)S(1)} %get-tuple-element.12.basis_ref), channel_id=1, source_target_pairs={{2,0},{3,1},{0,2},{1,3},{6,4},{7,5},{4,6},{5,7},{10,8},{11,9},{8,1... | collective-permute-start | bytes 196616 | tf_op jit(solution)/shard_map/ppermute | solution.py:642
  61.3 6.8 %collective-permute-start.15 = (bf16[2,32,512]{2,1,0:T(8,128)(2,1)S(1)}, bf16[2,32,512]{2,1,0:T(8,128)(2,1)S(1)}, u32[]{:S(2)}, u32[]{:S(2)}) collective-permute-start(bf16[2,32,512]{2,1,0:T(8,128)(2,1)S(1)} %get-tuple-element.12.basis_ref), channel_id=1, source_target_pairs={{1,0},{0,1},{3,2},{2,3},{5,4},{4,5},{7,6},{6,7},{9,8},{8,9},{11,10... | collective-permute-start | bytes 196616 | tf_op jit(solution)/shard_map/ppermute | solution.py:642
  69.8 5.8 %collective-permute-start.17 = (f32[2,32,32]{2,1,0:T(8,128)S(1)}, f32[2,32,32]{2,1,0:T(8,128)S(1)}, u32[]{:S(2)}, u32[]{:S(2)}) collective-permute-start(f32[2,32,32]{2,1,0:T(8,128)S(1)} %apply_score.1), channel_id=1, source_target_pairs={{3,0},{2,1},{1,2},{0,3},{7,4},{6,5},{5,6},{4,7},{11,8},{10,9},{9,1... | collective-permute-start | bytes 24584 | tf_op jit(solution)/shard_map/ppermute | solution.py:642
  71.7 4.8 %collective-permute-start.18 = (f32[2,32,32]{2,1,0:T(8,128)S(1)}, f32[2,32,32]{2,1,0:T(8,128)S(1)}, u32[]{:S(2)}, u32[]{:S(2)}) collective-permute-start(f32[2,32,32]{2,1,0:T(8,128)S(1)} %apply_score.1), channel_id=1, source_target_pairs={{2,0},{3,1},{0,2},{1,3},{6,4},{7,5},{4,6},{5,7},{10,8},{11,9},{8,1... | collective-permute-start | bytes 24584 | tf_op jit(solution)/shard_map/ppermute | solution.py:642
  71.7 4.8 %collective-permute-start.16 = (f32[2,32,32]{2,1,0:T(8,128)S(1)}, f32[2,32,32]{2,1,0:T(8,128)S(1)}, u32[]{:S(2)}, u32[]{:S(2)}) collective-permute-start(f32[2,32,32]{2,1,0:T(8,128)S(1)} %apply_score.1), channel_id=1, source_target_pairs={{1,0},{0,1},{3,2},{2,3},{5,4},{4,5},{7,6},{6,7},{9,8},{8,9},{11,10... | collective-permute-start | bytes 24584 | tf_op jit(solution)/shard_map/ppermute | solution.py:642

commit v17 on v16

--- a/solution.py
+++ b/solution.py
@@ -20,6 +20,7 @@
 TRANS_B = (((1,), (1,)), ((), ()))
 TRANS_A = (((0,), (0,)), ((), ()))
 SPREAD = (2, 88, 128)
+TAIL = 16
 
 
 def params(mib):
@@ -537,56 +538,55 @@
     )(gram, image)
 
 
-def cross_kernel(k, images_ref, out_ref, packed):
+def cross_kernel(images_ref, out_ref, packed):
     g = lax.axis_index("layer")
     every = images_ref[...].reshape(-1, images_ref.shape[2])
     gram = split_dot(every, every, TRANS_B)
     half = gram.shape[0] // 2
     first, last = gram[:half, :half], gram[half:, half:]
-    row = lax.broadcasted_iota(jnp.int32, (half, half), 0) // k
-    col = lax.broadcasted_iota(jnp.int32, (half, half), 1) // k
+    row = lax.broadcasted_iota(jnp.int32, (half, half), 0)
+    col = lax.broadcasted_iota(jnp.int32, (half, half), 1)
     packed[:half] = gram[:half, half:]
     packed[half : 2 * half] = jnp.where(col >= row, first, last)
-    diagonal = jnp.where(col == row, last, 0.0)
-    packed[2 * half :] = sum(diagonal[r * k : r * k + k] for r in range(half // k))
+    diagonal = jnp.sum(jnp.where(col == row, last, 0.0), axis=0, keepdims=True)
+    packed[2 * half :] = jnp.broadcast_to(diagonal, (TAIL, half))
     rows = out_ref.shape[0]
-    out_ref[...] = packed[pl.ds(pl.multiple_of((g & 1) * rows, 16), rows)]
+    out_ref[...] = packed[pl.ds(pl.multiple_of((g & 1) * rows, 8), rows)]
 
 
 def cross(images):
     layers, k, _ = images.shape
     size = layers * k
     return pl.pallas_call(
-        functools.partial(cross_kernel, k),
+        cross_kernel,
         in_specs=vmem_specs(1),
         out_specs=pl.BlockSpec(memory_space=pltpu.VMEM),
-        out_shape=jax.ShapeDtypeStruct(((size + k) // 2, size // 2), F32),
-        scratch_shapes=[pltpu.VMEM((size + k, size // 2), F32)],
+        out_shape=jax.ShapeDtypeStruct(((size + TAIL) // 2, size // 2), F32),
+        scratch_shapes=[pltpu.VMEM((size + TAIL, size // 2), F32)],
         compiler_params=params(6),
         name="cross_gram",
     )(images)
 
 
-def unpack(packed, k, work):
+def unpack(packed, work):
     half = packed.shape[1]
-    row = lax.broadcasted_iota(jnp.int32, (half, half), 0) // k
-    col = lax.broadcasted_iota(jnp.int32, (half, half), 1) // k
+    row = lax.broadcasted_iota(jnp.int32, (half, half), 0)
+    col = lax.broadcasted_iota(jnp.int32, (half, half), 1)
     mixed = packed[half : 2 * half]
-    under = jnp.where(col < row, mixed, 0.0)
-    diagonal = jnp.concatenate([packed[2 * half :]] * (half // k), axis=0)
-    work[:half, :half] = jnp.where(col >= row, mixed, 0.0)
+    over, under = jnp.where(col > row, mixed, 0.0), jnp.where(col < row, mixed, 0.0)
+    work[:half, :half] = jnp.where(col >= row, mixed, over.T)
     work[:half, half:] = packed[:half]
     work[half:, :half] = jnp.zeros((half, half), F32)
-    work[half:, half:] = under.T + jnp.where(col == row, diagonal, 0.0)
+    work[half:, half:] = under + under.T + jnp.where(col == row, packed[2 * half : 2 * half + 1], 0.0)
 
 
 def joint_kernel(k, *refs):
     own_ref, other_ref, images_ref, out_ref, again_ref, rounded_ref, work, packed, scratch = refs
     rows = own_ref.shape[0]
     odd = lax.axis_index("layer") & 1
-    packed[pl.ds(pl.multiple_of(odd * rows, 16), rows)] = own_ref[...]
-    packed[pl.ds(pl.multiple_of((1 - odd) * rows, 16), rows)] = other_ref[...]
-    unpack(packed[...], k, work)
+    packed[pl.ds(pl.multiple_of(odd * rows, 8), rows)] = own_ref[...]
+    packed[pl.ds(pl.multiple_of((1 - odd) * rows, 8), rows)] = other_ref[...]
+    unpack(packed[...], work)
     size = work.shape[0]
     steps = size // k
     lane = lax.broadcasted_iota(jnp.int32, (k, size), 1)
@@ -630,7 +630,7 @@
         ],
         scratch_shapes=[
             pltpu.VMEM((size, size), F32),
-            pltpu.VMEM((size + k, size // 2), F32),
+            pltpu.VMEM((size + TAIL, size // 2), F32),
             pltpu.VMEM((2, *SPREAD), F32),
         ],
         compiler_params=params(8),

time: 77.3 us -> 77.1 us (level)
  no operation moved by 1% of the time
where the time goes in v17:
time: 77.1 us; the launch traced here: 77 us
  starting transfers between devices  27.9 us (36%)
  Pallas kernels  26.3 us (34%)
  waiting for transfers between devices  13.1 us (17%)
  blocking collectives  7.37 us (10%)
  other arithmetic  1.56 us (2%)
    ppermute x19, starting transfers between devices, swap(): return lax.ppermute(x, axis, [(m ^ d, m) for m in range(count)])  27.9 us
    ppermute x19, waiting for transfers between devices, swap(): return lax.ppermute(x, axis, [(m ^ d, m) for m in range(count)])  13.1 us
    pallas_call x4, Pallas kernels, apply_whole(): pl.pallas_call(kernel, in_specs=vmem_specs(len(operands)), out_specs=pl.B...  9.07 us
    pallas_call x1, Pallas kernels, joint_solve(): pl.pallas_call(functools.partial(joint_kernel, k), in_specs=vmem_specs(3)...  7.87 us
    all_gather x1, blocking collectives, per_device(): images = lax.all_gather(image, 'layer', axis=0, tiled=True)  7.37 us
    pallas_call x1, Pallas kernels, build_whole(): pl.pallas_call(build_whole_kernel, in_specs=[pl.BlockSpec(memory_space=pl...  5.44 us
    pallas_call x1, Pallas kernels, apply_score(): pl.pallas_call(functools.partial(score_kernel, len(dense), ORDER[2:]), in...  1.64 us
  transfers between devices with their start and end apart: 19, of which 9 were waited for; matrix products, arithmetic and copies ran while one was open for 0% of the time, Pallas kernels for 15%

profile of v17, /device:TPU:0, one launch (start us, length us, event | category | flops | bytes accessed | tf_op | source)
XLA Modules:
  0.0 77.0 jit_solution(7613479025474605471)
XLA Ops:
  1.5 3.1 %collective-permute-start = (bf16[2,32,512]{2,1,0:T(8,128)(2,1)S(1)}, bf16[2,32,512]{2,1,0:T(8,128)(2,1)S(1)}, u32[]{:S(2)}, u32[]{:S(2)}) collective-permute-start(bf16[2,32,512]{2,1,0:T(8,128)(2,1)S(1)} %convert_element_type.3.refs_0_), channel_id=1, source_target_pairs={{1,0},{0,1},{3,2},{2,3},{5,4},{4,5},{7,6},{6,7},{9,8},{8,9},{11,10... | collective-permute-start | bytes 196616 | tf_op jit(solution)/shard_map/ppermute | solution.py:642
  4.6 2.5 %collective-permute-start.1 = (bf16[2,32,512]{2,1,0:T(8,128)(2,1)S(1)}, bf16[2,32,512]{2,1,0:T(8,128)(2,1)S(1)}, u32[]{:S(2)}, u32[]{:S(2)}) collective-permute-start(bf16[2,32,512]{2,1,0:T(8,128)(2,1)S(1)} %convert_element_type.3.refs_0_), channel_id=1, source_target_pairs={{3,0},{2,1},{1,2},{0,3},{7,4},{6,5},{5,6},{4,7},{11,8},{10,9},{9,1... | collective-permute-start | bytes 196616 | tf_op jit(solution)/shard_map/ppermute | solution.py:642
  7.2 5.4 %build_whole.1 = (bf16[4,512,1024]{2,1,0:T(8,128)(2,1)S(1)}, bf16[4,512,1024]{2,1,0:T(8,128)(2,1)S(1)}) custom-call(s32[2,512]{1,0:T(2,128)} %rows_hbm.1, s32[2,512]{1,0:T(2,128)} %cols_hbm.1, s32[1,2]{1,0:T(1,128)} %bitcast.1, bf16[2,512,4096]{2,1,0:T(8,128)(2,1)} %blocks_ref.1), custom_call_target="tpu_custom_call" | custom-call | bytes 20971520 | tf_op jit(solution)/shard_map/build_whole/pallas_call | solution.py:126
  13.6 1.5 %apply_first.3.refs_0_ = f32[32,512]{1,0:T(8,128)S(1)} custom-call(bf16[2,32,512]{2,1,0:T(8,128)(2,1)S(1)} %convert_element_type.3.refs_0_, bf16[2,32,512]{2,1,0:T(8,128)(2,1)S(1)} %collective-permute-done.refs_1_, bf16[2,32,512]{2,1,0:T(8,128)(2,1)S(1)} %collective-permute-done.1.refs_2_, bf16[2,32,512]{2,1,0:T(8,128)(2,1)S(1)} %collective-permute-done.2.refs_3_, ...), custom_call_target="tpu_custom_call" | custom-call | bytes 4194304 | tf_op jit(solution)/shard_map/apply_first/pallas_call | solution.py:315
  15.1 2.5 %collective-permute-start.6 = (f32[32,512]{1,0:T(8,128)S(1)}, f32[32,512]{1,0:T(8,128)S(1)}, u32[]{:S(2)}, u32[]{:S(2)}) collective-permute-start(f32[32,512]{1,0:T(8,128)S(1)} %apply_first.3.refs_0_), channel_id=1, source_target_pairs={{3,0},{2,1},{1,2},{0,3},{7,4},{6,5},{5,6},{4,7},{11,8},{10,9},{9,1... | collective-permute-start | bytes 196616 | tf_op jit(solution)/shard_map/ppermute | solution.py:642
  17.6 2.0 %collective-permute-start.8 = (f32[32,512]{1,0:T(8,128)S(1)}, f32[32,512]{1,0:T(8,128)S(1)}, u32[]{:S(2)}, u32[]{:S(2)}) collective-permute-start(f32[32,512]{1,0:T(8,128)S(1)} %apply_first.3.refs_0_), channel_id=1, source_target_pairs={{1,0},{0,1},{3,2},{2,3},{5,4},{4,5},{7,6},{6,7},{9,8},{8,9},{11,10... | collective-permute-start | bytes 196616 | tf_op jit(solution)/shard_map/ppermute | solution.py:642
  19.5 1.5 %apply_first.2.refs_0_ = f32[32,512]{1,0:T(8,128)S(1)} custom-call(bf16[2,32,512]{2,1,0:T(8,128)(2,1)S(1)} %convert_element_type.3.refs_0_, bf16[2,32,512]{2,1,0:T(8,128)(2,1)S(1)} %collective-permute-done.refs_1_, bf16[2,32,512]{2,1,0:T(8,128)(2,1)S(1)} %collective-permute-done.1.refs_2_, bf16[2,32,512]{2,1,0:T(8,128)(2,1)S(1)} %collective-permute-done.2.refs_3_, ...), custom_call_target="tpu_custom_call" | custom-call | bytes 4194304 | tf_op jit(solution)/shard_map/apply_first/pallas_call | solution.py:315
  21.0 2.5 %collective-permute-start.3 = (f32[32,512]{1,0:T(8,128)S(1)}, f32[32,512]{1,0:T(8,128)S(1)}, u32[]{:S(2)}, u32[]{:S(2)}) collective-permute-start(f32[32,512]{1,0:T(8,128)S(1)} %apply_first.2.refs_0_), channel_id=1, source_target_pairs={{3,0},{2,1},{1,2},{0,3},{7,4},{6,5},{5,6},{4,7},{11,8},{10,9},{9,1... | collective-permute-start | bytes 196616 | tf_op jit(solution)/shard_map/ppermute | solution.py:642
  23.5 2.0 %collective-permute-start.5 = (f32[32,512]{1,0:T(8,128)S(1)}, f32[32,512]{1,0:T(8,128)S(1)}, u32[]{:S(2)}, u32[]{:S(2)}) collective-permute-start(f32[32,512]{1,0:T(8,128)S(1)} %apply_first.2.refs_0_), channel_id=1, source_target_pairs={{1,0},{0,1},{3,2},{2,3},{5,4},{4,5},{7,6},{6,7},{9,8},{8,9},{11,10... | collective-permute-start | bytes 196616 | tf_op jit(solution)/shard_map/ppermute | solution.py:642
  25.5 3.0 %apply_second.2.refs_5_ = f32[1,32,512]{2,1,0:T(8,128)S(1)} custom-call(f32[32,512]{1,0:T(8,128)S(1)} %apply_first.3.refs_0_, f32[32,512]{1,0:T(8,128)S(1)} %collective-permute-done.6.refs_1_, f32[32,512]{1,0:T(8,128)S(1)} %collective-permute-done.7.refs_2_, f32[32,512]{1,0:T(8,128)S(1)} %collective-permute-done.8.refs_3_, ...), custom_call_target="tpu_custom_call" | custom-call | bytes 4194304 | tf_op jit(solution)/shard_map/apply_second/pallas_call | solution.py:315
  29.6 3.0 %apply_second.3 = f32[2,32,512]{2,1,0:T(8,128)S(1)} custom-call(f32[32,512]{1,0:T(8,128)S(1)} %apply_first.2.refs_0_, f32[32,512]{1,0:T(8,128)S(1)} %collective-permute-done.3.refs_1_, f32[32,512]{1,0:T(8,128)S(1)} %collective-permute-done.4.refs_2_, f32[32,512]{1,0:T(8,128)S(1)} %collective-permute-done.5.refs_3_, ...), custom_call_target="tpu_custom_call" | custom-call | bytes 4194304 | tf_op jit(solution)/shard_map/apply_second/pallas_call | solution.py:315
  32.6 7.4 %all_gather.3.images_ref.refs_2_ = f32[8,32,512]{2,1,0:T(8,128)S(1)} all-gather(f32[2,32,512]{2,1,0:T(8,128)S(1)} %apply_second.3), channel_id=1, replica_groups=mesh['parts'=2,'layer'=4,'node'=4] {'layer'}, dimensions={0}, use_global_device_ids=true | all-gather | bytes 655360 | tf_op jit(solution)/shard_map/all_gather | solution.py:681
  40.7 2.0 %collective-permute-start.10 = (f32[136,128]{1,0:T(8,128)S(1)}, f32[136,128]{1,0:T(8,128)S(1)}, u32[]{:S(2)}, u32[]{:S(2)}) collective-permute-start(f32[136,128]{1,0:T(8,128)S(1)} %cross_gram.1), channel_id=1, source_target_pairs={{3,0},{2,1},{1,2},{0,3},{7,4},{6,5},{5,6},{4,7},{11,8},{10,9},{9,1... | collective-permute-start | bytes 208904 | tf_op jit(solution)/shard_map/ppermute | solution.py:642
  42.6 2.5 %collective-permute-start.9 = (f32[136,128]{1,0:T(8,128)S(1)}, f32[136,128]{1,0:T(8,128)S(1)}, u32[]{:S(2)}, u32[]{:S(2)}) collective-permute-start(f32[136,128]{1,0:T(8,128)S(1)} %cross_gram.1), channel_id=1, source_target_pairs={{1,0},{0,1},{3,2},{2,3},{5,4},{4,5},{7,6},{6,7},{9,8},{8,9},{11,10... | collective-permute-start | bytes 208904 | tf_op jit(solution)/shard_map/ppermute | solution.py:642
  45.1 2.5 %collective-permute-done.10 = f32[136,128]{1,0:T(8,128)S(1)} collective-permute-done((f32[136,128]{1,0:T(8,128)S(1)}, f32[136,128]{1,0:T(8,128)S(1)}, u32[]{:S(2)}, u32[]{:S(2)}) %collective-permute-start.10) | collective-permute-done | bytes 69664 | tf_op jit(solution)/shard_map/ppermute | solution.py:642
  47.6 2.3 %collective-permute-done.11 = f32[136,128]{1,0:T(8,128)S(1)} collective-permute-done((f32[136,128]{1,0:T(8,128)S(1)}, f32[136,128]{1,0:T(8,128)S(1)}, u32[]{:S(2)}, u32[]{:S(2)}) %collective-permute-start.11) | collective-permute-done | bytes 69664 | tf_op jit(solution)/shard_map/ppermute | solution.py:642
  51.3 7.9 %joint_solve.1 = (f32[2,32,512]{2,1,0:T(8,128)}, f32[2,32,512]{2,1,0:T(8,128)S(1)}, bf16[2,32,512]{2,1,0:T(8,128)(2,1)S(1)}) custom-call(f32[136,128]{1,0:T(8,128)S(1)} %add_add_fusion.refs_0_, f32[136,128]{1,0:T(8,128)S(1)} %collective-permute-done.12.refs_1_, f32[8,32,512]{2,1,0:T(8,128)S(1)} %all_gather.3.images_ref.refs_2_), custom_call_target="tpu_custom_call" | custom-call | tf_op jit(solution)/shard_map/joint_solve/pallas_call | solution.py:622
  59.1 1.9 %collective-permute-start.13 = (bf16[2,32,512]{2,1,0:T(8,128)(2,1)S(1)}, bf16[2,32,512]{2,1,0:T(8,128)(2,1)S(1)}, u32[]{:S(2)}, u32[]{:S(2)}) collective-permute-start(bf16[2,32,512]{2,1,0:T(8,128)(2,1)S(1)} %get-tuple-element.12.basis_ref), channel_id=1, source_target_pairs={{3,0},{2,1},{1,2},{0,3},{7,4},{6,5},{5,6},{4,7},{11,8},{10,9},{9,1... | collective-permute-start | bytes 196616 | tf_op jit(solution)/shard_map/ppermute | solution.py:642
  61.1 2.5 %collective-permute-start.15 = (bf16[2,32,512]{2,1,0:T(8,128)(2,1)S(1)}, bf16[2,32,512]{2,1,0:T(8,128)(2,1)S(1)}, u32[]{:S(2)}, u32[]{:S(2)}) collective-permute-start(bf16[2,32,512]{2,1,0:T(8,128)(2,1)S(1)} %get-tuple-element.12.basis_ref), channel_id=1, source_target_pairs={{1,0},{0,1},{3,2},{2,3},{5,4},{4,5},{7,6},{6,7},{9,8},{8,9},{11,10... | collective-permute-start | bytes 196616 | tf_op jit(solution)/shard_map/ppermute | solution.py:642
  64.4 1.5 %collective-permute-done.13.basis_ref = bf16[2,32,512]{2,1,0:T(8,128)(2,1)S(1)} collective-permute-done((bf16[2,32,512]{2,1,0:T(8,128)(2,1)S(1)}, bf16[2,32,512]{2,1,0:T(8,128)(2,1)S(1)}, u32[]{:S(2)}, u32[]{:S(2)}) %collective-permute-start.13) | collective-permute-done | bytes 65568 | tf_op jit(solution)/shard_map/ppermute | solution.py:642
  67.9 1.6 %apply_score.1 = f32[2,32,32]{2,1,0:T(8,128)S(1)} custom-call(f32[2,512,64]{2,1,0:T(8,128)S(1)} %apply_some_3.1.so_far_ref, bf16[2,32,512]{2,1,0:T(8,128)(2,1)S(1)} %collective-permute-done.14.refs_0_, bf16[2,32,512]{2,1,0:T(8,128)(2,1)S(1)} %collective-permute-done.15.refs_1_, f32[2,64,256]{2,1,0:T(8,128)S(1)} %get-tuple-element.15.refs_2_, ...), custom_call_target="tpu_custom_call" | custom-call | bytes 2097152 | tf_op jit(solution)/shard_map/apply_score/pallas_call | solution.py:378
  69.6 2.0 %collective-permute-start.17 = (f32[2,32,32]{2,1,0:T(8,128)S(1)}, f32[2,32,32]{2,1,0:T(8,128)S(1)}, u32[]{:S(2)}, u32[]{:S(2)}) collective-permute-start(f32[2,32,32]{2,1,0:T(8,128)S(1)} %apply_score.1), channel_id=1, source_target_pairs={{3,0},{2,1},{1,2},{0,3},{7,4},{6,5},{5,6},{4,7},{11,8},{10,9},{9,1... | collective-permute-start | bytes 24584 | tf_op jit(solution)/shard_map/ppermute | solution.py:642
  71.5 2.5 %collective-permute-start.16 = (f32[2,32,32]{2,1,0:T(8,128)S(1)}, f32[2,32,32]{2,1,0:T(8,128)S(1)}, u32[]{:S(2)}, u32[]{:S(2)}) collective-permute-start(f32[2,32,32]{2,1,0:T(8,128)S(1)} %apply_score.1), channel_id=1, source_target_pairs={{1,0},{0,1},{3,2},{2,3},{5,4},{4,5},{7,6},{6,7},{9,8},{8,9},{11,10... | collective-permute-start | bytes 24584 | tf_op jit(solution)/shard_map/ppermute | solution.py:642
  74.0 1.4 %collective-permute-done.17 = f32[2,32,32]{2,1,0:T(8,128)S(1)} collective-permute-done((f32[2,32,32]{2,1,0:T(8,128)S(1)}, f32[2,32,32]{2,1,0:T(8,128)S(1)}, u32[]{:S(2)}, u32[]{:S(2)}) %collective-permute-start.17) | collective-permute-done | bytes 8224 | tf_op jit(solution)/shard_map/ppermute | solution.py:642
  (28 shorter events, 9.4 us)
Async XLA Ops:
  1.5 11.1 %collective-permute-start = (bf16[2,32,512]{2,1,0:T(8,128)(2,1)S(1)}, bf16[2,32,512]{2,1,0:T(8,128)(2,1)S(1)}, u32[]{:S(2)}, u32[]{:S(2)}) collective-permute-start(bf16[2,32,512]{2,1,0:T(8,128)(2,1)S(1)} %convert_element_type.3.refs_0_), channel_id=1, source_target_pairs={{1,0},{0,1},{3,2},{2,3},{5,4},{4,5},{7,6},{6,7},{9,8},{8,9},{11,10... | collective-permute-start | bytes 196616 | tf_op jit(solution)/shard_map/ppermute | solution.py:642
  4.6 8.1 %collective-permute-start.1 = (bf16[2,32,512]{2,1,0:T(8,128)(2,1)S(1)}, bf16[2,32,512]{2,1,0:T(8,128)(2,1)S(1)}, u32[]{:S(2)}, u32[]{:S(2)}) collective-permute-start(bf16[2,32,512]{2,1,0:T(8,128)(2,1)S(1)} %convert_element_type.3.refs_0_), channel_id=1, source_target_pairs={{3,0},{2,1},{1,2},{0,3},{7,4},{6,5},{5,6},{4,7},{11,8},{10,9},{9,1... | collective-permute-start | bytes 196616 | tf_op jit(solution)/shard_map/ppermute | solution.py:642
  7.1 6.4 %collective-permute-start.2 = (bf16[2,32,512]{2,1,0:T(8,128)(2,1)S(1)}, bf16[2,32,512]{2,1,0:T(8,128)(2,1)S(1)}, u32[]{:S(2)}, u32[]{:S(2)}) collective-permute-start(bf16[2,32,512]{2,1,0:T(8,128)(2,1)S(1)} %convert_element_type.3.refs_0_), channel_id=1, source_target_pairs={{2,0},{3,1},{0,2},{1,3},{6,4},{7,5},{4,6},{5,7},{10,8},{11,9},{8,1... | collective-permute-start | bytes 196616 | tf_op jit(solution)/shard_map/ppermute | solution.py:642
  15.1 8.4 %collective-permute-start.6 = (f32[32,512]{1,0:T(8,128)S(1)}, f32[32,512]{1,0:T(8,128)S(1)}, u32[]{:S(2)}, u32[]{:S(2)}) collective-permute-start(f32[32,512]{1,0:T(8,128)S(1)} %apply_first.3.refs_0_), channel_id=1, source_target_pairs={{3,0},{2,1},{1,2},{0,3},{7,4},{6,5},{5,6},{4,7},{11,8},{10,9},{9,1... | collective-permute-start | bytes 196616 | tf_op jit(solution)/shard_map/ppermute | solution.py:642
  17.6 7.9 %collective-permute-start.7 = (f32[32,512]{1,0:T(8,128)S(1)}, f32[32,512]{1,0:T(8,128)S(1)}, u32[]{:S(2)}, u32[]{:S(2)}) collective-permute-start(f32[32,512]{1,0:T(8,128)S(1)} %apply_first.3.refs_0_), channel_id=1, source_target_pairs={{2,0},{3,1},{0,2},{1,3},{6,4},{7,5},{4,6},{5,7},{10,8},{11,9},{8,1... | collective-permute-start | bytes 196616 | tf_op jit(solution)/shard_map/ppermute | solution.py:642
  17.6 7.9 %collective-permute-start.8 = (f32[32,512]{1,0:T(8,128)S(1)}, f32[32,512]{1,0:T(8,128)S(1)}, u32[]{:S(2)}, u32[]{:S(2)}) collective-permute-start(f32[32,512]{1,0:T(8,128)S(1)} %apply_first.3.refs_0_), channel_id=1, source_target_pairs={{1,0},{0,1},{3,2},{2,3},{5,4},{4,5},{7,6},{6,7},{9,8},{8,9},{11,10... | collective-permute-start | bytes 196616 | tf_op jit(solution)/shard_map/ppermute | solution.py:642
  21.0 7.5 %collective-permute-start.3 = (f32[32,512]{1,0:T(8,128)S(1)}, f32[32,512]{1,0:T(8,128)S(1)}, u32[]{:S(2)}, u32[]{:S(2)}) collective-permute-start(f32[32,512]{1,0:T(8,128)S(1)} %apply_first.2.refs_0_), channel_id=1, source_target_pairs={{3,0},{2,1},{1,2},{0,3},{7,4},{6,5},{5,6},{4,7},{11,8},{10,9},{9,1... | collective-permute-start | bytes 196616 | tf_op jit(solution)/shard_map/ppermute | solution.py:642
  23.5 6.1 %collective-permute-start.4 = (f32[32,512]{1,0:T(8,128)S(1)}, f32[32,512]{1,0:T(8,128)S(1)}, u32[]{:S(2)}, u32[]{:S(2)}) collective-permute-start(f32[32,512]{1,0:T(8,128)S(1)} %apply_first.2.refs_0_), channel_id=1, source_target_pairs={{2,0},{3,1},{0,2},{1,3},{6,4},{7,5},{4,6},{5,7},{10,8},{11,9},{8,1... | collective-permute-start | bytes 196616 | tf_op jit(solution)/shard_map/ppermute | solution.py:642
  23.5 6.1 %collective-permute-start.5 = (f32[32,512]{1,0:T(8,128)S(1)}, f32[32,512]{1,0:T(8,128)S(1)}, u32[]{:S(2)}, u32[]{:S(2)}) collective-permute-start(f32[32,512]{1,0:T(8,128)S(1)} %apply_first.2.refs_0_), channel_id=1, source_target_pairs={{1,0},{0,1},{3,2},{2,3},{5,4},{4,5},{7,6},{6,7},{9,8},{8,9},{11,10... | collective-permute-start | bytes 196616 | tf_op jit(solution)/shard_map/ppermute | solution.py:642
  40.7 7.0 %collective-permute-start.10 = (f32[136,128]{1,0:T(8,128)S(1)}, f32[136,128]{1,0:T(8,128)S(1)}, u32[]{:S(2)}, u32[]{:S(2)}) collective-permute-start(f32[136,128]{1,0:T(8,128)S(1)} %cross_gram.1), channel_id=1, source_target_pairs={{3,0},{2,1},{1,2},{0,3},{7,4},{6,5},{5,6},{4,7},{11,8},{10,9},{9,1... | collective-permute-start | bytes 208904 | tf_op jit(solution)/shard_map/ppermute | solution.py:642
  42.6 7.3 %collective-permute-start.11 = (f32[136,128]{1,0:T(8,128)S(1)}, f32[136,128]{1,0:T(8,128)S(1)}, u32[]{:S(2)}, u32[]{:S(2)}) collective-permute-start(f32[136,128]{1,0:T(8,128)S(1)} %cross_gram.1), channel_id=1, source_target_pairs={{2,0},{3,1},{0,2},{1,3},{6,4},{7,5},{4,6},{5,7},{10,8},{11,9},{8,1... | collective-permute-start | bytes 208904 | tf_op jit(solution)/shard_map/ppermute | solution.py:642
  42.6 7.3 %collective-permute-start.9 = (f32[136,128]{1,0:T(8,128)S(1)}, f32[136,128]{1,0:T(8,128)S(1)}, u32[]{:S(2)}, u32[]{:S(2)}) collective-permute-start(f32[136,128]{1,0:T(8,128)S(1)} %cross_gram.1), channel_id=1, source_target_pairs={{1,0},{0,1},{3,2},{2,3},{5,4},{4,5},{7,6},{6,7},{9,8},{8,9},{11,10... | collective-permute-start | bytes 208904 | tf_op jit(solution)/shard_map/ppermute | solution.py:642
  50.0 1.3 %collective-permute-start.12 = (f32[136,128]{1,0:T(8,128)S(1)}, f32[136,128]{1,0:T(8,128)S(1)}, u32[]{:S(2)}, u32[]{:S(2)}) collective-permute-start(f32[136,128]{1,0:T(8,128)S(1)} %add_add_fusion.refs_0_), channel_id=1, source_target_pairs={{4,0},{0,4},{12,8},{8,12},{5,1},{1,5},{13,9},{9,13},{6,2},{2,6},{1... | collective-permute-start | bytes 208904 | tf_op jit(solution)/shard_map/ppermute | solution.py:642
  59.1 6.8 %collective-permute-start.13 = (bf16[2,32,512]{2,1,0:T(8,128)(2,1)S(1)}, bf16[2,32,512]{2,1,0:T(8,128)(2,1)S(1)}, u32[]{:S(2)}, u32[]{:S(2)}) collective-permute-start(bf16[2,32,512]{2,1,0:T(8,128)(2,1)S(1)} %get-tuple-element.12.basis_ref), channel_id=1, source_target_pairs={{3,0},{2,1},{1,2},{0,3},{7,4},{6,5},{5,6},{4,7},{11,8},{10,9},{9,1... | collective-permute-start | bytes 196616 | tf_op jit(solution)/shard_map/ppermute | solution.py:642
  61.1 6.8 %collective-permute-start.14 = (bf16[2,32,512]{2,1,0:T(8,128)(2,1)S(1)}, bf16[2,32,512]{2,1,0:T(8,128)(2,1)S(1)}, u32[]{:S(2)}, u32[]{:S(2)}) collective-permute-start(bf16[2,32,512]{2,1,0:T(8,128)(2,1)S(1)} %get-tuple-element.12.basis_ref), channel_id=1, source_target_pairs={{2,0},{3,1},{0,2},{1,3},{6,4},{7,5},{4,6},{5,7},{10,8},{11,9},{8,1... | collective-permute-start | bytes 196616 | tf_op jit(solution)/shard_map/ppermute | solution.py:642
  61.1 6.8 %collective-permute-start.15 = (bf16[2,32,512]{2,1,0:T(8,128)(2,1)S(1)}, bf16[2,32,512]{2,1,0:T(8,128)(2,1)S(1)}, u32[]{:S(2)}, u32[]{:S(2)}) collective-permute-start(bf16[2,32,512]{2,1,0:T(8,128)(2,1)S(1)} %get-tuple-element.12.basis_ref), channel_id=1, source_target_pairs={{1,0},{0,1},{3,2},{2,3},{5,4},{4,5},{7,6},{6,7},{9,8},{8,9},{11,10... | collective-permute-start | bytes 196616 | tf_op jit(solution)/shard_map/ppermute | solution.py:642
  69.6 5.8 %collective-permute-start.17 = (f32[2,32,32]{2,1,0:T(8,128)S(1)}, f32[2,32,32]{2,1,0:T(8,128)S(1)}, u32[]{:S(2)}, u32[]{:S(2)}) collective-permute-start(f32[2,32,32]{2,1,0:T(8,128)S(1)} %apply_score.1), channel_id=1, source_target_pairs={{3,0},{2,1},{1,2},{0,3},{7,4},{6,5},{5,6},{4,7},{11,8},{10,9},{9,1... | collective-permute-start | bytes 24584 | tf_op jit(solution)/shard_map/ppermute | solution.py:642
  71.5 4.8 %collective-permute-start.18 = (f32[2,32,32]{2,1,0:T(8,128)S(1)}, f32[2,32,32]{2,1,0:T(8,128)S(1)}, u32[]{:S(2)}, u32[]{:S(2)}) collective-permute-start(f32[2,32,32]{2,1,0:T(8,128)S(1)} %apply_score.1), channel_id=1, source_target_pairs={{2,0},{3,1},{0,2},{1,3},{6,4},{7,5},{4,6},{5,7},{10,8},{11,9},{8,1... | collective-permute-start | bytes 24584 | tf_op jit(solution)/shard_map/ppermute | solution.py:642
  71.5 4.8 %collective-permute-start.16 = (f32[2,32,32]{2,1,0:T(8,128)S(1)}, f32[2,32,32]{2,1,0:T(8,128)S(1)}, u32[]{:S(2)}, u32[]{:S(2)}) collective-permute-start(f32[2,32,32]{2,1,0:T(8,128)S(1)} %apply_score.1), channel_id=1, source_target_pairs={{1,0},{0,1},{3,2},{2,3},{5,4},{4,5},{7,6},{6,7},{9,8},{8,9},{11,10... | collective-permute-start | bytes 24584 | tf_op jit(solution)/shard_map/ppermute | solution.py:642

commit v18 on v17

--- a/solution.py
+++ b/solution.py
@@ -97,8 +97,9 @@
     for copy in index_copies:
         copy.wait()
     flip = lax.axis_index("node") * CHUNK_COLS
-    for layer, dense_ref in enumerate(dense_refs):
-        onehot = one_hot(rows_ref, cols_ref, counts_ref, layer, flip, 0, dense_ref.shape[0] * CHUNK_COLS * BROWS)
+    positions = dense_refs[0].shape[0] * CHUNK_COLS * BROWS
+    onehots = [one_hot(rows_ref, cols_ref, counts_ref, layer, flip, 0, positions) for layer in range(layers)]
+    for layer, (dense_ref, onehot) in enumerate(zip(dense_refs, onehots)):
 
         def step(piece, carry):
             fetch(layer, piece).wait()

time: 77.1 us -> 77.1 us (level)
  no operation moved by 1% of the time
where the time goes in v18:
time: 77.1 us; the launch traced here: 77 us
  starting transfers between devices  27.9 us (36%)
  Pallas kernels  26.2 us (34%)
  waiting for transfers between devices  13.2 us (17%)
  blocking collectives  7.41 us (10%)
  other arithmetic  1.56 us (2%)
    ppermute x19, starting transfers between devices, swap(): return lax.ppermute(x, axis, [(m ^ d, m) for m in range(count)])  27.9 us
    ppermute x19, waiting for transfers between devices, swap(): return lax.ppermute(x, axis, [(m ^ d, m) for m in range(count)])  13.2 us
    pallas_call x4, Pallas kernels, apply_whole(): pl.pallas_call(kernel, in_specs=vmem_specs(len(operands)), out_specs=pl.B...  9.07 us
    pallas_call x1, Pallas kernels, joint_solve(): pl.pallas_call(functools.partial(joint_kernel, k), in_specs=vmem_specs(3)...  7.87 us
    all_gather x1, blocking collectives, per_device(): images = lax.all_gather(image, 'layer', axis=0, tiled=True)  7.41 us
    pallas_call x1, Pallas kernels, build_whole(): pl.pallas_call(build_whole_kernel, in_specs=[pl.BlockSpec(memory_space=pl...  5.36 us
    pallas_call x1, Pallas kernels, apply_score(): pl.pallas_call(functools.partial(score_kernel, len(dense), ORDER[2:]), in...  1.64 us
  transfers between devices with their start and end apart: 19, of which 9 were waited for; matrix products, arithmetic and copies ran while one was open for 0% of the time, Pallas kernels for 15%

profile of v18, /device:TPU:0, one launch (start us, length us, event | category | flops | bytes accessed | tf_op | source)
XLA Modules:
  0.0 77.0 jit_solution(13171737513117529792)
XLA Ops:
  1.5 3.1 %collective-permute-start = (bf16[2,32,512]{2,1,0:T(8,128)(2,1)S(1)}, bf16[2,32,512]{2,1,0:T(8,128)(2,1)S(1)}, u32[]{:S(2)}, u32[]{:S(2)}) collective-permute-start(bf16[2,32,512]{2,1,0:T(8,128)(2,1)S(1)} %convert_element_type.3.refs_0_), channel_id=1, source_target_pairs={{1,0},{0,1},{3,2},{2,3},{5,4},{4,5},{7,6},{6,7},{9,8},{8,9},{11,10... | collective-permute-start | bytes 196616 | tf_op jit(solution)/shard_map/ppermute | solution.py:643
  4.6 2.5 %collective-permute-start.1 = (bf16[2,32,512]{2,1,0:T(8,128)(2,1)S(1)}, bf16[2,32,512]{2,1,0:T(8,128)(2,1)S(1)}, u32[]{:S(2)}, u32[]{:S(2)}) collective-permute-start(bf16[2,32,512]{2,1,0:T(8,128)(2,1)S(1)} %convert_element_type.3.refs_0_), channel_id=1, source_target_pairs={{3,0},{2,1},{1,2},{0,3},{7,4},{6,5},{5,6},{4,7},{11,8},{10,9},{9,1... | collective-permute-start | bytes 196616 | tf_op jit(solution)/shard_map/ppermute | solution.py:643
  7.2 5.4 %build_whole.1 = (bf16[4,512,1024]{2,1,0:T(8,128)(2,1)S(1)}, bf16[4,512,1024]{2,1,0:T(8,128)(2,1)S(1)}) custom-call(s32[2,512]{1,0:T(2,128)} %rows_hbm.1, s32[2,512]{1,0:T(2,128)} %cols_hbm.1, s32[1,2]{1,0:T(1,128)} %bitcast.1, bf16[2,512,4096]{2,1,0:T(8,128)(2,1)} %blocks_ref.1), custom_call_target="tpu_custom_call" | custom-call | bytes 20971520 | tf_op jit(solution)/shard_map/build_whole/pallas_call | solution.py:127
  13.6 1.5 %apply_first.3.refs_0_ = f32[32,512]{1,0:T(8,128)S(1)} custom-call(bf16[2,32,512]{2,1,0:T(8,128)(2,1)S(1)} %convert_element_type.3.refs_0_, bf16[2,32,512]{2,1,0:T(8,128)(2,1)S(1)} %collective-permute-done.refs_1_, bf16[2,32,512]{2,1,0:T(8,128)(2,1)S(1)} %collective-permute-done.1.refs_2_, bf16[2,32,512]{2,1,0:T(8,128)(2,1)S(1)} %collective-permute-done.2.refs_3_, ...), custom_call_target="tpu_custom_call" | custom-call | bytes 4194304 | tf_op jit(solution)/shard_map/apply_first/pallas_call | solution.py:316
  15.1 2.5 %collective-permute-start.6 = (f32[32,512]{1,0:T(8,128)S(1)}, f32[32,512]{1,0:T(8,128)S(1)}, u32[]{:S(2)}, u32[]{:S(2)}) collective-permute-start(f32[32,512]{1,0:T(8,128)S(1)} %apply_first.3.refs_0_), channel_id=1, source_target_pairs={{3,0},{2,1},{1,2},{0,3},{7,4},{6,5},{5,6},{4,7},{11,8},{10,9},{9,1... | collective-permute-start | bytes 196616 | tf_op jit(solution)/shard_map/ppermute | solution.py:643
  17.6 2.0 %collective-permute-start.8 = (f32[32,512]{1,0:T(8,128)S(1)}, f32[32,512]{1,0:T(8,128)S(1)}, u32[]{:S(2)}, u32[]{:S(2)}) collective-permute-start(f32[32,512]{1,0:T(8,128)S(1)} %apply_first.3.refs_0_), channel_id=1, source_target_pairs={{1,0},{0,1},{3,2},{2,3},{5,4},{4,5},{7,6},{6,7},{9,8},{8,9},{11,10... | collective-permute-start | bytes 196616 | tf_op jit(solution)/shard_map/ppermute | solution.py:643
  19.5 1.5 %apply_first.2.refs_0_ = f32[32,512]{1,0:T(8,128)S(1)} custom-call(bf16[2,32,512]{2,1,0:T(8,128)(2,1)S(1)} %convert_element_type.3.refs_0_, bf16[2,32,512]{2,1,0:T(8,128)(2,1)S(1)} %collective-permute-done.refs_1_, bf16[2,32,512]{2,1,0:T(8,128)(2,1)S(1)} %collective-permute-done.1.refs_2_, bf16[2,32,512]{2,1,0:T(8,128)(2,1)S(1)} %collective-permute-done.2.refs_3_, ...), custom_call_target="tpu_custom_call" | custom-call | bytes 4194304 | tf_op jit(solution)/shard_map/apply_first/pallas_call | solution.py:316
  21.0 2.5 %collective-permute-start.3 = (f32[32,512]{1,0:T(8,128)S(1)}, f32[32,512]{1,0:T(8,128)S(1)}, u32[]{:S(2)}, u32[]{:S(2)}) collective-permute-start(f32[32,512]{1,0:T(8,128)S(1)} %apply_first.2.refs_0_), channel_id=1, source_target_pairs={{3,0},{2,1},{1,2},{0,3},{7,4},{6,5},{5,6},{4,7},{11,8},{10,9},{9,1... | collective-permute-start | bytes 196616 | tf_op jit(solution)/shard_map/ppermute | solution.py:643
  23.5 2.0 %collective-permute-start.5 = (f32[32,512]{1,0:T(8,128)S(1)}, f32[32,512]{1,0:T(8,128)S(1)}, u32[]{:S(2)}, u32[]{:S(2)}) collective-permute-start(f32[32,512]{1,0:T(8,128)S(1)} %apply_first.2.refs_0_), channel_id=1, source_target_pairs={{1,0},{0,1},{3,2},{2,3},{5,4},{4,5},{7,6},{6,7},{9,8},{8,9},{11,10... | collective-permute-start | bytes 196616 | tf_op jit(solution)/shard_map/ppermute | solution.py:643
  25.5 3.0 %apply_second.2.refs_5_ = f32[1,32,512]{2,1,0:T(8,128)S(1)} custom-call(f32[32,512]{1,0:T(8,128)S(1)} %apply_first.3.refs_0_, f32[32,512]{1,0:T(8,128)S(1)} %collective-permute-done.6.refs_1_, f32[32,512]{1,0:T(8,128)S(1)} %collective-permute-done.7.refs_2_, f32[32,512]{1,0:T(8,128)S(1)} %collective-permute-done.8.refs_3_, ...), custom_call_target="tpu_custom_call" | custom-call | bytes 4194304 | tf_op jit(solution)/shard_map/apply_second/pallas_call | solution.py:316
  29.5 3.0 %apply_second.3 = f32[2,32,512]{2,1,0:T(8,128)S(1)} custom-call(f32[32,512]{1,0:T(8,128)S(1)} %apply_first.2.refs_0_, f32[32,512]{1,0:T(8,128)S(1)} %collective-permute-done.3.refs_1_, f32[32,512]{1,0:T(8,128)S(1)} %collective-permute-done.4.refs_2_, f32[32,512]{1,0:T(8,128)S(1)} %collective-permute-done.5.refs_3_, ...), custom_call_target="tpu_custom_call" | custom-call | bytes 4194304 | tf_op jit(solution)/shard_map/apply_second/pallas_call | solution.py:316
  32.5 7.4 %all_gather.3.images_ref.refs_2_ = f32[8,32,512]{2,1,0:T(8,128)S(1)} all-gather(f32[2,32,512]{2,1,0:T(8,128)S(1)} %apply_second.3), channel_id=1, replica_groups=mesh['parts'=2,'layer'=4,'node'=4] {'layer'}, dimensions={0}, use_global_device_ids=true | all-gather | bytes 655360 | tf_op jit(solution)/shard_map/all_gather | solution.py:682
  40.6 2.1 %collective-permute-start.10 = (f32[136,128]{1,0:T(8,128)S(1)}, f32[136,128]{1,0:T(8,128)S(1)}, u32[]{:S(2)}, u32[]{:S(2)}) collective-permute-start(f32[136,128]{1,0:T(8,128)S(1)} %cross_gram.1), channel_id=1, source_target_pairs={{3,0},{2,1},{1,2},{0,3},{7,4},{6,5},{5,6},{4,7},{11,8},{10,9},{9,1... | collective-permute-start | bytes 208904 | tf_op jit(solution)/shard_map/ppermute | solution.py:643
  42.6 2.4 %collective-permute-start.9 = (f32[136,128]{1,0:T(8,128)S(1)}, f32[136,128]{1,0:T(8,128)S(1)}, u32[]{:S(2)}, u32[]{:S(2)}) collective-permute-start(f32[136,128]{1,0:T(8,128)S(1)} %cross_gram.1), channel_id=1, source_target_pairs={{1,0},{0,1},{3,2},{2,3},{5,4},{4,5},{7,6},{6,7},{9,8},{8,9},{11,10... | collective-permute-start | bytes 208904 | tf_op jit(solution)/shard_map/ppermute | solution.py:643
  45.0 2.5 %collective-permute-done.10 = f32[136,128]{1,0:T(8,128)S(1)} collective-permute-done((f32[136,128]{1,0:T(8,128)S(1)}, f32[136,128]{1,0:T(8,128)S(1)}, u32[]{:S(2)}, u32[]{:S(2)}) %collective-permute-start.10) | collective-permute-done | bytes 69664 | tf_op jit(solution)/shard_map/ppermute | solution.py:643
  47.5 2.3 %collective-permute-done.11 = f32[136,128]{1,0:T(8,128)S(1)} collective-permute-done((f32[136,128]{1,0:T(8,128)S(1)}, f32[136,128]{1,0:T(8,128)S(1)}, u32[]{:S(2)}, u32[]{:S(2)}) %collective-permute-start.11) | collective-permute-done | bytes 69664 | tf_op jit(solution)/shard_map/ppermute | solution.py:643
  51.2 7.9 %joint_solve.1 = (f32[2,32,512]{2,1,0:T(8,128)}, f32[2,32,512]{2,1,0:T(8,128)S(1)}, bf16[2,32,512]{2,1,0:T(8,128)(2,1)S(1)}) custom-call(f32[136,128]{1,0:T(8,128)S(1)} %add_add_fusion.refs_0_, f32[136,128]{1,0:T(8,128)S(1)} %collective-permute-done.12.refs_1_, f32[8,32,512]{2,1,0:T(8,128)S(1)} %all_gather.3.images_ref.refs_2_), custom_call_target="tpu_custom_call" | custom-call | tf_op jit(solution)/shard_map/joint_solve/pallas_call | solution.py:623
  59.1 2.0 %collective-permute-start.13 = (bf16[2,32,512]{2,1,0:T(8,128)(2,1)S(1)}, bf16[2,32,512]{2,1,0:T(8,128)(2,1)S(1)}, u32[]{:S(2)}, u32[]{:S(2)}) collective-permute-start(bf16[2,32,512]{2,1,0:T(8,128)(2,1)S(1)} %get-tuple-element.12.basis_ref), channel_id=1, source_target_pairs={{3,0},{2,1},{1,2},{0,3},{7,4},{6,5},{5,6},{4,7},{11,8},{10,9},{9,1... | collective-permute-start | bytes 196616 | tf_op jit(solution)/shard_map/ppermute | solution.py:643
  61.1 2.4 %collective-permute-start.15 = (bf16[2,32,512]{2,1,0:T(8,128)(2,1)S(1)}, bf16[2,32,512]{2,1,0:T(8,128)(2,1)S(1)}, u32[]{:S(2)}, u32[]{:S(2)}) collective-permute-start(bf16[2,32,512]{2,1,0:T(8,128)(2,1)S(1)} %get-tuple-element.12.basis_ref), channel_id=1, source_target_pairs={{1,0},{0,1},{3,2},{2,3},{5,4},{4,5},{7,6},{6,7},{9,8},{8,9},{11,10... | collective-permute-start | bytes 196616 | tf_op jit(solution)/shard_map/ppermute | solution.py:643
  64.3 1.5 %collective-permute-done.13.basis_ref = bf16[2,32,512]{2,1,0:T(8,128)(2,1)S(1)} collective-permute-done((bf16[2,32,512]{2,1,0:T(8,128)(2,1)S(1)}, bf16[2,32,512]{2,1,0:T(8,128)(2,1)S(1)}, u32[]{:S(2)}, u32[]{:S(2)}) %collective-permute-start.13) | collective-permute-done | bytes 65568 | tf_op jit(solution)/shard_map/ppermute | solution.py:643
  67.8 1.6 %apply_score.1 = f32[2,32,32]{2,1,0:T(8,128)S(1)} custom-call(f32[2,512,64]{2,1,0:T(8,128)S(1)} %apply_some_3.1.so_far_ref, bf16[2,32,512]{2,1,0:T(8,128)(2,1)S(1)} %collective-permute-done.14.refs_0_, bf16[2,32,512]{2,1,0:T(8,128)(2,1)S(1)} %collective-permute-done.15.refs_1_, f32[2,64,256]{2,1,0:T(8,128)S(1)} %get-tuple-element.15.refs_2_, ...), custom_call_target="tpu_custom_call" | custom-call | bytes 2097152 | tf_op jit(solution)/shard_map/apply_score/pallas_call | solution.py:379
  69.5 2.0 %collective-permute-start.17 = (f32[2,32,32]{2,1,0:T(8,128)S(1)}, f32[2,32,32]{2,1,0:T(8,128)S(1)}, u32[]{:S(2)}, u32[]{:S(2)}) collective-permute-start(f32[2,32,32]{2,1,0:T(8,128)S(1)} %apply_score.1), channel_id=1, source_target_pairs={{3,0},{2,1},{1,2},{0,3},{7,4},{6,5},{5,6},{4,7},{11,8},{10,9},{9,1... | collective-permute-start | bytes 24584 | tf_op jit(solution)/shard_map/ppermute | solution.py:643
  71.5 2.4 %collective-permute-start.16 = (f32[2,32,32]{2,1,0:T(8,128)S(1)}, f32[2,32,32]{2,1,0:T(8,128)S(1)}, u32[]{:S(2)}, u32[]{:S(2)}) collective-permute-start(f32[2,32,32]{2,1,0:T(8,128)S(1)} %apply_score.1), channel_id=1, source_target_pairs={{1,0},{0,1},{3,2},{2,3},{5,4},{4,5},{7,6},{6,7},{9,8},{8,9},{11,10... | collective-permute-start | bytes 24584 | tf_op jit(solution)/shard_map/ppermute | solution.py:643
  73.9 1.4 %collective-permute-done.17 = f32[2,32,32]{2,1,0:T(8,128)S(1)} collective-permute-done((f32[2,32,32]{2,1,0:T(8,128)S(1)}, f32[2,32,32]{2,1,0:T(8,128)S(1)}, u32[]{:S(2)}, u32[]{:S(2)}) %collective-permute-start.17) | collective-permute-done | bytes 8224 | tf_op jit(solution)/shard_map/ppermute | solution.py:643
  (28 shorter events, 9.4 us)
Async XLA Ops:
  1.5 11.0 %collective-permute-start = (bf16[2,32,512]{2,1,0:T(8,128)(2,1)S(1)}, bf16[2,32,512]{2,1,0:T(8,128)(2,1)S(1)}, u32[]{:S(2)}, u32[]{:S(2)}) collective-permute-start(bf16[2,32,512]{2,1,0:T(8,128)(2,1)S(1)} %convert_element_type.3.refs_0_), channel_id=1, source_target_pairs={{1,0},{0,1},{3,2},{2,3},{5,4},{4,5},{7,6},{6,7},{9,8},{8,9},{11,10... | collective-permute-start | bytes 196616 | tf_op jit(solution)/shard_map/ppermute | solution.py:643
  4.6 8.0 %collective-permute-start.1 = (bf16[2,32,512]{2,1,0:T(8,128)(2,1)S(1)}, bf16[2,32,512]{2,1,0:T(8,128)(2,1)S(1)}, u32[]{:S(2)}, u32[]{:S(2)}) collective-permute-start(bf16[2,32,512]{2,1,0:T(8,128)(2,1)S(1)} %convert_element_type.3.refs_0_), channel_id=1, source_target_pairs={{3,0},{2,1},{1,2},{0,3},{7,4},{6,5},{5,6},{4,7},{11,8},{10,9},{9,1... | collective-permute-start | bytes 196616 | tf_op jit(solution)/shard_map/ppermute | solution.py:643
  7.1 6.4 %collective-permute-start.2 = (bf16[2,32,512]{2,1,0:T(8,128)(2,1)S(1)}, bf16[2,32,512]{2,1,0:T(8,128)(2,1)S(1)}, u32[]{:S(2)}, u32[]{:S(2)}) collective-permute-start(bf16[2,32,512]{2,1,0:T(8,128)(2,1)S(1)} %convert_element_type.3.refs_0_), channel_id=1, source_target_pairs={{2,0},{3,1},{0,2},{1,3},{6,4},{7,5},{4,6},{5,7},{10,8},{11,9},{8,1... | collective-permute-start | bytes 196616 | tf_op jit(solution)/shard_map/ppermute | solution.py:643
  15.1 8.4 %collective-permute-start.6 = (f32[32,512]{1,0:T(8,128)S(1)}, f32[32,512]{1,0:T(8,128)S(1)}, u32[]{:S(2)}, u32[]{:S(2)}) collective-permute-start(f32[32,512]{1,0:T(8,128)S(1)} %apply_first.3.refs_0_), channel_id=1, source_target_pairs={{3,0},{2,1},{1,2},{0,3},{7,4},{6,5},{5,6},{4,7},{11,8},{10,9},{9,1... | collective-permute-start | bytes 196616 | tf_op jit(solution)/shard_map/ppermute | solution.py:643
  17.6 7.9 %collective-permute-start.7 = (f32[32,512]{1,0:T(8,128)S(1)}, f32[32,512]{1,0:T(8,128)S(1)}, u32[]{:S(2)}, u32[]{:S(2)}) collective-permute-start(f32[32,512]{1,0:T(8,128)S(1)} %apply_first.3.refs_0_), channel_id=1, source_target_pairs={{2,0},{3,1},{0,2},{1,3},{6,4},{7,5},{4,6},{5,7},{10,8},{11,9},{8,1... | collective-permute-start | bytes 196616 | tf_op jit(solution)/shard_map/ppermute | solution.py:643
  17.6 7.9 %collective-permute-start.8 = (f32[32,512]{1,0:T(8,128)S(1)}, f32[32,512]{1,0:T(8,128)S(1)}, u32[]{:S(2)}, u32[]{:S(2)}) collective-permute-start(f32[32,512]{1,0:T(8,128)S(1)} %apply_first.3.refs_0_), channel_id=1, source_target_pairs={{1,0},{0,1},{3,2},{2,3},{5,4},{4,5},{7,6},{6,7},{9,8},{8,9},{11,10... | collective-permute-start | bytes 196616 | tf_op jit(solution)/shard_map/ppermute | solution.py:643
  21.0 7.5 %collective-permute-start.3 = (f32[32,512]{1,0:T(8,128)S(1)}, f32[32,512]{1,0:T(8,128)S(1)}, u32[]{:S(2)}, u32[]{:S(2)}) collective-permute-start(f32[32,512]{1,0:T(8,128)S(1)} %apply_first.2.refs_0_), channel_id=1, source_target_pairs={{3,0},{2,1},{1,2},{0,3},{7,4},{6,5},{5,6},{4,7},{11,8},{10,9},{9,1... | collective-permute-start | bytes 196616 | tf_op jit(solution)/shard_map/ppermute | solution.py:643
  23.5 6.0 %collective-permute-start.4 = (f32[32,512]{1,0:T(8,128)S(1)}, f32[32,512]{1,0:T(8,128)S(1)}, u32[]{:S(2)}, u32[]{:S(2)}) collective-permute-start(f32[32,512]{1,0:T(8,128)S(1)} %apply_first.2.refs_0_), channel_id=1, source_target_pairs={{2,0},{3,1},{0,2},{1,3},{6,4},{7,5},{4,6},{5,7},{10,8},{11,9},{8,1... | collective-permute-start | bytes 196616 | tf_op jit(solution)/shard_map/ppermute | solution.py:643
  23.5 6.0 %collective-permute-start.5 = (f32[32,512]{1,0:T(8,128)S(1)}, f32[32,512]{1,0:T(8,128)S(1)}, u32[]{:S(2)}, u32[]{:S(2)}) collective-permute-start(f32[32,512]{1,0:T(8,128)S(1)} %apply_first.2.refs_0_), channel_id=1, source_target_pairs={{1,0},{0,1},{3,2},{2,3},{5,4},{4,5},{7,6},{6,7},{9,8},{8,9},{11,10... | collective-permute-start | bytes 196616 | tf_op jit(solution)/shard_map/ppermute | solution.py:643
  40.6 7.0 %collective-permute-start.10 = (f32[136,128]{1,0:T(8,128)S(1)}, f32[136,128]{1,0:T(8,128)S(1)}, u32[]{:S(2)}, u32[]{:S(2)}) collective-permute-start(f32[136,128]{1,0:T(8,128)S(1)} %cross_gram.1), channel_id=1, source_target_pairs={{3,0},{2,1},{1,2},{0,3},{7,4},{6,5},{5,6},{4,7},{11,8},{10,9},{9,1... | collective-permute-start | bytes 208904 | tf_op jit(solution)/shard_map/ppermute | solution.py:643
  42.6 7.2 %collective-permute-start.11 = (f32[136,128]{1,0:T(8,128)S(1)}, f32[136,128]{1,0:T(8,128)S(1)}, u32[]{:S(2)}, u32[]{:S(2)}) collective-permute-start(f32[136,128]{1,0:T(8,128)S(1)} %cross_gram.1), channel_id=1, source_target_pairs={{2,0},{3,1},{0,2},{1,3},{6,4},{7,5},{4,6},{5,7},{10,8},{11,9},{8,1... | collective-permute-start | bytes 208904 | tf_op jit(solution)/shard_map/ppermute | solution.py:643
  42.6 7.2 %collective-permute-start.9 = (f32[136,128]{1,0:T(8,128)S(1)}, f32[136,128]{1,0:T(8,128)S(1)}, u32[]{:S(2)}, u32[]{:S(2)}) collective-permute-start(f32[136,128]{1,0:T(8,128)S(1)} %cross_gram.1), channel_id=1, source_target_pairs={{1,0},{0,1},{3,2},{2,3},{5,4},{4,5},{7,6},{6,7},{9,8},{8,9},{11,10... | collective-permute-start | bytes 208904 | tf_op jit(solution)/shard_map/ppermute | solution.py:643
  49.9 1.3 %collective-permute-start.12 = (f32[136,128]{1,0:T(8,128)S(1)}, f32[136,128]{1,0:T(8,128)S(1)}, u32[]{:S(2)}, u32[]{:S(2)}) collective-permute-start(f32[136,128]{1,0:T(8,128)S(1)} %add_add_fusion.refs_0_), channel_id=1, source_target_pairs={{4,0},{0,4},{12,8},{8,12},{5,1},{1,5},{13,9},{9,13},{6,2},{2,6},{1... | collective-permute-start | bytes 208904 | tf_op jit(solution)/shard_map/ppermute | solution.py:643
  59.1 6.8 %collective-permute-start.13 = (bf16[2,32,512]{2,1,0:T(8,128)(2,1)S(1)}, bf16[2,32,512]{2,1,0:T(8,128)(2,1)S(1)}, u32[]{:S(2)}, u32[]{:S(2)}) collective-permute-start(bf16[2,32,512]{2,1,0:T(8,128)(2,1)S(1)} %get-tuple-element.12.basis_ref), channel_id=1, source_target_pairs={{3,0},{2,1},{1,2},{0,3},{7,4},{6,5},{5,6},{4,7},{11,8},{10,9},{9,1... | collective-permute-start | bytes 196616 | tf_op jit(solution)/shard_map/ppermute | solution.py:643
  61.1 6.8 %collective-permute-start.14 = (bf16[2,32,512]{2,1,0:T(8,128)(2,1)S(1)}, bf16[2,32,512]{2,1,0:T(8,128)(2,1)S(1)}, u32[]{:S(2)}, u32[]{:S(2)}) collective-permute-start(bf16[2,32,512]{2,1,0:T(8,128)(2,1)S(1)} %get-tuple-element.12.basis_ref), channel_id=1, source_target_pairs={{2,0},{3,1},{0,2},{1,3},{6,4},{7,5},{4,6},{5,7},{10,8},{11,9},{8,1... | collective-permute-start | bytes 196616 | tf_op jit(solution)/shard_map/ppermute | solution.py:643
  61.1 6.8 %collective-permute-start.15 = (bf16[2,32,512]{2,1,0:T(8,128)(2,1)S(1)}, bf16[2,32,512]{2,1,0:T(8,128)(2,1)S(1)}, u32[]{:S(2)}, u32[]{:S(2)}) collective-permute-start(bf16[2,32,512]{2,1,0:T(8,128)(2,1)S(1)} %get-tuple-element.12.basis_ref), channel_id=1, source_target_pairs={{1,0},{0,1},{3,2},{2,3},{5,4},{4,5},{7,6},{6,7},{9,8},{8,9},{11,10... | collective-permute-start | bytes 196616 | tf_op jit(solution)/shard_map/ppermute | solution.py:643
  69.5 5.8 %collective-permute-start.17 = (f32[2,32,32]{2,1,0:T(8,128)S(1)}, f32[2,32,32]{2,1,0:T(8,128)S(1)}, u32[]{:S(2)}, u32[]{:S(2)}) collective-permute-start(f32[2,32,32]{2,1,0:T(8,128)S(1)} %apply_score.1), channel_id=1, source_target_pairs={{3,0},{2,1},{1,2},{0,3},{7,4},{6,5},{5,6},{4,7},{11,8},{10,9},{9,1... | collective-permute-start | bytes 24584 | tf_op jit(solution)/shard_map/ppermute | solution.py:643
  71.5 4.8 %collective-permute-start.18 = (f32[2,32,32]{2,1,0:T(8,128)S(1)}, f32[2,32,32]{2,1,0:T(8,128)S(1)}, u32[]{:S(2)}, u32[]{:S(2)}) collective-permute-start(f32[2,32,32]{2,1,0:T(8,128)S(1)} %apply_score.1), channel_id=1, source_target_pairs={{2,0},{3,1},{0,2},{1,3},{6,4},{7,5},{4,6},{5,7},{10,8},{11,9},{8,1... | collective-permute-start | bytes 24584 | tf_op jit(solution)/shard_map/ppermute | solution.py:643
  71.5 4.8 %collective-permute-start.16 = (f32[2,32,32]{2,1,0:T(8,128)S(1)}, f32[2,32,32]{2,1,0:T(8,128)S(1)}, u32[]{:S(2)}, u32[]{:S(2)}) collective-permute-start(f32[2,32,32]{2,1,0:T(8,128)S(1)} %apply_score.1), channel_id=1, source_target_pairs={{1,0},{0,1},{3,2},{2,3},{5,4},{4,5},{7,6},{6,7},{9,8},{8,9},{11,10... | collective-permute-start | bytes 24584 | tf_op jit(solution)/shard_map/ppermute | solution.py:643
